TPU v7x, 32 devices: a whole 2x2x4 slice. The times are simulated.
32 devices in a mesh: group: 2 (over y), aperture: 8 (over z, x), wave: 2 (over core).
Axes of the slice: x: 2, y: 2, z: 4, core: 2. Of those that a mesh axis runs over, the one named last changes fastest.
Arguments:
- widths: float32 [512, 4096], P(('group', 'aperture')), parts along dimension 0, may hold values from -0.95 to 0.95
- coef_table: float32 [256, 16], replicated, may hold values from -3 to 3
- wave_ids: int32 [8], P(('group', 'wave')), parts along dimension 0, may hold values from 0 to 255
- angle_ids: int32 [8], P(('group', 'wave')), parts along dimension 0, may hold values from 0 to 3
- targets: int32 [8, 2], P(('group', 'wave')), parts along dimension 0, may hold values from 32 to 223
Outputs:
- width_grad: float32 [512, 4096], P(('group', 'aperture'), 'wave'), parts along dimension 0
- efficiency: float32 [8], P(('group', 'wave')), parts along dimension 0
There are 2 independent parts, one for each index of `group`. A program takes and returns all parts, laid end to end along the dimension named above; an argument that names none is the same for every part. Nothing has to cross between parts.
All inputs are finite; a program needn't handle non-finite values.
Results may differ from a plain program's by a relative error of at most 0.0045.
The roundings to bfloat16 on the way count: a program that leaves them out, or rounds other values in their place, can miss the bound.
Values may be sent and summed in bfloat16 or wider, within the bound.
No kernel may reach another device: no remote copies, remote signals or barrier semaphores. Data moves between devices by JAX's collectives and lax.ppermute only.
A program may use at most 64 MiB of HBM per device.

v0:
```python
import math

import jax
import jax.numpy as jnp
from jax import lax
from jax.sharding import PartitionSpec as P

FOCAL = 256
SPOT = 4
SHIFT = 32


def phase_table(positions, frequencies, period):
    turns = jnp.mod(positions[:, None] * frequencies[None, :], period)
    angle = turns.astype(jnp.float32) * (2.0 * math.pi / period)
    return jnp.concatenate([jnp.cos(angle), -jnp.sin(angle)], axis=1).astype(jnp.bfloat16)


def near_field(widths, coef):
    order_count = coef.shape[0] // 2
    before, current = (jnp.ones_like(widths), widths)
    real = coef[0] * before + coef[1] * current
    imag = coef[order_count] * before + coef[order_count + 1] * current
    for order in range(2, order_count):
        before, current = (current, 2.0 * widths * current - before)
        real = real + coef[order] * current
        imag = imag + coef[order_count + order] * current
    return (real, imag)


def near_slope(widths, coef):
    order_count = coef.shape[0] // 2
    before, current = (jnp.zeros_like(widths), jnp.ones_like(widths))
    real = jnp.zeros_like(widths)
    imag = jnp.zeros_like(widths)
    for order in range(1, order_count):
        real = real + order * coef[order] * current
        imag = imag + order * coef[order_count + order] * current
        before, current = (current, 2.0 * widths * current - before)
    return (real, imag)


def spot_map(target, count):
    rows_off = (jnp.arange(count, dtype=jnp.int32) - target[0]).astype(jnp.float32)
    cols_off = (jnp.arange(FOCAL, dtype=jnp.int32) - target[1]).astype(jnp.float32)
    return jnp.exp(-(rows_off[:, None] ** 2 + cols_off[None, :] ** 2) / (2.0 * SPOT * SPOT))


def spread_rows(tables, seed):
    real_tab = tables[:, :, :FOCAL]
    imag_tab = tables[:, :, FOCAL:]
    real_seed = seed[:, 0]
    imag_seed = seed[:, 1]
    first = jnp.einsum("nrj,njk->nrk", real_tab, real_seed, preferred_element_type=jnp.float32)
    first = first + jnp.einsum(
        "nrj,njk->nrk", imag_tab, imag_seed, preferred_element_type=jnp.float32
    )
    second = jnp.einsum("nrj,njk->nrk", real_tab, imag_seed, preferred_element_type=jnp.float32)
    second = second - jnp.einsum(
        "nrj,njk->nrk", imag_tab, real_seed, preferred_element_type=jnp.float32
    )
    return jnp.concatenate([first, second], axis=2)


def focal_adjoint(partials, tables, aims):
    full_spot = jax.vmap(lambda aim: spot_map(aim, FOCAL))(aims)
    factor = FOCAL * FOCAL / jnp.sum(full_spot, axis=(1, 2))
    field = lax.psum(partials, "aperture")
    intensity = field[:, 0] ** 2 + field[:, 1] ** 2
    spot_power = jnp.sum(full_spot * intensity, axis=(1, 2))
    all_power = jnp.sum(intensity, axis=(1, 2))
    all_power = all_power + 1e-06
    ratio = spot_power / all_power
    weight = (
        factor[:, None, None] * 2.0 * (full_spot - ratio[:, None, None]) / all_power[:, None, None]
    )
    seed = (weight[:, None] * field).astype(jnp.bfloat16)
    back = spread_rows(tables, seed)
    return (back.astype(jnp.bfloat16), ratio * factor)


def on_device(widths, coef_table, wave_ids, angle_ids, targets):
    rows_dev, cols = widths.shape
    pairs_dev = wave_ids.shape[0]
    rows = rows_dev * lax.axis_size("aperture")
    row_start = lax.axis_index("aperture") * rows_dev
    picks = (wave_ids[:, None] == jnp.arange(coef_table.shape[0], dtype=jnp.int32)[None, :]).astype(
        jnp.float32
    )
    coefs = jnp.dot(picks, coef_table, precision=lax.Precision.HIGHEST)
    focal_pos = jnp.arange(FOCAL, dtype=jnp.int32) - FOCAL // 2
    row_pos = row_start + jnp.arange(rows_dev, dtype=jnp.int32) - rows // 2
    col_pos = jnp.arange(cols, dtype=jnp.int32) - cols // 2
    row_tables = []
    col_tables = []
    partial_list = []
    for pair in range(pairs_dev):
        wave_freq = 256 + wave_ids[pair]
        row_tab = phase_table(row_pos, focal_pos * wave_freq, 256 * rows)
        col_tab = phase_table(
            col_pos, (focal_pos + SHIFT * angle_ids[pair]) * wave_freq, 256 * cols
        )
        real_near, imag_near = near_field(widths, coefs[pair])
        near = jnp.concatenate([real_near, imag_near], axis=0).astype(jnp.bfloat16)
        section = jnp.dot(near, col_tab, preferred_element_type=jnp.float32)
        section_r = section[:rows_dev, :FOCAL] - section[rows_dev:, FOCAL:]
        section_i = section[:rows_dev, FOCAL:] + section[rows_dev:, :FOCAL]
        section_cat = jnp.concatenate([section_r, section_i], axis=1).astype(jnp.bfloat16)
        mixed = lax.dot_general(
            row_tab, section_cat, (((0,), (0,)), ((), ())), preferred_element_type=jnp.float32
        )
        field_r = mixed[:FOCAL, :FOCAL] - mixed[FOCAL:, FOCAL:]
        field_i = mixed[:FOCAL, FOCAL:] + mixed[FOCAL:, :FOCAL]
        partial_list.append(jnp.stack([field_r, field_i]))
        row_tables.append(row_tab)
        col_tables.append(col_tab)
    tables = jnp.stack(row_tables)
    partials = jnp.stack(partial_list)
    results = [
        focal_adjoint(partials[pair : pair + 1], tables[pair : pair + 1], targets[pair : pair + 1])
        for pair in range(pairs_dev)
    ]
    backs = jnp.concatenate([item[0] for item in results], axis=0)
    scores = jnp.concatenate([item[1] for item in results], axis=0)
    local_grad = jnp.zeros((rows_dev, cols), jnp.float32)
    for pair in range(pairs_dev):
        back = backs[pair]
        left = jnp.concatenate(
            [back, jnp.concatenate([back[:, FOCAL:], -back[:, :FOCAL]], axis=1)], axis=0
        )
        grad_near = lax.dot_general(
            left, col_tables[pair], (((1,), (1,)), ((), ())), preferred_element_type=jnp.float32
        )
        slope_r, slope_i = near_slope(widths, coefs[pair])
        local_grad = local_grad + grad_near[:rows_dev] * slope_r + grad_near[rows_dev:] * slope_i
    summed = lax.psum_scatter(local_grad, "wave", scatter_dimension=1, tiled=True)
    return (summed * math.sqrt(rows * cols), scores)


def solution(mesh):
    in_specs = (
        P(("group", "aperture"), None),
        P(),
        P(("group", "wave")),
        P(("group", "wave")),
        P(("group", "wave"), None),
    )
    out_specs = (P(("group", "aperture"), "wave"), P(("group", "wave")))
    return jax.shard_map(
        on_device, mesh=mesh, in_specs=in_specs, out_specs=out_specs, check_vma=False
    )
```

profile of v0, /device:TPU:0, one launch (start us, length us, event | category | flops | bytes accessed | tf_op | source)
XLA Modules:
  0.0 194.8 jit_solution(12690372881907297040)
XLA Ops:
  7.2 0.0 copy-start
  7.2 0.0 all-reduce.3.cloned.1.call-start
  7.2 1.4 fusion.150
  8.6 0.0 copy-done
  8.6 0.8 fusion.102
  9.4 0.7 fusion.148
  10.2 0.7 fusion.147
  10.9 1.3 fusion.149
  14.8 0.0 copy-start.2
  14.8 35.4 %cosine_convert_fusion.1 = (bf16[4096,256]{1,0:T(8,128)(2,1)S(1)}, bf16[4096,256]{1,0:T(8,128)(2,1)S(1)}, bf16[4096,256]{1,0:T(8,128)(2,1)S(1)}, bf16[4096,256]{1,0:T(8,128)(2,1)S(1)}) fusion(s32[256]{0:T(256)S(1)} %get-tuple-element.76, s32[4096]{0:T(1024)S(1)} %iota_add_fusion, s32[256]{0:T(256)S(1)} %get-tuple-element.78), kind=kLoop, calls=%fused_computation.21 | loop fusion | flops 35651584 | bytes 8407040 | tf_op jit(solution)/shard_map/convert.18
  50.2 0.0 copy-start.3
  50.2 0.0 copy-start.5
  50.2 0.0 copy-start.7
  50.2 0.0 copy-done.2
  50.2 10.5 %add_convert_fusion.3 = (bf16[32,4096]{1,0:T(8,128)(2,1)S(1)}, bf16[32,4096]{1,0:T(8,128)(2,1)S(1)}) fusion(f32[32,4096]{1,0:T(8,128)S(1)} %copy-done.2, f32[]{:T(128)} %bitcast.10, f32[]{:T(128)} %bitcast.9, f32[]{:T(128)} %bitcast.8, f32[]{:T(128)} %bitcast.7, f32[]{:T(128)} %bitcast.6, f32[]{:T(128)} %bitcast.5, f32[]{:T(128)} %bitcast.4, f32[]{:T(128)} %bitcast.3, ...), kind=kLoop, calls=%fused_computation.94 | loop fusion | flops 5636096 | bytes 1048640 | tf_op jit(solution)/shard_map/convert.20
  60.8 10.4 %add_convert_fusion.2 = (bf16[32,4096]{1,0:T(8,128)(2,1)S(1)}, bf16[32,4096]{1,0:T(8,128)(2,1)S(1)}) fusion(f32[32,4096]{1,0:T(8,128)S(1)} %copy-done.2, f32[]{:T(128)} %bitcast.18, f32[]{:T(128)} %bitcast.17, f32[]{:T(128)} %bitcast.16, f32[]{:T(128)} %bitcast.15, f32[]{:T(128)} %bitcast.14, f32[]{:T(128)} %bitcast.13, f32[]{:T(128)} %bitcast.12, ...), kind=kLoop, calls=%fused_computation.93 | loop fusion | flops 5636096 | bytes 1048640 | tf_op jit(solution)/shard_map/convert.21
  71.1 0.9 fusion.7
  72.0 0.0 copy-done.3
  72.0 0.0 copy-done.5
  72.0 0.0 copy-done.7
  72.0 0.8 fusion.9
  72.9 0.3 cosine_convert_fusion.3
  73.3 0.3 fusion.95
  73.6 0.1 fusion.50
  73.6 0.3 fusion.88
  74.0 0.0 copy-start.8
  74.0 0.1 fusion.53
  74.0 0.8 maximum_bitcast_fusion.1
  74.9 0.9 maximum_bitcast_fusion
  75.7 0.0 all-reduce.3.cloned.1.call-update
  75.8 0.2 reduce-scatter.2.cloned.1.call-start
  90.7 0.0 copy-done.8
  90.7 0.6 fusion.146
  91.3 1.3 convert_multiply_fusion.2
  92.6 1.2 convert_multiply_fusion
  93.8 63.1 %all-reduce.3.cloned.1.call-done = (f32[1,2,256,256]{3,2,1,0:T(8,128)}, f32[1,2,256,256]{3,2,1,0:T(8,128)}) async-done(((f32[1,2,256,256]{3,2,1,0:T(8,128)}, f32[1,2,256,256]{3,2,1,0:T(8,128)}), (f32[1,2,256,256]{3,2,1,0:T(8,128)}, f32[1,2,256,256]{3,2,1,0:T(8,128)})) %all-reduce.3.cloned.1.call-update) | async-done | bytes 1048592 | tf_op jit(solution)/shard_map/psum | solution.py:68
  156.9 0.0 copy-start.1
  156.9 1.8 fusion.76
  159.3 1.8 fusion.57
  162.5 0.1 multiply_divide_fusion.1
  162.6 1.1 multiply_convert_fusion.1
  163.7 0.3 fusion.59
  164.0 0.3 fusion.58
  164.3 0.0 copy-done.1
  164.3 0.7 fusion.77
  165.7 0.8 fusion.56
  167.8 0.0 copy-start.6
  167.8 0.1 multiply_divide_fusion
  167.9 0.1 multiply_convert_fusion
  168.0 0.3 fusion.61
  168.3 0.3 fusion.60
  168.6 0.3 fusion.11
  168.9 0.3 fusion.152
  169.3 0.3 fusion.13
  169.6 0.3 fusion.151
  169.9 0.0 copy-done.6
  169.9 3.1 %fusion.8 = f32[64,4096]{1,0:T(8,128)S(1)} fusion(bf16[4096,256]{1,0:T(8,128)(2,1)} %copy-done.7, bf16[4096,256]{1,0:T(8,128)(2,1)S(1)} %copy-done.6, bf16[32,256]{1,0:T(8,128)(2,1)S(1)} %get-tuple-element.74, bf16[32,256]{1,0:T(8,128)(2,1)S(1)} %fusion.11, bf16[32,256]{1,0:T(8,128)(2,1)S(1)} %get-tuple-element.75), kind=kOutput, calls=%fused_computation.24 | convolution fusion | flops 277086208 | bytes 5292032 | tf_op jit(solution)/shard_map/dot_general | solution.py:131
  173.0 0.0 copy-done.4
  173.1 1.4 fusion.6
  174.4 4.3 %fusion.14 = f32[32,4096]{1,0:T(8,128)} fusion(f32[64,4096]{1,0:T(8,128)S(1)} %fusion.6, f32[64,4096]{1,0:T(8,128)S(1)} %fusion.8, f32[32,4096]{1,0:T(8,128)S(1)} %copy-done.2, f32[]{:T(128)S(6)} %mul.918, f32[]{:T(128)S(6)} %mul.915, f32[]{:T(128)S(6)} %mul.912, f32[]{:T(128)S(6)} %mul.909, f32[]{:T(128)S(6)} %mul.906, f32[]{:T(128)S(6)} %mul.903, ...), kind=kLoop, calls=%fused_computation.36 | loop fusion | flops 8650752 | bytes 3145840 | tf_op jit(solution)/shard_map/add | solution.py:135
  178.7 0.0 reduce-scatter.2.cloned.1.call-update
  178.8 0.6 pad_maximum_fusion.6
  179.3 6.9 %reduce-scatter.2.cloned.1.call-done = f32[32,2048]{1,0:T(8,128)} async-done(((f32[32,4096]{1,0:T(8,128)}), f32[32,2048]{1,0:T(8,128)}) %reduce-scatter.2.cloned.1.call-update) | async-done | bytes 262160 | tf_op jit(solution)/shard_map/reduce_scatter | solution.py:136
  186.3 1.7 broadcast_multiply_fusion
  (7 shorter events, 0.0 us)
Async XLA Ops:
  7.2 1.4 copy-start
  7.2 149.7 %all-reduce.3.cloned.1.call-start = ((), (), s32[]{:S(2)}) async-start(), calls=%async_computation.2 | async-start | bytes 2097152 | tf_op jit(solution)/shard_map/psum | solution.py:68
  14.8 35.4 %copy-start.2 = (f32[32,4096]{1,0:T(8,128)S(1)}, f32[32,4096]{1,0:T(8,128)}, u32[]{:S(2)}) copy-start(f32[32,4096]{1,0:T(8,128)} %param.5) | copy-start | bytes 1572868
  50.2 21.8 %copy-start.3 = (bf16[4096,256]{1,0:T(8,128)(2,1)}, bf16[4096,256]{1,0:T(8,128)(2,1)S(1)}, u32[]{:S(2)}) copy-start(bf16[4096,256]{1,0:T(8,128)(2,1)S(1)} %get-tuple-element.25) | copy-start | bytes 6291460
  50.2 21.8 %copy-start.5 = (bf16[4096,256]{1,0:T(8,128)(2,1)}, bf16[4096,256]{1,0:T(8,128)(2,1)S(1)}, u32[]{:S(2)}) copy-start(bf16[4096,256]{1,0:T(8,128)(2,1)S(1)} %get-tuple-element.20) | copy-start | bytes 6291460
  50.2 21.8 %copy-start.7 = (bf16[4096,256]{1,0:T(8,128)(2,1)}, bf16[4096,256]{1,0:T(8,128)(2,1)S(1)}, u32[]{:S(2)}) copy-start(bf16[4096,256]{1,0:T(8,128)(2,1)S(1)} %get-tuple-element.21) | copy-start | bytes 6291460
  74.0 16.7 %copy-start.8 = (s32[2,2]{1,0:T(2,128)S(1)}, s32[2,2]{1,0:T(2,128)}, u32[]{:S(2)}) copy-start(s32[2,2]{1,0:T(2,128)} %param.9) | copy-start | bytes 52
  75.8 110.5 %reduce-scatter.2.cloned.1.call-start = ((), (), s32[]{:S(2)}) async-start(), calls=%async_computation.1 | async-start | bytes 786432 | tf_op jit(solution)/shard_map/reduce_scatter | solution.py:136
  156.9 7.4 %copy-start.1 = (f32[1,2,256,256]{3,2,1,0:T(8,128)S(1)}, f32[1,2,256,256]{3,2,1,0:T(8,128)}, u32[]{:S(2)}) copy-start(f32[1,2,256,256]{3,2,1,0:T(8,128)} %get-tuple-element.6) | copy-start | bytes 1572868
  167.8 2.2 %copy-start.6 = (bf16[4096,256]{1,0:T(8,128)(2,1)S(1)}, bf16[4096,256]{1,0:T(8,128)(2,1)}, u32[]{:S(2)}) copy-start(bf16[4096,256]{1,0:T(8,128)(2,1)} %copy-done.5) | copy-start | bytes 6291460
  169.9 3.1 %copy-start.4 = (bf16[4096,256]{1,0:T(8,128)(2,1)S(1)}, bf16[4096,256]{1,0:T(8,128)(2,1)}, u32[]{:S(2)}) copy-start(bf16[4096,256]{1,0:T(8,128)(2,1)} %copy-done.3) | copy-start | bytes 6291460
Sparse Core Ops, SparseCore 0:
  75.9 80.9 all-reduce.2
  178.9 7.3 reduce-scatter.1
where the time goes:
time: 196 us; the launch traced here: 195 us
  other arithmetic  73.9 us (38%)
  waiting for transfers between devices  70.1 us (36%)
  between operations  35.5 us (18%)
  matrix products  10.2 us (5%)
  local copies, waits for them, and re-layouts  4.75 us (2%)
    psum x1, waiting for transfers between devices, focal_adjoint(): field = lax.psum(partials, 'aperture')  63.1 us
    another operation x6, other arithmetic  56.6 us
    reduce_scatter x1, waiting for transfers between devices, on_device(): lax.psum_scatter(local_grad, 'wave', scatter_dimension=1, tiled=True)  6.91 us
    dot_general x2, matrix products, on_device(): lax.dot_general(left, col_tables[pair], (((1,), (1,)), ((), ())), preferr...  4.49 us
    add x1, other arithmetic, on_device(): local_grad + grad_near[:rows_dev] * slope_r + grad_near[rows_dev:] * slope_i  4.29 us
  transfers between devices with their start and end apart: 2, of which 2 were waited for; matrix products, arithmetic and copies ran while one was open for 2% of the time, Pallas kernels for 0%

commit v1 on v0

v1 whole, which is shorter than its diff:
```python
import functools
import math

import jax
import jax.numpy as jnp
from jax import lax
from jax.experimental import pallas as pl
from jax.experimental.pallas import tpu as pltpu
from jax.sharding import PartitionSpec as P

FOCAL = 256
SPOT = 4
SHIFT = 32
TERMS = 8
BLOCK = 256
GRAIN = 16
VMEM_LIMIT = 24 * 1024 * 1024

COS = (
    1.0, -19.7392088015709, 64.93939395773512, -85.45681453397417, 60.24458621302471,
    -26.425616460281425, 7.8991596631575085, -1.6968741456712442, 0.2437618617467591,
)
SIN = (
    6.2831853071792665, -41.34170224019464, 81.60524925425943, -76.70585885700535,
    42.05867547580699, -15.094428387947755, 3.818490079304055, -0.7122771247541972,
    0.09149844789363434,
)


def horner(terms, u):
    value = terms[-1] * u + terms[-2]
    for term in terms[-3::-1]:
        value = value * u + term
    return value


def unit_waves(counts, period):
    half = period // 2
    centred = ((counts + half) & (period - 1)) - half
    t = centred.astype(jnp.float32) * (1.0 / period)
    u = t * t
    return horner(COS, u), -(t * horner(SIN, u))


def iota(shape, axis):
    return lax.broadcasted_iota(jnp.int32, shape, axis)


def pick_coef(table_ref, wave):
    table = table_ref[...]
    chosen = jnp.where(iota(table.shape, 1) == wave, table, 0.0)
    return jnp.sum(chosen, axis=1, keepdims=True)


def column_freq(wave, angle):
    return (iota((1, FOCAL), 1) - FOCAL // 2 + SHIFT * angle) * (BLOCK + wave)


def fill_base(freq, shift, period, base_ref, centre_ref):
    low_r, low_i = unit_waves(iota((GRAIN, 1), 0) * freq, period)
    steps = BLOCK // GRAIN
    high_r, high_i = unit_waves((iota((steps, 1), 0) * GRAIN - BLOCK // 2 + shift) * freq, period)
    for step in range(steps):
        one_r, one_i = high_r[step : step + 1], high_i[step : step + 1]
        rows = slice(step * GRAIN, (step + 1) * GRAIN)
        base_ref[0, rows, :] = one_r * low_r - one_i * low_i
        base_ref[1, rows, :] = one_r * low_i + one_i * low_r
    count = centre_ref.shape[1]
    cent_r, cent_i = unit_waves((iota((count, 1), 0) * BLOCK + BLOCK // 2) * freq, period)
    centre_ref[0] = cent_r
    centre_ref[1] = cent_i


def block_pair(base_ref, centre_ref, index):
    cent_r = centre_ref[0, pl.ds(index, 1), :]
    cent_i = centre_ref[1, pl.ds(index, 1), :]
    base_r, base_i = base_ref[0], base_ref[1]
    rr, ii = base_r * cent_r, base_i * cent_i
    ri, ir = base_r * cent_i, base_i * cent_r
    before = ((rr + ii).astype(jnp.bfloat16), (ir - ri).astype(jnp.bfloat16))
    after = ((rr - ii).astype(jnp.bfloat16), (ir + ri).astype(jnp.bfloat16))
    return before, after


def near_fields(s, coefs):
    outs = [[c[0:1] + c[1:2] * s, c[TERMS : TERMS + 1] + c[TERMS + 1 : TERMS + 2] * s] for c in coefs]
    twice = s + s
    before, current = jnp.ones_like(s), s
    for order in range(2, TERMS):
        before, current = current, twice * current - before
        for out, c in zip(outs, coefs):
            out[0] = out[0] + c[order : order + 1] * current
            out[1] = out[1] + c[TERMS + order : TERMS + order + 1] * current
    return outs


def near_slopes(s, coefs):
    outs = [[jnp.broadcast_to(c[1:2], s.shape), jnp.broadcast_to(c[TERMS + 1 : TERMS + 2], s.shape)] for c in coefs]
    twice = s + s
    before, current = jnp.ones_like(s), twice
    for order in range(2, TERMS):
        for out, c in zip(outs, coefs):
            out[0] = out[0] + c[order : order + 1] * current
            out[1] = out[1] + c[TERMS + order : TERMS + order + 1] * current
        before, current = current, twice * current - before
    return outs


def forward_kernel(wave_ref, angle_ref, coef_ref, width_ref, out_ref, base_ref, centre_ref, acc_ref):
    rows_dev, cols = width_ref.shape
    pairs = wave_ref.shape[0]
    period = 256 * cols
    peers, _, lanes = out_ref.shape
    width = lanes // (2 * pairs)
    coefs = [pick_coef(coef_ref, wave_ref[pair]) for pair in range(pairs)]
    for pair in range(pairs):
        freq = column_freq(wave_ref[pair], angle_ref[pair])
        fill_base(freq, 0, period, base_ref.at[pair], centre_ref.at[pair])
    acc_ref[...] = jnp.zeros_like(acc_ref)

    def step(index, carry):
        left = pl.multiple_of(cols // 2 - (index + 1) * BLOCK, BLOCK)
        right = pl.multiple_of(cols // 2 + index * BLOCK, BLOCK)
        nears = []
        for start in (left, right):
            outs = near_fields(width_ref[:, pl.ds(start, BLOCK)], coefs)
            nears.append([jnp.concatenate(out, axis=0).astype(jnp.bfloat16) for out in outs])
        for pair in range(pairs):
            before, after = block_pair(base_ref.at[pair], centre_ref.at[pair], index)
            near = jnp.concatenate([nears[0][pair], nears[1][pair]], axis=1)
            for part in range(2):
                table = jnp.concatenate([before[part], after[part]], axis=0)
                acc_ref[pair, part] += jnp.dot(near, table, preferred_element_type=jnp.float32)
        return carry

    lax.fori_loop(0, cols // (2 * BLOCK), step, 0)
    sections = []
    for pair in range(pairs):
        sections.append(acc_ref[pair, 0, :rows_dev] - acc_ref[pair, 1, rows_dev:])
        sections.append(acc_ref[pair, 1, :rows_dev] + acc_ref[pair, 0, rows_dev:])
    for peer in range(peers):
        part = [section[:, peer * width : (peer + 1) * width] for section in sections]
        out_ref[peer] = jnp.concatenate(part, axis=1).astype(jnp.bfloat16)


def row_kernel(wave_ref, flat_ref, tall_ref):
    pairs, rows, _ = flat_ref.shape
    period = 256 * rows
    size = min(rows, FOCAL)
    for pair in range(pairs):
        freq = BLOCK + wave_ref[pair]

        def step(index, carry):
            start = pl.multiple_of(index * size, size)
            first = start - rows // 2
            focal = (iota((1, FOCAL), 1) - FOCAL // 2) * freq
            real, imag = unit_waves((iota((size, 1), 0) + first) * focal, period)
            flat_ref[pair, pl.ds(start, size), :FOCAL] = real.astype(jnp.bfloat16)
            flat_ref[pair, pl.ds(start, size), FOCAL:] = imag.astype(jnp.bfloat16)
            if rows != FOCAL:
                focal = (iota((FOCAL, 1), 0) - FOCAL // 2) * freq
                real, imag = unit_waves((iota((1, size), 1) + first) * focal, period)
            tall_ref[pair, :FOCAL, pl.ds(start, size)] = real.astype(jnp.bfloat16)
            tall_ref[pair, FOCAL:, pl.ds(start, size)] = imag.astype(jnp.bfloat16)
            return carry

        if rows == size:
            step(0, 0)
        else:
            lax.fori_loop(0, rows // size, step, 0)


def lane_facts(lanes, pairs):
    width = lanes // (2 * pairs)
    lane = iota((1, lanes), 1)
    second = lane >= 2 * width
    imag = (lane % (2 * width)) >= width
    return width, lane, second, imag


def swap_parts(value, width, imag):
    lanes = value.shape[1]
    ahead = pltpu.roll(value, lanes - width, 1)
    behind = pltpu.roll(value, width, 1)
    return jnp.where(imag, behind, -ahead)


def spot_lanes(aim_ref, first_col, lanes, pairs):
    width, lane, second, _ = lane_facts(lanes, pairs)
    col = first_col + lane % width
    aim_row = jnp.where(second, aim_ref[1, 0], aim_ref[0, 0])
    aim_col = jnp.where(second, aim_ref[1, 1], aim_ref[0, 1])
    rows_off = (iota((FOCAL, lanes), 0) - aim_row).astype(jnp.float32)
    cols_off = (col - aim_col).astype(jnp.float32)
    return jnp.exp(-(rows_off * rows_off + cols_off * cols_off) / (2.0 * SPOT * SPOT))


def field_kernel(aim_ref, sect_ref, tall_ref, field_ref, power_ref):
    peers, rows_dev, lanes = sect_ref.shape
    pairs = tall_ref.shape[0]
    width, _, second, imag = lane_facts(lanes, pairs)
    sect = sect_ref[...].reshape(peers * rows_dev, lanes)
    mixed = [
        jnp.dot(tall_ref[pair], sect, preferred_element_type=jnp.float32) for pair in range(pairs)
    ]
    mixed = jnp.where(second, mixed[1], mixed[0])
    field = mixed[:FOCAL] + swap_parts(mixed[FOCAL:], width, imag)
    spot = spot_lanes(aim_ref, lax.axis_index("aperture") * width, lanes, pairs)
    power = field * field
    spot_power = jnp.sum(spot * power, axis=0, keepdims=True)
    all_power = jnp.sum(power, axis=0, keepdims=True)
    both = jnp.concatenate([spot_power, all_power, jnp.zeros((6, lanes), jnp.float32)], axis=0)
    field_ref[...] = field
    power_ref[...] = jnp.broadcast_to(both[None], power_ref.shape)


def seed_kernel(aim_ref, power_ref, field_ref, flat_ref, back_ref, score_ref):
    lanes = field_ref.shape[1]
    pairs, rows, _ = flat_ref.shape
    peers, copies, rows_dev, _ = back_ref.shape
    width, _, second, imag = lane_facts(lanes, pairs)
    total = jnp.sum(power_ref[...], axis=0)
    ratios, scales = [], []
    for pair in range(pairs):
        mine = jnp.where(second == (pair == 1), total, 0.0)
        sums = jnp.sum(mine, axis=1, keepdims=True)
        all_power = sums[1:2] + 1e-06
        ratio = sums[0:1] / all_power
        place = iota((1, FOCAL), 1)
        spans = []
        for axis in range(2):
            off = (place - aim_ref[pair, axis]).astype(jnp.float32)
            spans.append(jnp.sum(jnp.exp(-(off * off) / (2.0 * SPOT * SPOT)), axis=1, keepdims=True))
        factor = FOCAL * FOCAL / (spans[0] * spans[1])
        ratios.append(ratio)
        scales.append(factor * 2.0 / all_power)
        score_ref[pair] = jnp.sum(ratio * factor)
    spot = spot_lanes(aim_ref, lax.axis_index("aperture") * width, lanes, pairs)
    ratio = jnp.where(second, ratios[1], ratios[0])
    scale = jnp.where(second, scales[1], scales[0])
    seed = (scale * (spot - ratio)) * field_ref[...]
    turned = -swap_parts(seed, width, imag)
    stack = jnp.concatenate([seed, turned], axis=0).astype(jnp.bfloat16)
    backs = [
        jnp.dot(flat_ref[pair], stack, preferred_element_type=jnp.float32) for pair in range(pairs)
    ]
    back = jnp.where(second, backs[1], backs[0]).astype(jnp.bfloat16)
    back = back.reshape(peers, rows_dev, lanes)
    for copy in range(copies):
        back_ref[:, copy] = back


def table_kernel(scale, wave_ref, angle_ref, far_ref, coef_ref, width_ref, table_ref, slope_ref, base_ref, centre_ref):
    rows_dev, cols = width_ref.shape
    near_pairs = wave_ref.shape[0]
    pairs, own_cols, _ = table_ref.shape
    period = 256 * cols
    first = lax.axis_index("wave") * own_cols
    middle = own_cols // 2
    coefs = []
    for pair in range(pairs):
        if pair < near_pairs:
            wave, angle = wave_ref[pair], angle_ref[pair]
        else:
            wave, angle = far_ref[0, pair - near_pairs], far_ref[1, pair - near_pairs]
        coef = pick_coef(coef_ref, wave)
        order = (iota(coef.shape, 0) % TERMS).astype(jnp.float32) * scale
        coefs.append(coef * order)
        shift = first + middle - cols // 2
        fill_base(column_freq(wave, angle), shift, period, base_ref.at[pair], centre_ref.at[pair])

    def step(index, carry):
        left = pl.multiple_of(middle - (index + 1) * BLOCK, BLOCK)
        right = pl.multiple_of(middle + index * BLOCK, BLOCK)
        for pair in range(pairs):
            tables = block_pair(base_ref.at[pair], centre_ref.at[pair], index)
            for start, table in zip((left, right), tables):
                table_ref[pair, pl.ds(start, BLOCK), :FOCAL] = table[0]
                table_ref[pair, pl.ds(start, BLOCK), FOCAL:] = table[1]
        for start in (left, right):
            whole = pl.multiple_of(first + start, BLOCK)
            slopes = near_slopes(width_ref[:, pl.ds(whole, BLOCK)], coefs)
            for pair in range(pairs):
                slope_ref[pair, 0, :, pl.ds(start, BLOCK)] = slopes[pair][0]
                slope_ref[pair, 1, :, pl.ds(start, BLOCK)] = slopes[pair][1]
        return carry

    lax.fori_loop(0, own_cols // (2 * BLOCK), step, 0)


def grad_kernel(peers, back_ref, table_ref, slope_ref, out_ref, left_ref):
    rows_dev, own_cols = out_ref.shape
    pairs = table_ref.shape[0]
    copies = back_ref.shape[0] // peers
    pairs_dev = pairs // copies
    lanes = back_ref.shape[2]
    width = lanes // (2 * pairs_dev)
    me = lax.axis_index("wave")
    for pair in range(pairs):
        wave = lax.rem(me + pair // pairs_dev, copies)
        lane = (pair % pairs_dev) * 2 * width
        parts = [back_ref[peer * copies + wave] for peer in range(peers)]
        real = jnp.concatenate([part[:, lane : lane + width] for part in parts], axis=1)
        imag = jnp.concatenate([part[:, lane + width : lane + 2 * width] for part in parts], axis=1)
        left_ref[pair, :rows_dev, :FOCAL] = real
        left_ref[pair, :rows_dev, FOCAL:] = imag
        left_ref[pair, rows_dev:, :FOCAL] = imag
        left_ref[pair, rows_dev:, FOCAL:] = -real
    size = 2 * BLOCK

    def step(index, carry):
        start = pl.multiple_of(index * size, size)
        total = jnp.zeros((rows_dev, size), jnp.float32)
        for pair in range(pairs):
            grad = lax.dot_general(
                left_ref[pair],
                table_ref[pair, pl.ds(start, size), :],
                (((1,), (1,)), ((), ())),
                preferred_element_type=jnp.float32,
            )
            total += grad[:rows_dev] * slope_ref[pair, 0, :, pl.ds(start, size)]
            total += grad[rows_dev:] * slope_ref[pair, 1, :, pl.ds(start, size)]
        out_ref[:, pl.ds(start, size)] = total
        return carry

    lax.fori_loop(0, own_cols // size, step, 0)


VMEM = pl.BlockSpec(memory_space=pltpu.VMEM)
SMEM = pl.BlockSpec(memory_space=pltpu.SMEM)


def call(kernel, name, outs, in_specs, out_specs, scratch, flops, moved):
    return pl.pallas_call(
        kernel,
        name=name,
        out_shape=outs,
        in_specs=in_specs,
        out_specs=out_specs,
        scratch_shapes=scratch,
        cost_estimate=pl.CostEstimate(flops=flops, bytes_accessed=moved, transcendentals=0),
        compiler_params=pltpu.CompilerParams(vmem_limit_bytes=VMEM_LIMIT),
    )


def on_device(widths, coef_table, wave_ids, angle_ids, targets):
    rows_dev, cols = widths.shape
    pairs_dev = wave_ids.shape[0]
    peers = lax.axis_size("aperture")
    copies = lax.axis_size("wave")
    rows = rows_dev * peers
    pairs = pairs_dev * copies
    lanes = 2 * pairs_dev * FOCAL // peers
    own_cols = cols // copies
    f32, bf16 = jnp.float32, jnp.bfloat16
    coefs = coef_table.T
    ring = [(index, (index + 1) % copies) for index in range(copies)]
    far_ids = lax.ppermute(jnp.stack([wave_ids, angle_ids]), "wave", ring)

    sections = call(
        forward_kernel, "forward", jax.ShapeDtypeStruct((peers, rows_dev, lanes), bf16),
        [SMEM, SMEM, VMEM, VMEM], VMEM,
        [
            pltpu.VMEM((pairs_dev, 2, BLOCK, FOCAL), f32),
            pltpu.VMEM((pairs_dev, 2, cols // (2 * BLOCK), FOCAL), f32),
            pltpu.VMEM((pairs_dev, 2, 2 * rows_dev, FOCAL), f32),
        ],
        10**9, 10**7,
    )(wave_ids, angle_ids, coefs, widths)
    sections = lax.all_to_all(sections, "aperture", 0, 0, tiled=True)

    flat, tall = call(
        row_kernel, "row_tables",
        (pltpu.VMEM((pairs_dev, rows, 2 * FOCAL), bf16), pltpu.VMEM((pairs_dev, 2 * FOCAL, rows), bf16)),
        [SMEM], (VMEM, VMEM), [], 10**8, 10**6,
    )(wave_ids)
    tables, slopes = call(
        functools.partial(table_kernel, math.sqrt(rows * cols)), "column_tables",
        (pltpu.VMEM((pairs, own_cols, 2 * FOCAL), bf16), pltpu.VMEM((pairs, 2, rows_dev, own_cols), f32)),
        [SMEM, SMEM, SMEM, VMEM, VMEM], (VMEM, VMEM),
        [
            pltpu.VMEM((pairs, 2, BLOCK, FOCAL), f32),
            pltpu.VMEM((pairs, 2, own_cols // (2 * BLOCK), FOCAL), f32),
        ],
        10**9, 10**7,
    )(wave_ids, angle_ids, far_ids, coefs, widths)

    field, power = call(
        field_kernel, "field",
        (pltpu.VMEM((FOCAL, lanes), f32), jax.ShapeDtypeStruct((peers, 8, lanes), f32)),
        [SMEM, VMEM, VMEM], (VMEM, VMEM), [], 10**8, 10**6,
    )(targets, sections, tall)
    power = lax.all_to_all(power, "aperture", 0, 0, tiled=True)
    backs, scores = call(
        seed_kernel, "seed",
        (jax.ShapeDtypeStruct((peers, copies, rows_dev, lanes), bf16), jax.ShapeDtypeStruct((pairs_dev,), f32)),
        [SMEM, VMEM, VMEM, VMEM], (VMEM, SMEM), [], 10**8, 10**6,
    )(targets, power, field, flat)
    backs = backs.reshape(peers * copies, rows_dev, lanes)
    backs = lax.all_to_all(backs, ("aperture", "wave"), 0, 0, tiled=True)
    grad = call(
        functools.partial(grad_kernel, peers), "gradient",
        jax.ShapeDtypeStruct((rows_dev, own_cols), f32),
        [VMEM, VMEM, VMEM], VMEM,
        [pltpu.VMEM((pairs, 2 * rows_dev, 2 * FOCAL), bf16)],
        10**9, 10**7,
    )(backs, tables, slopes)
    return grad, scores


def solution(mesh):
    in_specs = (
        P(("group", "aperture"), None),
        P(),
        P(("group", "wave")),
        P(("group", "wave")),
        P(("group", "wave"), None),
    )
    out_specs = (P(("group", "aperture"), "wave"), P(("group", "wave")))
    return jax.shard_map(
        on_device, mesh=mesh, in_specs=in_specs, out_specs=out_specs, check_vma=False
    )
```

time: 196 us -> 59.5 us (0.30)
  other arithmetic: 73.9 us -> 0.68 us
  waiting for transfers between devices: 70.1 us -> 5.8 us
  between operations: 35.5 us -> 0.69 us
  Pallas kernels: 0 us -> 17.5 us
  starting transfers between devices: 0.26 us -> 11.1 us
  matrix products: 10.2 us -> 0 us
  local copies, waits for them, and re-layouts: 4.75 us -> 14.1 us
  blocking collectives: 0 us -> 9.06 us
    psum x1 -> x0, waiting for transfers between devices: 63.1 us -> none  [focal_adjoint(): field = lax.psum(partials, 'aperture')]
    another operation x10 -> x1, other arithmetic: 58.5 us -> 0.68 us  [on_device(): far_ids = lax.ppermute(jnp.stack([wave_ids, angle_ids]), 'wave', ring)]
    pallas_call x0 -> x6, Pallas kernels: none -> 17.5 us  [the longest x1 5.72 us: on_device(): call(forward_kernel, 'forward', jax.ShapeDtypeStruct((peers, rows_dev, la...]
    unnamed x18 -> x24, local copies, waits for them, and re-layouts: 0.05 us -> 14.1 us
    all_to_all x0 -> x2, starting transfers between devices: none -> 10.8 us  [the longest x1 7.25 us: on_device(): sections = lax.all_to_all(sections, 'aperture', 0, 0, tiled=True)]
    dot_general x15 -> x0, matrix products: 10.2 us -> none  [the longest x2 4.49 us: on_device(): lax.dot_general(left, col_tables[pair], (((1,), (1,)), ((), ())), preferr...]
    all_to_all x0 -> x1, blocking collectives: none -> 9.06 us  [on_device(): power = lax.all_to_all(power, 'aperture', 0, 0, tiled=True)]
    reduce_scatter x1 -> x0, waiting for transfers between devices: 6.91 us -> none  [on_device(): lax.psum_scatter(local_grad, 'wave', scatter_dimension=1, tiled=True)]
  transfers between devices with their start and end apart: 2 -> 3, of which waited for: 2 -> 2; matrix products, arithmetic and copies ran while one was open for 2% -> 1% of each run, Pallas kernels for 0% -> 9%
where the time goes in v1:
time: 59.5 us; the launch traced here: 58.9 us
  Pallas kernels  17.5 us (29%)
  local copies, waits for them, and re-layouts  14.1 us (24%)
  starting transfers between devices  11.1 us (19%)
  blocking collectives  9.06 us (15%)
  waiting for transfers between devices  5.8 us (10%)
  between operations  0.69 us (1%)
  other arithmetic  0.68 us (1%)
    unnamed x24, local copies, waits for them, and re-layouts  14.1 us
    all_to_all x1, blocking collectives, on_device(): power = lax.all_to_all(power, 'aperture', 0, 0, tiled=True)  9.06 us
    all_to_all x1, starting transfers between devices, on_device(): sections = lax.all_to_all(sections, 'aperture', 0, 0, tiled=True)  7.25 us
    pallas_call x1, Pallas kernels, on_device(): call(forward_kernel, 'forward', jax.ShapeDtypeStruct((peers, rows_dev, la...  5.72 us
    all_to_all x1, waiting for transfers between devices, on_device(): sections = lax.all_to_all(sections, 'aperture', 0, 0, tiled=True)  4.94 us
    pallas_call x1, Pallas kernels, on_device(): call(functools.partial(grad_kernel, peers), 'gradient', jax.ShapeDtypeStr...  3.9 us
    pallas_call x1, Pallas kernels, on_device(): call(functools.partial(table_kernel, math.sqrt(rows * cols)), 'column_tab...  3.88 us
    all_to_all x1, starting transfers between devices, on_device(): backs = lax.all_to_all(backs, ('aperture', 'wave'), 0, 0, tiled=True)  3.52 us
  transfers between devices with their start and end apart: 3, of which 2 were waited for; matrix products, arithmetic and copies ran while one was open for 1% of the time, Pallas kernels for 9%

profile of v1, /device:TPU:0, one launch (start us, length us, event | category | flops | bytes accessed | tf_op | source)
XLA Modules:
  0.0 58.9 jit_solution(17228474986970684729)
XLA Ops:
  0.6 0.0 copy-start.3
  0.6 0.6 %copy-done.3 = s32[2]{0:T(128)S(1)} copy-done((s32[2]{0:T(128)S(1)}, s32[2]{0:T(128)}, u32[]{:S(2)}) %copy-start.3) | copy-done | bytes 32
  1.3 0.0 copy-start.6
  1.3 0.7 %copy-done.6 = s32[2]{0:T(128)S(1)} copy-done((s32[2]{0:T(128)S(1)}, s32[2]{0:T(128)}, u32[]{:S(2)}) %copy-start.6) | copy-done | bytes 32
  1.9 0.0 copy-start.8
  1.9 1.0 %copy-done.8 = f32[32,4096]{1,0:T(8,128)S(1)} copy-done((f32[32,4096]{1,0:T(8,128)S(1)}, f32[32,4096]{1,0:T(8,128)}, u32[]{:S(2)}) %copy-start.8) | copy-done | bytes 524312
  3.0 0.0 copy-start.10
  3.0 0.7 %copy-done.10 = f32[256,16]{0,1:T(8,128)S(1)} copy-done((f32[256,16]{0,1:T(8,128)S(1)}, f32[256,16]{0,1:T(8,128)}, u32[]{:S(2)}) %copy-start.10) | copy-done | bytes 16408
  3.7 5.7 %forward.1 = bf16[8,32,128]{2,1,0:T(8,128)(2,1)} custom-call(s32[2]{0:T(128)S(1)} %copy-done.3, s32[2]{0:T(128)S(1)} %copy-done.6, f32[16,256]{1,0:T(8,128)S(1)} %bitcast.6, f32[32,4096]{1,0:T(8,128)S(1)} %copy-done.8), custom_call_target="tpu_custom_call" | custom-call | flops 1000000000 | bytes 10000000 | tf_op jit(solution)/shard_map/forward/pallas_call | solution.py:360
  9.4 7.3 %all-to-all-start = ((bf16[8,32,128]{2,1,0:T(8,128)(2,1)}), bf16[8,32,128]{2,1,0:T(8,128)(2,1)S(1)}, u32[]{:S(2)}, u32[]{:S(2)}) async-start(bf16[8,32,128]{2,1,0:T(8,128)(2,1)} %forward.1), calls=%async_computation | async-start | bytes 131072 | tf_op jit(solution)/shard_map/all_to_all | solution.py:370
  16.7 0.0 copy-start.4
  16.7 0.7 %copy-done.4 = s32[2]{0:T(128)S(1)} copy-done((s32[2]{0:T(128)S(1)}, s32[2]{0:T(128)}, u32[]{:S(2)}) %copy-start.4) | copy-done | bytes 32
  17.3 1.3 %row_tables.1 = (bf16[2,256,512]{2,1,0:T(8,128)(2,1)S(1)}, bf16[2,512,256]{2,1,0:T(8,128)(2,1)S(1)}) custom-call(s32[2]{0:T(128)S(1)} %copy-done.4), custom_call_target="tpu_custom_call" | custom-call | flops 100000000 | bytes 1000000 | tf_op jit(solution)/shard_map/row_tables/pallas_call | solution.py:372
  18.6 4.9 %all-to-all-done.sect_ref = bf16[8,32,128]{2,1,0:T(8,128)(2,1)S(1)} async-done(((bf16[8,32,128]{2,1,0:T(8,128)(2,1)}), bf16[8,32,128]{2,1,0:T(8,128)(2,1)S(1)}, u32[]{:S(2)}, u32[]{:S(2)}) %all-to-all-start) | async-done | bytes 65568 | tf_op jit(solution)/shard_map/all_to_all | solution.py:370
  23.6 0.0 copy-start.2
  23.6 0.7 %copy-done.2 = s32[2,2]{1,0:T(2,128)S(1)} copy-done((s32[2,2]{1,0:T(2,128)S(1)}, s32[2,2]{1,0:T(2,128)}, u32[]{:S(2)}) %copy-start.2) | copy-done | bytes 40
  24.3 0.9 %field.1 = (f32[256,128]{1,0:T(8,128)S(1)}, f32[8,8,128]{2,1,0:T(8,128)S(1)}) custom-call(s32[2,2]{1,0:T(2,128)S(1)} %copy-done.2, bf16[8,32,128]{2,1,0:T(8,128)(2,1)S(1)} %all-to-all-done.sect_ref, bf16[2,512,256]{2,1,0:T(8,128)(2,1)S(1)} %get-tuple-element.10.tall_ref), custom_call_target="tpu_custom_call" | custom-call | flops 100000000 | bytes 1000000 | tf_op jit(solution)/shard_map/field/pallas_call | solution.py:388
  25.2 9.1 %all_to_all.15.power_ref = f32[8,8,128]{2,1,0:T(8,128)S(1)} all-to-all(f32[8,8,128]{2,1,0:T(8,128)S(1)} %get-tuple-element.11), channel_id=1, replica_groups=mesh['group'=2,'aperture'=8,'wave'=2] {'aperture'}, dimensions={0} | all-to-all | bytes 65536 | tf_op jit(solution)/shard_map/all_to_all | solution.py:393
  34.3 1.8 %seed.1 = (bf16[8,2,32,128]{3,2,1,0:T(8,128)(2,1)}, f32[2]{0:T(128)}) custom-call(s32[2,2]{1,0:T(2,128)S(1)} %copy-done.2, f32[8,8,128]{2,1,0:T(8,128)S(1)} %all_to_all.15.power_ref, f32[256,128]{1,0:T(8,128)S(1)} %get-tuple-element.12.field_ref, bf16[2,256,512]{2,1,0:T(8,128)(2,1)S(1)} %get-tuple-element.13.flat_ref), custom_call_target="tpu_custom_call" | custom-call | flops 100000000 | bytes 1000000 | tf_op jit(solution)/shard_map/seed/pallas_call | solution.py:394
  36.1 3.5 %all-to-all-start.2 = ((bf16[16,32,128]{2,1,0:T(8,128)(2,1)}), bf16[16,32,128]{2,1,0:T(8,128)(2,1)S(1)}, u32[]{:S(2)}, u32[]{:S(2)}) async-start(bf16[16,32,128]{2,1,0:T(8,128)(2,1)} %bitcast.1), calls=%async_computation.2 | async-start | bytes 262144 | tf_op jit(solution)/shard_map/all_to_all | solution.py:400
  39.6 0.7 %pad_add_fusion = s32[2,2]{1,0:T(2,128)S(1)} fusion(s32[1,2]{1,0:T(1,128)} %bitcast.5, s32[1,2]{1,0:T(1,128)} %bitcast.4), kind=kLoop, calls=%fused_computation | loop fusion | flops 4 | bytes 32 | tf_op jit(solution)/shard_map/stack | solution.py:358
  40.3 0.3 collective-permute-start
  40.6 0.9 %collective-permute-done.far_ref = s32[2,2]{1,0:T(2,128)S(1)} collective-permute-done((s32[2,2]{1,0:T(2,128)S(1)}, s32[2,2]{1,0:T(2,128)S(1)}, u32[]{:S(2)}, u32[]{:S(2)}) %collective-permute-start) | collective-permute-done | bytes 48 | tf_op jit(solution)/shard_map/ppermute | solution.py:358
  41.4 0.0 copy-start.5
  41.4 0.7 %copy-done.5 = s32[2]{0:T(128)S(1)} copy-done((s32[2]{0:T(128)S(1)}, s32[2]{0:T(128)}, u32[]{:S(2)}) %copy-start.5) | copy-done | bytes 32
  42.1 0.0 copy-start.7
  42.1 0.7 %copy-done.7 = s32[2]{0:T(128)S(1)} copy-done((s32[2]{0:T(128)S(1)}, s32[2]{0:T(128)}, u32[]{:S(2)}) %copy-start.7) | copy-done | bytes 32
  42.7 0.0 copy-start.9
  42.7 1.0 %copy-done.9 = f32[32,4096]{1,0:T(8,128)S(1)} copy-done((f32[32,4096]{1,0:T(8,128)S(1)}, f32[32,4096]{1,0:T(8,128)}, u32[]{:S(2)}) %copy-start.9) | copy-done | bytes 524312
  43.8 0.0 copy-start.11
  43.8 0.7 %copy-done.11 = f32[256,16]{0,1:T(8,128)S(1)} copy-done((f32[256,16]{0,1:T(8,128)S(1)}, f32[256,16]{0,1:T(8,128)}, u32[]{:S(2)}) %copy-start.11) | copy-done | bytes 16408
  44.5 3.9 %column_tables.1 = (bf16[4,2048,512]{2,1,0:T(8,128)(2,1)S(1)}, f32[4,2,32,2048]{3,2,1,0:T(8,128)S(1)}) custom-call(s32[2]{0:T(128)S(1)} %copy-done.5, s32[2]{0:T(128)S(1)} %copy-done.7, s32[2,2]{1,0:T(2,128)S(1)} %collective-permute-done.far_ref, f32[16,256]{1,0:T(8,128)S(1)} %bitcast.7, f32[32,4096]{1,0:T(8,128)S(1)} %copy-done.9), custom_call_target="tpu_custom_call" | custom-call | flops 1000000000 | bytes 10000000 | tf_op jit(solution)/shard_map/column_tables/pallas_call | solution.py:377
  48.4 0.0 copy-start
  48.4 3.2 %copy-done = bf16[4,2048,512]{2,1,0:T(8,128)(2,1)} copy-done((bf16[4,2048,512]{2,1,0:T(8,128)(2,1)}, bf16[4,2048,512]{2,1,0:T(8,128)(2,1)S(1)}, u32[]{:S(2)}) %copy-start) | copy-done | bytes 8388632
  51.6 0.0 all-to-all-done.2.back_ref
  51.6 0.0 copy-start.1
  51.6 3.4 %copy-done.1 = bf16[4,2048,512]{2,1,0:T(8,128)(2,1)S(1)} copy-done((bf16[4,2048,512]{2,1,0:T(8,128)(2,1)S(1)}, bf16[4,2048,512]{2,1,0:T(8,128)(2,1)}, u32[]{:S(2)}) %copy-start.1) | copy-done | bytes 8388632
  55.0 3.9 %gradient.1 = f32[32,2048]{1,0:T(8,128)} custom-call(bf16[16,32,128]{2,1,0:T(8,128)(2,1)S(1)} %all-to-all-done.2.back_ref, bf16[4,2048,512]{2,1,0:T(8,128)(2,1)S(1)} %copy-done.1, f32[4,2,32,2048]{3,2,1,0:T(8,128)S(1)} %get-tuple-element.16.slope_ref), custom_call_target="tpu_custom_call" | custom-call | flops 1000000000 | bytes 10000000 | tf_op jit(solution)/shard_map/gradient/pallas_call | solution.py:401
Async XLA Ops:
  0.6 0.7 %copy-start.3 = (s32[2]{0:T(128)S(1)}, s32[2]{0:T(128)}, u32[]{:S(2)}) copy-start(s32[2]{0:T(128)} %wave_ref.5) | copy-start | bytes 28
  1.3 0.7 %copy-start.6 = (s32[2]{0:T(128)S(1)}, s32[2]{0:T(128)}, u32[]{:S(2)}) copy-start(s32[2]{0:T(128)} %angle_ref.3) | copy-start | bytes 28
  1.9 1.0 %copy-start.8 = (f32[32,4096]{1,0:T(8,128)S(1)}, f32[32,4096]{1,0:T(8,128)}, u32[]{:S(2)}) copy-start(f32[32,4096]{1,0:T(8,128)} %width_ref.3) | copy-start | bytes 1572868
  3.0 0.7 %copy-start.10 = (f32[256,16]{0,1:T(8,128)S(1)}, f32[256,16]{0,1:T(8,128)}, u32[]{:S(2)}) copy-start(f32[256,16]{0,1:T(8,128)} %param.6) | copy-start | bytes 49156
  9.4 14.2 %all-to-all-start = ((bf16[8,32,128]{2,1,0:T(8,128)(2,1)}), bf16[8,32,128]{2,1,0:T(8,128)(2,1)S(1)}, u32[]{:S(2)}, u32[]{:S(2)}) async-start(bf16[8,32,128]{2,1,0:T(8,128)(2,1)} %forward.1), calls=%async_computation | async-start | bytes 131072 | tf_op jit(solution)/shard_map/all_to_all | solution.py:370
  16.7 0.7 %copy-start.4 = (s32[2]{0:T(128)S(1)}, s32[2]{0:T(128)}, u32[]{:S(2)}) copy-start(s32[2]{0:T(128)} %wave_ref.5) | copy-start | bytes 28
  23.6 0.7 %copy-start.2 = (s32[2,2]{1,0:T(2,128)S(1)}, s32[2,2]{1,0:T(2,128)}, u32[]{:S(2)}) copy-start(s32[2,2]{1,0:T(2,128)} %aim_ref.3) | copy-start | bytes 52
  36.1 15.6 %all-to-all-start.2 = ((bf16[16,32,128]{2,1,0:T(8,128)(2,1)}), bf16[16,32,128]{2,1,0:T(8,128)(2,1)S(1)}, u32[]{:S(2)}, u32[]{:S(2)}) async-start(bf16[16,32,128]{2,1,0:T(8,128)(2,1)} %bitcast.1), calls=%async_computation.2 | async-start | bytes 262144 | tf_op jit(solution)/shard_map/all_to_all | solution.py:400
  40.3 1.1 %collective-permute-start = (s32[2,2]{1,0:T(2,128)S(1)}, s32[2,2]{1,0:T(2,128)S(1)}, u32[]{:S(2)}, u32[]{:S(2)}) collective-permute-start(s32[2,2]{1,0:T(2,128)S(1)} %pad_add_fusion), channel_id=1, source_target_pairs={{0,1},{1,0},{2,3},{3,2},{4,5},{5,4},{6,7},{7,6},{8,9},{9,8},{10,11... | collective-permute-start | bytes 56 | tf_op jit(solution)/shard_map/ppermute | solution.py:358
  41.4 0.7 %copy-start.5 = (s32[2]{0:T(128)S(1)}, s32[2]{0:T(128)}, u32[]{:S(2)}) copy-start(s32[2]{0:T(128)} %wave_ref.5) | copy-start | bytes 28
  42.1 0.7 %copy-start.7 = (s32[2]{0:T(128)S(1)}, s32[2]{0:T(128)}, u32[]{:S(2)}) copy-start(s32[2]{0:T(128)} %angle_ref.3) | copy-start | bytes 28
  42.7 1.0 %copy-start.9 = (f32[32,4096]{1,0:T(8,128)S(1)}, f32[32,4096]{1,0:T(8,128)}, u32[]{:S(2)}) copy-start(f32[32,4096]{1,0:T(8,128)} %width_ref.3) | copy-start | bytes 1572868
  43.8 0.7 %copy-start.11 = (f32[256,16]{0,1:T(8,128)S(1)}, f32[256,16]{0,1:T(8,128)}, u32[]{:S(2)}) copy-start(f32[256,16]{0,1:T(8,128)} %param.6) | copy-start | bytes 49156
  48.4 3.2 %copy-start = (bf16[4,2048,512]{2,1,0:T(8,128)(2,1)}, bf16[4,2048,512]{2,1,0:T(8,128)(2,1)S(1)}, u32[]{:S(2)}) copy-start(bf16[4,2048,512]{2,1,0:T(8,128)(2,1)S(1)} %get-tuple-element.15.table_ref) | copy-start | bytes 25165828
  51.6 3.4 %copy-start.1 = (bf16[4,2048,512]{2,1,0:T(8,128)(2,1)S(1)}, bf16[4,2048,512]{2,1,0:T(8,128)(2,1)}, u32[]{:S(2)}) copy-start(bf16[4,2048,512]{2,1,0:T(8,128)(2,1)} %copy-done) | copy-start | bytes 25165828

commit v2 on v1

v2 whole, which is shorter than its diff:
```python
import functools
import math

import jax
import jax.numpy as jnp
from jax import lax
from jax.experimental import pallas as pl
from jax.experimental.pallas import tpu as pltpu
from jax.sharding import PartitionSpec as P

FOCAL = 256
SPOT = 4
SHIFT = 32
TERMS = 8
BLOCK = 256
GRAIN = 16
VMEM_LIMIT = 16 * 1024 * 1024
HALF = FOCAL // 2
WAVE_ROW, ANGLE_ROW, AIM_ROW, INFO_ROWS = 16, 17, 18, 24
DIRECT = 16

COS = (
    1.0, -19.7392088015709, 64.93939395773512, -85.45681453397417, 60.24458621302471,
    -26.425616460281425, 7.8991596631575085, -1.6968741456712442, 0.2437618617467591,
)
SIN = (
    6.2831853071792665, -41.34170224019464, 81.60524925425943, -76.70585885700535,
    42.05867547580699, -15.094428387947755, 3.818490079304055, -0.7122771247541972,
    0.09149844789363434,
)


def horner(terms, u):
    value = terms[-1] * u + terms[-2]
    for term in terms[-3::-1]:
        value = value * u + term
    return value


def unit_waves(counts, period):
    half = period // 2
    centred = ((counts + half) & (period - 1)) - half
    t = centred.astype(jnp.float32) * (1.0 / period)
    u = t * t
    return horner(COS, u), -(t * horner(SIN, u))


def iota(shape, axis):
    return lax.broadcasted_iota(jnp.int32, shape, axis)


def pick_coef(table, wave):
    chosen = jnp.where(iota(table.shape, 1) == wave, table, 0.0)
    return jnp.sum(chosen, axis=1, keepdims=True)


def own_half():
    return lax.axis_index("aperture") % 2


def column_freq(info_ref, pair, first):
    wave = info_ref[pair, WAVE_ROW : WAVE_ROW + 1, :].astype(jnp.int32)
    angle = info_ref[pair, ANGLE_ROW : ANGLE_ROW + 1, :].astype(jnp.int32)
    focal = (iota((1, FOCAL), 1) + first) & (FOCAL - 1)
    return (focal - FOCAL // 2 + SHIFT * angle) * (BLOCK + wave)


def fill_base(freq, shift, period, base_ref, centre_ref):
    low_r, low_i = unit_waves(iota((GRAIN, 1), 0) * freq, period)
    steps = BLOCK // GRAIN
    high_r, high_i = unit_waves((iota((steps, 1), 0) * GRAIN - BLOCK // 2 + shift) * freq, period)
    for step in range(steps):
        one_r, one_i = high_r[step : step + 1], high_i[step : step + 1]
        rows = slice(step * GRAIN, (step + 1) * GRAIN)
        base_ref[0, rows, :] = one_r * low_r - one_i * low_i
        base_ref[1, rows, :] = one_r * low_i + one_i * low_r
    count = centre_ref.shape[1]
    cent_r, cent_i = unit_waves((iota((count, 1), 0) * BLOCK + BLOCK // 2) * freq, period)
    centre_ref[0] = cent_r
    centre_ref[1] = cent_i


def block_pair(base_ref, centre_ref, index):
    cent_r = centre_ref[0, index : index + 1, :]
    cent_i = centre_ref[1, index : index + 1, :]
    base_r, base_i = base_ref[0], base_ref[1]
    rr, ii = base_r * cent_r, base_i * cent_i
    ri, ir = base_r * cent_i, base_i * cent_r
    before = ((rr + ii).astype(jnp.bfloat16), (ir - ri).astype(jnp.bfloat16))
    after = ((rr - ii).astype(jnp.bfloat16), (ir + ri).astype(jnp.bfloat16))
    return before, after


def near_fields(s, info_ref, pairs):
    def coef(pair, row):
        return info_ref[pair, row : row + 1, :]

    outs = [[coef(p, k) + coef(p, k + 1) * s for k in (0, TERMS)] for p in range(pairs)]
    twice = s + s
    before, current = jnp.ones_like(s), s
    for order in range(2, TERMS):
        before, current = current, twice * current - before
        for pair, out in enumerate(outs):
            out[0] = out[0] + coef(pair, order) * current
            out[1] = out[1] + coef(pair, TERMS + order) * current
    return outs


def near_slopes(s, scale, info_ref, pairs):
    def coef(pair, row):
        return info_ref[pair, row : row + 1, :] * (scale * (row % TERMS))

    twice = s + s
    before, current = jnp.ones_like(s), twice
    outs = [[coef(p, k) + coef(p, k + 1) * twice for k in (1, TERMS + 1)] for p in range(pairs)]
    for order in range(3, TERMS):
        before, current = current, twice * current - before
        for pair, out in enumerate(outs):
            out[0] = out[0] + coef(pair, order) * current
            out[1] = out[1] + coef(pair, TERMS + order) * current
    return outs


def forward_kernel(
    wave_hbm, angle_hbm, aim_hbm, coef_hbm, width_hbm, mine_ref, other_ref, info_ref, own_ref,
    wave_ref, angle_ref, aim_ref, coef_ref, width_ref, base_ref, centre_ref, acc_ref, sems,
):
    rows_dev, cols = width_ref.shape
    pairs = wave_ref.shape[0]
    period = 256 * cols
    moves = [
        pltpu.make_async_copy(source, target, sems.at[index])
        for index, (source, target) in enumerate((
            (wave_hbm, wave_ref), (angle_hbm, angle_ref), (aim_hbm, aim_ref),
            (coef_hbm, coef_ref), (width_hbm, width_ref),
        ))
    ]
    for move in moves:
        move.start()
    for move in moves[:4]:
        move.wait()
    for pair in range(pairs):
        coef = pick_coef(coef_ref[...], wave_ref[pair])
        info_ref[pair, :WAVE_ROW, :] = jnp.broadcast_to(coef, (WAVE_ROW, FOCAL))
        row = iota((INFO_ROWS - WAVE_ROW, FOCAL), 0) + WAVE_ROW
        ids = jnp.where(row == WAVE_ROW, wave_ref[pair], 0)
        ids = jnp.where(row == ANGLE_ROW, angle_ref[pair], ids)
        ids = jnp.where(row == AIM_ROW, aim_ref[pair, 0], ids)
        ids = jnp.where(row == AIM_ROW + 1, aim_ref[pair, 1], ids)
        info_ref[pair, WAVE_ROW:, :] = ids.astype(jnp.float32)
    for pair in range(pairs):
        fill_base(column_freq(info_ref, pair, 0), 0, period, base_ref.at[pair], centre_ref.at[pair])
    acc_ref[...] = jnp.zeros_like(acc_ref)
    moves[4].wait()
    for index in range(cols // (2 * BLOCK)):
        left = cols // 2 - (index + 1) * BLOCK
        right = cols // 2 + index * BLOCK
        nears = []
        for start in (left, right):
            outs = near_fields(width_ref[:, start : start + BLOCK], info_ref, pairs)
            nears.append([jnp.concatenate(out, axis=0).astype(jnp.bfloat16) for out in outs])
        for pair in range(pairs):
            before, after = block_pair(base_ref.at[pair], centre_ref.at[pair], index)
            near = jnp.concatenate([nears[0][pair], nears[1][pair]], axis=1)
            for part in range(2):
                table = jnp.concatenate([before[part], after[part]], axis=0)
                acc_ref[pair, part] += jnp.dot(near, table, preferred_element_type=jnp.float32)
    own_cols = own_ref.shape[1]
    first = pl.multiple_of(lax.axis_index("wave") * own_cols, own_cols)
    own_ref[...] = width_ref[:, pl.ds(first, own_cols)]
    even = own_half() == 0
    for pair in range(pairs):
        real = acc_ref[pair, 0, :rows_dev] - acc_ref[pair, 1, rows_dev:]
        imag = acc_ref[pair, 1, :rows_dev] + acc_ref[pair, 0, rows_dev:]
        for part, value in enumerate((real, imag)):
            lanes = slice((2 * pair + part) * HALF, (2 * pair + part + 1) * HALF)
            mine_ref[:, lanes] = jnp.where(even, value[:, :HALF], value[:, HALF:]).astype(jnp.bfloat16)
            other_ref[:, lanes] = jnp.where(even, value[:, HALF:], value[:, :HALF]).astype(jnp.bfloat16)


def row_kernel(info_ref, tall_ref, flat_ref):
    pairs, _, rows = tall_ref.shape
    rows_dev = flat_ref.shape[1] // 2
    period = 256 * rows
    size = min(rows, FOCAL)
    me = lax.axis_index("aperture")
    for pair in range(pairs):
        wave = info_ref[pair, WAVE_ROW : WAVE_ROW + 1, :].astype(jnp.int32) + BLOCK
        focal = (iota((FOCAL, 1), 0) - FOCAL // 2) * wave

        def step(index, carry):
            start = pl.multiple_of(index * size, size)
            place = iota((1, size), 1) + (start - rows // 2)
            real, imag = unit_waves(focal[:, :size] * place, period)
            tall_ref[pair, :FOCAL, pl.ds(start, size)] = real.astype(jnp.bfloat16)
            tall_ref[pair, FOCAL:, pl.ds(start, size)] = imag.astype(jnp.bfloat16)
            return carry

        if rows == size:
            step(0, 0)
        else:
            lax.fori_loop(0, rows // size, step, 0)
        focal = (iota((1, FOCAL), 1) - FOCAL // 2) * wave
        for copy in range(2):
            first = (me ^ copy) * rows_dev - rows // 2
            real, imag = unit_waves((iota((rows_dev, 1), 0) + first) * focal, period)
            lines = slice(copy * rows_dev, (copy + 1) * rows_dev)
            flat_ref[pair, lines, :FOCAL] = real.astype(jnp.bfloat16)
            flat_ref[pair, lines, FOCAL:] = imag.astype(jnp.bfloat16)


def spot_half(info_ref, pair):
    aims = [info_ref[pair, row : row + 1, :HALF] for row in (AIM_ROW, AIM_ROW + 1)]
    rows_off = iota((FOCAL, HALF), 0).astype(jnp.float32) - aims[0]
    cols_off = (iota((1, HALF), 1) + own_half() * HALF).astype(jnp.float32) - aims[1]
    return jnp.exp(-(rows_off * rows_off + cols_off * cols_off) / (2.0 * SPOT * SPOT))


def field_kernel(info_ref, tall_ref, *refs):
    *sect_refs, field_ref, power_ref, rows_ref = refs
    pairs = tall_ref.shape[0]
    rows_dev = sect_refs[0].shape[0]
    if len(sect_refs) == 1:
        sect_ref = sect_refs[0]
    else:
        sect_ref = rows_ref
        me = lax.axis_index("aperture")
        for step, ref in enumerate(sect_refs):
            start = pl.multiple_of((me ^ step) * rows_dev, rows_dev)
            rows_ref[pl.ds(start, rows_dev), :] = ref[...]
    sums = []
    for pair in range(pairs):
        lanes = slice(pair * FOCAL, (pair + 1) * FOCAL)
        mixed = jnp.dot(tall_ref[pair], sect_ref[:, lanes], preferred_element_type=jnp.float32)
        real = mixed[:FOCAL, :HALF] - mixed[FOCAL:, HALF:]
        imag = mixed[:FOCAL, HALF:] + mixed[FOCAL:, :HALF]
        field_ref[pair, 0] = real
        field_ref[pair, 1] = imag
        power = real * real + imag * imag
        spot = spot_half(info_ref, pair)
        sums.append(jnp.sum(spot * power, axis=0, keepdims=True))
        sums.append(jnp.sum(power, axis=0, keepdims=True))
    sums.append(jnp.zeros((8 - len(sums), HALF), jnp.float32))
    power_ref[...] = jnp.concatenate(sums, axis=0)


def seed_kernel(info_ref, power_ref, far_ref, field_ref, flat_ref, mine_ref, other_ref, score_ref):
    rows_dev = mine_ref.shape[0]
    pairs = flat_ref.shape[0]
    sums = jnp.sum(power_ref[...] + far_ref[...], axis=1, keepdims=True)
    place = iota((1, FOCAL), 1).astype(jnp.float32)
    for pair in range(pairs):
        all_power = sums[2 * pair + 1 : 2 * pair + 2] + 1e-06
        ratio = sums[2 * pair : 2 * pair + 1] / all_power
        spans = []
        for row in (AIM_ROW, AIM_ROW + 1):
            off = place - info_ref[pair, row : row + 1, :]
            spans.append(jnp.sum(jnp.exp(-(off * off) / (2.0 * SPOT * SPOT)), axis=1, keepdims=True))
        factor = FOCAL * FOCAL / (spans[0] * spans[1])
        score_ref[pair] = jnp.sum(ratio * factor)
        weight = (factor * 2.0 / all_power) * (spot_half(info_ref, pair) - ratio)
        real = (weight * field_ref[pair, 0]).astype(jnp.bfloat16)
        imag = (weight * field_ref[pair, 1]).astype(jnp.bfloat16)
        stack = jnp.concatenate(
            [jnp.concatenate([real, imag], axis=1), jnp.concatenate([imag, -real], axis=1)], axis=0
        )
        back = jnp.dot(flat_ref[pair], stack, preferred_element_type=jnp.float32).astype(jnp.bfloat16)
        lanes = slice(pair * FOCAL, (pair + 1) * FOCAL)
        mine_ref[:, lanes] = back[:rows_dev]
        other_ref[:, lanes] = back[rows_dev:]


def table_kernel(scale, cols, info_ref, width_ref, *refs):
    *out_refs, base_ref, centre_ref = refs
    pairs = base_ref.shape[0]
    table_refs, slope_refs = out_refs[:pairs], out_refs[pairs:]
    own_cols = width_ref.shape[1]
    period = 256 * cols
    middle = own_cols // 2
    shift = lax.axis_index("wave") * own_cols + middle - cols // 2
    for pair in range(pairs):
        freq = column_freq(info_ref, pair, own_half() * HALF)
        fill_base(freq, shift, period, base_ref.at[pair], centre_ref.at[pair])
    for index in range(own_cols // (2 * BLOCK)):
        left = middle - (index + 1) * BLOCK
        right = middle + index * BLOCK
        for pair in range(pairs):
            tables = block_pair(base_ref.at[pair], centre_ref.at[pair], index)
            for start, table in zip((left, right), tables):
                table_refs[pair][start : start + BLOCK, :FOCAL] = table[0]
                table_refs[pair][start : start + BLOCK, FOCAL:] = table[1]
        for start in (left, right):
            slopes = near_slopes(width_ref[:, start : start + BLOCK], scale, info_ref, pairs)
            for pair in range(pairs):
                slope_refs[pair][0, :, start : start + BLOCK] = slopes[pair][0]
                slope_refs[pair][1, :, start : start + BLOCK] = slopes[pair][1]


def grad_kernel(pairs_dev, *refs):
    *in_refs, out_ref, left_ref = refs
    rows_dev, own_cols = out_ref.shape
    pairs = left_ref.shape[0]
    back_refs, in_refs = in_refs[: 2 * pairs // pairs_dev], in_refs[2 * pairs // pairs_dev :]
    table_refs, slope_refs = in_refs[:pairs], in_refs[pairs:]
    for pair in range(pairs):
        halves = back_refs[2 * (pair // pairs_dev) : 2 * (pair // pairs_dev) + 2]
        for half, ref in enumerate(halves):
            lane = (pair % pairs_dev) * FOCAL
            real, imag = ref[:, lane : lane + HALF], ref[:, lane + HALF : lane + FOCAL]
            for part, rows, value in ((0, 0, real), (1, 0, imag), (0, 1, imag), (1, 1, -real)):
                start = part * FOCAL + half * HALF
                left_ref[pair, rows * rows_dev : (rows + 1) * rows_dev, start : start + HALF] = value
    size = 2 * BLOCK
    for start in range(0, own_cols, size):
        total = jnp.zeros((rows_dev, size), jnp.float32)
        for pair in range(pairs):
            grad = lax.dot_general(
                left_ref[pair],
                table_refs[pair][start : start + size, :],
                (((1,), (1,)), ((), ())),
                preferred_element_type=jnp.float32,
            )
            total += grad[:rows_dev] * slope_refs[pair][0, :, start : start + size]
            total += grad[rows_dev:] * slope_refs[pair][1, :, start : start + size]
        out_ref[:, start : start + size] = total


VMEM = pl.BlockSpec(memory_space=pltpu.VMEM)
SMEM = pl.BlockSpec(memory_space=pltpu.SMEM)
HBM = pl.BlockSpec(memory_space=pltpu.HBM)


def call(kernel, name, outs, in_specs, out_specs, scratch, flops, moved):
    return pl.pallas_call(
        kernel,
        name=name,
        out_shape=outs,
        in_specs=in_specs,
        out_specs=out_specs,
        scratch_shapes=scratch,
        cost_estimate=pl.CostEstimate(flops=flops, bytes_accessed=moved, transcendentals=0),
        compiler_params=pltpu.CompilerParams(vmem_limit_bytes=VMEM_LIMIT),
    )


def on_device(widths, coef_table, wave_ids, angle_ids, targets):
    rows_dev, cols = widths.shape
    pairs_dev = wave_ids.shape[0]
    peers = lax.axis_size("aperture")
    copies = lax.axis_size("wave")
    rows = rows_dev * peers
    own_cols = cols // copies
    lanes = 2 * pairs_dev * HALF
    f32, bf16 = jnp.float32, jnp.bfloat16
    shape = jax.ShapeDtypeStruct

    def in_hbm(value):
        return pltpu.with_memory_space_constraint(value, pltpu.HBM)

    def exchange(value, step):
        return lax.ppermute(value, "aperture", [(index, index ^ step) for index in range(peers)])

    def to_core(value):
        return lax.ppermute(value, "wave", [(index, (index + 1) % copies) for index in range(copies)])

    def to_corner(value):
        places = [(index, core) for index in range(peers) for core in range(copies)]
        pairs = [
            (index * copies + core, (index ^ 1) * copies + (core + 1) % copies) for index, core in places
        ]
        return lax.ppermute(value, ("aperture", "wave"), pairs)

    mine, other, info, own = call(
        forward_kernel, "forward",
        (
            shape((rows_dev, lanes), bf16), shape((rows_dev, lanes), bf16),
            shape((pairs_dev, INFO_ROWS, FOCAL), f32), shape((rows_dev, own_cols), f32),
        ),
        [HBM] * 5, (VMEM,) * 4,
        [
            pltpu.SMEM(wave_ids.shape, jnp.int32),
            pltpu.SMEM(angle_ids.shape, jnp.int32),
            pltpu.SMEM(targets.shape, jnp.int32),
            pltpu.VMEM(coef_table.shape[::-1], f32),
            pltpu.VMEM(widths.shape, f32),
            pltpu.VMEM((pairs_dev, 2, BLOCK, FOCAL), f32),
            pltpu.VMEM((pairs_dev, 2, cols // (2 * BLOCK), FOCAL), f32),
            pltpu.VMEM((pairs_dev, 2, 2 * rows_dev, FOCAL), f32),
            pltpu.SemaphoreType.DMA((5,)),
        ],
        10**9, 10**7,
    )(*(in_hbm(value) for value in (wave_ids, angle_ids, targets, coef_table.T, widths)))
    far_info = to_core(info)
    if peers <= DIRECT:
        sections = [mine] + [exchange(other if step % 2 else mine, step) for step in range(1, peers)]
    else:
        even = lax.axis_index("aperture") % 2 == 0
        blocks = jnp.stack([jnp.where(even, mine, other), jnp.where(even, other, mine)])
        blocks = jnp.tile(blocks, (peers // 2, 1, 1))
        blocks = lax.all_to_all(blocks, "aperture", 0, 0, tiled=True)
        sections = [blocks.reshape(rows, lanes)]

    tall, flat = call(
        row_kernel, "row_tables",
        (shape((pairs_dev, 2 * FOCAL, rows), bf16), shape((pairs_dev, 2 * rows_dev, 2 * FOCAL), bf16)),
        [VMEM], (VMEM, VMEM), [], 10**8, 10**6,
    )(info)

    def column_tables(info, name):
        outs = [shape((own_cols, 2 * FOCAL), bf16)] * pairs_dev
        outs += [shape((2, rows_dev, own_cols), f32)] * pairs_dev
        got = call(
            functools.partial(table_kernel, math.sqrt(rows * cols), cols), name,
            outs, [VMEM, VMEM], [VMEM] * len(outs),
            [
                pltpu.VMEM((pairs_dev, 2, BLOCK, FOCAL), f32),
                pltpu.VMEM((pairs_dev, 2, own_cols // (2 * BLOCK), FOCAL), f32),
            ],
            10**9, 10**7,
        )(info, own)
        return got[:pairs_dev], got[pairs_dev:]

    tables, slopes = column_tables(info, "own_tables")
    far_tables, far_slopes = column_tables(far_info, "far_tables")

    field, power = call(
        field_kernel, "field",
        (shape((pairs_dev, 2, FOCAL, HALF), f32), shape((8, HALF), f32)),
        [VMEM] * (2 + len(sections)), (VMEM, VMEM), [pltpu.VMEM((rows, lanes), bf16)], 10**8, 10**6,
    )(info, tall, *sections)
    mine, other, scores = call(
        seed_kernel, "seed",
        (shape((rows_dev, lanes), bf16), shape((rows_dev, lanes), bf16), shape((pairs_dev,), f32)),
        [VMEM] * 5, (VMEM, VMEM, SMEM), [], 10**8, 10**6,
    )(info, power, exchange(power, 1), field, flat)
    backs = [mine, exchange(other, 1), to_core(mine), to_corner(other)]
    ins = [*backs, *tables, *far_tables, *slopes, *far_slopes]
    grad = call(
        functools.partial(grad_kernel, pairs_dev), "gradient",
        shape((rows_dev, own_cols), f32), [VMEM] * len(ins), VMEM,
        [pltpu.VMEM((copies * pairs_dev, 2 * rows_dev, 2 * FOCAL), bf16)],
        10**9, 10**7,
    )(*ins)
    return grad, scores


def solution(mesh):
    in_specs = (
        P(("group", "aperture"), None),
        P(),
        P(("group", "wave")),
        P(("group", "wave")),
        P(("group", "wave"), None),
    )
    out_specs = (P(("group", "aperture"), "wave"), P(("group", "wave")))
    return jax.shard_map(
        on_device, mesh=mesh, in_specs=in_specs, out_specs=out_specs, check_vma=False
    )
```

time: 59.5 us -> 34.1 us (0.57)
  local copies, waits for them, and re-layouts: 14.1 us -> 0 us
  blocking collectives: 9.06 us -> 0 us
  starting transfers between devices: 11.1 us -> 15 us
  Pallas kernels: 17.5 us -> 14.6 us
  waiting for transfers between devices: 5.8 us -> 3.68 us
  other arithmetic: 0.68 us -> 0 us
    ppermute x1 -> x12, starting transfers between devices: 0.29 us -> 15 us  [the longest x9 13.8 us: exchange(): lax.ppermute(value, 'aperture', [(index, index ^ step) for index in range...]
    unnamed x24 -> x0, local copies, waits for them, and re-layouts: 14.1 us -> none
    all_to_all x2 -> x0, starting transfers between devices: 10.8 us -> none  [the longest x1 7.25 us: on_device(): sections = lax.all_to_all(sections, 'aperture', 0, 0, tiled=True)]
    all_to_all x1 -> x0, blocking collectives: 9.06 us -> none  [on_device(): power = lax.all_to_all(power, 'aperture', 0, 0, tiled=True)]
    all_to_all x2 -> x0, waiting for transfers between devices: 4.95 us -> none  [the longest x1 4.94 us: on_device(): sections = lax.all_to_all(sections, 'aperture', 0, 0, tiled=True)]
    pallas_call x6 -> x7, Pallas kernels: 17.5 us -> 14.6 us  [the longest x2 4.7 us: column_tables(): call(functools.partial(table_kernel, math.sqrt(rows * cols), cols), name,...]
    ppermute x1 -> x12, waiting for transfers between devices: 0.85 us -> 3.68 us  [the longest x9 3.68 us: exchange(): lax.ppermute(value, 'aperture', [(index, index ^ step) for index in range...]
    another operation x1 -> x0, other arithmetic: 0.68 us -> none  [on_device(): far_ids = lax.ppermute(jnp.stack([wave_ids, angle_ids]), 'wave', ring)]
  transfers between devices with their start and end apart: 3 -> 12, of which waited for: 2 -> 3; matrix products, arithmetic and copies ran while one was open for 1% -> 0% of each run, Pallas kernels for 9% -> 20%
where the time goes in v2:
time: 34.1 us; the launch traced here: 34 us
  starting transfers between devices  15 us (44%)
  Pallas kernels  14.6 us (43%)
  waiting for transfers between devices  3.68 us (11%)
  between operations  0.73 us (2%)
    ppermute x9, starting transfers between devices, exchange(): lax.ppermute(value, 'aperture', [(index, index ^ step) for index in range...  13.8 us
    pallas_call x2, Pallas kernels, column_tables(): call(functools.partial(table_kernel, math.sqrt(rows * cols), cols), name,...  4.7 us
    pallas_call x1, Pallas kernels, on_device(): call(forward_kernel, 'forward', (shape((rows_dev, lanes), bf16), shape((r...  4.59 us
    ppermute x9, waiting for transfers between devices, exchange(): lax.ppermute(value, 'aperture', [(index, index ^ step) for index in range...  3.68 us
    pallas_call x1, Pallas kernels, on_device(): call(functools.partial(grad_kernel, pairs_dev), 'gradient', shape((rows_d...  3.34 us
    ppermute x2, starting transfers between devices, to_core(): lax.ppermute(value, 'wave', [(index, (index + 1) % copies) for index in r...  1.07 us
    pallas_call x1, Pallas kernels, on_device(): call(row_kernel, 'row_tables', (shape((pairs_dev, 2 * FOCAL, rows), bf16)...  0.96 us
  transfers between devices with their start and end apart: 12, of which 3 were waited for; matrix products, arithmetic and copies ran while one was open for 0% of the time, Pallas kernels for 20%

profile of v2, /device:TPU:0, one launch (start us, length us, event | category | flops | bytes accessed | tf_op | source)
XLA Modules:
  0.0 34.0 jit_solution(13443217945490460723)
XLA Ops:
  0.6 4.6 %forward.1 = (bf16[32,512]{1,0:T(8,128)(2,1)S(1)}, bf16[32,512]{1,0:T(8,128)(2,1)S(1)}, f32[2,24,256]{2,1,0:T(8,128)S(1)}, f32[32,2048]{1,0:T(8,128)S(1)}) custom-call(s32[2]{0:T(128)} %wave_hbm.1, s32[2]{0:T(128)} %angle_hbm.1, s32[2,2]{1,0:T(2,128)} %aim_hbm.1, f32[16,256]{1,0:T(8,128)} %bitcast.1, f32[32,4096]{1,0:T(8,128)} %width_hbm.1), custom_call_target="tpu_custom_call" | custom-call | flops 1000000000 | bytes 10000000 | tf_op jit(solution)/shard_map/forward/pallas_call | solution.py:373
  5.2 5.1 %collective-permute-start.5 = (bf16[32,512]{1,0:T(8,128)(2,1)S(1)}, bf16[32,512]{1,0:T(8,128)(2,1)S(1)}, u32[]{:S(2)}, u32[]{:S(2)}) collective-permute-start(bf16[32,512]{1,0:T(8,128)(2,1)S(1)} %get-tuple-element.23.refs_0_), channel_id=1, source_target_pairs={{0,12},{2,14},{4,8},{6,10},{8,4},{10,6},{12,0},{14,2},{1,13},{3,15... | collective-permute-start | bytes 98312 | tf_op jit(solution)/shard_map/ppermute | solution.py:361
  10.3 0.0 collective-permute-start.3
  10.3 0.6 %collective-permute-start.1 = (bf16[32,512]{1,0:T(8,128)(2,1)S(1)}, bf16[32,512]{1,0:T(8,128)(2,1)S(1)}, u32[]{:S(2)}, u32[]{:S(2)}) collective-permute-start(bf16[32,512]{1,0:T(8,128)(2,1)S(1)} %get-tuple-element.23.refs_0_), channel_id=1, source_target_pairs={{0,4},{2,6},{4,0},{6,2},{8,12},{10,14},{12,8},{14,10},{1,5},{3,7},... | collective-permute-start | bytes 98312 | tf_op jit(solution)/shard_map/ppermute | solution.py:361
  11.0 4.7 %collective-permute-start.6 = (bf16[32,512]{1,0:T(8,128)(2,1)S(1)}, bf16[32,512]{1,0:T(8,128)(2,1)S(1)}, u32[]{:S(2)}, u32[]{:S(2)}) collective-permute-start(bf16[32,512]{1,0:T(8,128)(2,1)S(1)} %get-tuple-element.24), channel_id=1, source_target_pairs={{0,14},{2,12},{4,10},{6,8},{8,6},{10,4},{12,2},{14,0},{1,15},{3,13... | collective-permute-start | bytes 98312 | tf_op jit(solution)/shard_map/ppermute | solution.py:361
  15.7 0.0 collective-permute-start.4
  15.7 0.0 collective-permute-done.5.refs_6_
  15.7 1.7 %collective-permute-start.2 = (bf16[32,512]{1,0:T(8,128)(2,1)S(1)}, bf16[32,512]{1,0:T(8,128)(2,1)S(1)}, u32[]{:S(2)}, u32[]{:S(2)}) collective-permute-start(bf16[32,512]{1,0:T(8,128)(2,1)S(1)} %get-tuple-element.24), channel_id=1, source_target_pairs={{0,6},{2,4},{4,2},{6,0},{8,14},{10,12},{12,10},{14,8},{1,7},{3,5},... | collective-permute-start | bytes 98312 | tf_op jit(solution)/shard_map/ppermute | solution.py:361
  17.4 0.0 collective-permute-done.3.refs_4_
  17.4 0.4 %collective-permute-start = (bf16[32,512]{1,0:T(8,128)(2,1)S(1)}, bf16[32,512]{1,0:T(8,128)(2,1)S(1)}, u32[]{:S(2)}, u32[]{:S(2)}) collective-permute-start(bf16[32,512]{1,0:T(8,128)(2,1)S(1)} %get-tuple-element.24), channel_id=1, source_target_pairs={{0,2},{2,0},{4,6},{6,4},{8,10},{10,8},{12,14},{14,12},{1,3},{3,1},... | collective-permute-start | bytes 98312 | tf_op jit(solution)/shard_map/ppermute | solution.py:361
  17.7 1.0 %row_tables.1 = (bf16[2,512,256]{2,1,0:T(8,128)(2,1)S(1)}, bf16[2,64,512]{2,1,0:T(8,128)(2,1)S(1)}) custom-call(f32[2,24,256]{2,1,0:T(8,128)S(1)} %get-tuple-element.21.info_ref), custom_call_target="tpu_custom_call" | custom-call | flops 100000000 | bytes 1000000 | tf_op jit(solution)/shard_map/row_tables/pallas_call | solution.py:403
  18.7 0.0 collective-permute-done.1.refs_2_
  18.7 0.1 collective-permute-start.11
  18.8 0.0 collective-permute-done.6.refs_7_
  18.8 2.7 %collective-permute-done.4.refs_5_ = bf16[32,512]{1,0:T(8,128)(2,1)S(1)} collective-permute-done((bf16[32,512]{1,0:T(8,128)(2,1)S(1)}, bf16[32,512]{1,0:T(8,128)(2,1)S(1)}, u32[]{:S(2)}, u32[]{:S(2)}) %collective-permute-start.4) | collective-permute-done | bytes 32800 | tf_op jit(solution)/shard_map/ppermute | solution.py:361
  21.5 0.0 collective-permute-done.2.refs_3_
  21.5 0.1 collective-permute-done.refs_1_
  21.6 0.3 field.1
  22.0 0.5 %collective-permute-start.7 = (f32[8,128]{1,0:T(8,128)S(1)}, f32[8,128]{1,0:T(8,128)S(1)}, u32[]{:S(2)}, u32[]{:S(2)}) collective-permute-start(f32[8,128]{1,0:T(8,128)S(1)} %get-tuple-element.25.power_ref), channel_id=1, source_target_pairs={{0,2},{2,0},{4,6},{6,4},{8,10},{10,8},{12,14},{14,12},{1,3},{3,1},... | collective-permute-start | bytes 12296 | tf_op jit(solution)/shard_map/ppermute | solution.py:361
  22.4 2.3 %own_tables.1 = (bf16[2048,512]{1,0:T(8,128)(2,1)S(1)}, bf16[2048,512]{1,0:T(8,128)(2,1)S(1)}, f32[2,32,2048]{2,1,0:T(8,128)S(1)}, f32[2,32,2048]{2,1,0:T(8,128)S(1)}) custom-call(f32[2,24,256]{2,1,0:T(8,128)S(1)} %get-tuple-element.21.info_ref, f32[32,2048]{1,0:T(8,128)S(1)} %get-tuple-element.30.width_ref), custom_call_target="tpu_custom_call" | custom-call | flops 1000000000 | bytes 10000000 | tf_op jit(solution)/shard_map/own_tables/pallas_call | solution.py:412
  24.8 0.8 %collective-permute-done.7.far_ref = f32[8,128]{1,0:T(8,128)S(1)} collective-permute-done((f32[8,128]{1,0:T(8,128)S(1)}, f32[8,128]{1,0:T(8,128)S(1)}, u32[]{:S(2)}, u32[]{:S(2)}) %collective-permute-start.7) | collective-permute-done | bytes 4128 | tf_op jit(solution)/shard_map/ppermute | solution.py:361
  25.6 0.7 %seed.1 = (bf16[32,512]{1,0:T(8,128)(2,1)S(1)}, bf16[32,512]{1,0:T(8,128)(2,1)S(1)}, f32[2]{0:T(128)}) custom-call(f32[2,24,256]{2,1,0:T(8,128)S(1)} %get-tuple-element.21.info_ref, f32[8,128]{1,0:T(8,128)S(1)} %get-tuple-element.25.power_ref, f32[8,128]{1,0:T(8,128)S(1)} %collective-permute-done.7.far_ref, ...), custom_call_target="tpu_custom_call" | custom-call | flops 100000000 | bytes 1000000 | tf_op jit(solution)/shard_map/seed/pallas_call | solution.py:431
  26.3 0.1 collective-permute-start.10
  26.4 0.9 %collective-permute-start.8 = (bf16[32,512]{1,0:T(8,128)(2,1)S(1)}, bf16[32,512]{1,0:T(8,128)(2,1)S(1)}, u32[]{:S(2)}, u32[]{:S(2)}) collective-permute-start(bf16[32,512]{1,0:T(8,128)(2,1)S(1)} %get-tuple-element.29), channel_id=1, source_target_pairs={{0,2},{2,0},{4,6},{6,4},{8,10},{10,8},{12,14},{14,12},{1,3},{3,1},... | collective-permute-start | bytes 98312 | tf_op jit(solution)/shard_map/ppermute | solution.py:361
  27.2 1.0 %collective-permute-start.9 = (bf16[32,512]{1,0:T(8,128)(2,1)S(1)}, bf16[32,512]{1,0:T(8,128)(2,1)S(1)}, u32[]{:S(2)}, u32[]{:S(2)}) collective-permute-start(bf16[32,512]{1,0:T(8,128)(2,1)S(1)} %get-tuple-element.28.refs_0_), channel_id=1, source_target_pairs={{0,1},{1,0},{2,3},{3,2},{4,5},{5,4},{6,7},{7,6},{8,9},{9,8},{10,11... | collective-permute-start | bytes 98312 | tf_op jit(solution)/shard_map/ppermute | solution.py:364
  28.2 0.0 collective-permute-done.11.info_ref
  28.2 2.3 %far_tables.1 = (bf16[2048,512]{1,0:T(8,128)(2,1)S(1)}, bf16[2048,512]{1,0:T(8,128)(2,1)S(1)}, f32[2,32,2048]{2,1,0:T(8,128)S(1)}, f32[2,32,2048]{2,1,0:T(8,128)S(1)}) custom-call(f32[2,24,256]{2,1,0:T(8,128)S(1)} %collective-permute-done.11.info_ref, f32[32,2048]{1,0:T(8,128)S(1)} %get-tuple-element.30.width_ref), custom_call_target="tpu_custom_call" | custom-call | flops 1000000000 | bytes 10000000 | tf_op jit(solution)/shard_map/far_tables/pallas_call | solution.py:412
  30.6 0.0 collective-permute-done.9.refs_2_
  30.6 0.0 collective-permute-done.10.refs_3_
  30.6 0.0 collective-permute-done.8.refs_1_
  30.6 3.3 %gradient.1 = f32[32,2048]{1,0:T(8,128)} custom-call(bf16[32,512]{1,0:T(8,128)(2,1)S(1)} %get-tuple-element.28.refs_0_, bf16[32,512]{1,0:T(8,128)(2,1)S(1)} %collective-permute-done.8.refs_1_, bf16[32,512]{1,0:T(8,128)(2,1)S(1)} %collective-permute-done.9.refs_2_, bf16[32,512]{1,0:T(8,128)(2,1)S(1)} %collective-permute-done.10.refs_3_, ...), custom_call_target="tpu_custom_call" | custom-call | flops 1000000000 | bytes 10000000 | tf_op jit(solution)/shard_map/gradient/pallas_call | solution.py:438
Async XLA Ops:
  5.2 10.4 %collective-permute-start.5 = (bf16[32,512]{1,0:T(8,128)(2,1)S(1)}, bf16[32,512]{1,0:T(8,128)(2,1)S(1)}, u32[]{:S(2)}, u32[]{:S(2)}) collective-permute-start(bf16[32,512]{1,0:T(8,128)(2,1)S(1)} %get-tuple-element.23.refs_0_), channel_id=1, source_target_pairs={{0,12},{2,14},{4,8},{6,10},{8,4},{10,6},{12,0},{14,2},{1,13},{3,15... | collective-permute-start | bytes 98312 | tf_op jit(solution)/shard_map/ppermute | solution.py:361
  10.3 7.0 %collective-permute-start.3 = (bf16[32,512]{1,0:T(8,128)(2,1)S(1)}, bf16[32,512]{1,0:T(8,128)(2,1)S(1)}, u32[]{:S(2)}, u32[]{:S(2)}) collective-permute-start(bf16[32,512]{1,0:T(8,128)(2,1)S(1)} %get-tuple-element.23.refs_0_), channel_id=1, source_target_pairs={{0,8},{2,10},{4,12},{6,14},{8,0},{10,2},{12,4},{14,6},{1,9},{3,11}... | collective-permute-start | bytes 98312 | tf_op jit(solution)/shard_map/ppermute | solution.py:361
  10.3 8.4 %collective-permute-start.1 = (bf16[32,512]{1,0:T(8,128)(2,1)S(1)}, bf16[32,512]{1,0:T(8,128)(2,1)S(1)}, u32[]{:S(2)}, u32[]{:S(2)}) collective-permute-start(bf16[32,512]{1,0:T(8,128)(2,1)S(1)} %get-tuple-element.23.refs_0_), channel_id=1, source_target_pairs={{0,4},{2,6},{4,0},{6,2},{8,12},{10,14},{12,8},{14,10},{1,5},{3,7},... | collective-permute-start | bytes 98312 | tf_op jit(solution)/shard_map/ppermute | solution.py:361
  11.0 7.8 %collective-permute-start.6 = (bf16[32,512]{1,0:T(8,128)(2,1)S(1)}, bf16[32,512]{1,0:T(8,128)(2,1)S(1)}, u32[]{:S(2)}, u32[]{:S(2)}) collective-permute-start(bf16[32,512]{1,0:T(8,128)(2,1)S(1)} %get-tuple-element.24), channel_id=1, source_target_pairs={{0,14},{2,12},{4,10},{6,8},{8,6},{10,4},{12,2},{14,0},{1,15},{3,13... | collective-permute-start | bytes 98312 | tf_op jit(solution)/shard_map/ppermute | solution.py:361
  15.7 5.8 %collective-permute-start.4 = (bf16[32,512]{1,0:T(8,128)(2,1)S(1)}, bf16[32,512]{1,0:T(8,128)(2,1)S(1)}, u32[]{:S(2)}, u32[]{:S(2)}) collective-permute-start(bf16[32,512]{1,0:T(8,128)(2,1)S(1)} %get-tuple-element.24), channel_id=1, source_target_pairs={{0,10},{2,8},{4,14},{6,12},{8,2},{10,0},{12,6},{14,4},{1,11},{3,9}... | collective-permute-start | bytes 98312 | tf_op jit(solution)/shard_map/ppermute | solution.py:361
  15.7 5.8 %collective-permute-start.2 = (bf16[32,512]{1,0:T(8,128)(2,1)S(1)}, bf16[32,512]{1,0:T(8,128)(2,1)S(1)}, u32[]{:S(2)}, u32[]{:S(2)}) collective-permute-start(bf16[32,512]{1,0:T(8,128)(2,1)S(1)} %get-tuple-element.24), channel_id=1, source_target_pairs={{0,6},{2,4},{4,2},{6,0},{8,14},{10,12},{12,10},{14,8},{1,7},{3,5},... | collective-permute-start | bytes 98312 | tf_op jit(solution)/shard_map/ppermute | solution.py:361
  17.4 4.3 %collective-permute-start = (bf16[32,512]{1,0:T(8,128)(2,1)S(1)}, bf16[32,512]{1,0:T(8,128)(2,1)S(1)}, u32[]{:S(2)}, u32[]{:S(2)}) collective-permute-start(bf16[32,512]{1,0:T(8,128)(2,1)S(1)} %get-tuple-element.24), channel_id=1, source_target_pairs={{0,2},{2,0},{4,6},{6,4},{8,10},{10,8},{12,14},{14,12},{1,3},{3,1},... | collective-permute-start | bytes 98312 | tf_op jit(solution)/shard_map/ppermute | solution.py:361
  18.7 9.5 %collective-permute-start.11 = (f32[2,24,256]{2,1,0:T(8,128)S(1)}, f32[2,24,256]{2,1,0:T(8,128)S(1)}, u32[]{:S(2)}, u32[]{:S(2)}) collective-permute-start(f32[2,24,256]{2,1,0:T(8,128)S(1)} %get-tuple-element.21.info_ref), channel_id=1, source_target_pairs={{0,1},{1,0},{2,3},{3,2},{4,5},{5,4},{6,7},{7,6},{8,9},{9,8},{10,11... | collective-permute-start | bytes 147464 | tf_op jit(solution)/shard_map/ppermute | solution.py:364
  22.0 3.7 %collective-permute-start.7 = (f32[8,128]{1,0:T(8,128)S(1)}, f32[8,128]{1,0:T(8,128)S(1)}, u32[]{:S(2)}, u32[]{:S(2)}) collective-permute-start(f32[8,128]{1,0:T(8,128)S(1)} %get-tuple-element.25.power_ref), channel_id=1, source_target_pairs={{0,2},{2,0},{4,6},{6,4},{8,10},{10,8},{12,14},{14,12},{1,3},{3,1},... | collective-permute-start | bytes 12296 | tf_op jit(solution)/shard_map/ppermute | solution.py:361
  26.3 4.3 %collective-permute-start.10 = (bf16[32,512]{1,0:T(8,128)(2,1)S(1)}, bf16[32,512]{1,0:T(8,128)(2,1)S(1)}, u32[]{:S(2)}, u32[]{:S(2)}) collective-permute-start(bf16[32,512]{1,0:T(8,128)(2,1)S(1)} %get-tuple-element.29), channel_id=1, source_target_pairs={{0,3},{1,2},{2,1},{3,0},{4,7},{5,6},{6,5},{7,4},{8,11},{9,10},{10,... | collective-permute-start | bytes 98312 | tf_op jit(solution)/shard_map/ppermute | solution.py:371
  26.4 4.2 %collective-permute-start.8 = (bf16[32,512]{1,0:T(8,128)(2,1)S(1)}, bf16[32,512]{1,0:T(8,128)(2,1)S(1)}, u32[]{:S(2)}, u32[]{:S(2)}) collective-permute-start(bf16[32,512]{1,0:T(8,128)(2,1)S(1)} %get-tuple-element.29), channel_id=1, source_target_pairs={{0,2},{2,0},{4,6},{6,4},{8,10},{10,8},{12,14},{14,12},{1,3},{3,1},... | collective-permute-start | bytes 98312 | tf_op jit(solution)/shard_map/ppermute | solution.py:361
  27.2 3.4 %collective-permute-start.9 = (bf16[32,512]{1,0:T(8,128)(2,1)S(1)}, bf16[32,512]{1,0:T(8,128)(2,1)S(1)}, u32[]{:S(2)}, u32[]{:S(2)}) collective-permute-start(bf16[32,512]{1,0:T(8,128)(2,1)S(1)} %get-tuple-element.28.refs_0_), channel_id=1, source_target_pairs={{0,1},{1,0},{2,3},{3,2},{4,5},{5,4},{6,7},{7,6},{8,9},{9,8},{10,11... | collective-permute-start | bytes 98312 | tf_op jit(solution)/shard_map/ppermute | solution.py:364

commit v3 on v2

--- a/solution.py
+++ b/solution.py
@@ -216,18 +216,27 @@
     return jnp.exp(-(rows_off * rows_off + cols_off * cols_off) / (2.0 * SPOT * SPOT))
 
 
-def field_kernel(info_ref, tall_ref, *refs):
+def merge_kernel(mine_ref, near_ref, after_ref, out_ref):
+    del after_ref
+    rows_dev = mine_ref.shape[0]
+    place = own_half()
+    out_ref[pl.ds(pl.multiple_of(place * rows_dev, rows_dev), rows_dev), :] = mine_ref[...]
+    out_ref[pl.ds(pl.multiple_of((1 - place) * rows_dev, rows_dev), rows_dev), :] = near_ref[...]
+
+
+def field_kernel(info_ref, tall_ref, after_ref, *refs):
+    del after_ref
     *sect_refs, field_ref, power_ref, rows_ref = refs
     pairs = tall_ref.shape[0]
-    rows_dev = sect_refs[0].shape[0]
+    count = sect_refs[0].shape[0]
     if len(sect_refs) == 1:
         sect_ref = sect_refs[0]
     else:
         sect_ref = rows_ref
-        me = lax.axis_index("aperture")
+        me = lax.axis_index("aperture") // 2
         for step, ref in enumerate(sect_refs):
-            start = pl.multiple_of((me ^ step) * rows_dev, rows_dev)
-            rows_ref[pl.ds(start, rows_dev), :] = ref[...]
+            start = pl.multiple_of((me ^ step) * count, count)
+            rows_ref[pl.ds(start, count), :] = ref[...]
     sums = []
     for pair in range(pairs):
         lanes = slice(pair * FOCAL, (pair + 1) * FOCAL)
@@ -270,7 +279,8 @@
         other_ref[:, lanes] = back[rows_dev:]
 
 
-def table_kernel(scale, cols, info_ref, width_ref, *refs):
+def table_kernel(scale, cols, info_ref, width_ref, after_ref, *refs):
+    del after_ref
     *out_refs, base_ref, centre_ref = refs
     pairs = base_ref.shape[0]
     table_refs, slope_refs = out_refs[:pairs], out_refs[pairs:]
@@ -327,6 +337,7 @@
 
 VMEM = pl.BlockSpec(memory_space=pltpu.VMEM)
 SMEM = pl.BlockSpec(memory_space=pltpu.SMEM)
+ANY = pl.BlockSpec(memory_space=pl.ANY)
 HBM = pl.BlockSpec(memory_space=pltpu.HBM)
 
 
@@ -391,8 +402,16 @@
         10**9, 10**7,
     )(*(in_hbm(value) for value in (wave_ids, angle_ids, targets, coef_table.T, widths)))
     far_info = to_core(info)
+    tall, flat = call(
+        row_kernel, "row_tables",
+        (shape((pairs_dev, 2 * FOCAL, rows), bf16), shape((pairs_dev, 2 * rows_dev, 2 * FOCAL), bf16)),
+        [VMEM], (VMEM, VMEM), [], 10**8, 10**6,
+    )(info)
     if peers <= DIRECT:
-        sections = [mine] + [exchange(other if step % 2 else mine, step) for step in range(1, peers)]
+        merged = call(
+            merge_kernel, "merge", shape((2 * rows_dev, lanes), bf16), [VMEM, VMEM, ANY], VMEM, [], 10**6, 10**6
+        )(mine, exchange(other, 1), flat)
+        sections = [merged] + [exchange(merged, step) for step in range(2, peers, 2)]
     else:
         even = lax.axis_index("aperture") % 2 == 0
         blocks = jnp.stack([jnp.where(even, mine, other), jnp.where(even, other, mine)])
@@ -400,34 +419,27 @@
         blocks = lax.all_to_all(blocks, "aperture", 0, 0, tiled=True)
         sections = [blocks.reshape(rows, lanes)]
 
-    tall, flat = call(
-        row_kernel, "row_tables",
-        (shape((pairs_dev, 2 * FOCAL, rows), bf16), shape((pairs_dev, 2 * rows_dev, 2 * FOCAL), bf16)),
-        [VMEM], (VMEM, VMEM), [], 10**8, 10**6,
-    )(info)
-
-    def column_tables(info, name):
+    def column_tables(info, after, name):
         outs = [shape((own_cols, 2 * FOCAL), bf16)] * pairs_dev
         outs += [shape((2, rows_dev, own_cols), f32)] * pairs_dev
         got = call(
             functools.partial(table_kernel, math.sqrt(rows * cols), cols), name,
-            outs, [VMEM, VMEM], [VMEM] * len(outs),
+            outs, [VMEM, VMEM, ANY], [VMEM] * len(outs),
             [
                 pltpu.VMEM((pairs_dev, 2, BLOCK, FOCAL), f32),
                 pltpu.VMEM((pairs_dev, 2, own_cols // (2 * BLOCK), FOCAL), f32),
             ],
             10**9, 10**7,
-        )(info, own)
+        )(info, own, after)
         return got[:pairs_dev], got[pairs_dev:]
 
-    tables, slopes = column_tables(info, "own_tables")
-    far_tables, far_slopes = column_tables(far_info, "far_tables")
-
+    tables, slopes = column_tables(info, sections[0], "own_tables")
     field, power = call(
         field_kernel, "field",
         (shape((pairs_dev, 2, FOCAL, HALF), f32), shape((8, HALF), f32)),
-        [VMEM] * (2 + len(sections)), (VMEM, VMEM), [pltpu.VMEM((rows, lanes), bf16)], 10**8, 10**6,
-    )(info, tall, *sections)
+        [VMEM, VMEM, ANY] + [VMEM] * len(sections), (VMEM, VMEM), [pltpu.VMEM((rows, lanes), bf16)], 10**8, 10**6,
+    )(info, tall, slopes[0], *sections)
+    far_tables, far_slopes = column_tables(far_info, power, "far_tables")
     mine, other, scores = call(
         seed_kernel, "seed",
         (shape((rows_dev, lanes), bf16), shape((rows_dev, lanes), bf16), shape((pairs_dev,), f32)),

time: 34.1 us -> 32.3 us (0.947)
  starting transfers between devices: 15 us -> 11.1 us
  waiting for transfers between devices: 3.68 us -> 5.52 us
    ppermute x9 -> x6, starting transfers between devices: 13.8 us -> 10.6 us  [exchange(): lax.ppermute(value, 'aperture', [(index, index ^ step) for index in range...]
    ppermute x9 -> x6, waiting for transfers between devices: 3.68 us -> 5.52 us  [exchange(): lax.ppermute(value, 'aperture', [(index, index ^ step) for index in range...]
    ppermute x2, starting transfers between devices: 1.07 us -> 0.47 us  [to_core(): lax.ppermute(value, 'wave', [(index, (index + 1) % copies) for index in r...]
  transfers between devices with their start and end apart: 12 -> 9, of which waited for: 3 -> 3; matrix products, arithmetic and copies ran while one was open for 0% -> 0% of each run, Pallas kernels for 20% -> 21%
where the time goes in v3:
time: 32.3 us; the launch traced here: 32.2 us
  Pallas kernels  14.8 us (46%)
  starting transfers between devices  11.1 us (34%)
  waiting for transfers between devices  5.52 us (17%)
  between operations  0.72 us (2%)
    ppermute x6, starting transfers between devices, exchange(): lax.ppermute(value, 'aperture', [(index, index ^ step) for index in range...  10.6 us
    ppermute x6, waiting for transfers between devices, exchange(): lax.ppermute(value, 'aperture', [(index, index ^ step) for index in range...  5.52 us
    pallas_call x2, Pallas kernels, column_tables(): call(functools.partial(table_kernel, math.sqrt(rows * cols), cols), name,...  4.78 us
    pallas_call x1, Pallas kernels, on_device(): call(forward_kernel, 'forward', (shape((rows_dev, lanes), bf16), shape((r...  4.67 us
    pallas_call x1, Pallas kernels, on_device(): call(functools.partial(grad_kernel, pairs_dev), 'gradient', shape((rows_d...  3.38 us
    pallas_call x1, Pallas kernels, on_device(): call(row_kernel, 'row_tables', (shape((pairs_dev, 2 * FOCAL, rows), bf16)...  0.96 us
    pallas_call x1, Pallas kernels, on_device(): call(seed_kernel, 'seed', (shape((rows_dev, lanes), bf16), shape((rows_de...  0.66 us
  transfers between devices with their start and end apart: 9, of which 3 were waited for; matrix products, arithmetic and copies ran while one was open for 0% of the time, Pallas kernels for 21%

profile of v3, /device:TPU:0, one launch (start us, length us, event | category | flops | bytes accessed | tf_op | source)
XLA Modules:
  0.0 32.2 jit_solution(10305887719366423071)
XLA Ops:
  0.6 4.7 %forward.1 = (bf16[32,512]{1,0:T(8,128)(2,1)S(1)}, bf16[32,512]{1,0:T(8,128)(2,1)S(1)}, f32[2,24,256]{2,1,0:T(8,128)S(1)}, f32[32,2048]{1,0:T(8,128)S(1)}) custom-call(s32[2]{0:T(128)} %wave_hbm.1, s32[2]{0:T(128)} %angle_hbm.1, s32[2,2]{1,0:T(2,128)} %aim_hbm.1, f32[16,256]{1,0:T(8,128)} %bitcast.1, f32[32,4096]{1,0:T(8,128)} %width_hbm.1), custom_call_target="tpu_custom_call" | custom-call | flops 1000000000 | bytes 10000000 | tf_op jit(solution)/shard_map/forward/pallas_call | solution.py:384
  5.3 3.0 %collective-permute-start = (bf16[32,512]{1,0:T(8,128)(2,1)S(1)}, bf16[32,512]{1,0:T(8,128)(2,1)S(1)}, u32[]{:S(2)}, u32[]{:S(2)}) collective-permute-start(bf16[32,512]{1,0:T(8,128)(2,1)S(1)} %get-tuple-element.25), channel_id=1, source_target_pairs={{0,2},{2,0},{4,6},{6,4},{8,10},{10,8},{12,14},{14,12},{1,3},{3,1},... | collective-permute-start | bytes 98312 | tf_op jit(solution)/shard_map/ppermute | solution.py:372
  8.3 0.0 collective-permute-start.8
  8.3 1.0 %row_tables.1 = (bf16[2,512,256]{2,1,0:T(8,128)(2,1)S(1)}, bf16[2,64,512]{2,1,0:T(8,128)(2,1)S(1)}) custom-call(f32[2,24,256]{2,1,0:T(8,128)S(1)} %get-tuple-element.21.info_ref), custom_call_target="tpu_custom_call" | custom-call | flops 100000000 | bytes 1000000 | tf_op jit(solution)/shard_map/row_tables/pallas_call | solution.py:405
  9.3 0.9 %collective-permute-done.near_ref = bf16[32,512]{1,0:T(8,128)(2,1)S(1)} collective-permute-done((bf16[32,512]{1,0:T(8,128)(2,1)S(1)}, bf16[32,512]{1,0:T(8,128)(2,1)S(1)}, u32[]{:S(2)}, u32[]{:S(2)}) %collective-permute-start) | collective-permute-done | bytes 32800 | tf_op jit(solution)/shard_map/ppermute | solution.py:372
  10.2 4.2 %collective-permute-start.3 = (bf16[64,512]{1,0:T(8,128)(2,1)S(1)}, bf16[64,512]{1,0:T(8,128)(2,1)S(1)}, u32[]{:S(2)}, u32[]{:S(2)}) collective-permute-start(bf16[64,512]{1,0:T(8,128)(2,1)S(1)} %merge.1.after_ref.refs_0_), channel_id=1, source_target_pairs={{0,12},{2,14},{4,8},{6,10},{8,4},{10,6},{12,0},{14,2},{1,13},{3,15... | collective-permute-start | bytes 196616 | tf_op jit(solution)/shard_map/ppermute | solution.py:372
  14.4 0.0 collective-permute-start.2
  14.4 0.6 %collective-permute-start.1 = (bf16[64,512]{1,0:T(8,128)(2,1)S(1)}, bf16[64,512]{1,0:T(8,128)(2,1)S(1)}, u32[]{:S(2)}, u32[]{:S(2)}) collective-permute-start(bf16[64,512]{1,0:T(8,128)(2,1)S(1)} %merge.1.after_ref.refs_0_), channel_id=1, source_target_pairs={{0,4},{2,6},{4,0},{6,2},{8,12},{10,14},{12,8},{14,10},{1,5},{3,7},... | collective-permute-start | bytes 196616 | tf_op jit(solution)/shard_map/ppermute | solution.py:372
  15.1 2.4 %own_tables.1 = (bf16[2048,512]{1,0:T(8,128)(2,1)S(1)}, bf16[2048,512]{1,0:T(8,128)(2,1)S(1)}, f32[2,32,2048]{2,1,0:T(8,128)S(1)}, f32[2,32,2048]{2,1,0:T(8,128)S(1)}) custom-call(f32[2,24,256]{2,1,0:T(8,128)S(1)} %get-tuple-element.21.info_ref, f32[32,2048]{1,0:T(8,128)S(1)} %get-tuple-element.23.width_ref, bf16[64,512]{1,0:T(8,128)(2,1)S(1)} %merge.1.after_ref.refs_0_), custom_call_target="tpu_custom_call" | custom-call | flops 1000000000 | bytes 10000000 | tf_op jit(solution)/shard_map/own_tables/pallas_call | solution.py:425
  17.5 0.0 collective-permute-done.3.refs_3_
  17.5 2.3 %collective-permute-done.2.refs_2_ = bf16[64,512]{1,0:T(8,128)(2,1)S(1)} collective-permute-done((bf16[64,512]{1,0:T(8,128)(2,1)S(1)}, bf16[64,512]{1,0:T(8,128)(2,1)S(1)}, u32[]{:S(2)}, u32[]{:S(2)}) %collective-permute-start.2) | collective-permute-done | bytes 65568 | tf_op jit(solution)/shard_map/ppermute | solution.py:372
  19.8 0.0 collective-permute-done.1.refs_1_
  19.8 0.3 %field.1 = (f32[2,2,256,128]{3,2,1,0:T(8,128)S(1)}, f32[8,128]{1,0:T(8,128)S(1)}) custom-call(f32[2,24,256]{2,1,0:T(8,128)S(1)} %get-tuple-element.21.info_ref, bf16[2,512,256]{2,1,0:T(8,128)(2,1)S(1)} %get-tuple-element.22.tall_ref, f32[2,32,2048]{2,1,0:T(8,128)S(1)} %get-tuple-element.27.after_ref.refs_8_, bf16[64,512]{1,0:T(8,128)(2,1)S(1)} %merge.1.after_ref.refs_0_, ...), custom_call_target="tpu_custom_call" | custom-call | flops 100000000 | bytes 1000000 | tf_op jit(solution)/shard_map/field/pallas_call | solution.py:437
  20.1 1.4 %collective-permute-start.4 = (f32[8,128]{1,0:T(8,128)S(1)}, f32[8,128]{1,0:T(8,128)S(1)}, u32[]{:S(2)}, u32[]{:S(2)}) collective-permute-start(f32[8,128]{1,0:T(8,128)S(1)} %get-tuple-element.28.power_ref.after_ref), channel_id=1, source_target_pairs={{0,2},{2,0},{4,6},{6,4},{8,10},{10,8},{12,14},{14,12},{1,3},{3,1},... | collective-permute-start | bytes 12296 | tf_op jit(solution)/shard_map/ppermute | solution.py:372
  21.5 2.3 %collective-permute-done.4.far_ref = f32[8,128]{1,0:T(8,128)S(1)} collective-permute-done((f32[8,128]{1,0:T(8,128)S(1)}, f32[8,128]{1,0:T(8,128)S(1)}, u32[]{:S(2)}, u32[]{:S(2)}) %collective-permute-start.4) | collective-permute-done | bytes 4128 | tf_op jit(solution)/shard_map/ppermute | solution.py:372
  23.8 0.7 %seed.1 = (bf16[32,512]{1,0:T(8,128)(2,1)S(1)}, bf16[32,512]{1,0:T(8,128)(2,1)S(1)}, f32[2]{0:T(128)}) custom-call(f32[2,24,256]{2,1,0:T(8,128)S(1)} %get-tuple-element.21.info_ref, f32[8,128]{1,0:T(8,128)S(1)} %get-tuple-element.28.power_ref.after_ref, f32[8,128]{1,0:T(8,128)S(1)} %collective-permute-done.4.far_ref, ...), custom_call_target="tpu_custom_call" | custom-call | flops 100000000 | bytes 1000000 | tf_op jit(solution)/shard_map/seed/pallas_call | solution.py:443
  24.5 0.1 collective-permute-start.7
  24.5 1.4 %collective-permute-start.5 = (bf16[32,512]{1,0:T(8,128)(2,1)S(1)}, bf16[32,512]{1,0:T(8,128)(2,1)S(1)}, u32[]{:S(2)}, u32[]{:S(2)}) collective-permute-start(bf16[32,512]{1,0:T(8,128)(2,1)S(1)} %get-tuple-element.31), channel_id=1, source_target_pairs={{0,2},{2,0},{4,6},{6,4},{8,10},{10,8},{12,14},{14,12},{1,3},{3,1},... | collective-permute-start | bytes 98312 | tf_op jit(solution)/shard_map/ppermute | solution.py:372
  25.9 0.5 %collective-permute-start.6 = (bf16[32,512]{1,0:T(8,128)(2,1)S(1)}, bf16[32,512]{1,0:T(8,128)(2,1)S(1)}, u32[]{:S(2)}, u32[]{:S(2)}) collective-permute-start(bf16[32,512]{1,0:T(8,128)(2,1)S(1)} %get-tuple-element.30.refs_0_), channel_id=1, source_target_pairs={{0,1},{1,0},{2,3},{3,2},{4,5},{5,4},{6,7},{7,6},{8,9},{9,8},{10,11... | collective-permute-start | bytes 98312 | tf_op jit(solution)/shard_map/ppermute | solution.py:375
  26.4 0.0 collective-permute-done.8.info_ref
  26.4 2.4 %far_tables.1 = (bf16[2048,512]{1,0:T(8,128)(2,1)S(1)}, bf16[2048,512]{1,0:T(8,128)(2,1)S(1)}, f32[2,32,2048]{2,1,0:T(8,128)S(1)}, f32[2,32,2048]{2,1,0:T(8,128)S(1)}) custom-call(f32[2,24,256]{2,1,0:T(8,128)S(1)} %collective-permute-done.8.info_ref, f32[32,2048]{1,0:T(8,128)S(1)} %get-tuple-element.23.width_ref, ...), custom_call_target="tpu_custom_call" | custom-call | flops 1000000000 | bytes 10000000 | tf_op jit(solution)/shard_map/far_tables/pallas_call | solution.py:425
  28.8 0.0 collective-permute-done.6.refs_2_
  28.8 0.0 collective-permute-done.7.refs_3_
  28.8 0.0 collective-permute-done.5.refs_1_
  28.8 3.4 %gradient.1 = f32[32,2048]{1,0:T(8,128)} custom-call(bf16[32,512]{1,0:T(8,128)(2,1)S(1)} %get-tuple-element.30.refs_0_, bf16[32,512]{1,0:T(8,128)(2,1)S(1)} %collective-permute-done.5.refs_1_, bf16[32,512]{1,0:T(8,128)(2,1)S(1)} %collective-permute-done.6.refs_2_, bf16[32,512]{1,0:T(8,128)(2,1)S(1)} %collective-permute-done.7.refs_3_, ...), custom_call_target="tpu_custom_call" | custom-call | flops 1000000000 | bytes 10000000 | tf_op jit(solution)/shard_map/gradient/pallas_call | solution.py:450
  (1 shorter events, 0.0 us)
Async XLA Ops:
  5.3 4.9 %collective-permute-start = (bf16[32,512]{1,0:T(8,128)(2,1)S(1)}, bf16[32,512]{1,0:T(8,128)(2,1)S(1)}, u32[]{:S(2)}, u32[]{:S(2)}) collective-permute-start(bf16[32,512]{1,0:T(8,128)(2,1)S(1)} %get-tuple-element.25), channel_id=1, source_target_pairs={{0,2},{2,0},{4,6},{6,4},{8,10},{10,8},{12,14},{14,12},{1,3},{3,1},... | collective-permute-start | bytes 98312 | tf_op jit(solution)/shard_map/ppermute | solution.py:372
  8.3 18.1 %collective-permute-start.8 = (f32[2,24,256]{2,1,0:T(8,128)S(1)}, f32[2,24,256]{2,1,0:T(8,128)S(1)}, u32[]{:S(2)}, u32[]{:S(2)}) collective-permute-start(f32[2,24,256]{2,1,0:T(8,128)S(1)} %get-tuple-element.21.info_ref), channel_id=1, source_target_pairs={{0,1},{1,0},{2,3},{3,2},{4,5},{5,4},{6,7},{7,6},{8,9},{9,8},{10,11... | collective-permute-start | bytes 147464 | tf_op jit(solution)/shard_map/ppermute | solution.py:375
  10.2 7.2 %collective-permute-start.3 = (bf16[64,512]{1,0:T(8,128)(2,1)S(1)}, bf16[64,512]{1,0:T(8,128)(2,1)S(1)}, u32[]{:S(2)}, u32[]{:S(2)}) collective-permute-start(bf16[64,512]{1,0:T(8,128)(2,1)S(1)} %merge.1.after_ref.refs_0_), channel_id=1, source_target_pairs={{0,12},{2,14},{4,8},{6,10},{8,4},{10,6},{12,0},{14,2},{1,13},{3,15... | collective-permute-start | bytes 196616 | tf_op jit(solution)/shard_map/ppermute | solution.py:372
  14.4 5.4 %collective-permute-start.2 = (bf16[64,512]{1,0:T(8,128)(2,1)S(1)}, bf16[64,512]{1,0:T(8,128)(2,1)S(1)}, u32[]{:S(2)}, u32[]{:S(2)}) collective-permute-start(bf16[64,512]{1,0:T(8,128)(2,1)S(1)} %merge.1.after_ref.refs_0_), channel_id=1, source_target_pairs={{0,8},{2,10},{4,12},{6,14},{8,0},{10,2},{12,4},{14,6},{1,9},{3,11}... | collective-permute-start | bytes 196616 | tf_op jit(solution)/shard_map/ppermute | solution.py:372
  14.4 5.4 %collective-permute-start.1 = (bf16[64,512]{1,0:T(8,128)(2,1)S(1)}, bf16[64,512]{1,0:T(8,128)(2,1)S(1)}, u32[]{:S(2)}, u32[]{:S(2)}) collective-permute-start(bf16[64,512]{1,0:T(8,128)(2,1)S(1)} %merge.1.after_ref.refs_0_), channel_id=1, source_target_pairs={{0,4},{2,6},{4,0},{6,2},{8,12},{10,14},{12,8},{14,10},{1,5},{3,7},... | collective-permute-start | bytes 196616 | tf_op jit(solution)/shard_map/ppermute | solution.py:372
  20.1 3.7 %collective-permute-start.4 = (f32[8,128]{1,0:T(8,128)S(1)}, f32[8,128]{1,0:T(8,128)S(1)}, u32[]{:S(2)}, u32[]{:S(2)}) collective-permute-start(f32[8,128]{1,0:T(8,128)S(1)} %get-tuple-element.28.power_ref.after_ref), channel_id=1, source_target_pairs={{0,2},{2,0},{4,6},{6,4},{8,10},{10,8},{12,14},{14,12},{1,3},{3,1},... | collective-permute-start | bytes 12296 | tf_op jit(solution)/shard_map/ppermute | solution.py:372
  24.5 4.3 %collective-permute-start.7 = (bf16[32,512]{1,0:T(8,128)(2,1)S(1)}, bf16[32,512]{1,0:T(8,128)(2,1)S(1)}, u32[]{:S(2)}, u32[]{:S(2)}) collective-permute-start(bf16[32,512]{1,0:T(8,128)(2,1)S(1)} %get-tuple-element.31), channel_id=1, source_target_pairs={{0,3},{1,2},{2,1},{3,0},{4,7},{5,6},{6,5},{7,4},{8,11},{9,10},{10,... | collective-permute-start | bytes 98312 | tf_op jit(solution)/shard_map/ppermute | solution.py:382
  24.5 4.3 %collective-permute-start.5 = (bf16[32,512]{1,0:T(8,128)(2,1)S(1)}, bf16[32,512]{1,0:T(8,128)(2,1)S(1)}, u32[]{:S(2)}, u32[]{:S(2)}) collective-permute-start(bf16[32,512]{1,0:T(8,128)(2,1)S(1)} %get-tuple-element.31), channel_id=1, source_target_pairs={{0,2},{2,0},{4,6},{6,4},{8,10},{10,8},{12,14},{14,12},{1,3},{3,1},... | collective-permute-start | bytes 98312 | tf_op jit(solution)/shard_map/ppermute | solution.py:372
  25.9 2.9 %collective-permute-start.6 = (bf16[32,512]{1,0:T(8,128)(2,1)S(1)}, bf16[32,512]{1,0:T(8,128)(2,1)S(1)}, u32[]{:S(2)}, u32[]{:S(2)}) collective-permute-start(bf16[32,512]{1,0:T(8,128)(2,1)S(1)} %get-tuple-element.30.refs_0_), channel_id=1, source_target_pairs={{0,1},{1,0},{2,3},{3,2},{4,5},{5,4},{6,7},{7,6},{8,9},{9,8},{10,11... | collective-permute-start | bytes 98312 | tf_op jit(solution)/shard_map/ppermute | solution.py:375

commit v4 on v3

--- a/solution.py
+++ b/solution.py
@@ -253,7 +253,10 @@
     power_ref[...] = jnp.concatenate(sums, axis=0)
 
 
-def seed_kernel(info_ref, power_ref, far_ref, field_ref, flat_ref, mine_ref, other_ref, score_ref):
+def seed_kernel(
+    info_ref, power_ref, far_ref, field_ref, flat_ref, after_ref, mine_ref, other_ref, score_ref
+):
+    del after_ref
     rows_dev = mine_ref.shape[0]
     pairs = flat_ref.shape[0]
     sums = jnp.sum(power_ref[...] + far_ref[...], axis=1, keepdims=True)
@@ -281,7 +284,7 @@
 
 def table_kernel(scale, cols, info_ref, width_ref, after_ref, *refs):
     del after_ref
-    *out_refs, base_ref, centre_ref = refs
+    *out_refs, base_ref, centre_ref, turned_ref = refs
     pairs = base_ref.shape[0]
     table_refs, slope_refs = out_refs[:pairs], out_refs[pairs:]
     own_cols = width_ref.shape[1]
@@ -291,14 +294,24 @@
     for pair in range(pairs):
         freq = column_freq(info_ref, pair, own_half() * HALF)
         fill_base(freq, shift, period, base_ref.at[pair], centre_ref.at[pair])
+        for part in range(2):
+            turned_ref[pair, part] = base_ref[pair, part].T
+    centres = [[centre_ref[pair, part].T for part in range(2)] for pair in range(pairs)]
     for index in range(own_cols // (2 * BLOCK)):
         left = middle - (index + 1) * BLOCK
         right = middle + index * BLOCK
         for pair in range(pairs):
-            tables = block_pair(base_ref.at[pair], centre_ref.at[pair], index)
-            for start, table in zip((left, right), tables):
-                table_refs[pair][start : start + BLOCK, :FOCAL] = table[0]
-                table_refs[pair][start : start + BLOCK, FOCAL:] = table[1]
+            cent_r, cent_i = (centre[:, index : index + 1] for centre in centres[pair])
+            for half in range(2):
+                lines = slice(half * HALF, (half + 1) * HALF)
+                one_r, one_i = cent_r[lines], cent_i[lines]
+                base_r, base_i = turned_ref[pair, 0, lines, :], turned_ref[pair, 1, lines, :]
+                rr, ii = base_r * one_r, base_i * one_i
+                ri, ir = base_r * one_i, base_i * one_r
+                for start, values in ((left, (rr + ii, ir - ri)), (right, (rr - ii, ir + ri))):
+                    for part, value in enumerate(values):
+                        row = (2 * half + part) * HALF
+                        table_refs[pair][row : row + HALF, start : start + BLOCK] = value.astype(jnp.bfloat16)
         for start in (left, right):
             slopes = near_slopes(width_ref[:, start : start + BLOCK], scale, info_ref, pairs)
             for pair in range(pairs):
@@ -306,33 +319,29 @@
                 slope_refs[pair][1, :, start : start + BLOCK] = slopes[pair][1]
 
 
-def grad_kernel(pairs_dev, *refs):
-    *in_refs, out_ref, left_ref = refs
+def grad_kernel(pairs, half, back_ref, *refs):
+    *in_refs, out_ref = refs
+    table_refs, slope_refs, total_ref = in_refs[:pairs], in_refs[pairs : 2 * pairs], in_refs[2 * pairs :]
     rows_dev, own_cols = out_ref.shape
-    pairs = left_ref.shape[0]
-    back_refs, in_refs = in_refs[: 2 * pairs // pairs_dev], in_refs[2 * pairs // pairs_dev :]
-    table_refs, slope_refs = in_refs[:pairs], in_refs[pairs:]
-    for pair in range(pairs):
-        halves = back_refs[2 * (pair // pairs_dev) : 2 * (pair // pairs_dev) + 2]
-        for half, ref in enumerate(halves):
-            lane = (pair % pairs_dev) * FOCAL
-            real, imag = ref[:, lane : lane + HALF], ref[:, lane + HALF : lane + FOCAL]
-            for part, rows, value in ((0, 0, real), (1, 0, imag), (0, 1, imag), (1, 1, -real)):
-                start = part * FOCAL + half * HALF
-                left_ref[pair, rows * rows_dev : (rows + 1) * rows_dev, start : start + HALF] = value
+    lefts = []
+    for pair in range(pairs):
+        lane = pair * FOCAL
+        real, imag = back_ref[:, lane : lane + HALF], back_ref[:, lane + HALF : lane + FOCAL]
+        lefts.append(
+            jnp.concatenate(
+                [jnp.concatenate([real, imag], axis=1), jnp.concatenate([imag, -real], axis=1)], axis=0
+            )
+        )
     size = 2 * BLOCK
+    lines = slice(half * FOCAL, (half + 1) * FOCAL)
     for start in range(0, own_cols, size):
-        total = jnp.zeros((rows_dev, size), jnp.float32)
+        place = slice(start, start + size)
+        total = total_ref[0][:, place] if total_ref else jnp.zeros((rows_dev, size), jnp.float32)
         for pair in range(pairs):
-            grad = lax.dot_general(
-                left_ref[pair],
-                table_refs[pair][start : start + size, :],
-                (((1,), (1,)), ((), ())),
-                preferred_element_type=jnp.float32,
-            )
-            total += grad[:rows_dev] * slope_refs[pair][0, :, start : start + size]
-            total += grad[rows_dev:] * slope_refs[pair][1, :, start : start + size]
-        out_ref[:, start : start + size] = total
+            grad = jnp.dot(lefts[pair], table_refs[pair][lines, place], preferred_element_type=jnp.float32)
+            total += grad[:rows_dev] * slope_refs[pair][0, :, place]
+            total += grad[rows_dev:] * slope_refs[pair][1, :, place]
+        out_ref[:, place] = total
 
 
 VMEM = pl.BlockSpec(memory_space=pltpu.VMEM)
@@ -373,13 +382,6 @@
 
     def to_core(value):
         return lax.ppermute(value, "wave", [(index, (index + 1) % copies) for index in range(copies)])
-
-    def to_corner(value):
-        places = [(index, core) for index in range(peers) for core in range(copies)]
-        pairs = [
-            (index * copies + core, (index ^ 1) * copies + (core + 1) % copies) for index, core in places
-        ]
-        return lax.ppermute(value, ("aperture", "wave"), pairs)
 
     mine, other, info, own = call(
         forward_kernel, "forward",
@@ -420,7 +422,7 @@
         sections = [blocks.reshape(rows, lanes)]
 
     def column_tables(info, after, name):
-        outs = [shape((own_cols, 2 * FOCAL), bf16)] * pairs_dev
+        outs = [shape((2 * FOCAL, own_cols), bf16)] * pairs_dev
         outs += [shape((2, rows_dev, own_cols), f32)] * pairs_dev
         got = call(
             functools.partial(table_kernel, math.sqrt(rows * cols), cols), name,
@@ -428,6 +430,7 @@
             [
                 pltpu.VMEM((pairs_dev, 2, BLOCK, FOCAL), f32),
                 pltpu.VMEM((pairs_dev, 2, own_cols // (2 * BLOCK), FOCAL), f32),
+                pltpu.VMEM((pairs_dev, 2, FOCAL, BLOCK), f32),
             ],
             10**9, 10**7,
         )(info, own, after)
@@ -443,16 +446,23 @@
     mine, other, scores = call(
         seed_kernel, "seed",
         (shape((rows_dev, lanes), bf16), shape((rows_dev, lanes), bf16), shape((pairs_dev,), f32)),
-        [VMEM] * 5, (VMEM, VMEM, SMEM), [], 10**8, 10**6,
-    )(info, power, exchange(power, 1), field, flat)
-    backs = [mine, exchange(other, 1), to_core(mine), to_corner(other)]
-    ins = [*backs, *tables, *far_tables, *slopes, *far_slopes]
-    grad = call(
-        functools.partial(grad_kernel, pairs_dev), "gradient",
-        shape((rows_dev, own_cols), f32), [VMEM] * len(ins), VMEM,
-        [pltpu.VMEM((copies * pairs_dev, 2 * rows_dev, 2 * FOCAL), bf16)],
-        10**9, 10**7,
-    )(*ins)
+        [VMEM] * 5 + [ANY], (VMEM, VMEM, SMEM), [], 10**8, 10**6,
+    )(info, power, exchange(power, 1), field, flat, far_slopes[0])
+
+    def add_grad(back, half, tables, slopes, name, *total):
+        ins = [back, *tables, *slopes, *total]
+        return call(
+            functools.partial(grad_kernel, pairs_dev, half), name,
+            shape((rows_dev, own_cols), f32), [VMEM] * len(ins), VMEM, [], 10**9, 10**7,
+        )(*ins)
+
+    from_core = to_core(mine)
+    from_near = exchange(other, 1)
+    grad = add_grad(mine, 0, tables, slopes, "gradient_own")
+    grad = add_grad(from_core, 0, far_tables, far_slopes, "gradient_core", grad)
+    from_near, grad = lax.optimization_barrier((from_near, grad))
+    grad = add_grad(from_near, 1, tables, slopes, "gradient_near", grad)
+    grad = add_grad(to_core(from_near), 1, far_tables, far_slopes, "gradient_last", grad)
     return grad, scores
 
 

time: 32.3 us -> 32.4 us (level)
  waiting for transfers between devices: 5.52 us -> 7.02 us
  Pallas kernels: 14.8 us -> 13.5 us
    ppermute x6, waiting for transfers between devices: 5.52 us -> 6.32 us  [exchange(): lax.ppermute(value, 'aperture', [(index, index ^ step) for index in range...]
    ppermute x2 -> x3, waiting for transfers between devices: 0.01 us -> 0.7 us  [to_core(): lax.ppermute(value, 'wave', [(index, (index + 1) % copies) for index in r...]
    pallas_call x1 -> x4, Pallas kernels: 3.38 us -> 2.71 us  [add_grad(): call(functools.partial(grad_kernel, pairs_dev, half), name, shape((rows_d...]
    pallas_call x2, Pallas kernels: 4.78 us -> 4.16 us  [column_tables(): call(functools.partial(table_kernel, math.sqrt(rows * cols), cols), name,...]
    ppermute x2 -> x3, starting transfers between devices: 0.47 us -> 0.08 us  [to_core(): lax.ppermute(value, 'wave', [(index, (index + 1) % copies) for index in r...]
  transfers between devices with their start and end apart: 9 -> 9, of which waited for: 3 -> 5; matrix products, arithmetic and copies ran while one was open for 0% -> 0% of each run, Pallas kernels for 21% -> 22%
where the time goes in v4:
time: 32.4 us; the launch traced here: 32.2 us
  Pallas kernels  13.5 us (42%)
  starting transfers between devices  10.9 us (34%)
  waiting for transfers between devices  7.02 us (22%)
  between operations  0.72 us (2%)
    ppermute x6, starting transfers between devices, exchange(): lax.ppermute(value, 'aperture', [(index, index ^ step) for index in range...  10.9 us
    ppermute x6, waiting for transfers between devices, exchange(): lax.ppermute(value, 'aperture', [(index, index ^ step) for index in range...  6.32 us
    pallas_call x1, Pallas kernels, on_device(): call(forward_kernel, 'forward', (shape((rows_dev, lanes), bf16), shape((r...  4.67 us
    pallas_call x2, Pallas kernels, column_tables(): call(functools.partial(table_kernel, math.sqrt(rows * cols), cols), name,...  4.16 us
    pallas_call x4, Pallas kernels, add_grad(): call(functools.partial(grad_kernel, pairs_dev, half), name, shape((rows_d...  2.71 us
    pallas_call x1, Pallas kernels, on_device(): call(row_kernel, 'row_tables', (shape((pairs_dev, 2 * FOCAL, rows), bf16)...  0.96 us
    ppermute x3, waiting for transfers between devices, to_core(): lax.ppermute(value, 'wave', [(index, (index + 1) % copies) for index in r...  0.7 us
    pallas_call x1, Pallas kernels, on_device(): call(seed_kernel, 'seed', (shape((rows_dev, lanes), bf16), shape((rows_de...  0.66 us
  transfers between devices with their start and end apart: 9, of which 5 were waited for; matrix products, arithmetic and copies ran while one was open for 0% of the time, Pallas kernels for 22%

profile of v4, /device:TPU:0, one launch (start us, length us, event | category | flops | bytes accessed | tf_op | source)
XLA Modules:
  0.0 32.2 jit_solution(9336326998075650721)
XLA Ops:
  0.6 4.7 %forward.1 = (bf16[32,512]{1,0:T(8,128)(2,1)S(1)}, bf16[32,512]{1,0:T(8,128)(2,1)S(1)}, f32[2,24,256]{2,1,0:T(8,128)S(1)}, f32[32,2048]{1,0:T(8,128)S(1)}) custom-call(s32[2]{0:T(128)} %wave_hbm.1, s32[2]{0:T(128)} %angle_hbm.1, s32[2,2]{1,0:T(2,128)} %aim_hbm.1, f32[16,256]{1,0:T(8,128)} %bitcast.1, f32[32,4096]{1,0:T(8,128)} %width_hbm.1), custom_call_target="tpu_custom_call" | custom-call | flops 1000000000 | bytes 10000000 | tf_op jit(solution)/shard_map/forward/pallas_call | solution.py:386
  5.3 3.0 %collective-permute-start = (bf16[32,512]{1,0:T(8,128)(2,1)S(1)}, bf16[32,512]{1,0:T(8,128)(2,1)S(1)}, u32[]{:S(2)}, u32[]{:S(2)}) collective-permute-start(bf16[32,512]{1,0:T(8,128)(2,1)S(1)} %get-tuple-element.27), channel_id=1, source_target_pairs={{0,2},{2,0},{4,6},{6,4},{8,10},{10,8},{12,14},{14,12},{1,3},{3,1},... | collective-permute-start | bytes 98312 | tf_op jit(solution)/shard_map/ppermute | solution.py:381
  8.3 0.0 collective-permute-start.5
  8.3 1.0 %row_tables.1 = (bf16[2,512,256]{2,1,0:T(8,128)(2,1)S(1)}, bf16[2,64,512]{2,1,0:T(8,128)(2,1)S(1)}) custom-call(f32[2,24,256]{2,1,0:T(8,128)S(1)} %get-tuple-element.23.info_ref), custom_call_target="tpu_custom_call" | custom-call | flops 100000000 | bytes 1000000 | tf_op jit(solution)/shard_map/row_tables/pallas_call | solution.py:407
  9.3 0.9 %collective-permute-done.near_ref = bf16[32,512]{1,0:T(8,128)(2,1)S(1)} collective-permute-done((bf16[32,512]{1,0:T(8,128)(2,1)S(1)}, bf16[32,512]{1,0:T(8,128)(2,1)S(1)}, u32[]{:S(2)}, u32[]{:S(2)}) %collective-permute-start) | collective-permute-done | bytes 32800 | tf_op jit(solution)/shard_map/ppermute | solution.py:381
  10.2 2.2 %collective-permute-start.1 = (bf16[64,512]{1,0:T(8,128)(2,1)S(1)}, bf16[64,512]{1,0:T(8,128)(2,1)S(1)}, u32[]{:S(2)}, u32[]{:S(2)}) collective-permute-start(bf16[64,512]{1,0:T(8,128)(2,1)S(1)} %merge.1.after_ref.refs_0_), channel_id=1, source_target_pairs={{0,4},{2,6},{4,0},{6,2},{8,12},{10,14},{12,8},{14,10},{1,5},{3,7},... | collective-permute-start | bytes 196616 | tf_op jit(solution)/shard_map/ppermute | solution.py:381
  12.4 2.6 %collective-permute-start.2 = (bf16[64,512]{1,0:T(8,128)(2,1)S(1)}, bf16[64,512]{1,0:T(8,128)(2,1)S(1)}, u32[]{:S(2)}, u32[]{:S(2)}) collective-permute-start(bf16[64,512]{1,0:T(8,128)(2,1)S(1)} %merge.1.after_ref.refs_0_), channel_id=1, source_target_pairs={{0,8},{2,10},{4,12},{6,14},{8,0},{10,2},{12,4},{14,6},{1,9},{3,11}... | collective-permute-start | bytes 196616 | tf_op jit(solution)/shard_map/ppermute | solution.py:381
  15.0 0.0 collective-permute-start.3
  15.0 2.1 %own_tables.1 = (bf16[512,2048]{1,0:T(8,128)(2,1)S(1)}, bf16[512,2048]{1,0:T(8,128)(2,1)S(1)}, f32[2,32,2048]{2,1,0:T(8,128)S(1)}, f32[2,32,2048]{2,1,0:T(8,128)S(1)}) custom-call(f32[2,24,256]{2,1,0:T(8,128)S(1)} %get-tuple-element.23.info_ref, f32[32,2048]{1,0:T(8,128)S(1)} %get-tuple-element.25.width_ref, bf16[64,512]{1,0:T(8,128)(2,1)S(1)} %merge.1.after_ref.refs_0_), custom_call_target="tpu_custom_call" | custom-call | flops 1000000000 | bytes 10000000 | tf_op jit(solution)/shard_map/own_tables/pallas_call | solution.py:427
  17.1 0.0 collective-permute-done.1.refs_1_
  17.1 1.9 %collective-permute-done.2.refs_2_ = bf16[64,512]{1,0:T(8,128)(2,1)S(1)} collective-permute-done((bf16[64,512]{1,0:T(8,128)(2,1)S(1)}, bf16[64,512]{1,0:T(8,128)(2,1)S(1)}, u32[]{:S(2)}, u32[]{:S(2)}) %collective-permute-start.2) | collective-permute-done | bytes 65568 | tf_op jit(solution)/shard_map/ppermute | solution.py:381
  19.0 2.1 %collective-permute-done.3.refs_3_ = bf16[64,512]{1,0:T(8,128)(2,1)S(1)} collective-permute-done((bf16[64,512]{1,0:T(8,128)(2,1)S(1)}, bf16[64,512]{1,0:T(8,128)(2,1)S(1)}, u32[]{:S(2)}, u32[]{:S(2)}) %collective-permute-start.3) | collective-permute-done | bytes 65568 | tf_op jit(solution)/shard_map/ppermute | solution.py:381
  21.0 0.3 %field.1 = (f32[2,2,256,128]{3,2,1,0:T(8,128)S(1)}, f32[8,128]{1,0:T(8,128)S(1)}) custom-call(f32[2,24,256]{2,1,0:T(8,128)S(1)} %get-tuple-element.23.info_ref, bf16[2,512,256]{2,1,0:T(8,128)(2,1)S(1)} %get-tuple-element.24.tall_ref, f32[2,32,2048]{2,1,0:T(8,128)S(1)} %get-tuple-element.29.after_ref.refs_2_, bf16[64,512]{1,0:T(8,128)(2,1)S(1)} %merge.1.after_ref.refs_0_, ...), custom_call_target="tpu_custom_call" | custom-call | flops 100000000 | bytes 1000000 | tf_op jit(solution)/shard_map/field/pallas_call | solution.py:440
  21.4 1.6 %collective-permute-start.4 = (f32[8,128]{1,0:T(8,128)S(1)}, f32[8,128]{1,0:T(8,128)S(1)}, u32[]{:S(2)}, u32[]{:S(2)}) collective-permute-start(f32[8,128]{1,0:T(8,128)S(1)} %get-tuple-element.30.after_ref.power_ref), channel_id=1, source_target_pairs={{0,2},{2,0},{4,6},{6,4},{8,10},{10,8},{12,14},{14,12},{1,3},{3,1},... | collective-permute-start | bytes 12296 | tf_op jit(solution)/shard_map/ppermute | solution.py:381
  22.9 0.0 collective-permute-done.5.info_ref
  23.0 2.1 %far_tables.1 = (bf16[512,2048]{1,0:T(8,128)(2,1)S(1)}, bf16[512,2048]{1,0:T(8,128)(2,1)S(1)}, f32[2,32,2048]{2,1,0:T(8,128)S(1)}, f32[2,32,2048]{2,1,0:T(8,128)S(1)}) custom-call(f32[2,24,256]{2,1,0:T(8,128)S(1)} %collective-permute-done.5.info_ref, f32[32,2048]{1,0:T(8,128)S(1)} %get-tuple-element.25.width_ref, ...), custom_call_target="tpu_custom_call" | custom-call | flops 1000000000 | bytes 10000000 | tf_op jit(solution)/shard_map/far_tables/pallas_call | solution.py:427
  25.0 0.0 collective-permute-done.4.far_ref
  25.1 0.7 %seed.1 = (bf16[32,512]{1,0:T(8,128)(2,1)S(1)}, bf16[32,512]{1,0:T(8,128)(2,1)S(1)}, f32[2]{0:T(128)}) custom-call(f32[2,24,256]{2,1,0:T(8,128)S(1)} %get-tuple-element.23.info_ref, f32[8,128]{1,0:T(8,128)S(1)} %get-tuple-element.30.after_ref.power_ref, f32[8,128]{1,0:T(8,128)S(1)} %collective-permute-done.4.far_ref, ...), custom_call_target="tpu_custom_call" | custom-call | flops 100000000 | bytes 1000000 | tf_op jit(solution)/shard_map/seed/pallas_call | solution.py:446
  25.7 0.1 collective-permute-start.7
  25.8 1.6 %collective-permute-start.6 = (bf16[32,512]{1,0:T(8,128)(2,1)S(1)}, bf16[32,512]{1,0:T(8,128)(2,1)S(1)}, u32[]{:S(2)}, u32[]{:S(2)}) collective-permute-start(bf16[32,512]{1,0:T(8,128)(2,1)S(1)} %get-tuple-element.33), channel_id=1, source_target_pairs={{0,2},{2,0},{4,6},{6,4},{8,10},{10,8},{12,14},{14,12},{1,3},{3,1},... | collective-permute-start | bytes 98312 | tf_op jit(solution)/shard_map/ppermute | solution.py:381
  27.4 0.5 %gradient_own.1.refs_4_ = f32[32,2048]{1,0:T(8,128)S(1)} custom-call(bf16[32,512]{1,0:T(8,128)(2,1)S(1)} %get-tuple-element.34.back_ref, bf16[512,2048]{1,0:T(8,128)(2,1)S(1)} %get-tuple-element.38.refs_0_, bf16[512,2048]{1,0:T(8,128)(2,1)S(1)} %get-tuple-element.39.refs_1_, f32[2,32,2048]{2,1,0:T(8,128)S(1)} %get-tuple-element.29.after_ref.refs_2_, ...), custom_call_target="tpu_custom_call" | custom-call | flops 1000000000 | bytes 10000000 | tf_op jit(solution)/shard_map/gradient_own/pallas_call | solution.py:454
  27.9 0.0 collective-permute-done.7.back_ref
  27.9 0.5 %gradient_core.1.refs_4_ = f32[32,2048]{1,0:T(8,128)S(1)} custom-call(bf16[32,512]{1,0:T(8,128)(2,1)S(1)} %collective-permute-done.7.back_ref, bf16[512,2048]{1,0:T(8,128)(2,1)S(1)} %get-tuple-element.35.refs_0_, bf16[512,2048]{1,0:T(8,128)(2,1)S(1)} %get-tuple-element.36.refs_1_, f32[2,32,2048]{2,1,0:T(8,128)S(1)} %get-tuple-element.32.after_ref.refs_2_, ...), custom_call_target="tpu_custom_call" | custom-call | flops 1000000000 | bytes 10000000 | tf_op jit(solution)/shard_map/gradient_core/pallas_call | solution.py:454
  28.4 1.4 %collective-permute-done.6.back_ref = bf16[32,512]{1,0:T(8,128)(2,1)S(1)} collective-permute-done((bf16[32,512]{1,0:T(8,128)(2,1)S(1)}, bf16[32,512]{1,0:T(8,128)(2,1)S(1)}, u32[]{:S(2)}, u32[]{:S(2)}) %collective-permute-start.6) | collective-permute-done | bytes 32800 | tf_op jit(solution)/shard_map/ppermute | solution.py:381
  29.8 0.0 collective-permute-start.8
  29.8 0.5 %gradient_near.1.refs_4_ = f32[32,2048]{1,0:T(8,128)S(1)} custom-call(bf16[32,512]{1,0:T(8,128)(2,1)S(1)} %collective-permute-done.6.back_ref, bf16[512,2048]{1,0:T(8,128)(2,1)S(1)} %get-tuple-element.38.refs_0_, bf16[512,2048]{1,0:T(8,128)(2,1)S(1)} %get-tuple-element.39.refs_1_, f32[2,32,2048]{2,1,0:T(8,128)S(1)} %get-tuple-element.29.after_ref.refs_2_, ...), custom_call_target="tpu_custom_call" | custom-call | flops 1000000000 | bytes 10000000 | tf_op jit(solution)/shard_map/gradient_near/pallas_call | solution.py:454
  30.3 0.7 %collective-permute-done.8.back_ref = bf16[32,512]{1,0:T(8,128)(2,1)S(1)} collective-permute-done((bf16[32,512]{1,0:T(8,128)(2,1)S(1)}, bf16[32,512]{1,0:T(8,128)(2,1)S(1)}, u32[]{:S(2)}, u32[]{:S(2)}) %collective-permute-start.8) | collective-permute-done | bytes 32800 | tf_op jit(solution)/shard_map/ppermute | solution.py:384
  31.0 1.2 %gradient_last.1 = f32[32,2048]{1,0:T(8,128)} custom-call(bf16[32,512]{1,0:T(8,128)(2,1)S(1)} %collective-permute-done.8.back_ref, bf16[512,2048]{1,0:T(8,128)(2,1)S(1)} %get-tuple-element.35.refs_0_, bf16[512,2048]{1,0:T(8,128)(2,1)S(1)} %get-tuple-element.36.refs_1_, f32[2,32,2048]{2,1,0:T(8,128)S(1)} %get-tuple-element.32.after_ref.refs_2_, ...), custom_call_target="tpu_custom_call" | custom-call | flops 1000000000 | bytes 10000000 | tf_op jit(solution)/shard_map/gradient_last/pallas_call | solution.py:454
  (1 shorter events, 0.0 us)
Async XLA Ops:
  5.3 4.9 %collective-permute-start = (bf16[32,512]{1,0:T(8,128)(2,1)S(1)}, bf16[32,512]{1,0:T(8,128)(2,1)S(1)}, u32[]{:S(2)}, u32[]{:S(2)}) collective-permute-start(bf16[32,512]{1,0:T(8,128)(2,1)S(1)} %get-tuple-element.27), channel_id=1, source_target_pairs={{0,2},{2,0},{4,6},{6,4},{8,10},{10,8},{12,14},{14,12},{1,3},{3,1},... | collective-permute-start | bytes 98312 | tf_op jit(solution)/shard_map/ppermute | solution.py:381
  8.3 14.6 %collective-permute-start.5 = (f32[2,24,256]{2,1,0:T(8,128)S(1)}, f32[2,24,256]{2,1,0:T(8,128)S(1)}, u32[]{:S(2)}, u32[]{:S(2)}) collective-permute-start(f32[2,24,256]{2,1,0:T(8,128)S(1)} %get-tuple-element.23.info_ref), channel_id=1, source_target_pairs={{0,1},{1,0},{2,3},{3,2},{4,5},{5,4},{6,7},{7,6},{8,9},{9,8},{10,11... | collective-permute-start | bytes 147464 | tf_op jit(solution)/shard_map/ppermute | solution.py:384
  10.2 6.9 %collective-permute-start.1 = (bf16[64,512]{1,0:T(8,128)(2,1)S(1)}, bf16[64,512]{1,0:T(8,128)(2,1)S(1)}, u32[]{:S(2)}, u32[]{:S(2)}) collective-permute-start(bf16[64,512]{1,0:T(8,128)(2,1)S(1)} %merge.1.after_ref.refs_0_), channel_id=1, source_target_pairs={{0,4},{2,6},{4,0},{6,2},{8,12},{10,14},{12,8},{14,10},{1,5},{3,7},... | collective-permute-start | bytes 196616 | tf_op jit(solution)/shard_map/ppermute | solution.py:381
  12.4 6.6 %collective-permute-start.2 = (bf16[64,512]{1,0:T(8,128)(2,1)S(1)}, bf16[64,512]{1,0:T(8,128)(2,1)S(1)}, u32[]{:S(2)}, u32[]{:S(2)}) collective-permute-start(bf16[64,512]{1,0:T(8,128)(2,1)S(1)} %merge.1.after_ref.refs_0_), channel_id=1, source_target_pairs={{0,8},{2,10},{4,12},{6,14},{8,0},{10,2},{12,4},{14,6},{1,9},{3,11}... | collective-permute-start | bytes 196616 | tf_op jit(solution)/shard_map/ppermute | solution.py:381
  15.0 6.1 %collective-permute-start.3 = (bf16[64,512]{1,0:T(8,128)(2,1)S(1)}, bf16[64,512]{1,0:T(8,128)(2,1)S(1)}, u32[]{:S(2)}, u32[]{:S(2)}) collective-permute-start(bf16[64,512]{1,0:T(8,128)(2,1)S(1)} %merge.1.after_ref.refs_0_), channel_id=1, source_target_pairs={{0,12},{2,14},{4,8},{6,10},{8,4},{10,6},{12,0},{14,2},{1,13},{3,15... | collective-permute-start | bytes 196616 | tf_op jit(solution)/shard_map/ppermute | solution.py:381
  21.4 3.7 %collective-permute-start.4 = (f32[8,128]{1,0:T(8,128)S(1)}, f32[8,128]{1,0:T(8,128)S(1)}, u32[]{:S(2)}, u32[]{:S(2)}) collective-permute-start(f32[8,128]{1,0:T(8,128)S(1)} %get-tuple-element.30.after_ref.power_ref), channel_id=1, source_target_pairs={{0,2},{2,0},{4,6},{6,4},{8,10},{10,8},{12,14},{14,12},{1,3},{3,1},... | collective-permute-start | bytes 12296 | tf_op jit(solution)/shard_map/ppermute | solution.py:381
  25.7 2.1 %collective-permute-start.7 = (bf16[32,512]{1,0:T(8,128)(2,1)S(1)}, bf16[32,512]{1,0:T(8,128)(2,1)S(1)}, u32[]{:S(2)}, u32[]{:S(2)}) collective-permute-start(bf16[32,512]{1,0:T(8,128)(2,1)S(1)} %get-tuple-element.34.back_ref), channel_id=1, source_target_pairs={{0,1},{1,0},{2,3},{3,2},{4,5},{5,4},{6,7},{7,6},{8,9},{9,8},{10,11... | collective-permute-start | bytes 98312 | tf_op jit(solution)/shard_map/ppermute | solution.py:384
  25.8 4.0 %collective-permute-start.6 = (bf16[32,512]{1,0:T(8,128)(2,1)S(1)}, bf16[32,512]{1,0:T(8,128)(2,1)S(1)}, u32[]{:S(2)}, u32[]{:S(2)}) collective-permute-start(bf16[32,512]{1,0:T(8,128)(2,1)S(1)} %get-tuple-element.33), channel_id=1, source_target_pairs={{0,2},{2,0},{4,6},{6,4},{8,10},{10,8},{12,14},{14,12},{1,3},{3,1},... | collective-permute-start | bytes 98312 | tf_op jit(solution)/shard_map/ppermute | solution.py:381
  29.8 1.2 %collective-permute-start.8 = (bf16[32,512]{1,0:T(8,128)(2,1)S(1)}, bf16[32,512]{1,0:T(8,128)(2,1)S(1)}, u32[]{:S(2)}, u32[]{:S(2)}) collective-permute-start(bf16[32,512]{1,0:T(8,128)(2,1)S(1)} %collective-permute-done.6.back_ref), channel_id=1, source_target_pairs={{0,1},{1,0},{2,3},{3,2},{4,5},{5,4},{6,7},{7,6},{8,9},{9,8},{10,11... | collective-permute-start | bytes 98312 | tf_op jit(solution)/shard_map/ppermute | solution.py:384

commit v5 on v4

v5 whole, which is shorter than its diff:
```python
import functools
import math

import jax
import jax.numpy as jnp
from jax import lax
from jax.experimental import pallas as pl
from jax.experimental.pallas import tpu as pltpu
from jax.sharding import PartitionSpec as P

FOCAL = 256
SPOT = 4
SHIFT = 32
TERMS = 8
BLOCK = 256
GRAIN = 16
VMEM_LIMIT = 16 * 1024 * 1024
WAVE_ROW, ANGLE_ROW, AIM_ROW, INFO_ROWS = 16, 17, 18, 24
DIRECT = 16

COS = (
    1.0, -19.7392088015709, 64.93939395773512, -85.45681453397417, 60.24458621302471,
    -26.425616460281425, 7.8991596631575085, -1.6968741456712442, 0.2437618617467591,
)
SIN = (
    6.2831853071792665, -41.34170224019464, 81.60524925425943, -76.70585885700535,
    42.05867547580699, -15.094428387947755, 3.818490079304055, -0.7122771247541972,
    0.09149844789363434,
)


def horner(terms, u):
    value = terms[-1] * u + terms[-2]
    for term in terms[-3::-1]:
        value = value * u + term
    return value


def unit_waves(counts, period):
    half = period // 2
    centred = ((counts + half) & (period - 1)) - half
    t = centred.astype(jnp.float32) * (1.0 / period)
    u = t * t
    return horner(COS, u), -(t * horner(SIN, u))


def iota(shape, axis):
    return lax.broadcasted_iota(jnp.int32, shape, axis)


def pick_coef(table, wave):
    chosen = jnp.where(iota(table.shape, 1) == wave, table, 0.0)
    return jnp.sum(chosen, axis=1, keepdims=True)


def column_freq(info_ref, pair):
    wave = info_ref[pair, WAVE_ROW : WAVE_ROW + 1, :].astype(jnp.int32)
    angle = info_ref[pair, ANGLE_ROW : ANGLE_ROW + 1, :].astype(jnp.int32)
    return (iota((1, FOCAL), 1) - FOCAL // 2 + SHIFT * angle) * (BLOCK + wave)


def fill_base(freq, shift, period, base_ref, centre_ref):
    low_r, low_i = unit_waves(iota((GRAIN, 1), 0) * freq, period)
    steps = BLOCK // GRAIN
    high_r, high_i = unit_waves((iota((steps, 1), 0) * GRAIN - BLOCK // 2 + shift) * freq, period)
    for step in range(steps):
        one_r, one_i = high_r[step : step + 1], high_i[step : step + 1]
        rows = slice(step * GRAIN, (step + 1) * GRAIN)
        base_ref[0, rows, :] = one_r * low_r - one_i * low_i
        base_ref[1, rows, :] = one_r * low_i + one_i * low_r
    count = centre_ref.shape[1]
    cent_r, cent_i = unit_waves((iota((count, 1), 0) * BLOCK + BLOCK // 2) * freq, period)
    centre_ref[0] = cent_r
    centre_ref[1] = cent_i


def block_pair(base_ref, centre_ref, index):
    cent_r = centre_ref[0, index : index + 1, :]
    cent_i = centre_ref[1, index : index + 1, :]
    base_r, base_i = base_ref[0], base_ref[1]
    rr, ii = base_r * cent_r, base_i * cent_i
    ri, ir = base_r * cent_i, base_i * cent_r
    before = ((rr + ii).astype(jnp.bfloat16), (ir - ri).astype(jnp.bfloat16))
    after = ((rr - ii).astype(jnp.bfloat16), (ir + ri).astype(jnp.bfloat16))
    return before, after


def near_fields(s, info_ref, pairs):
    def coef(pair, row):
        return info_ref[pair, row : row + 1, :]

    outs = [[coef(p, k) + coef(p, k + 1) * s for k in (0, TERMS)] for p in range(pairs)]
    twice = s + s
    before, current = jnp.ones_like(s), s
    for order in range(2, TERMS):
        before, current = current, twice * current - before
        for pair, out in enumerate(outs):
            out[0] = out[0] + coef(pair, order) * current
            out[1] = out[1] + coef(pair, TERMS + order) * current
    return outs


def near_slopes(s, scale, info_ref, pairs):
    def coef(pair, row):
        return info_ref[pair, row : row + 1, :] * (scale * (row % TERMS))

    twice = s + s
    before, current = jnp.ones_like(s), twice
    outs = [[coef(p, k) + coef(p, k + 1) * twice for k in (1, TERMS + 1)] for p in range(pairs)]
    for order in range(3, TERMS):
        before, current = current, twice * current - before
        for pair, out in enumerate(outs):
            out[0] = out[0] + coef(pair, order) * current
            out[1] = out[1] + coef(pair, TERMS + order) * current
    return outs


def forward_kernel(
    wave_hbm, angle_hbm, aim_hbm, coef_hbm, width_hbm, mine_ref, info_ref, own_ref,
    wave_ref, angle_ref, aim_ref, coef_ref, width_ref, base_ref, centre_ref, acc_ref, sems,
):
    rows_dev, cols = width_ref.shape
    pairs = wave_ref.shape[0]
    period = 256 * cols
    moves = [
        pltpu.make_async_copy(source, target, sems.at[index])
        for index, (source, target) in enumerate((
            (wave_hbm, wave_ref), (angle_hbm, angle_ref), (aim_hbm, aim_ref),
            (coef_hbm, coef_ref), (width_hbm, width_ref),
        ))
    ]
    for move in moves:
        move.start()
    for move in moves[:4]:
        move.wait()
    for pair in range(pairs):
        coef = pick_coef(coef_ref[...], wave_ref[pair])
        info_ref[pair, :WAVE_ROW, :] = jnp.broadcast_to(coef, (WAVE_ROW, FOCAL))
        row = iota((INFO_ROWS - WAVE_ROW, FOCAL), 0) + WAVE_ROW
        ids = jnp.where(row == WAVE_ROW, wave_ref[pair], 0)
        ids = jnp.where(row == ANGLE_ROW, angle_ref[pair], ids)
        ids = jnp.where(row == AIM_ROW, aim_ref[pair, 0], ids)
        ids = jnp.where(row == AIM_ROW + 1, aim_ref[pair, 1], ids)
        info_ref[pair, WAVE_ROW:, :] = ids.astype(jnp.float32)
    for pair in range(pairs):
        fill_base(column_freq(info_ref, pair), 0, period, base_ref.at[pair], centre_ref.at[pair])
    acc_ref[...] = jnp.zeros_like(acc_ref)
    moves[4].wait()
    for index in range(cols // (2 * BLOCK)):
        left = cols // 2 - (index + 1) * BLOCK
        right = cols // 2 + index * BLOCK
        nears = []
        for start in (left, right):
            outs = near_fields(width_ref[:, start : start + BLOCK], info_ref, pairs)
            nears.append([jnp.concatenate(out, axis=0).astype(jnp.bfloat16) for out in outs])
        for pair in range(pairs):
            before, after = block_pair(base_ref.at[pair], centre_ref.at[pair], index)
            near = jnp.concatenate([nears[0][pair], nears[1][pair]], axis=1)
            for part in range(2):
                table = jnp.concatenate([before[part], after[part]], axis=0)
                acc_ref[pair, part] += jnp.dot(near, table, preferred_element_type=jnp.float32)
    own_cols = own_ref.shape[1]
    first = pl.multiple_of(lax.axis_index("wave") * own_cols, own_cols)
    own_ref[...] = width_ref[:, pl.ds(first, own_cols)]
    for pair in range(pairs):
        real = acc_ref[pair, 0, :rows_dev] - acc_ref[pair, 1, rows_dev:]
        imag = acc_ref[pair, 1, :rows_dev] + acc_ref[pair, 0, rows_dev:]
        for part, value in enumerate((real, imag)):
            lane = (2 * pair + part) * FOCAL
            mine_ref[:, lane : lane + FOCAL] = value.astype(jnp.bfloat16)


def row_kernel(info_ref, after_ref, tall_ref, flat_ref):
    del after_ref
    pairs, _, rows = tall_ref.shape
    rows_dev = flat_ref.shape[1]
    period = 256 * rows
    size = min(rows, FOCAL)
    for pair in range(pairs):
        wave = info_ref[pair, WAVE_ROW : WAVE_ROW + 1, :].astype(jnp.int32) + BLOCK
        focal = (iota((FOCAL, 1), 0) - FOCAL // 2) * wave

        def step(index, carry):
            start = pl.multiple_of(index * size, size)
            place = iota((1, size), 1) + (start - rows // 2)
            real, imag = unit_waves(focal[:, :size] * place, period)
            tall_ref[pair, :FOCAL, pl.ds(start, size)] = real.astype(jnp.bfloat16)
            tall_ref[pair, FOCAL:, pl.ds(start, size)] = imag.astype(jnp.bfloat16)
            return carry

        if rows == size:
            step(0, 0)
        else:
            lax.fori_loop(0, rows // size, step, 0)
        focal = (iota((1, FOCAL), 1) - FOCAL // 2) * wave
        first = lax.axis_index("aperture") * rows_dev - rows // 2
        real, imag = unit_waves((iota((rows_dev, 1), 0) + first) * focal, period)
        flat_ref[pair, :, :FOCAL] = real.astype(jnp.bfloat16)
        flat_ref[pair, :, FOCAL:] = imag.astype(jnp.bfloat16)


def spot_map(info_ref, pair):
    aims = [info_ref[pair, row : row + 1, :] for row in (AIM_ROW, AIM_ROW + 1)]
    rows_off = iota((FOCAL, FOCAL), 0).astype(jnp.float32) - aims[0]
    cols_off = iota((1, FOCAL), 1).astype(jnp.float32) - aims[1]
    return jnp.exp(-(rows_off * rows_off + cols_off * cols_off) / (2.0 * SPOT * SPOT))


def join_kernel(*refs):
    *in_refs, out_ref = refs
    count = in_refs[0].shape[0]
    for index, ref in enumerate(in_refs):
        out_ref[index * count : (index + 1) * count, :] = ref[...]


def total_of(value):
    return jnp.sum(jnp.sum(value, axis=0, keepdims=True), axis=1, keepdims=True)


def focus_kernel(steps, info_ref, tall_ref, flat_ref, after_ref, *refs):
    del after_ref
    *sect_refs, back_ref, score_ref, rows_ref = refs
    pairs = tall_ref.shape[0]
    rows_dev = back_ref.shape[0]
    if steps is None:
        rows_ref = sect_refs[0]
    else:
        me = lax.axis_index("aperture")
        blocks = [
            ref[index * rows_dev : (index + 1) * rows_dev, :]
            for ref in sect_refs
            for index in range(ref.shape[0] // rows_dev)
        ]
        for step, block in zip(steps, blocks, strict=True):
            start = pl.multiple_of((me ^ step) * rows_dev, rows_dev)
            rows_ref[pl.ds(start, rows_dev), :] = block
    for pair in range(pairs):
        lane = 2 * pair * FOCAL
        section = rows_ref[:, lane : lane + 2 * FOCAL]
        mixed = jnp.dot(tall_ref[pair], section, preferred_element_type=jnp.float32)
        real = mixed[:FOCAL, :FOCAL] - mixed[FOCAL:, FOCAL:]
        imag = mixed[:FOCAL, FOCAL:] + mixed[FOCAL:, :FOCAL]
        power = real * real + imag * imag
        spot = spot_map(info_ref, pair)
        spot_power = total_of(spot * power)
        all_power = total_of(power) + 1e-06
        ratio = spot_power / all_power
        factor = FOCAL * FOCAL / total_of(spot)
        score_ref[pair] = jnp.sum(ratio * factor)
        weight = (factor * 2.0 / all_power) * (spot - ratio)
        real = (weight * real).astype(jnp.bfloat16)
        imag = (weight * imag).astype(jnp.bfloat16)
        stack = jnp.concatenate(
            [jnp.concatenate([real, imag], axis=1), jnp.concatenate([imag, -real], axis=1)], axis=0
        )
        back = jnp.dot(flat_ref[pair], stack, preferred_element_type=jnp.float32)
        back_ref[:, lane : lane + 2 * FOCAL] = back.astype(jnp.bfloat16)


def table_kernel(scale, cols, info_ref, width_ref, after_ref, *refs):
    del after_ref
    *out_refs, base_ref, centre_ref, turned_ref = refs
    pairs = base_ref.shape[0]
    table_refs, slope_refs = out_refs[:pairs], out_refs[pairs:]
    own_cols = width_ref.shape[1]
    period = 256 * cols
    middle = own_cols // 2
    shift = lax.axis_index("wave") * own_cols + middle - cols // 2
    for pair in range(pairs):
        freq = column_freq(info_ref, pair)
        fill_base(freq, shift, period, base_ref.at[pair], centre_ref.at[pair])
        for part in range(2):
            turned_ref[pair, part] = base_ref[pair, part].T
    centres = [[centre_ref[pair, part].T for part in range(2)] for pair in range(pairs)]
    for index in range(own_cols // (2 * BLOCK)):
        left = middle - (index + 1) * BLOCK
        right = middle + index * BLOCK
        for pair in range(pairs):
            cent_r, cent_i = (centre[:, index : index + 1] for centre in centres[pair])
            base_r, base_i = turned_ref[pair, 0], turned_ref[pair, 1]
            rr, ii = base_r * cent_r, base_i * cent_i
            ri, ir = base_r * cent_i, base_i * cent_r
            for start, values in ((left, (rr + ii, ir - ri)), (right, (rr - ii, ir + ri))):
                for part, value in enumerate(values):
                    row = part * FOCAL
                    table_refs[pair][row : row + FOCAL, start : start + BLOCK] = value.astype(jnp.bfloat16)
        for start in (left, right):
            slopes = near_slopes(width_ref[:, start : start + BLOCK], scale, info_ref, pairs)
            for pair in range(pairs):
                slope_refs[pair][0, :, start : start + BLOCK] = slopes[pair][0]
                slope_refs[pair][1, :, start : start + BLOCK] = slopes[pair][1]


def grad_kernel(pairs, back_ref, *refs):
    *in_refs, out_ref = refs
    table_refs, slope_refs, total_ref = in_refs[:pairs], in_refs[pairs : 2 * pairs], in_refs[2 * pairs :]
    rows_dev, own_cols = out_ref.shape
    lefts = []
    for pair in range(pairs):
        lane = 2 * pair * FOCAL
        real, imag = back_ref[:, lane : lane + FOCAL], back_ref[:, lane + FOCAL : lane + 2 * FOCAL]
        lefts.append(
            jnp.concatenate(
                [jnp.concatenate([real, imag], axis=1), jnp.concatenate([imag, -real], axis=1)], axis=0
            )
        )
    size = 2 * BLOCK
    for start in range(0, own_cols, size):
        place = slice(start, start + size)
        total = total_ref[0][:, place] if total_ref else jnp.zeros((rows_dev, size), jnp.float32)
        for pair in range(pairs):
            grad = jnp.dot(lefts[pair], table_refs[pair][:, place], preferred_element_type=jnp.float32)
            total += grad[:rows_dev] * slope_refs[pair][0, :, place]
            total += grad[rows_dev:] * slope_refs[pair][1, :, place]
        out_ref[:, place] = total


VMEM = pl.BlockSpec(memory_space=pltpu.VMEM)
SMEM = pl.BlockSpec(memory_space=pltpu.SMEM)
ANY = pl.BlockSpec(memory_space=pl.ANY)
HBM = pl.BlockSpec(memory_space=pltpu.HBM)


def call(kernel, name, outs, in_specs, out_specs, scratch, flops, moved):
    return pl.pallas_call(
        kernel,
        name=name,
        out_shape=outs,
        in_specs=in_specs,
        out_specs=out_specs,
        scratch_shapes=scratch,
        cost_estimate=pl.CostEstimate(flops=flops, bytes_accessed=moved, transcendentals=0),
        compiler_params=pltpu.CompilerParams(vmem_limit_bytes=VMEM_LIMIT),
    )


def on_device(widths, coef_table, wave_ids, angle_ids, targets):
    rows_dev, cols = widths.shape
    pairs_dev = wave_ids.shape[0]
    peers = lax.axis_size("aperture")
    copies = lax.axis_size("wave")
    rows = rows_dev * peers
    own_cols = cols // copies
    lanes = 2 * pairs_dev * FOCAL
    f32, bf16 = jnp.float32, jnp.bfloat16
    shape = jax.ShapeDtypeStruct

    def in_hbm(value):
        return pltpu.with_memory_space_constraint(value, pltpu.HBM)

    def exchange(value, step):
        return lax.ppermute(value, "aperture", [(index, index ^ step) for index in range(peers)])

    def to_core(value):
        return lax.ppermute(value, "wave", [(index, (index + 1) % copies) for index in range(copies)])

    mine, info, own = call(
        forward_kernel, "forward",
        (
            shape((rows_dev, lanes), bf16),
            shape((pairs_dev, INFO_ROWS, FOCAL), f32), shape((rows_dev, own_cols), f32),
        ),
        [HBM] * 5, (VMEM,) * 3,
        [
            pltpu.SMEM(wave_ids.shape, jnp.int32),
            pltpu.SMEM(angle_ids.shape, jnp.int32),
            pltpu.SMEM(targets.shape, jnp.int32),
            pltpu.VMEM(coef_table.shape[::-1], f32),
            pltpu.VMEM(widths.shape, f32),
            pltpu.VMEM((pairs_dev, 2, BLOCK, FOCAL), f32),
            pltpu.VMEM((pairs_dev, 2, cols // (2 * BLOCK), FOCAL), f32),
            pltpu.VMEM((pairs_dev, 2, 2 * rows_dev, FOCAL), f32),
            pltpu.SemaphoreType.DMA((5,)),
        ],
        10**9, 10**7,
    )(*(in_hbm(value) for value in (wave_ids, angle_ids, targets, coef_table.T, widths)))
    far_info = to_core(info)

    def column_tables(info, after, name):
        outs = [shape((2 * FOCAL, own_cols), bf16)] * pairs_dev
        outs += [shape((2, rows_dev, own_cols), f32)] * pairs_dev
        got = call(
            functools.partial(table_kernel, math.sqrt(rows * cols), cols), name,
            outs, [VMEM, VMEM, ANY], [VMEM] * len(outs),
            [
                pltpu.VMEM((pairs_dev, 2, BLOCK, FOCAL), f32),
                pltpu.VMEM((pairs_dev, 2, own_cols // (2 * BLOCK), FOCAL), f32),
                pltpu.VMEM((pairs_dev, 2, FOCAL, BLOCK), f32),
            ],
            10**9, 10**7,
        )(info, own, after)
        return list(got[:pairs_dev]), list(got[pairs_dev:])

    tables, slopes = column_tables(info, mine, "own_tables")
    if peers <= DIRECT:
        steps = list(range(peers - 2, 0, -2))
        got = [exchange(mine, step) for step in steps]
        near = exchange(mine, 1)
        *got, slopes[0] = lax.optimization_barrier((*got, slopes[0]))
        first = got[0]
        joined = call(join_kernel, "join", shape(((len(steps) - 1) * rows_dev, lanes), bf16),
                      [VMEM] * (len(steps) - 1), VMEM, [], 10**6, 10**6)(*got[1:])
        sections = [mine, near, first, joined, exchange(first, 1), exchange(joined, 1)]
        steps = [0, 1, *steps, *(step ^ 1 for step in steps)]
        after = joined
    else:
        blocks = jnp.tile(mine[None], (peers, 1, 1))
        blocks = lax.all_to_all(blocks, "aperture", 0, 0, tiled=True)
        sections, steps, after = [blocks.reshape(rows, lanes)], None, mine
    tall, flat = call(
        row_kernel, "row_tables",
        (shape((pairs_dev, 2 * FOCAL, rows), bf16), shape((pairs_dev, rows_dev, 2 * FOCAL), bf16)),
        [VMEM, ANY], (VMEM, VMEM), [], 10**8, 10**6,
    )(info, after)
    far_tables, far_slopes = column_tables(far_info, flat, "far_tables")

    back, scores = call(
        functools.partial(focus_kernel, steps), "focus",
        (shape((rows_dev, lanes), bf16), shape((pairs_dev,), f32)),
        [VMEM, VMEM, VMEM, ANY] + [VMEM] * len(sections), (VMEM, SMEM), [pltpu.VMEM((rows, lanes), bf16)],
        10**8, 10**6,
    )(info, tall, flat, far_slopes[0], *sections)

    def add_grad(back, tables, slopes, name, *total):
        ins = [back, *tables, *slopes, *total]
        return call(
            functools.partial(grad_kernel, pairs_dev), name,
            shape((rows_dev, own_cols), f32), [VMEM] * len(ins), VMEM, [], 10**9, 10**7,
        )(*ins)

    far_back = to_core(back)
    grad = add_grad(back, tables, slopes, "gradient_own")
    grad = add_grad(far_back, far_tables, far_slopes, "gradient_far", grad)
    return grad, scores


def solution(mesh):
    in_specs = (
        P(("group", "aperture"), None),
        P(),
        P(("group", "wave")),
        P(("group", "wave")),
        P(("group", "wave"), None),
    )
    out_specs = (P(("group", "aperture"), "wave"), P(("group", "wave")))
    return jax.shard_map(
        on_device, mesh=mesh, in_specs=in_specs, out_specs=out_specs, check_vma=False
    )
```

time: 32.4 us -> 28.8 us (0.89)
  waiting for transfers between devices: 7.02 us -> 4.6 us
  starting transfers between devices: 10.9 us -> 9.41 us
  Pallas kernels: 13.5 us -> 13.9 us
    ppermute x6, waiting for transfers between devices: 6.32 us -> 4.22 us  [exchange(): lax.ppermute(value, 'aperture', [(index, index ^ step) for index in range...]
    ppermute x6, starting transfers between devices: 10.9 us -> 9.34 us  [exchange(): lax.ppermute(value, 'aperture', [(index, index ^ step) for index in range...]
    pallas_call x8 -> x5, Pallas kernels: 8.39 us -> 8.88 us  [the longest x1 4.64 us: on_device(): call(forward_kernel, 'forward', (shape((rows_dev, lanes), bf16), shape((p...]
    ppermute x3 -> x2, waiting for transfers between devices: 0.7 us -> 0.39 us  [to_core(): lax.ppermute(value, 'wave', [(index, (index + 1) % copies) for index in r...]
  transfers between devices with their start and end apart: 9 -> 8, of which waited for: 5 -> 4; matrix products, arithmetic and copies ran while one was open for 0% -> 0% of each run, Pallas kernels for 22% -> 21%
where the time goes in v5:
time: 28.8 us; the launch traced here: 28.7 us
  Pallas kernels  13.9 us (48%)
  starting transfers between devices  9.41 us (33%)
  waiting for transfers between devices  4.6 us (16%)
  between operations  0.71 us (2%)
    ppermute x6, starting transfers between devices, exchange(): lax.ppermute(value, 'aperture', [(index, index ^ step) for index in range...  9.34 us
    pallas_call x1, Pallas kernels, on_device(): call(forward_kernel, 'forward', (shape((rows_dev, lanes), bf16), shape((p...  4.64 us
    ppermute x6, waiting for transfers between devices, exchange(): lax.ppermute(value, 'aperture', [(index, index ^ step) for index in range...  4.22 us
    pallas_call x2, Pallas kernels, column_tables(): call(functools.partial(table_kernel, math.sqrt(rows * cols), cols), name,...  4.2 us
    pallas_call x2, Pallas kernels, add_grad(): call(functools.partial(grad_kernel, pairs_dev), name, shape((rows_dev, ow...  2.4 us
    pallas_call x1, Pallas kernels, on_device(): call(functools.partial(focus_kernel, steps), 'focus', (shape((rows_dev, l...  1.82 us
    pallas_call x1, Pallas kernels, on_device(): call(row_kernel, 'row_tables', (shape((pairs_dev, 2 * FOCAL, rows), bf16)...  0.87 us
  transfers between devices with their start and end apart: 8, of which 4 were waited for; matrix products, arithmetic and copies ran while one was open for 0% of the time, Pallas kernels for 21%

profile of v5, /device:TPU:0, one launch (start us, length us, event | category | flops | bytes accessed | tf_op | source)
XLA Modules:
  0.0 28.7 jit_solution(15487329722995305443)
XLA Ops:
  0.6 4.6 %forward.1 = (bf16[32,1024]{1,0:T(8,128)(2,1)S(1)}, f32[2,24,256]{2,1,0:T(8,128)S(1)}, f32[32,2048]{1,0:T(8,128)S(1)}) custom-call(s32[2]{0:T(128)} %wave_hbm.1, s32[2]{0:T(128)} %angle_hbm.1, s32[2,2]{1,0:T(2,128)} %aim_hbm.1, f32[16,256]{1,0:T(8,128)} %bitcast.1, f32[32,4096]{1,0:T(8,128)} %width_hbm.1), custom_call_target="tpu_custom_call" | custom-call | flops 1000000000 | bytes 10000000 | tf_op jit(solution)/shard_map/forward/pallas_call | solution.py:357
  5.3 5.1 %collective-permute-start = (bf16[32,1024]{1,0:T(8,128)(2,1)S(1)}, bf16[32,1024]{1,0:T(8,128)(2,1)S(1)}, u32[]{:S(2)}, u32[]{:S(2)}) collective-permute-start(bf16[32,1024]{1,0:T(8,128)(2,1)S(1)} %get-tuple-element.22.after_ref.refs_0_), channel_id=1, source_target_pairs={{0,12},{2,14},{4,8},{6,10},{8,4},{10,6},{12,0},{14,2},{1,13},{3,15... | collective-permute-start | bytes 196616 | tf_op jit(solution)/shard_map/ppermute | solution.py:352
  10.4 0.0 collective-permute-start.1
  10.4 0.6 %collective-permute-start.2 = (bf16[32,1024]{1,0:T(8,128)(2,1)S(1)}, bf16[32,1024]{1,0:T(8,128)(2,1)S(1)}, u32[]{:S(2)}, u32[]{:S(2)}) collective-permute-start(bf16[32,1024]{1,0:T(8,128)(2,1)S(1)} %get-tuple-element.22.after_ref.refs_0_), channel_id=1, source_target_pairs={{0,4},{2,6},{4,0},{6,2},{8,12},{10,14},{12,8},{14,10},{1,5},{3,7},... | collective-permute-start | bytes 196616 | tf_op jit(solution)/shard_map/ppermute | solution.py:352
  11.0 0.0 collective-permute-start.3
  11.0 2.1 %own_tables.1 = (bf16[512,2048]{1,0:T(8,128)(2,1)S(1)}, bf16[512,2048]{1,0:T(8,128)(2,1)S(1)}, f32[2,32,2048]{2,1,0:T(8,128)S(1)}, f32[2,32,2048]{2,1,0:T(8,128)S(1)}) custom-call(f32[2,24,256]{2,1,0:T(8,128)S(1)} %get-tuple-element.21.info_ref, f32[32,2048]{1,0:T(8,128)S(1)} %get-tuple-element.23.width_ref, ...), custom_call_target="tpu_custom_call" | custom-call | flops 1000000000 | bytes 10000000 | tf_op jit(solution)/shard_map/own_tables/pallas_call | solution.py:382
  13.1 0.0 collective-permute-done.refs_2_
  13.2 2.8 %collective-permute-done.1.refs_0_ = bf16[32,1024]{1,0:T(8,128)(2,1)S(1)} collective-permute-done((bf16[32,1024]{1,0:T(8,128)(2,1)S(1)}, bf16[32,1024]{1,0:T(8,128)(2,1)S(1)}, u32[]{:S(2)}, u32[]{:S(2)}) %collective-permute-start.1) | collective-permute-done | bytes 65568 | tf_op jit(solution)/shard_map/ppermute | solution.py:352
  16.0 0.0 collective-permute-done.2.refs_1_
  16.0 1.6 %collective-permute-start.6 = (bf16[64,1024]{1,0:T(8,128)(2,1)S(1)}, bf16[64,1024]{1,0:T(8,128)(2,1)S(1)}, u32[]{:S(2)}, u32[]{:S(2)}) collective-permute-start(bf16[64,1024]{1,0:T(8,128)(2,1)S(1)} %join.1.after_ref.refs_3_), channel_id=1, source_target_pairs={{0,2},{2,0},{4,6},{6,4},{8,10},{10,8},{12,14},{14,12},{1,3},{3,1},... | collective-permute-start | bytes 393224 | tf_op jit(solution)/shard_map/ppermute | solution.py:352
  17.6 0.5 %collective-permute-start.4 = (bf16[32,1024]{1,0:T(8,128)(2,1)S(1)}, bf16[32,1024]{1,0:T(8,128)(2,1)S(1)}, u32[]{:S(2)}, u32[]{:S(2)}) collective-permute-start(bf16[32,1024]{1,0:T(8,128)(2,1)S(1)} %get-tuple-element.22.after_ref.refs_0_), channel_id=1, source_target_pairs={{0,2},{2,0},{4,6},{6,4},{8,10},{10,8},{12,14},{14,12},{1,3},{3,1},... | collective-permute-start | bytes 196616 | tf_op jit(solution)/shard_map/ppermute | solution.py:352
  18.1 1.5 %collective-permute-start.5 = (bf16[32,1024]{1,0:T(8,128)(2,1)S(1)}, bf16[32,1024]{1,0:T(8,128)(2,1)S(1)}, u32[]{:S(2)}, u32[]{:S(2)}) collective-permute-start(bf16[32,1024]{1,0:T(8,128)(2,1)S(1)} %collective-permute-done.refs_2_), channel_id=1, source_target_pairs={{0,2},{2,0},{4,6},{6,4},{8,10},{10,8},{12,14},{14,12},{1,3},{3,1},... | collective-permute-start | bytes 196616 | tf_op jit(solution)/shard_map/ppermute | solution.py:352
  19.6 0.9 %row_tables.1 = (bf16[2,512,256]{2,1,0:T(8,128)(2,1)S(1)}, bf16[2,32,512]{2,1,0:T(8,128)(2,1)S(1)}) custom-call(f32[2,24,256]{2,1,0:T(8,128)S(1)} %get-tuple-element.21.info_ref, bf16[64,1024]{1,0:T(8,128)(2,1)S(1)} %join.1.after_ref.refs_3_), custom_call_target="tpu_custom_call" | custom-call | flops 100000000 | bytes 1000000 | tf_op jit(solution)/shard_map/row_tables/pallas_call | solution.py:410
  20.5 0.0 collective-permute-done.3.info_ref
  20.5 2.1 %far_tables.1 = (bf16[512,2048]{1,0:T(8,128)(2,1)S(1)}, bf16[512,2048]{1,0:T(8,128)(2,1)S(1)}, f32[2,32,2048]{2,1,0:T(8,128)S(1)}, f32[2,32,2048]{2,1,0:T(8,128)S(1)}) custom-call(f32[2,24,256]{2,1,0:T(8,128)S(1)} %collective-permute-done.3.info_ref, f32[32,2048]{1,0:T(8,128)S(1)} %get-tuple-element.23.width_ref, ...), custom_call_target="tpu_custom_call" | custom-call | flops 1000000000 | bytes 10000000 | tf_op jit(solution)/shard_map/far_tables/pallas_call | solution.py:382
  22.6 0.7 %collective-permute-done.4.refs_1_ = bf16[32,1024]{1,0:T(8,128)(2,1)S(1)} collective-permute-done((bf16[32,1024]{1,0:T(8,128)(2,1)S(1)}, bf16[32,1024]{1,0:T(8,128)(2,1)S(1)}, u32[]{:S(2)}, u32[]{:S(2)}) %collective-permute-start.4) | collective-permute-done | bytes 65568 | tf_op jit(solution)/shard_map/ppermute | solution.py:352
  23.3 0.7 %collective-permute-done.5.refs_4_ = bf16[32,1024]{1,0:T(8,128)(2,1)S(1)} collective-permute-done((bf16[32,1024]{1,0:T(8,128)(2,1)S(1)}, bf16[32,1024]{1,0:T(8,128)(2,1)S(1)}, u32[]{:S(2)}, u32[]{:S(2)}) %collective-permute-start.5) | collective-permute-done | bytes 65568 | tf_op jit(solution)/shard_map/ppermute | solution.py:352
  24.0 0.0 collective-permute-done.6.refs_5_
  24.0 1.8 %focus.1 = (bf16[32,1024]{1,0:T(8,128)(2,1)S(1)}, f32[2]{0:T(128)}) custom-call(f32[2,24,256]{2,1,0:T(8,128)S(1)} %get-tuple-element.21.info_ref, bf16[2,512,256]{2,1,0:T(8,128)(2,1)S(1)} %get-tuple-element.27.tall_ref, bf16[2,32,512]{2,1,0:T(8,128)(2,1)S(1)} %get-tuple-element.28.after_ref.flat_ref, f32[2,32,2048]{2,1,0:T(8,128)S(1)} %get-tuple-element.29.after_ref.refs_2_, ...), custom_call_target="tpu_custom_call" | custom-call | flops 100000000 | bytes 1000000 | tf_op jit(solution)/shard_map/focus/pallas_call | solution.py:417
  25.8 0.1 collective-permute-start.7
  25.9 0.9 %gradient_own.1.refs_4_ = f32[32,2048]{1,0:T(8,128)S(1)} custom-call(bf16[32,1024]{1,0:T(8,128)(2,1)S(1)} %get-tuple-element.31.back_ref, bf16[512,2048]{1,0:T(8,128)(2,1)S(1)} %get-tuple-element.35.refs_0_, bf16[512,2048]{1,0:T(8,128)(2,1)S(1)} %get-tuple-element.36.refs_1_, f32[2,32,2048]{2,1,0:T(8,128)S(1)} %get-tuple-element.37.refs_2_, ...), custom_call_target="tpu_custom_call" | custom-call | flops 1000000000 | bytes 10000000 | tf_op jit(solution)/shard_map/gradient_own/pallas_call | solution.py:426
  26.7 0.4 %collective-permute-done.7.back_ref = bf16[32,1024]{1,0:T(8,128)(2,1)S(1)} collective-permute-done((bf16[32,1024]{1,0:T(8,128)(2,1)S(1)}, bf16[32,1024]{1,0:T(8,128)(2,1)S(1)}, u32[]{:S(2)}, u32[]{:S(2)}) %collective-permute-start.7) | collective-permute-done | bytes 65568 | tf_op jit(solution)/shard_map/ppermute | solution.py:355
  27.1 1.6 %gradient_far.1 = f32[32,2048]{1,0:T(8,128)} custom-call(bf16[32,1024]{1,0:T(8,128)(2,1)S(1)} %collective-permute-done.7.back_ref, bf16[512,2048]{1,0:T(8,128)(2,1)S(1)} %get-tuple-element.32.refs_0_, bf16[512,2048]{1,0:T(8,128)(2,1)S(1)} %get-tuple-element.33.refs_1_, f32[2,32,2048]{2,1,0:T(8,128)S(1)} %get-tuple-element.29.after_ref.refs_2_, ...), custom_call_target="tpu_custom_call" | custom-call | flops 1000000000 | bytes 10000000 | tf_op jit(solution)/shard_map/gradient_far/pallas_call | solution.py:426
  (1 shorter events, 0.0 us)
Async XLA Ops:
  5.3 7.9 %collective-permute-start = (bf16[32,1024]{1,0:T(8,128)(2,1)S(1)}, bf16[32,1024]{1,0:T(8,128)(2,1)S(1)}, u32[]{:S(2)}, u32[]{:S(2)}) collective-permute-start(bf16[32,1024]{1,0:T(8,128)(2,1)S(1)} %get-tuple-element.22.after_ref.refs_0_), channel_id=1, source_target_pairs={{0,12},{2,14},{4,8},{6,10},{8,4},{10,6},{12,0},{14,2},{1,13},{3,15... | collective-permute-start | bytes 196616 | tf_op jit(solution)/shard_map/ppermute | solution.py:352
  10.4 5.6 %collective-permute-start.1 = (bf16[32,1024]{1,0:T(8,128)(2,1)S(1)}, bf16[32,1024]{1,0:T(8,128)(2,1)S(1)}, u32[]{:S(2)}, u32[]{:S(2)}) collective-permute-start(bf16[32,1024]{1,0:T(8,128)(2,1)S(1)} %get-tuple-element.22.after_ref.refs_0_), channel_id=1, source_target_pairs={{0,8},{2,10},{4,12},{6,14},{8,0},{10,2},{12,4},{14,6},{1,9},{3,11}... | collective-permute-start | bytes 196616 | tf_op jit(solution)/shard_map/ppermute | solution.py:352
  10.4 5.6 %collective-permute-start.2 = (bf16[32,1024]{1,0:T(8,128)(2,1)S(1)}, bf16[32,1024]{1,0:T(8,128)(2,1)S(1)}, u32[]{:S(2)}, u32[]{:S(2)}) collective-permute-start(bf16[32,1024]{1,0:T(8,128)(2,1)S(1)} %get-tuple-element.22.after_ref.refs_0_), channel_id=1, source_target_pairs={{0,4},{2,6},{4,0},{6,2},{8,12},{10,14},{12,8},{14,10},{1,5},{3,7},... | collective-permute-start | bytes 196616 | tf_op jit(solution)/shard_map/ppermute | solution.py:352
  11.0 9.4 %collective-permute-start.3 = (f32[2,24,256]{2,1,0:T(8,128)S(1)}, f32[2,24,256]{2,1,0:T(8,128)S(1)}, u32[]{:S(2)}, u32[]{:S(2)}) collective-permute-start(f32[2,24,256]{2,1,0:T(8,128)S(1)} %get-tuple-element.21.info_ref), channel_id=1, source_target_pairs={{0,1},{1,0},{2,3},{3,2},{4,5},{5,4},{6,7},{7,6},{8,9},{9,8},{10,11... | collective-permute-start | bytes 147464 | tf_op jit(solution)/shard_map/ppermute | solution.py:355
  16.0 7.9 %collective-permute-start.6 = (bf16[64,1024]{1,0:T(8,128)(2,1)S(1)}, bf16[64,1024]{1,0:T(8,128)(2,1)S(1)}, u32[]{:S(2)}, u32[]{:S(2)}) collective-permute-start(bf16[64,1024]{1,0:T(8,128)(2,1)S(1)} %join.1.after_ref.refs_3_), channel_id=1, source_target_pairs={{0,2},{2,0},{4,6},{6,4},{8,10},{10,8},{12,14},{14,12},{1,3},{3,1},... | collective-permute-start | bytes 393224 | tf_op jit(solution)/shard_map/ppermute | solution.py:352
  17.6 5.7 %collective-permute-start.4 = (bf16[32,1024]{1,0:T(8,128)(2,1)S(1)}, bf16[32,1024]{1,0:T(8,128)(2,1)S(1)}, u32[]{:S(2)}, u32[]{:S(2)}) collective-permute-start(bf16[32,1024]{1,0:T(8,128)(2,1)S(1)} %get-tuple-element.22.after_ref.refs_0_), channel_id=1, source_target_pairs={{0,2},{2,0},{4,6},{6,4},{8,10},{10,8},{12,14},{14,12},{1,3},{3,1},... | collective-permute-start | bytes 196616 | tf_op jit(solution)/shard_map/ppermute | solution.py:352
  18.1 5.8 %collective-permute-start.5 = (bf16[32,1024]{1,0:T(8,128)(2,1)S(1)}, bf16[32,1024]{1,0:T(8,128)(2,1)S(1)}, u32[]{:S(2)}, u32[]{:S(2)}) collective-permute-start(bf16[32,1024]{1,0:T(8,128)(2,1)S(1)} %collective-permute-done.refs_2_), channel_id=1, source_target_pairs={{0,2},{2,0},{4,6},{6,4},{8,10},{10,8},{12,14},{14,12},{1,3},{3,1},... | collective-permute-start | bytes 196616 | tf_op jit(solution)/shard_map/ppermute | solution.py:352
  25.8 1.3 %collective-permute-start.7 = (bf16[32,1024]{1,0:T(8,128)(2,1)S(1)}, bf16[32,1024]{1,0:T(8,128)(2,1)S(1)}, u32[]{:S(2)}, u32[]{:S(2)}) collective-permute-start(bf16[32,1024]{1,0:T(8,128)(2,1)S(1)} %get-tuple-element.31.back_ref), channel_id=1, source_target_pairs={{0,1},{1,0},{2,3},{3,2},{4,5},{5,4},{6,7},{7,6},{8,9},{9,8},{10,11... | collective-permute-start | bytes 196616 | tf_op jit(solution)/shard_map/ppermute | solution.py:355

commit v6 on v5

--- a/solution.py
+++ b/solution.py
@@ -170,8 +170,18 @@
             mine_ref[:, lane : lane + FOCAL] = value.astype(jnp.bfloat16)
 
 
-def row_kernel(info_ref, after_ref, tall_ref, flat_ref):
-    del after_ref
+def spot_map(info_ref, pair):
+    aims = [info_ref[pair, row : row + 1, :] for row in (AIM_ROW, AIM_ROW + 1)]
+    rows_off = iota((FOCAL, FOCAL), 0).astype(jnp.float32) - aims[0]
+    cols_off = iota((1, FOCAL), 1).astype(jnp.float32) - aims[1]
+    return jnp.exp(-(rows_off * rows_off + cols_off * cols_off) / (2.0 * SPOT * SPOT))
+
+
+def total_of(value):
+    return jnp.sum(jnp.sum(value, axis=0, keepdims=True), axis=1, keepdims=True)
+
+
+def row_kernel(info_ref, tall_ref, flat_ref, spot_ref, gain_ref):
     pairs, _, rows = tall_ref.shape
     rows_dev = flat_ref.shape[1]
     period = 256 * rows
@@ -197,13 +207,9 @@
         real, imag = unit_waves((iota((rows_dev, 1), 0) + first) * focal, period)
         flat_ref[pair, :, :FOCAL] = real.astype(jnp.bfloat16)
         flat_ref[pair, :, FOCAL:] = imag.astype(jnp.bfloat16)
-
-
-def spot_map(info_ref, pair):
-    aims = [info_ref[pair, row : row + 1, :] for row in (AIM_ROW, AIM_ROW + 1)]
-    rows_off = iota((FOCAL, FOCAL), 0).astype(jnp.float32) - aims[0]
-    cols_off = iota((1, FOCAL), 1).astype(jnp.float32) - aims[1]
-    return jnp.exp(-(rows_off * rows_off + cols_off * cols_off) / (2.0 * SPOT * SPOT))
+        spot = spot_map(info_ref, pair)
+        spot_ref[pair] = spot
+        gain_ref[pair] = jnp.broadcast_to(FOCAL * FOCAL / total_of(spot), gain_ref.shape[1:])
 
 
 def join_kernel(*refs):
@@ -213,11 +219,7 @@
         out_ref[index * count : (index + 1) * count, :] = ref[...]
 
 
-def total_of(value):
-    return jnp.sum(jnp.sum(value, axis=0, keepdims=True), axis=1, keepdims=True)
-
-
-def focus_kernel(steps, info_ref, tall_ref, flat_ref, after_ref, *refs):
+def focus_kernel(steps, tall_ref, flat_ref, spot_ref, gain_ref, after_ref, *refs):
     del after_ref
     *sect_refs, back_ref, score_ref, rows_ref = refs
     pairs = tall_ref.shape[0]
@@ -234,6 +236,7 @@
         for step, block in zip(steps, blocks, strict=True):
             start = pl.multiple_of((me ^ step) * rows_dev, rows_dev)
             rows_ref[pl.ds(start, rows_dev), :] = block
+    fields, sums = [], []
     for pair in range(pairs):
         lane = 2 * pair * FOCAL
         section = rows_ref[:, lane : lane + 2 * FOCAL]
@@ -241,26 +244,27 @@
         real = mixed[:FOCAL, :FOCAL] - mixed[FOCAL:, FOCAL:]
         imag = mixed[:FOCAL, FOCAL:] + mixed[FOCAL:, :FOCAL]
         power = real * real + imag * imag
-        spot = spot_map(info_ref, pair)
-        spot_power = total_of(spot * power)
-        all_power = total_of(power) + 1e-06
+        fields.append((real, imag))
+        sums.append((total_of(spot_ref[pair] * power), total_of(power) + 1e-06))
+    for pair, ((real, imag), (spot_power, all_power)) in enumerate(zip(fields, sums)):
         ratio = spot_power / all_power
-        factor = FOCAL * FOCAL / total_of(spot)
-        score_ref[pair] = jnp.sum(ratio * factor)
-        weight = (factor * 2.0 / all_power) * (spot - ratio)
+        gain = gain_ref[pair, :1, :1]
+        score_ref[pair] = jnp.sum(ratio * gain)
+        weight = (gain * 2.0 / all_power) * (spot_ref[pair] - ratio)
         real = (weight * real).astype(jnp.bfloat16)
         imag = (weight * imag).astype(jnp.bfloat16)
         stack = jnp.concatenate(
             [jnp.concatenate([real, imag], axis=1), jnp.concatenate([imag, -real], axis=1)], axis=0
         )
         back = jnp.dot(flat_ref[pair], stack, preferred_element_type=jnp.float32)
+        lane = 2 * pair * FOCAL
         back_ref[:, lane : lane + 2 * FOCAL] = back.astype(jnp.bfloat16)
 
 
-def table_kernel(scale, cols, info_ref, width_ref, after_ref, *refs):
-    del after_ref
+def table_kernel(scale, cols, info_ref, width_ref, *refs):
     *out_refs, base_ref, centre_ref, turned_ref = refs
     pairs = base_ref.shape[0]
+    out_refs = out_refs[-2 * pairs :]
     table_refs, slope_refs = out_refs[:pairs], out_refs[pairs:]
     own_cols = width_ref.shape[1]
     period = 256 * cols
@@ -291,7 +295,23 @@
                 slope_refs[pair][1, :, start : start + BLOCK] = slopes[pair][1]
 
 
-def grad_kernel(pairs, back_ref, *refs):
+def last_grad_kernel(pairs, *refs):
+    *in_refs, out_hbm, out_ref, sems = refs
+    size = 2 * BLOCK
+    moves = []
+
+    def send(start):
+        place = slice(start, start + size)
+        index = start // size
+        moves.append(pltpu.make_async_copy(out_ref.at[:, place], out_hbm.at[:, place], sems.at[index]))
+        moves[-1].start()
+
+    grad_kernel(pairs, *in_refs, out_ref, send=send)
+    for move in moves:
+        move.wait()
+
+
+def grad_kernel(pairs, back_ref, *refs, send=None):
     *in_refs, out_ref = refs
     table_refs, slope_refs, total_ref = in_refs[:pairs], in_refs[pairs : 2 * pairs], in_refs[2 * pairs :]
     rows_dev, own_cols = out_ref.shape
@@ -313,6 +333,8 @@
             total += grad[:rows_dev] * slope_refs[pair][0, :, place]
             total += grad[rows_dev:] * slope_refs[pair][1, :, place]
         out_ref[:, place] = total
+        if send is not None:
+            send(start)
 
 
 VMEM = pl.BlockSpec(memory_space=pltpu.VMEM)
@@ -376,61 +398,65 @@
     )(*(in_hbm(value) for value in (wave_ids, angle_ids, targets, coef_table.T, widths)))
     far_info = to_core(info)
 
-    def column_tables(info, after, name):
+    def column_tables(info, name, *after):
         outs = [shape((2 * FOCAL, own_cols), bf16)] * pairs_dev
         outs += [shape((2, rows_dev, own_cols), f32)] * pairs_dev
         got = call(
             functools.partial(table_kernel, math.sqrt(rows * cols), cols), name,
-            outs, [VMEM, VMEM, ANY], [VMEM] * len(outs),
+            outs, [VMEM, VMEM] + [ANY] * len(after), [VMEM] * len(outs),
             [
                 pltpu.VMEM((pairs_dev, 2, BLOCK, FOCAL), f32),
                 pltpu.VMEM((pairs_dev, 2, own_cols // (2 * BLOCK), FOCAL), f32),
                 pltpu.VMEM((pairs_dev, 2, FOCAL, BLOCK), f32),
             ],
             10**9, 10**7,
-        )(info, own, after)
+        )(info, own, *after)
         return list(got[:pairs_dev]), list(got[pairs_dev:])
 
-    tables, slopes = column_tables(info, mine, "own_tables")
+    tall, flat, spots, gains = call(
+        row_kernel, "row_tables",
+        (
+            shape((pairs_dev, 2 * FOCAL, rows), bf16), shape((pairs_dev, rows_dev, 2 * FOCAL), bf16),
+            shape((pairs_dev, FOCAL, FOCAL), f32), shape((pairs_dev, 8, 128), f32),
+        ),
+        [VMEM], (VMEM,) * 4, [], 10**8, 10**6,
+    )(info)
     if peers <= DIRECT:
         steps = list(range(peers - 2, 0, -2))
         got = [exchange(mine, step) for step in steps]
         near = exchange(mine, 1)
-        *got, slopes[0] = lax.optimization_barrier((*got, slopes[0]))
-        first = got[0]
+        first, flat = lax.optimization_barrier((got[0], flat))
         joined = call(join_kernel, "join", shape(((len(steps) - 1) * rows_dev, lanes), bf16),
                       [VMEM] * (len(steps) - 1), VMEM, [], 10**6, 10**6)(*got[1:])
         sections = [mine, near, first, joined, exchange(first, 1), exchange(joined, 1)]
         steps = [0, 1, *steps, *(step ^ 1 for step in steps)]
-        after = joined
+        after = [near, joined]
     else:
         blocks = jnp.tile(mine[None], (peers, 1, 1))
         blocks = lax.all_to_all(blocks, "aperture", 0, 0, tiled=True)
-        sections, steps, after = [blocks.reshape(rows, lanes)], None, mine
-    tall, flat = call(
-        row_kernel, "row_tables",
-        (shape((pairs_dev, 2 * FOCAL, rows), bf16), shape((pairs_dev, rows_dev, 2 * FOCAL), bf16)),
-        [VMEM, ANY], (VMEM, VMEM), [], 10**8, 10**6,
-    )(info, after)
-    far_tables, far_slopes = column_tables(far_info, flat, "far_tables")
+        sections, steps, after = [blocks.reshape(rows, lanes)], None, []
+    tables, slopes = column_tables(info, "own_tables", *after)
+    far_tables, far_slopes = column_tables(far_info, "far_tables", slopes[0])
 
     back, scores = call(
         functools.partial(focus_kernel, steps), "focus",
         (shape((rows_dev, lanes), bf16), shape((pairs_dev,), f32)),
-        [VMEM, VMEM, VMEM, ANY] + [VMEM] * len(sections), (VMEM, SMEM), [pltpu.VMEM((rows, lanes), bf16)],
+        [VMEM] * 4 + [ANY] + [VMEM] * len(sections), (VMEM, SMEM), [pltpu.VMEM((rows, lanes), bf16)],
         10**8, 10**6,
-    )(info, tall, flat, far_slopes[0], *sections)
-
-    def add_grad(back, tables, slopes, name, *total):
-        ins = [back, *tables, *slopes, *total]
-        return call(
-            functools.partial(grad_kernel, pairs_dev), name,
-            shape((rows_dev, own_cols), f32), [VMEM] * len(ins), VMEM, [], 10**9, 10**7,
-        )(*ins)
-
-    far_back = to_core(back)
-    grad = add_grad(back, tables, slopes, "gradient_own")
-    grad = add_grad(far_back, far_tables, far_slopes, "gradient_far", grad)
+    )(tall, flat, spots, gains, far_slopes[0], *sections)
+
+    out = shape((rows_dev, own_cols), f32)
+    ins = [back, *tables, *slopes]
+    grad = call(
+        functools.partial(grad_kernel, pairs_dev), "gradient_own",
+        out, [VMEM] * len(ins), VMEM, [], 10**9, 10**7,
+    )(*ins)
+    ins = [to_core(back), *far_tables, *far_slopes, grad]
+    grad = call(
+        functools.partial(last_grad_kernel, pairs_dev), "gradient_far",
+        out, [VMEM] * len(ins), HBM,
+        [pltpu.VMEM(out.shape, f32), pltpu.SemaphoreType.DMA((own_cols // (2 * BLOCK),))], 10**9, 10**7,
+    )(*ins)
     return grad, scores
 
 

time: 28.8 us -> 26 us (0.903)
  waiting for transfers between devices: 4.6 us -> 1.55 us
  starting transfers between devices: 9.41 us -> 9.78 us
    ppermute x6, waiting for transfers between devices: 4.22 us -> 1.18 us  [exchange(): lax.ppermute(value, 'aperture', [(index, index ^ step) for index in range...]
    pallas_call x1, Pallas kernels: 1.82 us -> 1.22 us  [on_device(): call(functools.partial(focus_kernel, steps), 'focus', (shape((rows_dev, l...]
    pallas_call x1, Pallas kernels: 0.87 us -> 1.37 us  [on_device(): call(row_kernel, 'row_tables', (shape((pairs_dev, 2 * FOCAL, rows), bf16)...]
    ppermute x6, starting transfers between devices: 9.34 us -> 9.71 us  [exchange(): lax.ppermute(value, 'aperture', [(index, index ^ step) for index in range...]
  transfers between devices with their start and end apart: 8 -> 8, of which waited for: 4 -> 2; matrix products, arithmetic and copies ran while one was open for 0% -> 0% of each run, Pallas kernels for 21% -> 25%
where the time goes in v6:
time: 26 us; the launch traced here: 25.9 us
  Pallas kernels  13.8 us (53%)
  starting transfers between devices  9.78 us (38%)
  waiting for transfers between devices  1.55 us (6%)
  between operations  0.73 us (3%)
    ppermute x6, starting transfers between devices, exchange(): lax.ppermute(value, 'aperture', [(index, index ^ step) for index in range...  9.71 us
    pallas_call x1, Pallas kernels, on_device(): call(forward_kernel, 'forward', (shape((rows_dev, lanes), bf16), shape((p...  4.64 us
    pallas_call x2, Pallas kernels, column_tables(): call(functools.partial(table_kernel, math.sqrt(rows * cols), cols), name,...  4.2 us
    pallas_call x1, Pallas kernels, on_device(): call(functools.partial(last_grad_kernel, pairs_dev), 'gradient_far', out,...  1.53 us
    pallas_call x1, Pallas kernels, on_device(): call(row_kernel, 'row_tables', (shape((pairs_dev, 2 * FOCAL, rows), bf16)...  1.37 us
    pallas_call x1, Pallas kernels, on_device(): call(functools.partial(focus_kernel, steps), 'focus', (shape((rows_dev, l...  1.22 us
    ppermute x6, waiting for transfers between devices, exchange(): lax.ppermute(value, 'aperture', [(index, index ^ step) for index in range...  1.18 us
    pallas_call x1, Pallas kernels, on_device(): call(functools.partial(grad_kernel, pairs_dev), 'gradient_own', out, [VME...  0.87 us
  transfers between devices with their start and end apart: 8, of which 2 were waited for; matrix products, arithmetic and copies ran while one was open for 0% of the time, Pallas kernels for 25%

profile of v6, /device:TPU:0, one launch (start us, length us, event | category | flops | bytes accessed | tf_op | source)
XLA Modules:
  0.0 25.9 jit_solution(14886902742612254544)
XLA Ops:
  0.6 4.6 %forward.1 = (bf16[32,1024]{1,0:T(8,128)(2,1)S(1)}, f32[2,24,256]{2,1,0:T(8,128)S(1)}, f32[32,2048]{1,0:T(8,128)S(1)}) custom-call(s32[2]{0:T(128)} %wave_hbm.1, s32[2]{0:T(128)} %angle_hbm.1, s32[2,2]{1,0:T(2,128)} %aim_hbm.1, f32[16,256]{1,0:T(8,128)} %bitcast.1, f32[32,4096]{1,0:T(8,128)} %width_hbm.1), custom_call_target="tpu_custom_call" | custom-call | flops 1000000000 | bytes 10000000 | tf_op jit(solution)/shard_map/forward/pallas_call | solution.py:379
  5.3 5.1 %collective-permute-start = (bf16[32,1024]{1,0:T(8,128)(2,1)S(1)}, bf16[32,1024]{1,0:T(8,128)(2,1)S(1)}, u32[]{:S(2)}, u32[]{:S(2)}) collective-permute-start(bf16[32,1024]{1,0:T(8,128)(2,1)S(1)} %get-tuple-element.23.refs_0_), channel_id=1, source_target_pairs={{0,12},{2,14},{4,8},{6,10},{8,4},{10,6},{12,0},{14,2},{1,13},{3,15... | collective-permute-start | bytes 196616 | tf_op jit(solution)/shard_map/ppermute | solution.py:374
  10.4 0.0 collective-permute-start.3
  10.4 0.6 %collective-permute-start.4 = (bf16[32,1024]{1,0:T(8,128)(2,1)S(1)}, bf16[32,1024]{1,0:T(8,128)(2,1)S(1)}, u32[]{:S(2)}, u32[]{:S(2)}) collective-permute-start(bf16[32,1024]{1,0:T(8,128)(2,1)S(1)} %get-tuple-element.23.refs_0_), channel_id=1, source_target_pairs={{0,4},{2,6},{4,0},{6,2},{8,12},{10,14},{12,8},{14,10},{1,5},{3,7},... | collective-permute-start | bytes 196616 | tf_op jit(solution)/shard_map/ppermute | solution.py:374
  11.0 1.6 %collective-permute-start.2 = (bf16[32,1024]{1,0:T(8,128)(2,1)S(1)}, bf16[32,1024]{1,0:T(8,128)(2,1)S(1)}, u32[]{:S(2)}, u32[]{:S(2)}) collective-permute-start(bf16[32,1024]{1,0:T(8,128)(2,1)S(1)} %get-tuple-element.23.refs_0_), channel_id=1, source_target_pairs={{0,2},{2,0},{4,6},{6,4},{8,10},{10,8},{12,14},{14,12},{1,3},{3,1},... | collective-permute-start | bytes 196616 | tf_op jit(solution)/shard_map/ppermute | solution.py:374
  12.7 0.0 collective-permute-start.1
  12.7 1.4 %row_tables.1 = (bf16[2,512,256]{2,1,0:T(8,128)(2,1)S(1)}, bf16[2,32,512]{2,1,0:T(8,128)(2,1)S(1)}, f32[2,256,256]{2,1,0:T(8,128)S(1)}, f32[2,8,128]{2,1,0:T(8,128)S(1)}) custom-call(f32[2,24,256]{2,1,0:T(8,128)S(1)} %get-tuple-element.21.info_ref), custom_call_target="tpu_custom_call" | custom-call | flops 100000000 | bytes 1000000 | tf_op jit(solution)/shard_map/row_tables/pallas_call | solution.py:416
  14.1 0.0 collective-permute-done.refs_2_
  14.1 0.8 %collective-permute-start.5 = (bf16[32,1024]{1,0:T(8,128)(2,1)S(1)}, bf16[32,1024]{1,0:T(8,128)(2,1)S(1)}, u32[]{:S(2)}, u32[]{:S(2)}) collective-permute-start(bf16[32,1024]{1,0:T(8,128)(2,1)S(1)} %collective-permute-done.refs_2_), channel_id=1, source_target_pairs={{0,2},{2,0},{4,6},{6,4},{8,10},{10,8},{12,14},{14,12},{1,3},{3,1},... | collective-permute-start | bytes 196616 | tf_op jit(solution)/shard_map/ppermute | solution.py:374
  14.8 1.2 %collective-permute-done.3.refs_0_ = bf16[32,1024]{1,0:T(8,128)(2,1)S(1)} collective-permute-done((bf16[32,1024]{1,0:T(8,128)(2,1)S(1)}, bf16[32,1024]{1,0:T(8,128)(2,1)S(1)}, u32[]{:S(2)}, u32[]{:S(2)}) %collective-permute-start.3) | collective-permute-done | bytes 65568 | tf_op jit(solution)/shard_map/ppermute | solution.py:374
  16.0 0.0 collective-permute-done.4.refs_1_
  16.0 1.6 %collective-permute-start.6 = (bf16[64,1024]{1,0:T(8,128)(2,1)S(1)}, bf16[64,1024]{1,0:T(8,128)(2,1)S(1)}, u32[]{:S(2)}, u32[]{:S(2)}) collective-permute-start(bf16[64,1024]{1,0:T(8,128)(2,1)S(1)} %join.1.refs_1_.refs_3_), channel_id=1, source_target_pairs={{0,2},{2,0},{4,6},{6,4},{8,10},{10,8},{12,14},{14,12},{1,3},{3,1},... | collective-permute-start | bytes 393224 | tf_op jit(solution)/shard_map/ppermute | solution.py:374
  17.6 0.0 collective-permute-done.2.refs_0_.refs_1_
  17.6 2.1 %own_tables.1 = (bf16[512,2048]{1,0:T(8,128)(2,1)S(1)}, bf16[512,2048]{1,0:T(8,128)(2,1)S(1)}, f32[2,32,2048]{2,1,0:T(8,128)S(1)}, f32[2,32,2048]{2,1,0:T(8,128)S(1)}) custom-call(f32[2,24,256]{2,1,0:T(8,128)S(1)} %get-tuple-element.21.info_ref, f32[32,2048]{1,0:T(8,128)S(1)} %get-tuple-element.28.width_ref, ...), custom_call_target="tpu_custom_call" | custom-call | flops 1000000000 | bytes 10000000 | tf_op jit(solution)/shard_map/own_tables/pallas_call | solution.py:404
  19.7 0.0 collective-permute-done.1.info_ref
  19.7 2.1 %far_tables.1 = (bf16[512,2048]{1,0:T(8,128)(2,1)S(1)}, bf16[512,2048]{1,0:T(8,128)(2,1)S(1)}, f32[2,32,2048]{2,1,0:T(8,128)S(1)}, f32[2,32,2048]{2,1,0:T(8,128)S(1)}) custom-call(f32[2,24,256]{2,1,0:T(8,128)S(1)} %collective-permute-done.1.info_ref, f32[32,2048]{1,0:T(8,128)S(1)} %get-tuple-element.28.width_ref, ...), custom_call_target="tpu_custom_call" | custom-call | flops 1000000000 | bytes 10000000 | tf_op jit(solution)/shard_map/far_tables/pallas_call | solution.py:404
  21.8 0.0 collective-permute-done.5.refs_4_
  21.8 0.0 collective-permute-done.6.refs_5_
  21.8 1.2 %focus.1 = (bf16[32,1024]{1,0:T(8,128)(2,1)S(1)}, f32[2]{0:T(128)}) custom-call(bf16[2,512,256]{2,1,0:T(8,128)(2,1)S(1)} %get-tuple-element.22.tall_ref, bf16[2,32,512]{2,1,0:T(8,128)(2,1)S(1)} %get-tuple-element.25.flat_ref, f32[2,256,256]{2,1,0:T(8,128)S(1)} %get-tuple-element.26.spot_ref, f32[2,8,128]{2,1,0:T(8,128)S(1)} %get-tuple-element.27.gain_ref, ...), custom_call_target="tpu_custom_call" | custom-call | flops 100000000 | bytes 1000000 | tf_op jit(solution)/shard_map/focus/pallas_call | solution.py:441
  23.0 0.1 collective-permute-start.7
  23.1 0.9 %gradient_own.1.refs_5_ = f32[32,2048]{1,0:T(8,128)S(1)} custom-call(bf16[32,1024]{1,0:T(8,128)(2,1)S(1)} %get-tuple-element.32.back_ref, bf16[512,2048]{1,0:T(8,128)(2,1)S(1)} %get-tuple-element.36.refs_0_, bf16[512,2048]{1,0:T(8,128)(2,1)S(1)} %get-tuple-element.37.refs_1_, f32[2,32,2048]{2,1,0:T(8,128)S(1)} %get-tuple-element.29.refs_0_.refs_2_, ...), custom_call_target="tpu_custom_call" | custom-call | flops 1000000000 | bytes 10000000 | tf_op jit(solution)/shard_map/gradient_own/pallas_call | solution.py:450
  24.0 0.4 %collective-permute-done.7.refs_0_ = bf16[32,1024]{1,0:T(8,128)(2,1)S(1)} collective-permute-done((bf16[32,1024]{1,0:T(8,128)(2,1)S(1)}, bf16[32,1024]{1,0:T(8,128)(2,1)S(1)}, u32[]{:S(2)}, u32[]{:S(2)}) %collective-permute-start.7) | collective-permute-done | bytes 65568 | tf_op jit(solution)/shard_map/ppermute | solution.py:377
  24.4 1.5 %gradient_far.1 = f32[32,2048]{1,0:T(8,128)} custom-call(bf16[32,1024]{1,0:T(8,128)(2,1)S(1)} %collective-permute-done.7.refs_0_, bf16[512,2048]{1,0:T(8,128)(2,1)S(1)} %get-tuple-element.33.refs_1_, bf16[512,2048]{1,0:T(8,128)(2,1)S(1)} %get-tuple-element.34.refs_2_, f32[2,32,2048]{2,1,0:T(8,128)S(1)} %get-tuple-element.30.after_ref.refs_3_, ...), custom_call_target="tpu_custom_call" | custom-call | flops 1000000000 | bytes 10000000 | tf_op jit(solution)/shard_map/gradient_far/pallas_call | solution.py:455
  (1 shorter events, 0.0 us)
Async XLA Ops:
  5.3 8.8 %collective-permute-start = (bf16[32,1024]{1,0:T(8,128)(2,1)S(1)}, bf16[32,1024]{1,0:T(8,128)(2,1)S(1)}, u32[]{:S(2)}, u32[]{:S(2)}) collective-permute-start(bf16[32,1024]{1,0:T(8,128)(2,1)S(1)} %get-tuple-element.23.refs_0_), channel_id=1, source_target_pairs={{0,12},{2,14},{4,8},{6,10},{8,4},{10,6},{12,0},{14,2},{1,13},{3,15... | collective-permute-start | bytes 196616 | tf_op jit(solution)/shard_map/ppermute | solution.py:374
  10.4 5.6 %collective-permute-start.3 = (bf16[32,1024]{1,0:T(8,128)(2,1)S(1)}, bf16[32,1024]{1,0:T(8,128)(2,1)S(1)}, u32[]{:S(2)}, u32[]{:S(2)}) collective-permute-start(bf16[32,1024]{1,0:T(8,128)(2,1)S(1)} %get-tuple-element.23.refs_0_), channel_id=1, source_target_pairs={{0,8},{2,10},{4,12},{6,14},{8,0},{10,2},{12,4},{14,6},{1,9},{3,11}... | collective-permute-start | bytes 196616 | tf_op jit(solution)/shard_map/ppermute | solution.py:374
  10.4 5.6 %collective-permute-start.4 = (bf16[32,1024]{1,0:T(8,128)(2,1)S(1)}, bf16[32,1024]{1,0:T(8,128)(2,1)S(1)}, u32[]{:S(2)}, u32[]{:S(2)}) collective-permute-start(bf16[32,1024]{1,0:T(8,128)(2,1)S(1)} %get-tuple-element.23.refs_0_), channel_id=1, source_target_pairs={{0,4},{2,6},{4,0},{6,2},{8,12},{10,14},{12,8},{14,10},{1,5},{3,7},... | collective-permute-start | bytes 196616 | tf_op jit(solution)/shard_map/ppermute | solution.py:374
  11.0 6.5 %collective-permute-start.2 = (bf16[32,1024]{1,0:T(8,128)(2,1)S(1)}, bf16[32,1024]{1,0:T(8,128)(2,1)S(1)}, u32[]{:S(2)}, u32[]{:S(2)}) collective-permute-start(bf16[32,1024]{1,0:T(8,128)(2,1)S(1)} %get-tuple-element.23.refs_0_), channel_id=1, source_target_pairs={{0,2},{2,0},{4,6},{6,4},{8,10},{10,8},{12,14},{14,12},{1,3},{3,1},... | collective-permute-start | bytes 196616 | tf_op jit(solution)/shard_map/ppermute | solution.py:374
  12.7 7.0 %collective-permute-start.1 = (f32[2,24,256]{2,1,0:T(8,128)S(1)}, f32[2,24,256]{2,1,0:T(8,128)S(1)}, u32[]{:S(2)}, u32[]{:S(2)}) collective-permute-start(f32[2,24,256]{2,1,0:T(8,128)S(1)} %get-tuple-element.21.info_ref), channel_id=1, source_target_pairs={{0,1},{1,0},{2,3},{3,2},{4,5},{5,4},{6,7},{7,6},{8,9},{9,8},{10,11... | collective-permute-start | bytes 147464 | tf_op jit(solution)/shard_map/ppermute | solution.py:377
  14.1 7.7 %collective-permute-start.5 = (bf16[32,1024]{1,0:T(8,128)(2,1)S(1)}, bf16[32,1024]{1,0:T(8,128)(2,1)S(1)}, u32[]{:S(2)}, u32[]{:S(2)}) collective-permute-start(bf16[32,1024]{1,0:T(8,128)(2,1)S(1)} %collective-permute-done.refs_2_), channel_id=1, source_target_pairs={{0,2},{2,0},{4,6},{6,4},{8,10},{10,8},{12,14},{14,12},{1,3},{3,1},... | collective-permute-start | bytes 196616 | tf_op jit(solution)/shard_map/ppermute | solution.py:374
  16.0 5.8 %collective-permute-start.6 = (bf16[64,1024]{1,0:T(8,128)(2,1)S(1)}, bf16[64,1024]{1,0:T(8,128)(2,1)S(1)}, u32[]{:S(2)}, u32[]{:S(2)}) collective-permute-start(bf16[64,1024]{1,0:T(8,128)(2,1)S(1)} %join.1.refs_1_.refs_3_), channel_id=1, source_target_pairs={{0,2},{2,0},{4,6},{6,4},{8,10},{10,8},{12,14},{14,12},{1,3},{3,1},... | collective-permute-start | bytes 393224 | tf_op jit(solution)/shard_map/ppermute | solution.py:374
  23.0 1.3 %collective-permute-start.7 = (bf16[32,1024]{1,0:T(8,128)(2,1)S(1)}, bf16[32,1024]{1,0:T(8,128)(2,1)S(1)}, u32[]{:S(2)}, u32[]{:S(2)}) collective-permute-start(bf16[32,1024]{1,0:T(8,128)(2,1)S(1)} %get-tuple-element.32.back_ref), channel_id=1, source_target_pairs={{0,1},{1,0},{2,3},{3,2},{4,5},{5,4},{6,7},{7,6},{8,9},{9,8},{10,11... | collective-permute-start | bytes 196616 | tf_op jit(solution)/shard_map/ppermute | solution.py:377

commit v7 on v6

--- a/solution.py
+++ b/solution.py
@@ -14,6 +14,7 @@
 TERMS = 8
 BLOCK = 256
 GRAIN = 16
+LANES = 128
 VMEM_LIMIT = 16 * 1024 * 1024
 WAVE_ROW, ANGLE_ROW, AIM_ROW, INFO_ROWS = 16, 17, 18, 24
 DIRECT = 16
@@ -74,17 +75,6 @@
     centre_ref[1] = cent_i
 
 
-def block_pair(base_ref, centre_ref, index):
-    cent_r = centre_ref[0, index : index + 1, :]
-    cent_i = centre_ref[1, index : index + 1, :]
-    base_r, base_i = base_ref[0], base_ref[1]
-    rr, ii = base_r * cent_r, base_i * cent_i
-    ri, ir = base_r * cent_i, base_i * cent_r
-    before = ((rr + ii).astype(jnp.bfloat16), (ir - ri).astype(jnp.bfloat16))
-    after = ((rr - ii).astype(jnp.bfloat16), (ir + ri).astype(jnp.bfloat16))
-    return before, after
-
-
 def near_fields(s, info_ref, pairs):
     def coef(pair, row):
         return info_ref[pair, row : row + 1, :]
@@ -115,13 +105,49 @@
     return outs
 
 
+def turn_round(value):
+    rows, cols = value.shape
+    order = LANES - 1 - iota((rows, LANES), 1)
+    parts = [
+        jnp.take_along_axis(value[:, start : start + LANES], order, axis=1)
+        for start in range(cols - LANES, -1, -LANES)
+    ]
+    return jnp.concatenate(parts, axis=1)
+
+
+def write_tables(index, base_ref, centres, table_ref):
+    middle = table_ref.shape[1] // 2
+    cent_r, cent_i = (centre[:, index : index + 1] for centre in centres)
+    base_r, base_i = base_ref[0], base_ref[1]
+    rr, ii = base_r * cent_r, base_i * cent_i
+    ri, ir = base_r * cent_i, base_i * cent_r
+    left, right = middle - (index + 1) * BLOCK, middle + index * BLOCK
+    tables = []
+    for start, values in ((left, (rr + ii, ir - ri)), (right, (rr - ii, ir + ri))):
+        table = jnp.concatenate(values, axis=0).astype(jnp.bfloat16)
+        table_ref[:, start : start + BLOCK] = table
+        tables.append(table)
+    return tables
+
+
+def turned_waves(info_ref, pair, cols, base_ref, centre_ref, turned_ref):
+    shift = cols // 4 + 1 - lax.axis_index("wave")
+    fill_base(column_freq(info_ref, pair), shift, 256 * cols, base_ref, centre_ref)
+    for part in range(2):
+        turned_ref[part] = base_ref[part].T
+    return [centre_ref[part].T for part in range(2)]
+
+
 def forward_kernel(
-    wave_hbm, angle_hbm, aim_hbm, coef_hbm, width_hbm, mine_ref, info_ref, own_ref,
-    wave_ref, angle_ref, aim_ref, coef_ref, width_ref, base_ref, centre_ref, acc_ref, sems,
+    wave_hbm, angle_hbm, aim_hbm, coef_hbm, width_hbm, mine_ref, info_ref, own_ref, *refs
 ):
+    pairs = info_ref.shape[0]
+    table_refs, refs = refs[:pairs], refs[pairs:]
+    (
+        wave_ref, angle_ref, aim_ref, coef_ref, width_ref, far_ref, base_ref, centre_ref, turned_ref, acc_ref, sems,
+    ) = refs
     rows_dev, cols = width_ref.shape
-    pairs = wave_ref.shape[0]
-    period = 256 * cols
+    half = cols // 2
     moves = [
         pltpu.make_async_copy(source, target, sems.at[index])
         for index, (source, target) in enumerate((
@@ -142,29 +168,63 @@
         ids = jnp.where(row == AIM_ROW, aim_ref[pair, 0], ids)
         ids = jnp.where(row == AIM_ROW + 1, aim_ref[pair, 1], ids)
         info_ref[pair, WAVE_ROW:, :] = ids.astype(jnp.float32)
-    for pair in range(pairs):
-        fill_base(column_freq(info_ref, pair), 0, period, base_ref.at[pair], centre_ref.at[pair])
+    centres = [
+        turned_waves(info_ref, pair, cols, base_ref.at[pair], centre_ref.at[pair], turned_ref.at[pair])
+        for pair in range(pairs)
+    ]
     acc_ref[...] = jnp.zeros_like(acc_ref)
     moves[4].wait()
-    for index in range(cols // (2 * BLOCK)):
-        left = cols // 2 - (index + 1) * BLOCK
-        right = cols // 2 + index * BLOCK
-        nears = []
-        for start in (left, right):
-            outs = near_fields(width_ref[:, start : start + BLOCK], info_ref, pairs)
-            nears.append([jnp.concatenate(out, axis=0).astype(jnp.bfloat16) for out in outs])
+    core = lax.axis_index("wave")
+
+    @pl.when(core == 1)
+    def _():
+        own_ref[...] = width_ref[:, half:]
+        far_ref[...] = pltpu.roll(turn_round(width_ref[:, :half]), 1, 1)
+
+    @pl.when(core == 0)
+    def _():
+        own_ref[...] = turn_round(width_ref[:, :half])
+        far_ref[...] = pltpu.roll(width_ref[:, half:], half - 1, 1)
+
+    void = jnp.where(core == 1, 0, half - 1)
+    for index in range(half // (2 * BLOCK)):
+        nears = [[] for _ in range(pairs)]
+        for start in (half // 2 - (index + 1) * BLOCK, half // 2 + index * BLOCK):
+            sides = []
+            for ref in (own_ref, far_ref):
+                sides.append(near_fields(ref[:, start : start + BLOCK], info_ref, pairs))
+            if start in (0, half - BLOCK):
+                keep = iota((rows_dev, BLOCK), 1) + start != void
+                sides[1] = [[jnp.where(keep, part, 0.0) for part in out] for out in sides[1]]
+            for pair in range(pairs):
+                both = jnp.concatenate([*sides[0][pair], *sides[1][pair]], axis=0)
+                nears[pair].append(both.astype(jnp.bfloat16))
         for pair in range(pairs):
-            before, after = block_pair(base_ref.at[pair], centre_ref.at[pair], index)
-            near = jnp.concatenate([nears[0][pair], nears[1][pair]], axis=1)
-            for part in range(2):
-                table = jnp.concatenate([before[part], after[part]], axis=0)
-                acc_ref[pair, part] += jnp.dot(near, table, preferred_element_type=jnp.float32)
-    own_cols = own_ref.shape[1]
-    first = pl.multiple_of(lax.axis_index("wave") * own_cols, own_cols)
-    own_ref[...] = width_ref[:, pl.ds(first, own_cols)]
+            tables = write_tables(index, turned_ref.at[pair], centres[pair], table_refs[pair])
+            acc_ref[pair] += lax.dot_general(
+                jnp.concatenate(nears[pair], axis=1),
+                jnp.concatenate(tables, axis=1),
+                (((1,), (1,)), ((), ())),
+                preferred_element_type=jnp.float32,
+            )
+    alone = jnp.where(core == 1, 0, half)
+    column = width_ref[:, pl.ds(pl.multiple_of(alone, LANES), LANES)]
+    columns = near_fields(jnp.concatenate([column, column], axis=1), info_ref, pairs)
     for pair in range(pairs):
-        real = acc_ref[pair, 0, :rows_dev] - acc_ref[pair, 1, rows_dev:]
-        imag = acc_ref[pair, 1, :rows_dev] + acc_ref[pair, 0, rows_dev:]
+        acc = [acc_ref[pair, part * rows_dev : (part + 1) * rows_dev, :] for part in range(4)]
+        (own_rr, own_ri), (own_ir, own_ii), (far_rr, far_ri), (far_ir, far_ii) = (
+            (part[:, :FOCAL], part[:, FOCAL:]) for part in acc
+        )
+        cross_r, cross_i = far_ii - own_ii, own_ri - far_ri
+        real = own_rr + far_rr + jnp.where(core == 1, cross_r, -cross_r)
+        imag = own_ir + far_ir + jnp.where(core == 1, cross_i, -cross_i)
+        near_r, near_i = (part[:, :1].astype(jnp.bfloat16).astype(jnp.float32) for part in columns[pair])
+        wave_r, wave_i = (
+            part.astype(jnp.bfloat16).astype(jnp.float32)
+            for part in unit_waves((alone - half) * column_freq(info_ref, pair), 256 * cols)
+        )
+        real = real + (near_r * wave_r - near_i * wave_i)
+        imag = imag + (near_r * wave_i + near_i * wave_r)
         for part, value in enumerate((real, imag)):
             lane = (2 * pair + part) * FOCAL
             mine_ref[:, lane : lane + FOCAL] = value.astype(jnp.bfloat16)
@@ -261,47 +321,39 @@
         back_ref[:, lane : lane + 2 * FOCAL] = back.astype(jnp.bfloat16)
 
 
-def table_kernel(scale, cols, info_ref, width_ref, *refs):
+def table_kernel(scale, cols, info_ref, far_info_ref, width_ref, *refs):
     *out_refs, base_ref, centre_ref, turned_ref = refs
     pairs = base_ref.shape[0]
-    out_refs = out_refs[-2 * pairs :]
+    out_refs = out_refs[-3 * pairs :]
     table_refs, slope_refs = out_refs[:pairs], out_refs[pairs:]
     own_cols = width_ref.shape[1]
-    period = 256 * cols
-    middle = own_cols // 2
-    shift = lax.axis_index("wave") * own_cols + middle - cols // 2
-    for pair in range(pairs):
-        freq = column_freq(info_ref, pair)
-        fill_base(freq, shift, period, base_ref.at[pair], centre_ref.at[pair])
-        for part in range(2):
-            turned_ref[pair, part] = base_ref[pair, part].T
-    centres = [[centre_ref[pair, part].T for part in range(2)] for pair in range(pairs)]
+    centres = [
+        turned_waves(far_info_ref, pair, cols, base_ref.at[pair], centre_ref.at[pair], turned_ref.at[pair])
+        for pair in range(pairs)
+    ]
     for index in range(own_cols // (2 * BLOCK)):
-        left = middle - (index + 1) * BLOCK
-        right = middle + index * BLOCK
         for pair in range(pairs):
-            cent_r, cent_i = (centre[:, index : index + 1] for centre in centres[pair])
-            base_r, base_i = turned_ref[pair, 0], turned_ref[pair, 1]
-            rr, ii = base_r * cent_r, base_i * cent_i
-            ri, ir = base_r * cent_i, base_i * cent_r
-            for start, values in ((left, (rr + ii, ir - ri)), (right, (rr - ii, ir + ri))):
-                for part, value in enumerate(values):
-                    row = part * FOCAL
-                    table_refs[pair][row : row + FOCAL, start : start + BLOCK] = value.astype(jnp.bfloat16)
-        for start in (left, right):
-            slopes = near_slopes(width_ref[:, start : start + BLOCK], scale, info_ref, pairs)
-            for pair in range(pairs):
-                slope_refs[pair][0, :, start : start + BLOCK] = slopes[pair][0]
-                slope_refs[pair][1, :, start : start + BLOCK] = slopes[pair][1]
+            write_tables(index, turned_ref.at[pair], centres[pair], table_refs[pair])
+        for start in (2 * index * BLOCK, (2 * index + 1) * BLOCK):
+            place = slice(start, start + BLOCK)
+            for core, ref in enumerate((info_ref, far_info_ref)):
+                slopes = near_slopes(width_ref[:, place], scale, ref, pairs)
+                for pair in range(pairs):
+                    slope_refs[core * pairs + pair][0, :, place] = slopes[pair][0]
+                    slope_refs[core * pairs + pair][1, :, place] = slopes[pair][1]
 
 
 def last_grad_kernel(pairs, *refs):
     *in_refs, out_hbm, out_ref, sems = refs
+    rows_dev, own_cols = out_ref.shape
     size = 2 * BLOCK
+    core = lax.axis_index("wave")
     moves = []
 
-    def send(start):
-        place = slice(start, start + size)
+    def send(start, total):
+        place = pl.multiple_of(jnp.where(core == 1, start, own_cols - size - start), size)
+        place = pl.ds(place, size)
+        out_ref[:, place] = jnp.where(core == 1, total, turn_round(total))
         index = start // size
         moves.append(pltpu.make_async_copy(out_ref.at[:, place], out_hbm.at[:, place], sems.at[index]))
         moves[-1].start()
@@ -315,13 +367,16 @@
     *in_refs, out_ref = refs
     table_refs, slope_refs, total_ref = in_refs[:pairs], in_refs[pairs : 2 * pairs], in_refs[2 * pairs :]
     rows_dev, own_cols = out_ref.shape
+    core = lax.axis_index("wave")
     lefts = []
     for pair in range(pairs):
         lane = 2 * pair * FOCAL
         real, imag = back_ref[:, lane : lane + FOCAL], back_ref[:, lane + FOCAL : lane + 2 * FOCAL]
+        above = jnp.where(core == 1, imag, -imag)
+        below = jnp.where(core == 1, -real, real)
         lefts.append(
             jnp.concatenate(
-                [jnp.concatenate([real, imag], axis=1), jnp.concatenate([imag, -real], axis=1)], axis=0
+                [jnp.concatenate([real, above], axis=1), jnp.concatenate([imag, below], axis=1)], axis=0
             )
         )
     size = 2 * BLOCK
@@ -332,9 +387,10 @@
             grad = jnp.dot(lefts[pair], table_refs[pair][:, place], preferred_element_type=jnp.float32)
             total += grad[:rows_dev] * slope_refs[pair][0, :, place]
             total += grad[rows_dev:] * slope_refs[pair][1, :, place]
-        out_ref[:, place] = total
-        if send is not None:
-            send(start)
+        if send is None:
+            out_ref[:, place] = total
+        else:
+            send(start, total)
 
 
 VMEM = pl.BlockSpec(memory_space=pltpu.VMEM)
@@ -376,42 +432,33 @@
     def to_core(value):
         return lax.ppermute(value, "wave", [(index, (index + 1) % copies) for index in range(copies)])
 
-    mine, info, own = call(
+    waves = [
+        pltpu.VMEM((pairs_dev, 2, BLOCK, FOCAL), f32),
+        pltpu.VMEM((pairs_dev, 2, 8, FOCAL), f32),
+        pltpu.VMEM((pairs_dev, 2, FOCAL, BLOCK), f32),
+    ]
+    mine, info, own, *tables = call(
         forward_kernel, "forward",
         (
             shape((rows_dev, lanes), bf16),
             shape((pairs_dev, INFO_ROWS, FOCAL), f32), shape((rows_dev, own_cols), f32),
+            *[shape((2 * FOCAL, own_cols), bf16)] * pairs_dev,
         ),
-        [HBM] * 5, (VMEM,) * 3,
+        [HBM] * 5, (VMEM,) * (3 + pairs_dev),
         [
             pltpu.SMEM(wave_ids.shape, jnp.int32),
             pltpu.SMEM(angle_ids.shape, jnp.int32),
             pltpu.SMEM(targets.shape, jnp.int32),
             pltpu.VMEM(coef_table.shape[::-1], f32),
             pltpu.VMEM(widths.shape, f32),
-            pltpu.VMEM((pairs_dev, 2, BLOCK, FOCAL), f32),
-            pltpu.VMEM((pairs_dev, 2, cols // (2 * BLOCK), FOCAL), f32),
-            pltpu.VMEM((pairs_dev, 2, 2 * rows_dev, FOCAL), f32),
+            pltpu.VMEM((rows_dev, own_cols), f32),
+            *waves,
+            pltpu.VMEM((pairs_dev, 4 * rows_dev, 2 * FOCAL), f32),
             pltpu.SemaphoreType.DMA((5,)),
         ],
         10**9, 10**7,
     )(*(in_hbm(value) for value in (wave_ids, angle_ids, targets, coef_table.T, widths)))
     far_info = to_core(info)
-
-    def column_tables(info, name, *after):
-        outs = [shape((2 * FOCAL, own_cols), bf16)] * pairs_dev
-        outs += [shape((2, rows_dev, own_cols), f32)] * pairs_dev
-        got = call(
-            functools.partial(table_kernel, math.sqrt(rows * cols), cols), name,
-            outs, [VMEM, VMEM] + [ANY] * len(after), [VMEM] * len(outs),
-            [
-                pltpu.VMEM((pairs_dev, 2, BLOCK, FOCAL), f32),
-                pltpu.VMEM((pairs_dev, 2, own_cols // (2 * BLOCK), FOCAL), f32),
-                pltpu.VMEM((pairs_dev, 2, FOCAL, BLOCK), f32),
-            ],
-            10**9, 10**7,
-        )(info, own, *after)
-        return list(got[:pairs_dev]), list(got[pairs_dev:])
 
     tall, flat, spots, gains = call(
         row_kernel, "row_tables",
@@ -435,8 +482,12 @@
         blocks = jnp.tile(mine[None], (peers, 1, 1))
         blocks = lax.all_to_all(blocks, "aperture", 0, 0, tiled=True)
         sections, steps, after = [blocks.reshape(rows, lanes)], None, []
-    tables, slopes = column_tables(info, "own_tables", *after)
-    far_tables, far_slopes = column_tables(far_info, "far_tables", slopes[0])
+    outs = [shape((2 * FOCAL, own_cols), bf16)] * pairs_dev + [shape((2, rows_dev, own_cols), f32)] * 2 * pairs_dev
+    made = call(
+        functools.partial(table_kernel, math.sqrt(rows * cols), cols), "far_tables",
+        outs, [VMEM] * 3 + [ANY] * len(after), [VMEM] * len(outs), waves, 10**9, 10**7,
+    )(info, far_info, own, *after)
+    far_tables, slopes, far_slopes = made[:pairs_dev], made[pairs_dev : 2 * pairs_dev], made[2 * pairs_dev :]
 
     back, scores = call(
         functools.partial(focus_kernel, steps), "focus",

time: 26 us -> 25.5 us (0.981)
  Pallas kernels: 13.8 us -> 12.4 us
  starting transfers between devices: 9.78 us -> 10.5 us
    pallas_call x2 -> x1, Pallas kernels: 4.2 us -> 2.81 us  [on_device(): call(functools.partial(table_kernel, math.sqrt(rows * cols), cols), 'far_...]
    ppermute x6, starting transfers between devices: 9.71 us -> 10.4 us  [exchange(): lax.ppermute(value, 'aperture', [(index, index ^ step) for index in range...]
  transfers between devices with their start and end apart: 8 -> 8, of which waited for: 2 -> 3; matrix products, arithmetic and copies ran while one was open for 0% -> 0% of each run, Pallas kernels for 25% -> 20%
where the time goes in v7:
time: 25.5 us; the launch traced here: 25.3 us
  Pallas kernels  12.4 us (49%)
  starting transfers between devices  10.5 us (41%)
  waiting for transfers between devices  1.78 us (7%)
  between operations  0.7 us (3%)
    ppermute x6, starting transfers between devices, exchange(): lax.ppermute(value, 'aperture', [(index, index ^ step) for index in range...  10.4 us
    pallas_call x1, Pallas kernels, on_device(): call(forward_kernel, 'forward', (shape((rows_dev, lanes), bf16), shape((p...  4.47 us
    pallas_call x1, Pallas kernels, on_device(): call(functools.partial(table_kernel, math.sqrt(rows * cols), cols), 'far_...  2.81 us
    pallas_call x1, Pallas kernels, on_device(): call(functools.partial(last_grad_kernel, pairs_dev), 'gradient_far', out,...  1.6 us
    ppermute x6, waiting for transfers between devices, exchange(): lax.ppermute(value, 'aperture', [(index, index ^ step) for index in range...  1.41 us
    pallas_call x1, Pallas kernels, on_device(): call(row_kernel, 'row_tables', (shape((pairs_dev, 2 * FOCAL, rows), bf16)...  1.37 us
    pallas_call x1, Pallas kernels, on_device(): call(functools.partial(focus_kernel, steps), 'focus', (shape((rows_dev, l...  1.22 us
    pallas_call x1, Pallas kernels, on_device(): call(functools.partial(grad_kernel, pairs_dev), 'gradient_own', out, [VME...  0.86 us
  transfers between devices with their start and end apart: 8, of which 3 were waited for; matrix products, arithmetic and copies ran while one was open for 0% of the time, Pallas kernels for 20%

profile of v7, /device:TPU:0, one launch (start us, length us, event | category | flops | bytes accessed | tf_op | source)
XLA Modules:
  0.0 25.3 jit_solution(9828770478244998927)
XLA Ops:
  0.6 4.5 %forward.1 = (bf16[32,1024]{1,0:T(8,128)(2,1)S(1)}, f32[2,24,256]{2,1,0:T(8,128)S(1)}, f32[32,2048]{1,0:T(8,128)S(1)}, bf16[512,2048]{1,0:T(8,128)(2,1)S(1)}, bf16[512,2048]{1,0:T(8,128)(2,1)S(1)}) custom-call(s32[2]{0:T(128)} %wave_hbm.1, s32[2]{0:T(128)} %angle_hbm.1, s32[2,2]{1,0:T(2,128)} %aim_hbm.1, f32[16,256]{1,0:T(8,128)} %bitcast.1, ...), custom_call_target="tpu_custom_call" | custom-call | flops 1000000000 | bytes 10000000 | tf_op jit(solution)/shard_map/forward/pallas_call | solution.py:440
  5.1 4.1 %collective-permute-start.3 = (bf16[32,1024]{1,0:T(8,128)(2,1)S(1)}, bf16[32,1024]{1,0:T(8,128)(2,1)S(1)}, u32[]{:S(2)}, u32[]{:S(2)}) collective-permute-start(bf16[32,1024]{1,0:T(8,128)(2,1)S(1)} %get-tuple-element.23.refs_0_), channel_id=1, source_target_pairs={{0,8},{2,10},{4,12},{6,14},{8,0},{10,2},{12,4},{14,6},{1,9},{3,11}... | collective-permute-start | bytes 196616 | tf_op jit(solution)/shard_map/ppermute | solution.py:430
  9.2 1.6 %collective-permute-start.4 = (bf16[32,1024]{1,0:T(8,128)(2,1)S(1)}, bf16[32,1024]{1,0:T(8,128)(2,1)S(1)}, u32[]{:S(2)}, u32[]{:S(2)}) collective-permute-start(bf16[32,1024]{1,0:T(8,128)(2,1)S(1)} %get-tuple-element.23.refs_0_), channel_id=1, source_target_pairs={{0,4},{2,6},{4,0},{6,2},{8,12},{10,14},{12,8},{14,10},{1,5},{3,7},... | collective-permute-start | bytes 196616 | tf_op jit(solution)/shard_map/ppermute | solution.py:430
  10.8 0.0 collective-permute-start
  10.8 1.7 %collective-permute-start.2 = (bf16[32,1024]{1,0:T(8,128)(2,1)S(1)}, bf16[32,1024]{1,0:T(8,128)(2,1)S(1)}, u32[]{:S(2)}, u32[]{:S(2)}) collective-permute-start(bf16[32,1024]{1,0:T(8,128)(2,1)S(1)} %get-tuple-element.23.refs_0_), channel_id=1, source_target_pairs={{0,2},{2,0},{4,6},{6,4},{8,10},{10,8},{12,14},{14,12},{1,3},{3,1},... | collective-permute-start | bytes 196616 | tf_op jit(solution)/shard_map/ppermute | solution.py:430
  12.5 0.0 collective-permute-start.1
  12.5 0.0 collective-permute-done.3.refs_0_
  12.5 1.0 %collective-permute-done.4.refs_1_ = bf16[32,1024]{1,0:T(8,128)(2,1)S(1)} collective-permute-done((bf16[32,1024]{1,0:T(8,128)(2,1)S(1)}, bf16[32,1024]{1,0:T(8,128)(2,1)S(1)}, u32[]{:S(2)}, u32[]{:S(2)}) %collective-permute-start.4) | collective-permute-done | bytes 65568 | tf_op jit(solution)/shard_map/ppermute | solution.py:430
  13.5 1.6 %collective-permute-start.6 = (bf16[64,1024]{1,0:T(8,128)(2,1)S(1)}, bf16[64,1024]{1,0:T(8,128)(2,1)S(1)}, u32[]{:S(2)}, u32[]{:S(2)}) collective-permute-start(bf16[64,1024]{1,0:T(8,128)(2,1)S(1)} %join.1.refs_1_.refs_3_), channel_id=1, source_target_pairs={{0,2},{2,0},{4,6},{6,4},{8,10},{10,8},{12,14},{14,12},{1,3},{3,1},... | collective-permute-start | bytes 393224 | tf_op jit(solution)/shard_map/ppermute | solution.py:430
  15.1 1.4 %row_tables.1 = (bf16[2,512,256]{2,1,0:T(8,128)(2,1)S(1)}, bf16[2,32,512]{2,1,0:T(8,128)(2,1)S(1)}, f32[2,256,256]{2,1,0:T(8,128)S(1)}, f32[2,8,128]{2,1,0:T(8,128)S(1)}) custom-call(f32[2,24,256]{2,1,0:T(8,128)S(1)} %get-tuple-element.21.info_ref), custom_call_target="tpu_custom_call" | custom-call | flops 100000000 | bytes 1000000 | tf_op jit(solution)/shard_map/row_tables/pallas_call | solution.py:463
  16.4 0.4 %collective-permute-done.refs_2_ = bf16[32,1024]{1,0:T(8,128)(2,1)S(1)} collective-permute-done((bf16[32,1024]{1,0:T(8,128)(2,1)S(1)}, bf16[32,1024]{1,0:T(8,128)(2,1)S(1)}, u32[]{:S(2)}, u32[]{:S(2)}) %collective-permute-start) | collective-permute-done | bytes 65568 | tf_op jit(solution)/shard_map/ppermute | solution.py:430
  16.9 1.5 %collective-permute-start.5 = (bf16[32,1024]{1,0:T(8,128)(2,1)S(1)}, bf16[32,1024]{1,0:T(8,128)(2,1)S(1)}, u32[]{:S(2)}, u32[]{:S(2)}) collective-permute-start(bf16[32,1024]{1,0:T(8,128)(2,1)S(1)} %collective-permute-done.refs_2_), channel_id=1, source_target_pairs={{0,2},{2,0},{4,6},{6,4},{8,10},{10,8},{12,14},{14,12},{1,3},{3,1},... | collective-permute-start | bytes 196616 | tf_op jit(solution)/shard_map/ppermute | solution.py:430
  18.3 0.0 collective-permute-done.1.far_info_ref
  18.3 0.0 collective-permute-done.2.refs_0_.refs_1_
  18.4 2.8 %far_tables.1 = (bf16[512,2048]{1,0:T(8,128)(2,1)S(1)}, bf16[512,2048]{1,0:T(8,128)(2,1)S(1)}, f32[2,32,2048]{2,1,0:T(8,128)S(1)}, f32[2,32,2048]{2,1,0:T(8,128)...) custom-call(f32[2,24,256]{2,1,0:T(8,128)S(1)} %get-tuple-element.21.info_ref, ...), custom_call_target="tpu_custom_call" | custom-call | flops 1000000000 | bytes 10000000 | tf_op jit(solution)/shard_map/far_tables/pallas_call | solution.py:486
  21.2 0.0 collective-permute-done.5.refs_4_
  21.2 0.0 collective-permute-done.6.refs_5_
  21.2 1.2 %focus.1 = (bf16[32,1024]{1,0:T(8,128)(2,1)S(1)}, f32[2]{0:T(128)}) custom-call(bf16[2,512,256]{2,1,0:T(8,128)(2,1)S(1)} %get-tuple-element.22.tall_ref, bf16[2,32,512]{2,1,0:T(8,128)(2,1)S(1)} %get-tuple-element.25.flat_ref, f32[2,256,256]{2,1,0:T(8,128)S(1)} %get-tuple-element.26.spot_ref, f32[2,8,128]{2,1,0:T(8,128)S(1)} %get-tuple-element.27.gain_ref, ...), custom_call_target="tpu_custom_call" | custom-call | flops 100000000 | bytes 1000000 | tf_op jit(solution)/shard_map/focus/pallas_call | solution.py:492
  22.4 0.1 collective-permute-start.7
  22.5 0.9 %gradient_own.1.refs_5_ = f32[32,2048]{1,0:T(8,128)S(1)} custom-call(bf16[32,1024]{1,0:T(8,128)(2,1)S(1)} %get-tuple-element.31.back_ref, bf16[512,2048]{1,0:T(8,128)(2,1)S(1)} %get-tuple-element.35.refs_0_, bf16[512,2048]{1,0:T(8,128)(2,1)S(1)} %get-tuple-element.36.refs_1_, f32[2,32,2048]{2,1,0:T(8,128)S(1)} %get-tuple-element.37.refs_2_, ...), custom_call_target="tpu_custom_call" | custom-call | flops 1000000000 | bytes 10000000 | tf_op jit(solution)/shard_map/gradient_own/pallas_call | solution.py:501
  23.4 0.4 %collective-permute-done.7.refs_0_ = bf16[32,1024]{1,0:T(8,128)(2,1)S(1)} collective-permute-done((bf16[32,1024]{1,0:T(8,128)(2,1)S(1)}, bf16[32,1024]{1,0:T(8,128)(2,1)S(1)}, u32[]{:S(2)}, u32[]{:S(2)}) %collective-permute-start.7) | collective-permute-done | bytes 65568 | tf_op jit(solution)/shard_map/ppermute | solution.py:433
  23.7 1.6 %gradient_far.1 = f32[32,2048]{1,0:T(8,128)} custom-call(bf16[32,1024]{1,0:T(8,128)(2,1)S(1)} %collective-permute-done.7.refs_0_, bf16[512,2048]{1,0:T(8,128)(2,1)S(1)} %get-tuple-element.32.refs_1_, bf16[512,2048]{1,0:T(8,128)(2,1)S(1)} %get-tuple-element.33.refs_2_, f32[2,32,2048]{2,1,0:T(8,128)S(1)} %get-tuple-element.29.after_ref.refs_3_, ...), custom_call_target="tpu_custom_call" | custom-call | flops 1000000000 | bytes 10000000 | tf_op jit(solution)/shard_map/gradient_far/pallas_call | solution.py:506
  (1 shorter events, 0.0 us)
Async XLA Ops:
  5.1 7.4 %collective-permute-start.3 = (bf16[32,1024]{1,0:T(8,128)(2,1)S(1)}, bf16[32,1024]{1,0:T(8,128)(2,1)S(1)}, u32[]{:S(2)}, u32[]{:S(2)}) collective-permute-start(bf16[32,1024]{1,0:T(8,128)(2,1)S(1)} %get-tuple-element.23.refs_0_), channel_id=1, source_target_pairs={{0,8},{2,10},{4,12},{6,14},{8,0},{10,2},{12,4},{14,6},{1,9},{3,11}... | collective-permute-start | bytes 196616 | tf_op jit(solution)/shard_map/ppermute | solution.py:430
  9.2 4.3 %collective-permute-start.4 = (bf16[32,1024]{1,0:T(8,128)(2,1)S(1)}, bf16[32,1024]{1,0:T(8,128)(2,1)S(1)}, u32[]{:S(2)}, u32[]{:S(2)}) collective-permute-start(bf16[32,1024]{1,0:T(8,128)(2,1)S(1)} %get-tuple-element.23.refs_0_), channel_id=1, source_target_pairs={{0,4},{2,6},{4,0},{6,2},{8,12},{10,14},{12,8},{14,10},{1,5},{3,7},... | collective-permute-start | bytes 196616 | tf_op jit(solution)/shard_map/ppermute | solution.py:430
  10.8 6.1 %collective-permute-start = (bf16[32,1024]{1,0:T(8,128)(2,1)S(1)}, bf16[32,1024]{1,0:T(8,128)(2,1)S(1)}, u32[]{:S(2)}, u32[]{:S(2)}) collective-permute-start(bf16[32,1024]{1,0:T(8,128)(2,1)S(1)} %get-tuple-element.23.refs_0_), channel_id=1, source_target_pairs={{0,12},{2,14},{4,8},{6,10},{8,4},{10,6},{12,0},{14,2},{1,13},{3,15... | collective-permute-start | bytes 196616 | tf_op jit(solution)/shard_map/ppermute | solution.py:430
  10.8 7.6 %collective-permute-start.2 = (bf16[32,1024]{1,0:T(8,128)(2,1)S(1)}, bf16[32,1024]{1,0:T(8,128)(2,1)S(1)}, u32[]{:S(2)}, u32[]{:S(2)}) collective-permute-start(bf16[32,1024]{1,0:T(8,128)(2,1)S(1)} %get-tuple-element.23.refs_0_), channel_id=1, source_target_pairs={{0,2},{2,0},{4,6},{6,4},{8,10},{10,8},{12,14},{14,12},{1,3},{3,1},... | collective-permute-start | bytes 196616 | tf_op jit(solution)/shard_map/ppermute | solution.py:430
  12.5 5.8 %collective-permute-start.1 = (f32[2,24,256]{2,1,0:T(8,128)S(1)}, f32[2,24,256]{2,1,0:T(8,128)S(1)}, u32[]{:S(2)}, u32[]{:S(2)}) collective-permute-start(f32[2,24,256]{2,1,0:T(8,128)S(1)} %get-tuple-element.21.info_ref), channel_id=1, source_target_pairs={{0,1},{1,0},{2,3},{3,2},{4,5},{5,4},{6,7},{7,6},{8,9},{9,8},{10,11... | collective-permute-start | bytes 147464 | tf_op jit(solution)/shard_map/ppermute | solution.py:433
  13.5 7.7 %collective-permute-start.6 = (bf16[64,1024]{1,0:T(8,128)(2,1)S(1)}, bf16[64,1024]{1,0:T(8,128)(2,1)S(1)}, u32[]{:S(2)}, u32[]{:S(2)}) collective-permute-start(bf16[64,1024]{1,0:T(8,128)(2,1)S(1)} %join.1.refs_1_.refs_3_), channel_id=1, source_target_pairs={{0,2},{2,0},{4,6},{6,4},{8,10},{10,8},{12,14},{14,12},{1,3},{3,1},... | collective-permute-start | bytes 393224 | tf_op jit(solution)/shard_map/ppermute | solution.py:430
  16.9 4.3 %collective-permute-start.5 = (bf16[32,1024]{1,0:T(8,128)(2,1)S(1)}, bf16[32,1024]{1,0:T(8,128)(2,1)S(1)}, u32[]{:S(2)}, u32[]{:S(2)}) collective-permute-start(bf16[32,1024]{1,0:T(8,128)(2,1)S(1)} %collective-permute-done.refs_2_), channel_id=1, source_target_pairs={{0,2},{2,0},{4,6},{6,4},{8,10},{10,8},{12,14},{14,12},{1,3},{3,1},... | collective-permute-start | bytes 196616 | tf_op jit(solution)/shard_map/ppermute | solution.py:430
  22.4 1.3 %collective-permute-start.7 = (bf16[32,1024]{1,0:T(8,128)(2,1)S(1)}, bf16[32,1024]{1,0:T(8,128)(2,1)S(1)}, u32[]{:S(2)}, u32[]{:S(2)}) collective-permute-start(bf16[32,1024]{1,0:T(8,128)(2,1)S(1)} %get-tuple-element.31.back_ref), channel_id=1, source_target_pairs={{0,1},{1,0},{2,3},{3,2},{4,5},{5,4},{6,7},{7,6},{8,9},{9,8},{10,11... | collective-permute-start | bytes 196616 | tf_op jit(solution)/shard_map/ppermute | solution.py:433

commit v8 on v7

--- a/solution.py
+++ b/solution.py
@@ -485,7 +485,7 @@
     outs = [shape((2 * FOCAL, own_cols), bf16)] * pairs_dev + [shape((2, rows_dev, own_cols), f32)] * 2 * pairs_dev
     made = call(
         functools.partial(table_kernel, math.sqrt(rows * cols), cols), "far_tables",
-        outs, [VMEM] * 3 + [ANY] * len(after), [VMEM] * len(outs), waves, 10**9, 10**7,
+        outs, [VMEM] * 3 + [ANY] * len(after), [VMEM] * len(outs), waves, 30 * 10**8, 30 * 10**6,
     )(info, far_info, own, *after)
     far_tables, slopes, far_slopes = made[:pairs_dev], made[pairs_dev : 2 * pairs_dev], made[2 * pairs_dev :]
 

time: 25.5 us -> 25.6 us (level)
  waiting for transfers between devices: 1.78 us -> 2.63 us
  starting transfers between devices: 10.5 us -> 9.78 us
    ppermute x6, waiting for transfers between devices: 1.41 us -> 2.26 us  [exchange(): lax.ppermute(value, 'aperture', [(index, index ^ step) for index in range...]
    ppermute x6, starting transfers between devices: 10.4 us -> 9.7 us  [exchange(): lax.ppermute(value, 'aperture', [(index, index ^ step) for index in range...]
where the time goes in v8:
time: 25.6 us; the launch traced here: 25.4 us
  Pallas kernels  12.3 us (48%)
  starting transfers between devices  9.78 us (38%)
  waiting for transfers between devices  2.63 us (10%)
  between operations  0.7 us (3%)
    ppermute x6, starting transfers between devices, exchange(): lax.ppermute(value, 'aperture', [(index, index ^ step) for index in range...  9.7 us
    pallas_call x1, Pallas kernels, on_device(): call(forward_kernel, 'forward', (shape((rows_dev, lanes), bf16), shape((p...  4.47 us
    pallas_call x1, Pallas kernels, on_device(): call(functools.partial(table_kernel, math.sqrt(rows * cols), cols), 'far_...  2.78 us
    ppermute x6, waiting for transfers between devices, exchange(): lax.ppermute(value, 'aperture', [(index, index ^ step) for index in range...  2.26 us
    pallas_call x1, Pallas kernels, on_device(): call(functools.partial(last_grad_kernel, pairs_dev), 'gradient_far', out,...  1.6 us
    pallas_call x1, Pallas kernels, on_device(): call(row_kernel, 'row_tables', (shape((pairs_dev, 2 * FOCAL, rows), bf16)...  1.37 us
    pallas_call x1, Pallas kernels, on_device(): call(functools.partial(focus_kernel, steps), 'focus', (shape((rows_dev, l...  1.22 us
    pallas_call x1, Pallas kernels, on_device(): call(functools.partial(grad_kernel, pairs_dev), 'gradient_own', out, [VME...  0.86 us
  transfers between devices with their start and end apart: 8, of which 3 were waited for; matrix products, arithmetic and copies ran while one was open for 0% of the time, Pallas kernels for 20%

profile of v8, /device:TPU:0, one launch (start us, length us, event | category | flops | bytes accessed | tf_op | source)
XLA Modules:
  0.0 25.4 jit_solution(11352583451743196173)
XLA Ops:
  0.6 4.5 %forward.1 = (bf16[32,1024]{1,0:T(8,128)(2,1)S(1)}, f32[2,24,256]{2,1,0:T(8,128)S(1)}, f32[32,2048]{1,0:T(8,128)S(1)}, bf16[512,2048]{1,0:T(8,128)(2,1)S(1)}, bf16[512,2048]{1,0:T(8,128)(2,1)S(1)}) custom-call(s32[2]{0:T(128)} %wave_hbm.1, s32[2]{0:T(128)} %angle_hbm.1, s32[2,2]{1,0:T(2,128)} %aim_hbm.1, f32[16,256]{1,0:T(8,128)} %bitcast.1, ...), custom_call_target="tpu_custom_call" | custom-call | flops 1000000000 | bytes 10000000 | tf_op jit(solution)/shard_map/forward/pallas_call | solution.py:440
  5.1 5.1 %collective-permute-start = (bf16[32,1024]{1,0:T(8,128)(2,1)S(1)}, bf16[32,1024]{1,0:T(8,128)(2,1)S(1)}, u32[]{:S(2)}, u32[]{:S(2)}) collective-permute-start(bf16[32,1024]{1,0:T(8,128)(2,1)S(1)} %get-tuple-element.23.refs_0_), channel_id=1, source_target_pairs={{0,12},{2,14},{4,8},{6,10},{8,4},{10,6},{12,0},{14,2},{1,13},{3,15... | collective-permute-start | bytes 196616 | tf_op jit(solution)/shard_map/ppermute | solution.py:430
  10.2 0.0 collective-permute-start.3
  10.2 0.6 %collective-permute-start.4 = (bf16[32,1024]{1,0:T(8,128)(2,1)S(1)}, bf16[32,1024]{1,0:T(8,128)(2,1)S(1)}, u32[]{:S(2)}, u32[]{:S(2)}) collective-permute-start(bf16[32,1024]{1,0:T(8,128)(2,1)S(1)} %get-tuple-element.23.refs_0_), channel_id=1, source_target_pairs={{0,4},{2,6},{4,0},{6,2},{8,12},{10,14},{12,8},{14,10},{1,5},{3,7},... | collective-permute-start | bytes 196616 | tf_op jit(solution)/shard_map/ppermute | solution.py:430
  10.9 1.6 %collective-permute-start.2 = (bf16[32,1024]{1,0:T(8,128)(2,1)S(1)}, bf16[32,1024]{1,0:T(8,128)(2,1)S(1)}, u32[]{:S(2)}, u32[]{:S(2)}) collective-permute-start(bf16[32,1024]{1,0:T(8,128)(2,1)S(1)} %get-tuple-element.23.refs_0_), channel_id=1, source_target_pairs={{0,2},{2,0},{4,6},{6,4},{8,10},{10,8},{12,14},{14,12},{1,3},{3,1},... | collective-permute-start | bytes 196616 | tf_op jit(solution)/shard_map/ppermute | solution.py:430
  12.5 0.0 collective-permute-start.1
  12.5 1.4 %row_tables.1 = (bf16[2,512,256]{2,1,0:T(8,128)(2,1)S(1)}, bf16[2,32,512]{2,1,0:T(8,128)(2,1)S(1)}, f32[2,256,256]{2,1,0:T(8,128)S(1)}, f32[2,8,128]{2,1,0:T(8,128)S(1)}) custom-call(f32[2,24,256]{2,1,0:T(8,128)S(1)} %get-tuple-element.21.info_ref), custom_call_target="tpu_custom_call" | custom-call | flops 100000000 | bytes 1000000 | tf_op jit(solution)/shard_map/row_tables/pallas_call | solution.py:463
  13.9 0.0 collective-permute-done.refs_2_
  13.9 0.8 %collective-permute-start.5 = (bf16[32,1024]{1,0:T(8,128)(2,1)S(1)}, bf16[32,1024]{1,0:T(8,128)(2,1)S(1)}, u32[]{:S(2)}, u32[]{:S(2)}) collective-permute-start(bf16[32,1024]{1,0:T(8,128)(2,1)S(1)} %collective-permute-done.refs_2_), channel_id=1, source_target_pairs={{0,2},{2,0},{4,6},{6,4},{8,10},{10,8},{12,14},{14,12},{1,3},{3,1},... | collective-permute-start | bytes 196616 | tf_op jit(solution)/shard_map/ppermute | solution.py:430
  14.7 1.2 %collective-permute-done.3.refs_0_ = bf16[32,1024]{1,0:T(8,128)(2,1)S(1)} collective-permute-done((bf16[32,1024]{1,0:T(8,128)(2,1)S(1)}, bf16[32,1024]{1,0:T(8,128)(2,1)S(1)}, u32[]{:S(2)}, u32[]{:S(2)}) %collective-permute-start.3) | collective-permute-done | bytes 65568 | tf_op jit(solution)/shard_map/ppermute | solution.py:430
  15.8 0.0 collective-permute-done.4.refs_1_
  15.9 1.6 %collective-permute-start.6 = (bf16[64,1024]{1,0:T(8,128)(2,1)S(1)}, bf16[64,1024]{1,0:T(8,128)(2,1)S(1)}, u32[]{:S(2)}, u32[]{:S(2)}) collective-permute-start(bf16[64,1024]{1,0:T(8,128)(2,1)S(1)} %join.1.refs_1_.refs_3_), channel_id=1, source_target_pairs={{0,2},{2,0},{4,6},{6,4},{8,10},{10,8},{12,14},{14,12},{1,3},{3,1},... | collective-permute-start | bytes 393224 | tf_op jit(solution)/shard_map/ppermute | solution.py:430
  17.4 0.0 collective-permute-done.1.far_info_ref
  17.4 0.0 collective-permute-done.2.refs_0_.refs_1_
  17.4 2.8 %far_tables.1 = (bf16[512,2048]{1,0:T(8,128)(2,1)S(1)}, bf16[512,2048]{1,0:T(8,128)(2,1)S(1)}, f32[2,32,2048]{2,1,0:T(8,128)S(1)}, f32[2,32,2048]{2,1,0:T(8,128)...) custom-call(f32[2,24,256]{2,1,0:T(8,128)S(1)} %get-tuple-element.21.info_ref, ...), custom_call_target="tpu_custom_call" | custom-call | flops 3000000000 | bytes 30000000 | tf_op jit(solution)/shard_map/far_tables/pallas_call | solution.py:486
  20.2 0.0 collective-permute-done.5.refs_4_
  20.2 1.1 %collective-permute-done.6.refs_5_ = bf16[64,1024]{1,0:T(8,128)(2,1)S(1)} collective-permute-done((bf16[64,1024]{1,0:T(8,128)(2,1)S(1)}, bf16[64,1024]{1,0:T(8,128)(2,1)S(1)}, u32[]{:S(2)}, u32[]{:S(2)}) %collective-permute-start.6) | collective-permute-done | bytes 131104 | tf_op jit(solution)/shard_map/ppermute | solution.py:430
  21.3 1.2 %focus.1 = (bf16[32,1024]{1,0:T(8,128)(2,1)S(1)}, f32[2]{0:T(128)}) custom-call(bf16[2,512,256]{2,1,0:T(8,128)(2,1)S(1)} %get-tuple-element.22.tall_ref, bf16[2,32,512]{2,1,0:T(8,128)(2,1)S(1)} %get-tuple-element.25.flat_ref, f32[2,256,256]{2,1,0:T(8,128)S(1)} %get-tuple-element.26.spot_ref, f32[2,8,128]{2,1,0:T(8,128)S(1)} %get-tuple-element.27.gain_ref, ...), custom_call_target="tpu_custom_call" | custom-call | flops 100000000 | bytes 1000000 | tf_op jit(solution)/shard_map/focus/pallas_call | solution.py:492
  22.5 0.1 collective-permute-start.7
  22.6 0.9 %gradient_own.1.refs_5_ = f32[32,2048]{1,0:T(8,128)S(1)} custom-call(bf16[32,1024]{1,0:T(8,128)(2,1)S(1)} %get-tuple-element.31.back_ref, bf16[512,2048]{1,0:T(8,128)(2,1)S(1)} %get-tuple-element.35.refs_0_, bf16[512,2048]{1,0:T(8,128)(2,1)S(1)} %get-tuple-element.36.refs_1_, f32[2,32,2048]{2,1,0:T(8,128)S(1)} %get-tuple-element.37.refs_2_, ...), custom_call_target="tpu_custom_call" | custom-call | flops 1000000000 | bytes 10000000 | tf_op jit(solution)/shard_map/gradient_own/pallas_call | solution.py:501
  23.4 0.4 %collective-permute-done.7.refs_0_ = bf16[32,1024]{1,0:T(8,128)(2,1)S(1)} collective-permute-done((bf16[32,1024]{1,0:T(8,128)(2,1)S(1)}, bf16[32,1024]{1,0:T(8,128)(2,1)S(1)}, u32[]{:S(2)}, u32[]{:S(2)}) %collective-permute-start.7) | collective-permute-done | bytes 65568 | tf_op jit(solution)/shard_map/ppermute | solution.py:433
  23.8 1.6 %gradient_far.1 = f32[32,2048]{1,0:T(8,128)} custom-call(bf16[32,1024]{1,0:T(8,128)(2,1)S(1)} %collective-permute-done.7.refs_0_, bf16[512,2048]{1,0:T(8,128)(2,1)S(1)} %get-tuple-element.32.refs_1_, bf16[512,2048]{1,0:T(8,128)(2,1)S(1)} %get-tuple-element.33.refs_2_, f32[2,32,2048]{2,1,0:T(8,128)S(1)} %get-tuple-element.29.after_ref.refs_3_, ...), custom_call_target="tpu_custom_call" | custom-call | flops 1000000000 | bytes 10000000 | tf_op jit(solution)/shard_map/gradient_far/pallas_call | solution.py:506
  (1 shorter events, 0.0 us)
Async XLA Ops:
  5.1 8.8 %collective-permute-start = (bf16[32,1024]{1,0:T(8,128)(2,1)S(1)}, bf16[32,1024]{1,0:T(8,128)(2,1)S(1)}, u32[]{:S(2)}, u32[]{:S(2)}) collective-permute-start(bf16[32,1024]{1,0:T(8,128)(2,1)S(1)} %get-tuple-element.23.refs_0_), channel_id=1, source_target_pairs={{0,12},{2,14},{4,8},{6,10},{8,4},{10,6},{12,0},{14,2},{1,13},{3,15... | collective-permute-start | bytes 196616 | tf_op jit(solution)/shard_map/ppermute | solution.py:430
  10.2 5.6 %collective-permute-start.3 = (bf16[32,1024]{1,0:T(8,128)(2,1)S(1)}, bf16[32,1024]{1,0:T(8,128)(2,1)S(1)}, u32[]{:S(2)}, u32[]{:S(2)}) collective-permute-start(bf16[32,1024]{1,0:T(8,128)(2,1)S(1)} %get-tuple-element.23.refs_0_), channel_id=1, source_target_pairs={{0,8},{2,10},{4,12},{6,14},{8,0},{10,2},{12,4},{14,6},{1,9},{3,11}... | collective-permute-start | bytes 196616 | tf_op jit(solution)/shard_map/ppermute | solution.py:430
  10.2 5.6 %collective-permute-start.4 = (bf16[32,1024]{1,0:T(8,128)(2,1)S(1)}, bf16[32,1024]{1,0:T(8,128)(2,1)S(1)}, u32[]{:S(2)}, u32[]{:S(2)}) collective-permute-start(bf16[32,1024]{1,0:T(8,128)(2,1)S(1)} %get-tuple-element.23.refs_0_), channel_id=1, source_target_pairs={{0,4},{2,6},{4,0},{6,2},{8,12},{10,14},{12,8},{14,10},{1,5},{3,7},... | collective-permute-start | bytes 196616 | tf_op jit(solution)/shard_map/ppermute | solution.py:430
  10.9 6.5 %collective-permute-start.2 = (bf16[32,1024]{1,0:T(8,128)(2,1)S(1)}, bf16[32,1024]{1,0:T(8,128)(2,1)S(1)}, u32[]{:S(2)}, u32[]{:S(2)}) collective-permute-start(bf16[32,1024]{1,0:T(8,128)(2,1)S(1)} %get-tuple-element.23.refs_0_), channel_id=1, source_target_pairs={{0,2},{2,0},{4,6},{6,4},{8,10},{10,8},{12,14},{14,12},{1,3},{3,1},... | collective-permute-start | bytes 196616 | tf_op jit(solution)/shard_map/ppermute | solution.py:430
  12.5 4.9 %collective-permute-start.1 = (f32[2,24,256]{2,1,0:T(8,128)S(1)}, f32[2,24,256]{2,1,0:T(8,128)S(1)}, u32[]{:S(2)}, u32[]{:S(2)}) collective-permute-start(f32[2,24,256]{2,1,0:T(8,128)S(1)} %get-tuple-element.21.info_ref), channel_id=1, source_target_pairs={{0,1},{1,0},{2,3},{3,2},{4,5},{5,4},{6,7},{7,6},{8,9},{9,8},{10,11... | collective-permute-start | bytes 147464 | tf_op jit(solution)/shard_map/ppermute | solution.py:433
  13.9 6.3 %collective-permute-start.5 = (bf16[32,1024]{1,0:T(8,128)(2,1)S(1)}, bf16[32,1024]{1,0:T(8,128)(2,1)S(1)}, u32[]{:S(2)}, u32[]{:S(2)}) collective-permute-start(bf16[32,1024]{1,0:T(8,128)(2,1)S(1)} %collective-permute-done.refs_2_), channel_id=1, source_target_pairs={{0,2},{2,0},{4,6},{6,4},{8,10},{10,8},{12,14},{14,12},{1,3},{3,1},... | collective-permute-start | bytes 196616 | tf_op jit(solution)/shard_map/ppermute | solution.py:430
  15.9 5.4 %collective-permute-start.6 = (bf16[64,1024]{1,0:T(8,128)(2,1)S(1)}, bf16[64,1024]{1,0:T(8,128)(2,1)S(1)}, u32[]{:S(2)}, u32[]{:S(2)}) collective-permute-start(bf16[64,1024]{1,0:T(8,128)(2,1)S(1)} %join.1.refs_1_.refs_3_), channel_id=1, source_target_pairs={{0,2},{2,0},{4,6},{6,4},{8,10},{10,8},{12,14},{14,12},{1,3},{3,1},... | collective-permute-start | bytes 393224 | tf_op jit(solution)/shard_map/ppermute | solution.py:430
  22.5 1.3 %collective-permute-start.7 = (bf16[32,1024]{1,0:T(8,128)(2,1)S(1)}, bf16[32,1024]{1,0:T(8,128)(2,1)S(1)}, u32[]{:S(2)}, u32[]{:S(2)}) collective-permute-start(bf16[32,1024]{1,0:T(8,128)(2,1)S(1)} %get-tuple-element.31.back_ref), channel_id=1, source_target_pairs={{0,1},{1,0},{2,3},{3,2},{4,5},{5,4},{6,7},{7,6},{8,9},{9,8},{10,11... | collective-permute-start | bytes 196616 | tf_op jit(solution)/shard_map/ppermute | solution.py:433

commit v9 on v8

--- a/solution.py
+++ b/solution.py
@@ -1,4 +1,5 @@
 import functools
+import itertools
 import math
 
 import jax
@@ -15,6 +16,7 @@
 BLOCK = 256
 GRAIN = 16
 LANES = 128
+PIECE = 16
 VMEM_LIMIT = 16 * 1024 * 1024
 WAVE_ROW, ANGLE_ROW, AIM_ROW, INFO_ROWS = 16, 17, 18, 24
 DIRECT = 16
@@ -77,7 +79,7 @@
 
 def near_fields(s, info_ref, pairs):
     def coef(pair, row):
-        return info_ref[pair, row : row + 1, :]
+        return info_ref[pair, row : row + 1, :LANES]
 
     outs = [[coef(p, k) + coef(p, k + 1) * s for k in (0, TERMS)] for p in range(pairs)]
     twice = s + s
@@ -90,9 +92,9 @@
     return outs
 
 
-def near_slopes(s, scale, info_ref, pairs):
+def near_slopes(s, coef_ref, pairs):
     def coef(pair, row):
-        return info_ref[pair, row : row + 1, :] * (scale * (row % TERMS))
+        return coef_ref[pair, row : row + 1, :]
 
     twice = s + s
     before, current = jnp.ones_like(s), twice
@@ -115,27 +117,19 @@
     return jnp.concatenate(parts, axis=1)
 
 
-def write_tables(index, base_ref, centres, table_ref):
-    middle = table_ref.shape[1] // 2
-    cent_r, cent_i = (centre[:, index : index + 1] for centre in centres)
-    base_r, base_i = base_ref[0], base_ref[1]
+def block_starts(cols, index):
+    return cols // 2 - (index + 1) * BLOCK, cols // 2 + index * BLOCK
+
+
+def both_blocks(base_r, base_i, cent_r, cent_i):
     rr, ii = base_r * cent_r, base_i * cent_i
     ri, ir = base_r * cent_i, base_i * cent_r
-    left, right = middle - (index + 1) * BLOCK, middle + index * BLOCK
-    tables = []
-    for start, values in ((left, (rr + ii, ir - ri)), (right, (rr - ii, ir + ri))):
-        table = jnp.concatenate(values, axis=0).astype(jnp.bfloat16)
-        table_ref[:, start : start + BLOCK] = table
-        tables.append(table)
-    return tables
-
-
-def turned_waves(info_ref, pair, cols, base_ref, centre_ref, turned_ref):
+    return (rr + ii, ir - ri), (rr - ii, ir + ri)
+
+
+def own_waves(info_ref, pair, cols, base_ref, centre_ref):
     shift = cols // 4 + 1 - lax.axis_index("wave")
     fill_base(column_freq(info_ref, pair), shift, 256 * cols, base_ref, centre_ref)
-    for part in range(2):
-        turned_ref[part] = base_ref[part].T
-    return [centre_ref[part].T for part in range(2)]
 
 
 def forward_kernel(
@@ -144,7 +138,7 @@
     pairs = info_ref.shape[0]
     table_refs, refs = refs[:pairs], refs[pairs:]
     (
-        wave_ref, angle_ref, aim_ref, coef_ref, width_ref, far_ref, base_ref, centre_ref, turned_ref, acc_ref, sems,
+        wave_ref, angle_ref, aim_ref, coef_ref, width_ref, far_ref, base_ref, centre_ref, near_ref, acc_ref, sems,
     ) = refs
     rows_dev, cols = width_ref.shape
     half = cols // 2
@@ -168,10 +162,8 @@
         ids = jnp.where(row == AIM_ROW, aim_ref[pair, 0], ids)
         ids = jnp.where(row == AIM_ROW + 1, aim_ref[pair, 1], ids)
         info_ref[pair, WAVE_ROW:, :] = ids.astype(jnp.float32)
-    centres = [
-        turned_waves(info_ref, pair, cols, base_ref.at[pair], centre_ref.at[pair], turned_ref.at[pair])
-        for pair in range(pairs)
-    ]
+    for pair in range(pairs):
+        own_waves(info_ref, pair, cols, base_ref.at[pair], centre_ref.at[pair])
     acc_ref[...] = jnp.zeros_like(acc_ref)
     moves[4].wait()
     core = lax.axis_index("wave")
@@ -188,28 +180,32 @@
 
     void = jnp.where(core == 1, 0, half - 1)
     for index in range(half // (2 * BLOCK)):
-        nears = [[] for _ in range(pairs)]
-        for start in (half // 2 - (index + 1) * BLOCK, half // 2 + index * BLOCK):
-            sides = []
-            for ref in (own_ref, far_ref):
-                sides.append(near_fields(ref[:, start : start + BLOCK], info_ref, pairs))
-            if start in (0, half - BLOCK):
-                keep = iota((rows_dev, BLOCK), 1) + start != void
-                sides[1] = [[jnp.where(keep, part, 0.0) for part in out] for out in sides[1]]
-            for pair in range(pairs):
-                both = jnp.concatenate([*sides[0][pair], *sides[1][pair]], axis=0)
-                nears[pair].append(both.astype(jnp.bfloat16))
+        starts = block_starts(half, index)
+        for start in (start + step for start in starts for step in range(0, BLOCK, LANES)):
+            for side, ref in enumerate((own_ref, far_ref)):
+                outs = near_fields(ref[:, start : start + LANES], info_ref, pairs)
+                if side and start in (0, half - LANES):
+                    keep = iota((rows_dev, LANES), 1) + start != void
+                    outs = [[jnp.where(keep, part, 0.0) for part in out] for out in outs]
+                for pair, part in ((pair, part) for pair in range(pairs) for part in range(2)):
+                    row = (2 * side + part) * rows_dev
+                    near_ref[pair, row : row + rows_dev, start : start + LANES] = outs[pair][part].astype(jnp.bfloat16)
         for pair in range(pairs):
-            tables = write_tables(index, turned_ref.at[pair], centres[pair], table_refs[pair])
-            acc_ref[pair] += lax.dot_general(
-                jnp.concatenate(nears[pair], axis=1),
-                jnp.concatenate(tables, axis=1),
-                (((1,), (1,)), ((), ())),
+            cent_r, cent_i = (centre_ref[pair, part, index : index + 1, :] for part in range(2))
+            for row in range(0, BLOCK, GRAIN):
+                base_r, base_i = (base_ref[pair, part, row : row + GRAIN, :] for part in range(2))
+                for start, table in zip(starts, both_blocks(base_r, base_i, cent_r, cent_i)):
+                    rows = slice(start + row, start + row + GRAIN)
+                    table_refs[pair][rows, :FOCAL] = table[0].astype(jnp.bfloat16)
+                    table_refs[pair][rows, FOCAL:] = table[1].astype(jnp.bfloat16)
+            acc_ref[pair] += jnp.dot(
+                jnp.concatenate([near_ref[pair, :, start : start + BLOCK] for start in starts], axis=1),
+                jnp.concatenate([table_refs[pair][start : start + BLOCK, :] for start in starts], axis=0),
                 preferred_element_type=jnp.float32,
             )
     alone = jnp.where(core == 1, 0, half)
     column = width_ref[:, pl.ds(pl.multiple_of(alone, LANES), LANES)]
-    columns = near_fields(jnp.concatenate([column, column], axis=1), info_ref, pairs)
+    columns = near_fields(column, info_ref, pairs)
     for pair in range(pairs):
         acc = [acc_ref[pair, part * rows_dev : (part + 1) * rows_dev, :] for part in range(4)]
         (own_rr, own_ri), (own_ir, own_ii), (far_rr, far_ri), (far_ir, far_ii) = (
@@ -230,9 +226,9 @@
             mine_ref[:, lane : lane + FOCAL] = value.astype(jnp.bfloat16)
 
 
-def spot_map(info_ref, pair):
+def spot_rows(info_ref, pair, first):
     aims = [info_ref[pair, row : row + 1, :] for row in (AIM_ROW, AIM_ROW + 1)]
-    rows_off = iota((FOCAL, FOCAL), 0).astype(jnp.float32) - aims[0]
+    rows_off = (iota((PIECE, FOCAL), 0) + first).astype(jnp.float32) - aims[0]
     cols_off = iota((1, FOCAL), 1).astype(jnp.float32) - aims[1]
     return jnp.exp(-(rows_off * rows_off + cols_off * cols_off) / (2.0 * SPOT * SPOT))
 
@@ -253,9 +249,11 @@
         def step(index, carry):
             start = pl.multiple_of(index * size, size)
             place = iota((1, size), 1) + (start - rows // 2)
-            real, imag = unit_waves(focal[:, :size] * place, period)
-            tall_ref[pair, :FOCAL, pl.ds(start, size)] = real.astype(jnp.bfloat16)
-            tall_ref[pair, FOCAL:, pl.ds(start, size)] = imag.astype(jnp.bfloat16)
+            for row in range(0, FOCAL, PIECE):
+                real, imag = unit_waves(focal[row : row + PIECE, :size] * place, period)
+                tall_ref[pair, row : row + PIECE, pl.ds(start, size)] = real.astype(jnp.bfloat16)
+                row += FOCAL
+                tall_ref[pair, row : row + PIECE, pl.ds(start, size)] = imag.astype(jnp.bfloat16)
             return carry
 
         if rows == size:
@@ -267,9 +265,12 @@
         real, imag = unit_waves((iota((rows_dev, 1), 0) + first) * focal, period)
         flat_ref[pair, :, :FOCAL] = real.astype(jnp.bfloat16)
         flat_ref[pair, :, FOCAL:] = imag.astype(jnp.bfloat16)
-        spot = spot_map(info_ref, pair)
-        spot_ref[pair] = spot
-        gain_ref[pair] = jnp.broadcast_to(FOCAL * FOCAL / total_of(spot), gain_ref.shape[1:])
+        total = jnp.zeros((PIECE, FOCAL), jnp.float32)
+        for row in range(0, FOCAL, PIECE):
+            spot = spot_rows(info_ref, pair, row)
+            spot_ref[pair, row : row + PIECE, :] = spot
+            total += spot
+        gain_ref[pair] = jnp.broadcast_to(FOCAL * FOCAL / total_of(total), gain_ref.shape[1:])
 
 
 def join_kernel(*refs):
@@ -281,7 +282,7 @@
 
 def focus_kernel(steps, tall_ref, flat_ref, spot_ref, gain_ref, after_ref, *refs):
     del after_ref
-    *sect_refs, back_ref, score_ref, rows_ref = refs
+    *sect_refs, back_ref, score_ref, rows_ref, mixed_ref, field_ref, stack_ref = refs
     pairs = tall_ref.shape[0]
     rows_dev = back_ref.shape[0]
     if steps is None:
@@ -296,51 +297,76 @@
         for step, block in zip(steps, blocks, strict=True):
             start = pl.multiple_of((me ^ step) * rows_dev, rows_dev)
             rows_ref[pl.ds(start, rows_dev), :] = block
-    fields, sums = [], []
     for pair in range(pairs):
         lane = 2 * pair * FOCAL
         section = rows_ref[:, lane : lane + 2 * FOCAL]
-        mixed = jnp.dot(tall_ref[pair], section, preferred_element_type=jnp.float32)
-        real = mixed[:FOCAL, :FOCAL] - mixed[FOCAL:, FOCAL:]
-        imag = mixed[:FOCAL, FOCAL:] + mixed[FOCAL:, :FOCAL]
-        power = real * real + imag * imag
-        fields.append((real, imag))
-        sums.append((total_of(spot_ref[pair] * power), total_of(power) + 1e-06))
-    for pair, ((real, imag), (spot_power, all_power)) in enumerate(zip(fields, sums)):
+        mixed_ref[pair] = jnp.dot(tall_ref[pair], section, preferred_element_type=jnp.float32)
+    pieces = [slice(row, row + PIECE) for row in range(0, FOCAL, PIECE)]
+    sums = []
+    for pair in range(pairs):
+        totals = [jnp.zeros((PIECE, FOCAL), jnp.float32) for _ in range(2)]
+        for rows in pieces:
+            lower = slice(rows.start + FOCAL, rows.stop + FOCAL)
+            real = mixed_ref[pair, rows, :FOCAL] - mixed_ref[pair, lower, FOCAL:]
+            imag = mixed_ref[pair, rows, FOCAL:] + mixed_ref[pair, lower, :FOCAL]
+            field_ref[pair, 0, rows, :] = real
+            field_ref[pair, 1, rows, :] = imag
+            power = real * real + imag * imag
+            totals = [totals[0] + spot_ref[pair, rows, :] * power, totals[1] + power]
+        sums.append((total_of(totals[0]), total_of(totals[1]) + 1e-06))
+    for pair, (spot_power, all_power) in enumerate(sums):
         ratio = spot_power / all_power
         gain = gain_ref[pair, :1, :1]
         score_ref[pair] = jnp.sum(ratio * gain)
-        weight = (gain * 2.0 / all_power) * (spot_ref[pair] - ratio)
-        real = (weight * real).astype(jnp.bfloat16)
-        imag = (weight * imag).astype(jnp.bfloat16)
-        stack = jnp.concatenate(
-            [jnp.concatenate([real, imag], axis=1), jnp.concatenate([imag, -real], axis=1)], axis=0
-        )
-        back = jnp.dot(flat_ref[pair], stack, preferred_element_type=jnp.float32)
+        scale = gain * 2.0 / all_power
+        for rows in pieces:
+            lower = slice(rows.start + FOCAL, rows.stop + FOCAL)
+            weight = scale * (spot_ref[pair, rows, :] - ratio)
+            real = (weight * field_ref[pair, 0, rows, :]).astype(jnp.bfloat16)
+            imag = (weight * field_ref[pair, 1, rows, :]).astype(jnp.bfloat16)
+            stack_ref[pair, rows, :FOCAL] = real
+            stack_ref[pair, rows, FOCAL:] = imag
+            stack_ref[pair, lower, :FOCAL] = imag
+            stack_ref[pair, lower, FOCAL:] = -real
+        back = jnp.dot(flat_ref[pair], stack_ref[pair], preferred_element_type=jnp.float32)
         lane = 2 * pair * FOCAL
         back_ref[:, lane : lane + 2 * FOCAL] = back.astype(jnp.bfloat16)
 
 
 def table_kernel(scale, cols, info_ref, far_info_ref, width_ref, *refs):
-    *out_refs, base_ref, centre_ref, turned_ref = refs
+    *out_refs, base_ref, centre_ref, turned_ref, coef_ref = refs
     pairs = base_ref.shape[0]
     out_refs = out_refs[-3 * pairs :]
     table_refs, slope_refs = out_refs[:pairs], out_refs[pairs:]
     own_cols = width_ref.shape[1]
-    centres = [
-        turned_waves(far_info_ref, pair, cols, base_ref.at[pair], centre_ref.at[pair], turned_ref.at[pair])
-        for pair in range(pairs)
-    ]
+    for core, ref in enumerate((info_ref, far_info_ref)):
+        for pair in range(pairs):
+            coef = ref[pair, : 2 * TERMS, :LANES]
+            coef_ref[core * pairs + pair] = coef * ((iota(coef.shape, 0) % TERMS).astype(jnp.float32) * scale)
+    centres = []
+    for pair in range(pairs):
+        own_waves(far_info_ref, pair, cols, base_ref.at[pair], centre_ref.at[pair])
+        for part, row, lane in itertools.product(range(2), range(0, BLOCK, LANES), range(0, FOCAL, LANES)):
+            tile = base_ref[pair, part, row : row + LANES, lane : lane + LANES]
+            turned_ref[pair, part, lane : lane + LANES, row : row + LANES] = tile.T
+        centres.append([centre_ref[pair, part].T for part in range(2)])
     for index in range(own_cols // (2 * BLOCK)):
+        starts = block_starts(own_cols, index)
         for pair in range(pairs):
-            write_tables(index, turned_ref.at[pair], centres[pair], table_refs[pair])
-        for start in (2 * index * BLOCK, (2 * index + 1) * BLOCK):
-            place = slice(start, start + BLOCK)
-            for core, ref in enumerate((info_ref, far_info_ref)):
-                slopes = near_slopes(width_ref[:, place], scale, ref, pairs)
-                for pair in range(pairs):
-                    slope_refs[core * pairs + pair][0, :, place] = slopes[pair][0]
-                    slope_refs[core * pairs + pair][1, :, place] = slopes[pair][1]
+            for row in range(0, FOCAL, GRAIN):
+                rows = slice(row, row + GRAIN)
+                cent_r, cent_i = (centre[rows, index : index + 1] for centre in centres[pair])
+                base_r, base_i = (turned_ref[pair, part, rows, :] for part in range(2))
+                for start, table in zip(starts, both_blocks(base_r, base_i, cent_r, cent_i)):
+                    for part, value in enumerate(table):
+                        place = slice(row + part * FOCAL, row + part * FOCAL + GRAIN)
+                        table_refs[pair][place, start : start + BLOCK] = value.astype(jnp.bfloat16)
+        for start in (start + step for start in starts for step in range(0, BLOCK, LANES)):
+            place = slice(start, start + LANES)
+            slopes = near_slopes(width_ref[:, place], coef_ref, 2 * pairs)
+            for ref, slope in zip(slope_refs, slopes):
+                ref[0, :, place] = slope[0]
+                ref[1, :, place] = slope[1]
 
 
 def last_grad_kernel(pairs, *refs):
@@ -363,7 +389,7 @@
         move.wait()
 
 
-def grad_kernel(pairs, back_ref, *refs, send=None):
+def grad_kernel(pairs, back_ref, *refs, send=None, across=True):
     *in_refs, out_ref = refs
     table_refs, slope_refs, total_ref = in_refs[:pairs], in_refs[pairs : 2 * pairs], in_refs[2 * pairs :]
     rows_dev, own_cols = out_ref.shape
@@ -384,7 +410,11 @@
         place = slice(start, start + size)
         total = total_ref[0][:, place] if total_ref else jnp.zeros((rows_dev, size), jnp.float32)
         for pair in range(pairs):
-            grad = jnp.dot(lefts[pair], table_refs[pair][:, place], preferred_element_type=jnp.float32)
+            if across:
+                table, dims = table_refs[pair][:, place], ((1,), (0,))
+            else:
+                table, dims = table_refs[pair][place, :], ((1,), (1,))
+            grad = lax.dot_general(lefts[pair], table, (dims, ((), ())), preferred_element_type=jnp.float32)
             total += grad[:rows_dev] * slope_refs[pair][0, :, place]
             total += grad[rows_dev:] * slope_refs[pair][1, :, place]
         if send is None:
@@ -435,14 +465,13 @@
     waves = [
         pltpu.VMEM((pairs_dev, 2, BLOCK, FOCAL), f32),
         pltpu.VMEM((pairs_dev, 2, 8, FOCAL), f32),
-        pltpu.VMEM((pairs_dev, 2, FOCAL, BLOCK), f32),
     ]
     mine, info, own, *tables = call(
         forward_kernel, "forward",
         (
             shape((rows_dev, lanes), bf16),
             shape((pairs_dev, INFO_ROWS, FOCAL), f32), shape((rows_dev, own_cols), f32),
-            *[shape((2 * FOCAL, own_cols), bf16)] * pairs_dev,
+            *[shape((own_cols, 2 * FOCAL), bf16)] * pairs_dev,
         ),
         [HBM] * 5, (VMEM,) * (3 + pairs_dev),
         [
@@ -453,6 +482,7 @@
             pltpu.VMEM(widths.shape, f32),
             pltpu.VMEM((rows_dev, own_cols), f32),
             *waves,
+            pltpu.VMEM((pairs_dev, 4 * rows_dev, own_cols), bf16),
             pltpu.VMEM((pairs_dev, 4 * rows_dev, 2 * FOCAL), f32),
             pltpu.SemaphoreType.DMA((5,)),
         ],
@@ -485,21 +515,29 @@
     outs = [shape((2 * FOCAL, own_cols), bf16)] * pairs_dev + [shape((2, rows_dev, own_cols), f32)] * 2 * pairs_dev
     made = call(
         functools.partial(table_kernel, math.sqrt(rows * cols), cols), "far_tables",
-        outs, [VMEM] * 3 + [ANY] * len(after), [VMEM] * len(outs), waves, 30 * 10**8, 30 * 10**6,
+        outs, [VMEM] * 3 + [ANY] * len(after), [VMEM] * len(outs),
+        [*waves, pltpu.VMEM((pairs_dev, 2, FOCAL, BLOCK), f32), pltpu.VMEM((copies * pairs_dev, 2 * TERMS, LANES), f32)],
+        30 * 10**8, 30 * 10**6,
     )(info, far_info, own, *after)
     far_tables, slopes, far_slopes = made[:pairs_dev], made[pairs_dev : 2 * pairs_dev], made[2 * pairs_dev :]
 
     back, scores = call(
         functools.partial(focus_kernel, steps), "focus",
         (shape((rows_dev, lanes), bf16), shape((pairs_dev,), f32)),
-        [VMEM] * 4 + [ANY] + [VMEM] * len(sections), (VMEM, SMEM), [pltpu.VMEM((rows, lanes), bf16)],
+        [VMEM] * 4 + [ANY] + [VMEM] * len(sections), (VMEM, SMEM),
+        [
+            pltpu.VMEM((rows, lanes), bf16),
+            pltpu.VMEM((pairs_dev, 2 * FOCAL, 2 * FOCAL), f32),
+            pltpu.VMEM((pairs_dev, 2, FOCAL, FOCAL), f32),
+            pltpu.VMEM((pairs_dev, 2 * FOCAL, 2 * FOCAL), bf16),
+        ],
         10**8, 10**6,
     )(tall, flat, spots, gains, far_slopes[0], *sections)
 
     out = shape((rows_dev, own_cols), f32)
     ins = [back, *tables, *slopes]
     grad = call(
-        functools.partial(grad_kernel, pairs_dev), "gradient_own",
+        functools.partial(grad_kernel, pairs_dev, across=False), "gradient_own",
         out, [VMEM] * len(ins), VMEM, [], 10**9, 10**7,
     )(*ins)
     ins = [to_core(back), *far_tables, *far_slopes, grad]

time: 25.6 us -> 25.2 us (0.984)
  Pallas kernels: 12.3 us -> 11.8 us
  starting transfers between devices: 9.78 us -> 10.1 us
    pallas_call x1, Pallas kernels: 0.86 us -> 1.38 us  [on_device(): call(functools.partial(grad_kernel, pairs_dev, across=False), 'gradient_o...]
    pallas_call x1, Pallas kernels: 2.78 us -> 2.37 us  [on_device(): call(functools.partial(table_kernel, math.sqrt(rows * cols), cols), 'far_...]
    ppermute x2, waiting for transfers between devices: 0.38 us -> 0.01 us  [to_core(): lax.ppermute(value, 'wave', [(index, (index + 1) % copies) for index in r...]
    ppermute x6, starting transfers between devices: 9.7 us -> 10 us  [exchange(): lax.ppermute(value, 'aperture', [(index, index ^ step) for index in range...]
    pallas_call x1, Pallas kernels: 1.37 us -> 1.04 us  [on_device(): call(row_kernel, 'row_tables', (shape((pairs_dev, 2 * FOCAL, rows), bf16)...]
    pallas_call x1, Pallas kernels: 4.47 us -> 4.17 us  [on_device(): call(forward_kernel, 'forward', (shape((rows_dev, lanes), bf16), shape((p...]
  transfers between devices with their start and end apart: 8 -> 8, of which waited for: 3 -> 2; matrix products, arithmetic and copies ran while one was open for 0% -> 0% of each run, Pallas kernels for 20% -> 19%
where the time goes in v9:
time: 25.2 us; the launch traced here: 25 us
  Pallas kernels  11.8 us (47%)
  starting transfers between devices  10.1 us (40%)
  waiting for transfers between devices  2.38 us (9%)
  between operations  0.7 us (3%)
    ppermute x6, starting transfers between devices, exchange(): lax.ppermute(value, 'aperture', [(index, index ^ step) for index in range...  10 us
    pallas_call x1, Pallas kernels, on_device(): call(forward_kernel, 'forward', (shape((rows_dev, lanes), bf16), shape((p...  4.17 us
    ppermute x6, waiting for transfers between devices, exchange(): lax.ppermute(value, 'aperture', [(index, index ^ step) for index in range...  2.37 us
    pallas_call x1, Pallas kernels, on_device(): call(functools.partial(table_kernel, math.sqrt(rows * cols), cols), 'far_...  2.37 us
    pallas_call x1, Pallas kernels, on_device(): call(functools.partial(last_grad_kernel, pairs_dev), 'gradient_far', out,...  1.61 us
    pallas_call x1, Pallas kernels, on_device(): call(functools.partial(grad_kernel, pairs_dev, across=False), 'gradient_o...  1.38 us
    pallas_call x1, Pallas kernels, on_device(): call(functools.partial(focus_kernel, steps), 'focus', (shape((rows_dev, l...  1.21 us
    pallas_call x1, Pallas kernels, on_device(): call(row_kernel, 'row_tables', (shape((pairs_dev, 2 * FOCAL, rows), bf16)...  1.04 us
  transfers between devices with their start and end apart: 8, of which 2 were waited for; matrix products, arithmetic and copies ran while one was open for 0% of the time, Pallas kernels for 19%

profile of v9, /device:TPU:0, one launch (start us, length us, event | category | flops | bytes accessed | tf_op | source)
XLA Modules:
  0.0 25.0 jit_solution(11488950998734004217)
XLA Ops:
  0.6 4.2 %forward.1 = (bf16[32,1024]{1,0:T(8,128)(2,1)S(1)}, f32[2,24,256]{2,1,0:T(8,128)S(1)}, f32[32,2048]{1,0:T(8,128)S(1)}, bf16[2048,512]{1,0:T(8,128)(2,1)S(1)}, bf16[2048,512]{1,0:T(8,128)(2,1)S(1)}) custom-call(s32[2]{0:T(128)} %wave_hbm.1, s32[2]{0:T(128)} %angle_hbm.1, s32[2,2]{1,0:T(2,128)} %aim_hbm.1, f32[16,256]{1,0:T(8,128)} %bitcast.1, ...), custom_call_target="tpu_custom_call" | custom-call | flops 1000000000 | bytes 10000000 | tf_op jit(solution)/shard_map/forward/pallas_call | solution.py:469
  4.8 5.1 %collective-permute-start = (bf16[32,1024]{1,0:T(8,128)(2,1)S(1)}, bf16[32,1024]{1,0:T(8,128)(2,1)S(1)}, u32[]{:S(2)}, u32[]{:S(2)}) collective-permute-start(bf16[32,1024]{1,0:T(8,128)(2,1)S(1)} %get-tuple-element.23.refs_0_), channel_id=1, source_target_pairs={{0,12},{2,14},{4,8},{6,10},{8,4},{10,6},{12,0},{14,2},{1,13},{3,15... | collective-permute-start | bytes 196616 | tf_op jit(solution)/shard_map/ppermute | solution.py:460
  9.9 0.0 collective-permute-start.3
  9.9 0.6 %collective-permute-start.4 = (bf16[32,1024]{1,0:T(8,128)(2,1)S(1)}, bf16[32,1024]{1,0:T(8,128)(2,1)S(1)}, u32[]{:S(2)}, u32[]{:S(2)}) collective-permute-start(bf16[32,1024]{1,0:T(8,128)(2,1)S(1)} %get-tuple-element.23.refs_0_), channel_id=1, source_target_pairs={{0,4},{2,6},{4,0},{6,2},{8,12},{10,14},{12,8},{14,10},{1,5},{3,7},... | collective-permute-start | bytes 196616 | tf_op jit(solution)/shard_map/ppermute | solution.py:460
  10.6 1.6 %collective-permute-start.2 = (bf16[32,1024]{1,0:T(8,128)(2,1)S(1)}, bf16[32,1024]{1,0:T(8,128)(2,1)S(1)}, u32[]{:S(2)}, u32[]{:S(2)}) collective-permute-start(bf16[32,1024]{1,0:T(8,128)(2,1)S(1)} %get-tuple-element.23.refs_0_), channel_id=1, source_target_pairs={{0,2},{2,0},{4,6},{6,4},{8,10},{10,8},{12,14},{14,12},{1,3},{3,1},... | collective-permute-start | bytes 196616 | tf_op jit(solution)/shard_map/ppermute | solution.py:460
  12.2 0.0 collective-permute-start.1
  12.2 1.0 %row_tables.1 = (bf16[2,512,256]{2,1,0:T(8,128)(2,1)S(1)}, bf16[2,32,512]{2,1,0:T(8,128)(2,1)S(1)}, f32[2,256,256]{2,1,0:T(8,128)S(1)}, f32[2,8,128]{2,1,0:T(8,128)S(1)}) custom-call(f32[2,24,256]{2,1,0:T(8,128)S(1)} %get-tuple-element.21.info_ref), custom_call_target="tpu_custom_call" | custom-call | flops 100000000 | bytes 1000000 | tf_op jit(solution)/shard_map/row_tables/pallas_call | solution.py:493
  13.2 0.0 collective-permute-done.refs_2_
  13.3 1.1 %collective-permute-start.5 = (bf16[32,1024]{1,0:T(8,128)(2,1)S(1)}, bf16[32,1024]{1,0:T(8,128)(2,1)S(1)}, u32[]{:S(2)}, u32[]{:S(2)}) collective-permute-start(bf16[32,1024]{1,0:T(8,128)(2,1)S(1)} %collective-permute-done.refs_2_), channel_id=1, source_target_pairs={{0,2},{2,0},{4,6},{6,4},{8,10},{10,8},{12,14},{14,12},{1,3},{3,1},... | collective-permute-start | bytes 196616 | tf_op jit(solution)/shard_map/ppermute | solution.py:460
  14.4 1.2 %collective-permute-done.3.refs_0_ = bf16[32,1024]{1,0:T(8,128)(2,1)S(1)} collective-permute-done((bf16[32,1024]{1,0:T(8,128)(2,1)S(1)}, bf16[32,1024]{1,0:T(8,128)(2,1)S(1)}, u32[]{:S(2)}, u32[]{:S(2)}) %collective-permute-start.3) | collective-permute-done | bytes 65568 | tf_op jit(solution)/shard_map/ppermute | solution.py:460
  15.5 0.0 collective-permute-done.4.refs_1_
  15.5 1.6 %collective-permute-start.6 = (bf16[64,1024]{1,0:T(8,128)(2,1)S(1)}, bf16[64,1024]{1,0:T(8,128)(2,1)S(1)}, u32[]{:S(2)}, u32[]{:S(2)}) collective-permute-start(bf16[64,1024]{1,0:T(8,128)(2,1)S(1)} %join.1.refs_1_.refs_3_), channel_id=1, source_target_pairs={{0,2},{2,0},{4,6},{6,4},{8,10},{10,8},{12,14},{14,12},{1,3},{3,1},... | collective-permute-start | bytes 393224 | tf_op jit(solution)/shard_map/ppermute | solution.py:460
  17.1 0.0 collective-permute-done.1.far_info_ref
  17.1 0.0 collective-permute-done.2.refs_0_.refs_1_
  17.1 2.4 %far_tables.1 = (bf16[512,2048]{1,0:T(8,128)(2,1)S(1)}, bf16[512,2048]{1,0:T(8,128)(2,1)S(1)}, f32[2,32,2048]{2,1,0:T(8,128)S(1)}, f32[2,32,2048]{2,1,0:T(8,128)...) custom-call(f32[2,24,256]{2,1,0:T(8,128)S(1)} %get-tuple-element.21.info_ref, ...), custom_call_target="tpu_custom_call" | custom-call | flops 3000000000 | bytes 30000000 | tf_op jit(solution)/shard_map/far_tables/pallas_call | solution.py:516
  19.5 0.0 collective-permute-done.5.refs_4_
  19.5 1.2 %collective-permute-done.6.refs_5_ = bf16[64,1024]{1,0:T(8,128)(2,1)S(1)} collective-permute-done((bf16[64,1024]{1,0:T(8,128)(2,1)S(1)}, bf16[64,1024]{1,0:T(8,128)(2,1)S(1)}, u32[]{:S(2)}, u32[]{:S(2)}) %collective-permute-start.6) | collective-permute-done | bytes 131104 | tf_op jit(solution)/shard_map/ppermute | solution.py:460
  20.7 1.2 %focus.1 = (bf16[32,1024]{1,0:T(8,128)(2,1)S(1)}, f32[2]{0:T(128)}) custom-call(bf16[2,512,256]{2,1,0:T(8,128)(2,1)S(1)} %get-tuple-element.22.tall_ref, bf16[2,32,512]{2,1,0:T(8,128)(2,1)S(1)} %get-tuple-element.25.flat_ref, f32[2,256,256]{2,1,0:T(8,128)S(1)} %get-tuple-element.26.spot_ref, f32[2,8,128]{2,1,0:T(8,128)S(1)} %get-tuple-element.27.gain_ref, ...), custom_call_target="tpu_custom_call" | custom-call | flops 100000000 | bytes 1000000 | tf_op jit(solution)/shard_map/focus/pallas_call | solution.py:524
  21.9 0.1 collective-permute-start.7
  22.0 1.4 %gradient_own.1.refs_5_ = f32[32,2048]{1,0:T(8,128)S(1)} custom-call(bf16[32,1024]{1,0:T(8,128)(2,1)S(1)} %get-tuple-element.31.back_ref, bf16[2048,512]{1,0:T(8,128)(2,1)S(1)} %get-tuple-element.35.refs_0_, bf16[2048,512]{1,0:T(8,128)(2,1)S(1)} %get-tuple-element.36.refs_1_, f32[2,32,2048]{2,1,0:T(8,128)S(1)} %get-tuple-element.37.refs_2_, ...), custom_call_target="tpu_custom_call" | custom-call | flops 1000000000 | bytes 10000000 | tf_op jit(solution)/shard_map/gradient_own/pallas_call | solution.py:539
  23.4 0.0 collective-permute-done.7.refs_0_
  23.4 1.6 %gradient_far.1 = f32[32,2048]{1,0:T(8,128)} custom-call(bf16[32,1024]{1,0:T(8,128)(2,1)S(1)} %collective-permute-done.7.refs_0_, bf16[512,2048]{1,0:T(8,128)(2,1)S(1)} %get-tuple-element.32.refs_1_, bf16[512,2048]{1,0:T(8,128)(2,1)S(1)} %get-tuple-element.33.refs_2_, f32[2,32,2048]{2,1,0:T(8,128)S(1)} %get-tuple-element.29.after_ref.refs_3_, ...), custom_call_target="tpu_custom_call" | custom-call | flops 1000000000 | bytes 10000000 | tf_op jit(solution)/shard_map/gradient_far/pallas_call | solution.py:544
  (1 shorter events, 0.0 us)
Async XLA Ops:
  4.8 8.4 %collective-permute-start = (bf16[32,1024]{1,0:T(8,128)(2,1)S(1)}, bf16[32,1024]{1,0:T(8,128)(2,1)S(1)}, u32[]{:S(2)}, u32[]{:S(2)}) collective-permute-start(bf16[32,1024]{1,0:T(8,128)(2,1)S(1)} %get-tuple-element.23.refs_0_), channel_id=1, source_target_pairs={{0,12},{2,14},{4,8},{6,10},{8,4},{10,6},{12,0},{14,2},{1,13},{3,15... | collective-permute-start | bytes 196616 | tf_op jit(solution)/shard_map/ppermute | solution.py:460
  9.9 5.6 %collective-permute-start.3 = (bf16[32,1024]{1,0:T(8,128)(2,1)S(1)}, bf16[32,1024]{1,0:T(8,128)(2,1)S(1)}, u32[]{:S(2)}, u32[]{:S(2)}) collective-permute-start(bf16[32,1024]{1,0:T(8,128)(2,1)S(1)} %get-tuple-element.23.refs_0_), channel_id=1, source_target_pairs={{0,8},{2,10},{4,12},{6,14},{8,0},{10,2},{12,4},{14,6},{1,9},{3,11}... | collective-permute-start | bytes 196616 | tf_op jit(solution)/shard_map/ppermute | solution.py:460
  9.9 5.6 %collective-permute-start.4 = (bf16[32,1024]{1,0:T(8,128)(2,1)S(1)}, bf16[32,1024]{1,0:T(8,128)(2,1)S(1)}, u32[]{:S(2)}, u32[]{:S(2)}) collective-permute-start(bf16[32,1024]{1,0:T(8,128)(2,1)S(1)} %get-tuple-element.23.refs_0_), channel_id=1, source_target_pairs={{0,4},{2,6},{4,0},{6,2},{8,12},{10,14},{12,8},{14,10},{1,5},{3,7},... | collective-permute-start | bytes 196616 | tf_op jit(solution)/shard_map/ppermute | solution.py:460
  10.6 6.5 %collective-permute-start.2 = (bf16[32,1024]{1,0:T(8,128)(2,1)S(1)}, bf16[32,1024]{1,0:T(8,128)(2,1)S(1)}, u32[]{:S(2)}, u32[]{:S(2)}) collective-permute-start(bf16[32,1024]{1,0:T(8,128)(2,1)S(1)} %get-tuple-element.23.refs_0_), channel_id=1, source_target_pairs={{0,2},{2,0},{4,6},{6,4},{8,10},{10,8},{12,14},{14,12},{1,3},{3,1},... | collective-permute-start | bytes 196616 | tf_op jit(solution)/shard_map/ppermute | solution.py:460
  12.2 4.9 %collective-permute-start.1 = (f32[2,24,256]{2,1,0:T(8,128)S(1)}, f32[2,24,256]{2,1,0:T(8,128)S(1)}, u32[]{:S(2)}, u32[]{:S(2)}) collective-permute-start(f32[2,24,256]{2,1,0:T(8,128)S(1)} %get-tuple-element.21.info_ref), channel_id=1, source_target_pairs={{0,1},{1,0},{2,3},{3,2},{4,5},{5,4},{6,7},{7,6},{8,9},{9,8},{10,11... | collective-permute-start | bytes 147464 | tf_op jit(solution)/shard_map/ppermute | solution.py:463
  13.3 6.2 %collective-permute-start.5 = (bf16[32,1024]{1,0:T(8,128)(2,1)S(1)}, bf16[32,1024]{1,0:T(8,128)(2,1)S(1)}, u32[]{:S(2)}, u32[]{:S(2)}) collective-permute-start(bf16[32,1024]{1,0:T(8,128)(2,1)S(1)} %collective-permute-done.refs_2_), channel_id=1, source_target_pairs={{0,2},{2,0},{4,6},{6,4},{8,10},{10,8},{12,14},{14,12},{1,3},{3,1},... | collective-permute-start | bytes 196616 | tf_op jit(solution)/shard_map/ppermute | solution.py:460
  15.5 5.1 %collective-permute-start.6 = (bf16[64,1024]{1,0:T(8,128)(2,1)S(1)}, bf16[64,1024]{1,0:T(8,128)(2,1)S(1)}, u32[]{:S(2)}, u32[]{:S(2)}) collective-permute-start(bf16[64,1024]{1,0:T(8,128)(2,1)S(1)} %join.1.refs_1_.refs_3_), channel_id=1, source_target_pairs={{0,2},{2,0},{4,6},{6,4},{8,10},{10,8},{12,14},{14,12},{1,3},{3,1},... | collective-permute-start | bytes 393224 | tf_op jit(solution)/shard_map/ppermute | solution.py:460
  21.9 1.5 %collective-permute-start.7 = (bf16[32,1024]{1,0:T(8,128)(2,1)S(1)}, bf16[32,1024]{1,0:T(8,128)(2,1)S(1)}, u32[]{:S(2)}, u32[]{:S(2)}) collective-permute-start(bf16[32,1024]{1,0:T(8,128)(2,1)S(1)} %get-tuple-element.31.back_ref), channel_id=1, source_target_pairs={{0,1},{1,0},{2,3},{3,2},{4,5},{5,4},{6,7},{7,6},{8,9},{9,8},{10,11... | collective-permute-start | bytes 196616 | tf_op jit(solution)/shard_map/ppermute | solution.py:463

commit v10 on v9

--- a/solution.py
+++ b/solution.py
@@ -77,19 +77,33 @@
     centre_ref[1] = cent_i
 
 
-def near_fields(s, info_ref, pairs):
-    def coef(pair, row):
-        return info_ref[pair, row : row + 1, :LANES]
-
-    outs = [[coef(p, k) + coef(p, k + 1) * s for k in (0, TERMS)] for p in range(pairs)]
-    twice = s + s
-    before, current = jnp.ones_like(s), s
-    for order in range(2, TERMS):
-        before, current = current, twice * current - before
-        for pair, out in enumerate(outs):
-            out[0] = out[0] + coef(pair, order) * current
-            out[1] = out[1] + coef(pair, TERMS + order) * current
-    return outs
+def power_coefs(coef):
+    before, current = [1], [0, 1]
+    bases = [before, current]
+    for _ in range(2, TERMS):
+        doubled = [0] + [2 * term for term in current]
+        before, current = current, [a - b for a, b in itertools.zip_longest(doubled, before, fillvalue=0)]
+        bases.append(current)
+    rows = []
+    for part, power in itertools.product(range(2), range(TERMS)):
+        row = None
+        for order in range(power, TERMS, 2):
+            place = part * TERMS + order
+            term = coef[place : place + 1] * float(bases[order][power])
+            row = term if row is None else row + term
+        rows.append(row)
+    return jnp.concatenate(rows, axis=0)
+
+
+def near_fields(s, power_ref, pairs):
+    outs = []
+    for pair, part in itertools.product(range(pairs), range(2)):
+        row = (part + 1) * TERMS - 1
+        value = power_ref[pair, row : row + 1, :] * s + power_ref[pair, row - 1 : row, :]
+        for row in range(row - 2, part * TERMS - 1, -1):
+            value = value * s + power_ref[pair, row : row + 1, :]
+        outs.append(value)
+    return [outs[2 * pair : 2 * pair + 2] for pair in range(pairs)]
 
 
 def near_slopes(s, coef_ref, pairs):
@@ -138,7 +152,8 @@
     pairs = info_ref.shape[0]
     table_refs, refs = refs[:pairs], refs[pairs:]
     (
-        wave_ref, angle_ref, aim_ref, coef_ref, width_ref, far_ref, base_ref, centre_ref, near_ref, acc_ref, sems,
+        wave_ref, angle_ref, aim_ref, coef_ref, width_ref, far_ref, base_ref, centre_ref, power_ref, near_ref, acc_ref,
+        sems,
     ) = refs
     rows_dev, cols = width_ref.shape
     half = cols // 2
@@ -151,11 +166,13 @@
     ]
     for move in moves:
         move.start()
-    for move in moves[:4]:
+    for move in moves:
         move.wait()
     for pair in range(pairs):
         coef = pick_coef(coef_ref[...], wave_ref[pair])
-        info_ref[pair, :WAVE_ROW, :] = jnp.broadcast_to(coef, (WAVE_ROW, FOCAL))
+        coef = jnp.broadcast_to(coef, (WAVE_ROW, FOCAL))
+        info_ref[pair, :WAVE_ROW, :] = coef
+        power_ref[pair] = power_coefs(coef[:, :LANES])
         row = iota((INFO_ROWS - WAVE_ROW, FOCAL), 0) + WAVE_ROW
         ids = jnp.where(row == WAVE_ROW, wave_ref[pair], 0)
         ids = jnp.where(row == ANGLE_ROW, angle_ref[pair], ids)
@@ -164,26 +181,17 @@
         info_ref[pair, WAVE_ROW:, :] = ids.astype(jnp.float32)
     for pair in range(pairs):
         own_waves(info_ref, pair, cols, base_ref.at[pair], centre_ref.at[pair])
-    acc_ref[...] = jnp.zeros_like(acc_ref)
-    moves[4].wait()
     core = lax.axis_index("wave")
-
-    @pl.when(core == 1)
-    def _():
-        own_ref[...] = width_ref[:, half:]
-        far_ref[...] = pltpu.roll(turn_round(width_ref[:, :half]), 1, 1)
-
-    @pl.when(core == 0)
-    def _():
-        own_ref[...] = turn_round(width_ref[:, :half])
-        far_ref[...] = pltpu.roll(width_ref[:, half:], half - 1, 1)
+    left, right = turn_round(width_ref[:, :half]), width_ref[:, half:]
+    own_ref[...] = jnp.where(core == 1, right, left)
+    far_ref[...] = jnp.where(core == 1, pltpu.roll(left, 1, 1), pltpu.roll(right, half - 1, 1))
 
     void = jnp.where(core == 1, 0, half - 1)
     for index in range(half // (2 * BLOCK)):
         starts = block_starts(half, index)
         for start in (start + step for start in starts for step in range(0, BLOCK, LANES)):
             for side, ref in enumerate((own_ref, far_ref)):
-                outs = near_fields(ref[:, start : start + LANES], info_ref, pairs)
+                outs = near_fields(ref[:, start : start + LANES], power_ref, pairs)
                 if side and start in (0, half - LANES):
                     keep = iota((rows_dev, LANES), 1) + start != void
                     outs = [[jnp.where(keep, part, 0.0) for part in out] for out in outs]
@@ -198,14 +206,15 @@
                     rows = slice(start + row, start + row + GRAIN)
                     table_refs[pair][rows, :FOCAL] = table[0].astype(jnp.bfloat16)
                     table_refs[pair][rows, FOCAL:] = table[1].astype(jnp.bfloat16)
-            acc_ref[pair] += jnp.dot(
+            product = jnp.dot(
                 jnp.concatenate([near_ref[pair, :, start : start + BLOCK] for start in starts], axis=1),
                 jnp.concatenate([table_refs[pair][start : start + BLOCK, :] for start in starts], axis=0),
                 preferred_element_type=jnp.float32,
             )
+            acc_ref[pair] = product if index == 0 else acc_ref[pair] + product
     alone = jnp.where(core == 1, 0, half)
     column = width_ref[:, pl.ds(pl.multiple_of(alone, LANES), LANES)]
-    columns = near_fields(column, info_ref, pairs)
+    columns = near_fields(column, power_ref, pairs)
     for pair in range(pairs):
         acc = [acc_ref[pair, part * rows_dev : (part + 1) * rows_dev, :] for part in range(4)]
         (own_rr, own_ri), (own_ir, own_ii), (far_rr, far_ri), (far_ir, far_ii) = (
@@ -320,17 +329,16 @@
         score_ref[pair] = jnp.sum(ratio * gain)
         scale = gain * 2.0 / all_power
         for rows in pieces:
-            lower = slice(rows.start + FOCAL, rows.stop + FOCAL)
             weight = scale * (spot_ref[pair, rows, :] - ratio)
-            real = (weight * field_ref[pair, 0, rows, :]).astype(jnp.bfloat16)
-            imag = (weight * field_ref[pair, 1, rows, :]).astype(jnp.bfloat16)
-            stack_ref[pair, rows, :FOCAL] = real
-            stack_ref[pair, rows, FOCAL:] = imag
-            stack_ref[pair, lower, :FOCAL] = imag
-            stack_ref[pair, lower, FOCAL:] = -real
-        back = jnp.dot(flat_ref[pair], stack_ref[pair], preferred_element_type=jnp.float32)
+            stack_ref[pair, rows, :FOCAL] = (weight * field_ref[pair, 0, rows, :]).astype(jnp.bfloat16)
+            stack_ref[pair, rows, FOCAL:] = (weight * field_ref[pair, 1, rows, :]).astype(jnp.bfloat16)
+        flat = jnp.concatenate([flat_ref[pair, :, :FOCAL], flat_ref[pair, :, FOCAL:]], axis=0)
+        back = jnp.dot(flat, stack_ref[pair], preferred_element_type=jnp.float32)
+        real = back[:rows_dev, :FOCAL] + back[rows_dev:, FOCAL:]
+        imag = back[:rows_dev, FOCAL:] - back[rows_dev:, :FOCAL]
         lane = 2 * pair * FOCAL
-        back_ref[:, lane : lane + 2 * FOCAL] = back.astype(jnp.bfloat16)
+        back_ref[:, lane : lane + FOCAL] = real.astype(jnp.bfloat16)
+        back_ref[:, lane + FOCAL : lane + 2 * FOCAL] = imag.astype(jnp.bfloat16)
 
 
 def table_kernel(scale, cols, info_ref, far_info_ref, width_ref, *refs):
@@ -482,6 +490,7 @@
             pltpu.VMEM(widths.shape, f32),
             pltpu.VMEM((rows_dev, own_cols), f32),
             *waves,
+            pltpu.VMEM((pairs_dev, 2 * TERMS, LANES), f32),
             pltpu.VMEM((pairs_dev, 4 * rows_dev, own_cols), bf16),
             pltpu.VMEM((pairs_dev, 4 * rows_dev, 2 * FOCAL), f32),
             pltpu.SemaphoreType.DMA((5,)),
@@ -529,7 +538,7 @@
             pltpu.VMEM((rows, lanes), bf16),
             pltpu.VMEM((pairs_dev, 2 * FOCAL, 2 * FOCAL), f32),
             pltpu.VMEM((pairs_dev, 2, FOCAL, FOCAL), f32),
-            pltpu.VMEM((pairs_dev, 2 * FOCAL, 2 * FOCAL), bf16),
+            pltpu.VMEM((pairs_dev, FOCAL, 2 * FOCAL), bf16),
         ],
         10**8, 10**6,
     )(tall, flat, spots, gains, far_slopes[0], *sections)

time: 25.2 us -> 25.1 us (level)
  no operation moved by 1% of the time
where the time goes in v10:
time: 25.1 us; the launch traced here: 25 us
  Pallas kernels  11.8 us (47%)
  starting transfers between devices  10.1 us (40%)
  waiting for transfers between devices  2.37 us (9%)
  between operations  0.7 us (3%)
    ppermute x6, starting transfers between devices, exchange(): lax.ppermute(value, 'aperture', [(index, index ^ step) for index in range...  10 us
    pallas_call x1, Pallas kernels, on_device(): call(forward_kernel, 'forward', (shape((rows_dev, lanes), bf16), shape((p...  4.01 us
    pallas_call x1, Pallas kernels, on_device(): call(functools.partial(table_kernel, math.sqrt(rows * cols), cols), 'far_...  2.37 us
    ppermute x6, waiting for transfers between devices, exchange(): lax.ppermute(value, 'aperture', [(index, index ^ step) for index in range...  2.36 us
    pallas_call x1, Pallas kernels, on_device(): call(functools.partial(last_grad_kernel, pairs_dev), 'gradient_far', out,...  1.61 us
    pallas_call x1, Pallas kernels, on_device(): call(functools.partial(grad_kernel, pairs_dev, across=False), 'gradient_o...  1.38 us
    pallas_call x1, Pallas kernels, on_device(): call(functools.partial(focus_kernel, steps), 'focus', (shape((rows_dev, l...  1.36 us
    pallas_call x1, Pallas kernels, on_device(): call(row_kernel, 'row_tables', (shape((pairs_dev, 2 * FOCAL, rows), bf16)...  1.04 us
  transfers between devices with their start and end apart: 8, of which 2 were waited for; matrix products, arithmetic and copies ran while one was open for 0% of the time, Pallas kernels for 19%

profile of v10, /device:TPU:0, one launch (start us, length us, event | category | flops | bytes accessed | tf_op | source)
XLA Modules:
  0.0 25.0 jit_solution(7603673227177631260)
XLA Ops:
  0.6 4.0 %forward.1 = (bf16[32,1024]{1,0:T(8,128)(2,1)S(1)}, f32[2,24,256]{2,1,0:T(8,128)S(1)}, f32[32,2048]{1,0:T(8,128)S(1)}, bf16[2048,512]{1,0:T(8,128)(2,1)S(1)}, bf16[2048,512]{1,0:T(8,128)(2,1)S(1)}) custom-call(s32[2]{0:T(128)} %wave_hbm.1, s32[2]{0:T(128)} %angle_hbm.1, s32[2,2]{1,0:T(2,128)} %aim_hbm.1, f32[16,256]{1,0:T(8,128)} %bitcast.1, ...), custom_call_target="tpu_custom_call" | custom-call | flops 1000000000 | bytes 10000000 | tf_op jit(solution)/shard_map/forward/pallas_call | solution.py:477
  4.7 5.1 %collective-permute-start = (bf16[32,1024]{1,0:T(8,128)(2,1)S(1)}, bf16[32,1024]{1,0:T(8,128)(2,1)S(1)}, u32[]{:S(2)}, u32[]{:S(2)}) collective-permute-start(bf16[32,1024]{1,0:T(8,128)(2,1)S(1)} %get-tuple-element.23.refs_0_), channel_id=1, source_target_pairs={{0,12},{2,14},{4,8},{6,10},{8,4},{10,6},{12,0},{14,2},{1,13},{3,15... | collective-permute-start | bytes 196616 | tf_op jit(solution)/shard_map/ppermute | solution.py:468
  9.8 0.0 collective-permute-start.3
  9.8 0.6 %collective-permute-start.4 = (bf16[32,1024]{1,0:T(8,128)(2,1)S(1)}, bf16[32,1024]{1,0:T(8,128)(2,1)S(1)}, u32[]{:S(2)}, u32[]{:S(2)}) collective-permute-start(bf16[32,1024]{1,0:T(8,128)(2,1)S(1)} %get-tuple-element.23.refs_0_), channel_id=1, source_target_pairs={{0,4},{2,6},{4,0},{6,2},{8,12},{10,14},{12,8},{14,10},{1,5},{3,7},... | collective-permute-start | bytes 196616 | tf_op jit(solution)/shard_map/ppermute | solution.py:468
  10.4 1.6 %collective-permute-start.2 = (bf16[32,1024]{1,0:T(8,128)(2,1)S(1)}, bf16[32,1024]{1,0:T(8,128)(2,1)S(1)}, u32[]{:S(2)}, u32[]{:S(2)}) collective-permute-start(bf16[32,1024]{1,0:T(8,128)(2,1)S(1)} %get-tuple-element.23.refs_0_), channel_id=1, source_target_pairs={{0,2},{2,0},{4,6},{6,4},{8,10},{10,8},{12,14},{14,12},{1,3},{3,1},... | collective-permute-start | bytes 196616 | tf_op jit(solution)/shard_map/ppermute | solution.py:468
  12.0 0.0 collective-permute-start.1
  12.0 1.0 %row_tables.1 = (bf16[2,512,256]{2,1,0:T(8,128)(2,1)S(1)}, bf16[2,32,512]{2,1,0:T(8,128)(2,1)S(1)}, f32[2,256,256]{2,1,0:T(8,128)S(1)}, f32[2,8,128]{2,1,0:T(8,128)S(1)}) custom-call(f32[2,24,256]{2,1,0:T(8,128)S(1)} %get-tuple-element.21.info_ref), custom_call_target="tpu_custom_call" | custom-call | flops 100000000 | bytes 1000000 | tf_op jit(solution)/shard_map/row_tables/pallas_call | solution.py:502
  13.1 0.0 collective-permute-done.refs_2_
  13.1 1.1 %collective-permute-start.5 = (bf16[32,1024]{1,0:T(8,128)(2,1)S(1)}, bf16[32,1024]{1,0:T(8,128)(2,1)S(1)}, u32[]{:S(2)}, u32[]{:S(2)}) collective-permute-start(bf16[32,1024]{1,0:T(8,128)(2,1)S(1)} %collective-permute-done.refs_2_), channel_id=1, source_target_pairs={{0,2},{2,0},{4,6},{6,4},{8,10},{10,8},{12,14},{14,12},{1,3},{3,1},... | collective-permute-start | bytes 196616 | tf_op jit(solution)/shard_map/ppermute | solution.py:468
  14.2 1.2 %collective-permute-done.3.refs_0_ = bf16[32,1024]{1,0:T(8,128)(2,1)S(1)} collective-permute-done((bf16[32,1024]{1,0:T(8,128)(2,1)S(1)}, bf16[32,1024]{1,0:T(8,128)(2,1)S(1)}, u32[]{:S(2)}, u32[]{:S(2)}) %collective-permute-start.3) | collective-permute-done | bytes 65568 | tf_op jit(solution)/shard_map/ppermute | solution.py:468
  15.4 0.0 collective-permute-done.4.refs_1_
  15.4 1.6 %collective-permute-start.6 = (bf16[64,1024]{1,0:T(8,128)(2,1)S(1)}, bf16[64,1024]{1,0:T(8,128)(2,1)S(1)}, u32[]{:S(2)}, u32[]{:S(2)}) collective-permute-start(bf16[64,1024]{1,0:T(8,128)(2,1)S(1)} %join.1.refs_1_.refs_3_), channel_id=1, source_target_pairs={{0,2},{2,0},{4,6},{6,4},{8,10},{10,8},{12,14},{14,12},{1,3},{3,1},... | collective-permute-start | bytes 393224 | tf_op jit(solution)/shard_map/ppermute | solution.py:468
  16.9 0.0 collective-permute-done.1.far_info_ref
  16.9 0.0 collective-permute-done.2.refs_0_.refs_1_
  16.9 2.4 %far_tables.1 = (bf16[512,2048]{1,0:T(8,128)(2,1)S(1)}, bf16[512,2048]{1,0:T(8,128)(2,1)S(1)}, f32[2,32,2048]{2,1,0:T(8,128)S(1)}, f32[2,32,2048]{2,1,0:T(8,128)...) custom-call(f32[2,24,256]{2,1,0:T(8,128)S(1)} %get-tuple-element.21.info_ref, ...), custom_call_target="tpu_custom_call" | custom-call | flops 3000000000 | bytes 30000000 | tf_op jit(solution)/shard_map/far_tables/pallas_call | solution.py:525
  19.3 0.0 collective-permute-done.5.refs_4_
  19.3 1.2 %collective-permute-done.6.refs_5_ = bf16[64,1024]{1,0:T(8,128)(2,1)S(1)} collective-permute-done((bf16[64,1024]{1,0:T(8,128)(2,1)S(1)}, bf16[64,1024]{1,0:T(8,128)(2,1)S(1)}, u32[]{:S(2)}, u32[]{:S(2)}) %collective-permute-start.6) | collective-permute-done | bytes 131104 | tf_op jit(solution)/shard_map/ppermute | solution.py:468
  20.5 1.4 %focus.1 = (bf16[32,1024]{1,0:T(8,128)(2,1)S(1)}, f32[2]{0:T(128)}) custom-call(bf16[2,512,256]{2,1,0:T(8,128)(2,1)S(1)} %get-tuple-element.22.tall_ref, bf16[2,32,512]{2,1,0:T(8,128)(2,1)S(1)} %get-tuple-element.25.flat_ref, f32[2,256,256]{2,1,0:T(8,128)S(1)} %get-tuple-element.26.spot_ref, f32[2,8,128]{2,1,0:T(8,128)S(1)} %get-tuple-element.27.gain_ref, ...), custom_call_target="tpu_custom_call" | custom-call | flops 100000000 | bytes 1000000 | tf_op jit(solution)/shard_map/focus/pallas_call | solution.py:533
  21.9 0.1 collective-permute-start.7
  22.0 1.4 %gradient_own.1.refs_5_ = f32[32,2048]{1,0:T(8,128)S(1)} custom-call(bf16[32,1024]{1,0:T(8,128)(2,1)S(1)} %get-tuple-element.31.back_ref, bf16[2048,512]{1,0:T(8,128)(2,1)S(1)} %get-tuple-element.35.refs_0_, bf16[2048,512]{1,0:T(8,128)(2,1)S(1)} %get-tuple-element.36.refs_1_, f32[2,32,2048]{2,1,0:T(8,128)S(1)} %get-tuple-element.37.refs_2_, ...), custom_call_target="tpu_custom_call" | custom-call | flops 1000000000 | bytes 10000000 | tf_op jit(solution)/shard_map/gradient_own/pallas_call | solution.py:548
  23.3 0.0 collective-permute-done.7.refs_0_
  23.4 1.6 %gradient_far.1 = f32[32,2048]{1,0:T(8,128)} custom-call(bf16[32,1024]{1,0:T(8,128)(2,1)S(1)} %collective-permute-done.7.refs_0_, bf16[512,2048]{1,0:T(8,128)(2,1)S(1)} %get-tuple-element.32.refs_1_, bf16[512,2048]{1,0:T(8,128)(2,1)S(1)} %get-tuple-element.33.refs_2_, f32[2,32,2048]{2,1,0:T(8,128)S(1)} %get-tuple-element.29.after_ref.refs_3_, ...), custom_call_target="tpu_custom_call" | custom-call | flops 1000000000 | bytes 10000000 | tf_op jit(solution)/shard_map/gradient_far/pallas_call | solution.py:553
  (1 shorter events, 0.0 us)
Async XLA Ops:
  4.7 8.4 %collective-permute-start = (bf16[32,1024]{1,0:T(8,128)(2,1)S(1)}, bf16[32,1024]{1,0:T(8,128)(2,1)S(1)}, u32[]{:S(2)}, u32[]{:S(2)}) collective-permute-start(bf16[32,1024]{1,0:T(8,128)(2,1)S(1)} %get-tuple-element.23.refs_0_), channel_id=1, source_target_pairs={{0,12},{2,14},{4,8},{6,10},{8,4},{10,6},{12,0},{14,2},{1,13},{3,15... | collective-permute-start | bytes 196616 | tf_op jit(solution)/shard_map/ppermute | solution.py:468
  9.8 5.6 %collective-permute-start.3 = (bf16[32,1024]{1,0:T(8,128)(2,1)S(1)}, bf16[32,1024]{1,0:T(8,128)(2,1)S(1)}, u32[]{:S(2)}, u32[]{:S(2)}) collective-permute-start(bf16[32,1024]{1,0:T(8,128)(2,1)S(1)} %get-tuple-element.23.refs_0_), channel_id=1, source_target_pairs={{0,8},{2,10},{4,12},{6,14},{8,0},{10,2},{12,4},{14,6},{1,9},{3,11}... | collective-permute-start | bytes 196616 | tf_op jit(solution)/shard_map/ppermute | solution.py:468
  9.8 5.6 %collective-permute-start.4 = (bf16[32,1024]{1,0:T(8,128)(2,1)S(1)}, bf16[32,1024]{1,0:T(8,128)(2,1)S(1)}, u32[]{:S(2)}, u32[]{:S(2)}) collective-permute-start(bf16[32,1024]{1,0:T(8,128)(2,1)S(1)} %get-tuple-element.23.refs_0_), channel_id=1, source_target_pairs={{0,4},{2,6},{4,0},{6,2},{8,12},{10,14},{12,8},{14,10},{1,5},{3,7},... | collective-permute-start | bytes 196616 | tf_op jit(solution)/shard_map/ppermute | solution.py:468
  10.4 6.5 %collective-permute-start.2 = (bf16[32,1024]{1,0:T(8,128)(2,1)S(1)}, bf16[32,1024]{1,0:T(8,128)(2,1)S(1)}, u32[]{:S(2)}, u32[]{:S(2)}) collective-permute-start(bf16[32,1024]{1,0:T(8,128)(2,1)S(1)} %get-tuple-element.23.refs_0_), channel_id=1, source_target_pairs={{0,2},{2,0},{4,6},{6,4},{8,10},{10,8},{12,14},{14,12},{1,3},{3,1},... | collective-permute-start | bytes 196616 | tf_op jit(solution)/shard_map/ppermute | solution.py:468
  12.0 4.9 %collective-permute-start.1 = (f32[2,24,256]{2,1,0:T(8,128)S(1)}, f32[2,24,256]{2,1,0:T(8,128)S(1)}, u32[]{:S(2)}, u32[]{:S(2)}) collective-permute-start(f32[2,24,256]{2,1,0:T(8,128)S(1)} %get-tuple-element.21.info_ref), channel_id=1, source_target_pairs={{0,1},{1,0},{2,3},{3,2},{4,5},{5,4},{6,7},{7,6},{8,9},{9,8},{10,11... | collective-permute-start | bytes 147464 | tf_op jit(solution)/shard_map/ppermute | solution.py:471
  13.1 6.2 %collective-permute-start.5 = (bf16[32,1024]{1,0:T(8,128)(2,1)S(1)}, bf16[32,1024]{1,0:T(8,128)(2,1)S(1)}, u32[]{:S(2)}, u32[]{:S(2)}) collective-permute-start(bf16[32,1024]{1,0:T(8,128)(2,1)S(1)} %collective-permute-done.refs_2_), channel_id=1, source_target_pairs={{0,2},{2,0},{4,6},{6,4},{8,10},{10,8},{12,14},{14,12},{1,3},{3,1},... | collective-permute-start | bytes 196616 | tf_op jit(solution)/shard_map/ppermute | solution.py:468
  15.4 5.1 %collective-permute-start.6 = (bf16[64,1024]{1,0:T(8,128)(2,1)S(1)}, bf16[64,1024]{1,0:T(8,128)(2,1)S(1)}, u32[]{:S(2)}, u32[]{:S(2)}) collective-permute-start(bf16[64,1024]{1,0:T(8,128)(2,1)S(1)} %join.1.refs_1_.refs_3_), channel_id=1, source_target_pairs={{0,2},{2,0},{4,6},{6,4},{8,10},{10,8},{12,14},{14,12},{1,3},{3,1},... | collective-permute-start | bytes 393224 | tf_op jit(solution)/shard_map/ppermute | solution.py:468
  21.9 1.5 %collective-permute-start.7 = (bf16[32,1024]{1,0:T(8,128)(2,1)S(1)}, bf16[32,1024]{1,0:T(8,128)(2,1)S(1)}, u32[]{:S(2)}, u32[]{:S(2)}) collective-permute-start(bf16[32,1024]{1,0:T(8,128)(2,1)S(1)} %get-tuple-element.31.back_ref), channel_id=1, source_target_pairs={{0,1},{1,0},{2,3},{3,2},{4,5},{5,4},{6,7},{7,6},{8,9},{9,8},{10,11... | collective-permute-start | bytes 196616 | tf_op jit(solution)/shard_map/ppermute | solution.py:471

commit v11 on v10

--- a/solution.py
+++ b/solution.py
@@ -17,6 +17,7 @@
 GRAIN = 16
 LANES = 128
 PIECE = 16
+SPLITS = 4
 VMEM_LIMIT = 16 * 1024 * 1024
 WAVE_ROW, ANGLE_ROW, AIM_ROW, INFO_ROWS = 16, 17, 18, 24
 DIRECT = 16
@@ -131,6 +132,30 @@
     return jnp.concatenate(parts, axis=1)
 
 
+def both_sides(width_ref, core, start):
+    rows, cols = width_ref.shape
+    half = cols // 2
+    lane = iota((rows, LANES), 1)
+
+    def right(place):
+        place = half + place
+        return width_ref[:, place : place + LANES]
+
+    def left(place, turn):
+        place = half - LANES - place
+        return jnp.take_along_axis(width_ref[:, place : place + LANES], turn - lane, axis=1)
+
+    own = jnp.where(core == 1, right(start), left(start, LANES - 1))
+    mirrored = jnp.take_along_axis(
+        width_ref[:, half - LANES - start : half - start], (LANES - lane) % LANES, axis=1
+    )
+    edge = width_ref[:, half - start : half - start + 1]
+    mirrored = jnp.where(lane == 0, edge, mirrored)
+    after = min(start + LANES, half - LANES)
+    shifted = jnp.where(lane == LANES - 1, right(after)[:, :1], pltpu.roll(right(start), LANES - 1, 1))
+    return own, jnp.where(core == 1, mirrored, shifted)
+
+
 def block_starts(cols, index):
     return cols // 2 - (index + 1) * BLOCK, cols // 2 + index * BLOCK
 
@@ -152,17 +177,17 @@
     pairs = info_ref.shape[0]
     table_refs, refs = refs[:pairs], refs[pairs:]
     (
-        wave_ref, angle_ref, aim_ref, coef_ref, width_ref, far_ref, base_ref, centre_ref, power_ref, near_ref, acc_ref,
+        wave_ref, angle_ref, aim_ref, coef_ref, width_ref, base_ref, centre_ref, power_ref, near_ref, acc_ref,
         sems,
     ) = refs
     rows_dev, cols = width_ref.shape
     half = cols // 2
+    copies = [(wave_hbm, wave_ref), (angle_hbm, angle_ref), (aim_hbm, aim_ref), (coef_hbm, coef_ref)]
+    for start in range(0, cols, cols // SPLITS):
+        place = slice(start, start + cols // SPLITS)
+        copies.append((width_hbm.at[:, place], width_ref.at[:, place]))
     moves = [
-        pltpu.make_async_copy(source, target, sems.at[index])
-        for index, (source, target) in enumerate((
-            (wave_hbm, wave_ref), (angle_hbm, angle_ref), (aim_hbm, aim_ref),
-            (coef_hbm, coef_ref), (width_hbm, width_ref),
-        ))
+        pltpu.make_async_copy(source, target, sems.at[index]) for index, (source, target) in enumerate(copies)
     ]
     for move in moves:
         move.start()
@@ -182,16 +207,14 @@
     for pair in range(pairs):
         own_waves(info_ref, pair, cols, base_ref.at[pair], centre_ref.at[pair])
     core = lax.axis_index("wave")
-    left, right = turn_round(width_ref[:, :half]), width_ref[:, half:]
-    own_ref[...] = jnp.where(core == 1, right, left)
-    far_ref[...] = jnp.where(core == 1, pltpu.roll(left, 1, 1), pltpu.roll(right, half - 1, 1))
-
     void = jnp.where(core == 1, 0, half - 1)
     for index in range(half // (2 * BLOCK)):
         starts = block_starts(half, index)
         for start in (start + step for start in starts for step in range(0, BLOCK, LANES)):
-            for side, ref in enumerate((own_ref, far_ref)):
-                outs = near_fields(ref[:, start : start + LANES], power_ref, pairs)
+            sides = both_sides(width_ref, core, start)
+            own_ref[:, start : start + LANES] = sides[0]
+            for side, widths in enumerate(sides):
+                outs = near_fields(widths, power_ref, pairs)
                 if side and start in (0, half - LANES):
                     keep = iota((rows_dev, LANES), 1) + start != void
                     outs = [[jnp.where(keep, part, 0.0) for part in out] for out in outs]
@@ -282,13 +305,6 @@
         gain_ref[pair] = jnp.broadcast_to(FOCAL * FOCAL / total_of(total), gain_ref.shape[1:])
 
 
-def join_kernel(*refs):
-    *in_refs, out_ref = refs
-    count = in_refs[0].shape[0]
-    for index, ref in enumerate(in_refs):
-        out_ref[index * count : (index + 1) * count, :] = ref[...]
-
-
 def focus_kernel(steps, tall_ref, flat_ref, spot_ref, gain_ref, after_ref, *refs):
     del after_ref
     *sect_refs, back_ref, score_ref, rows_ref, mixed_ref, field_ref, stack_ref = refs
@@ -329,16 +345,17 @@
         score_ref[pair] = jnp.sum(ratio * gain)
         scale = gain * 2.0 / all_power
         for rows in pieces:
+            lower = slice(rows.start + FOCAL, rows.stop + FOCAL)
             weight = scale * (spot_ref[pair, rows, :] - ratio)
-            stack_ref[pair, rows, :FOCAL] = (weight * field_ref[pair, 0, rows, :]).astype(jnp.bfloat16)
-            stack_ref[pair, rows, FOCAL:] = (weight * field_ref[pair, 1, rows, :]).astype(jnp.bfloat16)
-        flat = jnp.concatenate([flat_ref[pair, :, :FOCAL], flat_ref[pair, :, FOCAL:]], axis=0)
-        back = jnp.dot(flat, stack_ref[pair], preferred_element_type=jnp.float32)
-        real = back[:rows_dev, :FOCAL] + back[rows_dev:, FOCAL:]
-        imag = back[:rows_dev, FOCAL:] - back[rows_dev:, :FOCAL]
+            real = (weight * field_ref[pair, 0, rows, :]).astype(jnp.bfloat16)
+            imag = (weight * field_ref[pair, 1, rows, :]).astype(jnp.bfloat16)
+            stack_ref[pair, rows, :FOCAL] = real
+            stack_ref[pair, rows, FOCAL:] = imag
+            stack_ref[pair, lower, :FOCAL] = imag
+            stack_ref[pair, lower, FOCAL:] = -real
+        back = jnp.dot(flat_ref[pair], stack_ref[pair], preferred_element_type=jnp.float32)
         lane = 2 * pair * FOCAL
-        back_ref[:, lane : lane + FOCAL] = real.astype(jnp.bfloat16)
-        back_ref[:, lane + FOCAL : lane + 2 * FOCAL] = imag.astype(jnp.bfloat16)
+        back_ref[:, lane : lane + 2 * FOCAL] = back.astype(jnp.bfloat16)
 
 
 def table_kernel(scale, cols, info_ref, far_info_ref, width_ref, *refs):
@@ -488,12 +505,11 @@
             pltpu.SMEM(targets.shape, jnp.int32),
             pltpu.VMEM(coef_table.shape[::-1], f32),
             pltpu.VMEM(widths.shape, f32),
-            pltpu.VMEM((rows_dev, own_cols), f32),
             *waves,
             pltpu.VMEM((pairs_dev, 2 * TERMS, LANES), f32),
             pltpu.VMEM((pairs_dev, 4 * rows_dev, own_cols), bf16),
             pltpu.VMEM((pairs_dev, 4 * rows_dev, 2 * FOCAL), f32),
-            pltpu.SemaphoreType.DMA((5,)),
+            pltpu.SemaphoreType.DMA((4 + SPLITS,)),
         ],
         10**9, 10**7,
     )(*(in_hbm(value) for value in (wave_ids, angle_ids, targets, coef_table.T, widths)))
@@ -511,12 +527,12 @@
         steps = list(range(peers - 2, 0, -2))
         got = [exchange(mine, step) for step in steps]
         near = exchange(mine, 1)
-        first, flat = lax.optimization_barrier((got[0], flat))
-        joined = call(join_kernel, "join", shape(((len(steps) - 1) * rows_dev, lanes), bf16),
-                      [VMEM] * (len(steps) - 1), VMEM, [], 10**6, 10**6)(*got[1:])
-        sections = [mine, near, first, joined, exchange(first, 1), exchange(joined, 1)]
+        got[0], flat = lax.optimization_barrier((got[0], flat))
+        for index in range(1, len(got) - 1):
+            got[index], _ = lax.optimization_barrier((got[index], got[index + 1]))
+        sections = [mine, near, *got, *(exchange(block, 1) for block in got)]
         steps = [0, 1, *steps, *(step ^ 1 for step in steps)]
-        after = [near, joined]
+        after = [near, *got]
     else:
         blocks = jnp.tile(mine[None], (peers, 1, 1))
         blocks = lax.all_to_all(blocks, "aperture", 0, 0, tiled=True)
@@ -538,7 +554,7 @@
             pltpu.VMEM((rows, lanes), bf16),
             pltpu.VMEM((pairs_dev, 2 * FOCAL, 2 * FOCAL), f32),
             pltpu.VMEM((pairs_dev, 2, FOCAL, FOCAL), f32),
-            pltpu.VMEM((pairs_dev, FOCAL, 2 * FOCAL), bf16),
+            pltpu.VMEM((pairs_dev, 2 * FOCAL, 2 * FOCAL), bf16),
         ],
         10**8, 10**6,
     )(tall, flat, spots, gains, far_slopes[0], *sections)

time: 25.1 us -> 27 us (1.076)
  waiting for transfers between devices: 2.37 us -> 3.44 us
  starting transfers between devices: 10.1 us -> 11 us
    ppermute x6 -> x7, waiting for transfers between devices: 2.36 us -> 3.44 us  [exchange(): lax.ppermute(value, 'aperture', [(index, index ^ step) for index in range...]
    ppermute x6 -> x7, starting transfers between devices: 10 us -> 10.9 us  [exchange(): lax.ppermute(value, 'aperture', [(index, index ^ step) for index in range...]
  transfers between devices with their start and end apart: 8 -> 9, of which waited for: 2 -> 3; matrix products, arithmetic and copies ran while one was open for 0% -> 0% of each run, Pallas kernels for 19% -> 18%
where the time goes in v11:
time: 27 us; the launch traced here: 26.8 us
  Pallas kernels  11.7 us (43%)
  starting transfers between devices  11 us (41%)
  waiting for transfers between devices  3.44 us (13%)
  between operations  0.7 us (3%)
    ppermute x7, starting transfers between devices, exchange(): lax.ppermute(value, 'aperture', [(index, index ^ step) for index in range...  10.9 us
    pallas_call x1, Pallas kernels, on_device(): call(forward_kernel, 'forward', (shape((rows_dev, lanes), bf16), shape((p...  4.11 us
    ppermute x7, waiting for transfers between devices, exchange(): lax.ppermute(value, 'aperture', [(index, index ^ step) for index in range...  3.44 us
    pallas_call x1, Pallas kernels, on_device(): call(functools.partial(table_kernel, math.sqrt(rows * cols), cols), 'far_...  2.37 us
    pallas_call x1, Pallas kernels, on_device(): call(functools.partial(last_grad_kernel, pairs_dev), 'gradient_far', out,...  1.61 us
    pallas_call x1, Pallas kernels, on_device(): call(functools.partial(grad_kernel, pairs_dev, across=False), 'gradient_o...  1.38 us
    pallas_call x1, Pallas kernels, on_device(): call(functools.partial(focus_kernel, steps), 'focus', (shape((rows_dev, l...  1.21 us
    pallas_call x1, Pallas kernels, on_device(): call(row_kernel, 'row_tables', (shape((pairs_dev, 2 * FOCAL, rows), bf16)...  1.04 us
  transfers between devices with their start and end apart: 9, of which 3 were waited for; matrix products, arithmetic and copies ran while one was open for 0% of the time, Pallas kernels for 18%

profile of v11, /device:TPU:0, one launch (start us, length us, event | category | flops | bytes accessed | tf_op | source)
XLA Modules:
  0.0 26.8 jit_solution(4967477807459261188)
XLA Ops:
  0.6 4.1 %forward.1 = (bf16[32,1024]{1,0:T(8,128)(2,1)S(1)}, f32[2,24,256]{2,1,0:T(8,128)S(1)}, f32[32,2048]{1,0:T(8,128)S(1)}, bf16[2048,512]{1,0:T(8,128)(2,1)S(1)}, bf16[2048,512]{1,0:T(8,128)(2,1)S(1)}) custom-call(s32[2]{0:T(128)} %wave_hbm.1, s32[2]{0:T(128)} %angle_hbm.1, s32[2,2]{1,0:T(2,128)} %aim_hbm.1, f32[16,256]{1,0:T(8,128)} %bitcast.1, ...), custom_call_target="tpu_custom_call" | custom-call | flops 1000000000 | bytes 10000000 | tf_op jit(solution)/shard_map/forward/pallas_call | solution.py:494
  4.7 5.1 %collective-permute-start = (bf16[32,1024]{1,0:T(8,128)(2,1)S(1)}, bf16[32,1024]{1,0:T(8,128)(2,1)S(1)}, u32[]{:S(2)}, u32[]{:S(2)}) collective-permute-start(bf16[32,1024]{1,0:T(8,128)(2,1)S(1)} %get-tuple-element.24.refs_0_), channel_id=1, source_target_pairs={{0,12},{2,14},{4,8},{6,10},{8,4},{10,6},{12,0},{14,2},{1,13},{3,15... | collective-permute-start | bytes 196616 | tf_op jit(solution)/shard_map/ppermute | solution.py:485
  9.9 0.0 collective-permute-start.3
  9.9 0.6 %collective-permute-start.4 = (bf16[32,1024]{1,0:T(8,128)(2,1)S(1)}, bf16[32,1024]{1,0:T(8,128)(2,1)S(1)}, u32[]{:S(2)}, u32[]{:S(2)}) collective-permute-start(bf16[32,1024]{1,0:T(8,128)(2,1)S(1)} %get-tuple-element.24.refs_0_), channel_id=1, source_target_pairs={{0,4},{2,6},{4,0},{6,2},{8,12},{10,14},{12,8},{14,10},{1,5},{3,7},... | collective-permute-start | bytes 196616 | tf_op jit(solution)/shard_map/ppermute | solution.py:485
  10.5 1.6 %collective-permute-start.2 = (bf16[32,1024]{1,0:T(8,128)(2,1)S(1)}, bf16[32,1024]{1,0:T(8,128)(2,1)S(1)}, u32[]{:S(2)}, u32[]{:S(2)}) collective-permute-start(bf16[32,1024]{1,0:T(8,128)(2,1)S(1)} %get-tuple-element.24.refs_0_), channel_id=1, source_target_pairs={{0,2},{2,0},{4,6},{6,4},{8,10},{10,8},{12,14},{14,12},{1,3},{3,1},... | collective-permute-start | bytes 196616 | tf_op jit(solution)/shard_map/ppermute | solution.py:485
  12.1 0.0 collective-permute-start.1
  12.1 1.0 %row_tables.1 = (bf16[2,512,256]{2,1,0:T(8,128)(2,1)S(1)}, bf16[2,32,512]{2,1,0:T(8,128)(2,1)S(1)}, f32[2,256,256]{2,1,0:T(8,128)S(1)}, f32[2,8,128]{2,1,0:T(8,128)S(1)}) custom-call(f32[2,24,256]{2,1,0:T(8,128)S(1)} %get-tuple-element.22.info_ref), custom_call_target="tpu_custom_call" | custom-call | flops 100000000 | bytes 1000000 | tf_op jit(solution)/shard_map/row_tables/pallas_call | solution.py:518
  13.2 0.0 collective-permute-done.refs_1_.refs_2_
  13.2 2.3 %collective-permute-done.3.refs_2_.refs_3_ = bf16[32,1024]{1,0:T(8,128)(2,1)S(1)} collective-permute-done((bf16[32,1024]{1,0:T(8,128)(2,1)S(1)}, bf16[32,1024]{1,0:T(8,128)(2,1)S(1)}, u32[]{:S(2)}, u32[]{:S(2)}) %collective-permute-start.3) | collective-permute-done | bytes 65568 | tf_op jit(solution)/shard_map/ppermute | solution.py:485
  15.5 0.0 collective-permute-done.4.refs_3_.refs_4_
  15.5 1.5 %collective-permute-start.5 = (bf16[32,1024]{1,0:T(8,128)(2,1)S(1)}, bf16[32,1024]{1,0:T(8,128)(2,1)S(1)}, u32[]{:S(2)}, u32[]{:S(2)}) collective-permute-start(bf16[32,1024]{1,0:T(8,128)(2,1)S(1)} %collective-permute-done.refs_1_.refs_2_), channel_id=1, source_target_pairs={{0,2},{2,0},{4,6},{6,4},{8,10},{10,8},{12,14},{14,12},{1,3},{3,1},... | collective-permute-start | bytes 196616 | tf_op jit(solution)/shard_map/ppermute | solution.py:485
  17.0 0.5 %collective-permute-start.6 = (bf16[32,1024]{1,0:T(8,128)(2,1)S(1)}, bf16[32,1024]{1,0:T(8,128)(2,1)S(1)}, u32[]{:S(2)}, u32[]{:S(2)}) collective-permute-start(bf16[32,1024]{1,0:T(8,128)(2,1)S(1)} %collective-permute-done.3.refs_2_.refs_3_), channel_id=1, source_target_pairs={{0,2},{2,0},{4,6},{6,4},{8,10},{10,8},{12,14},{14,12},{1,3},{3,1},... | collective-permute-start | bytes 196616 | tf_op jit(solution)/shard_map/ppermute | solution.py:485
  17.5 1.5 %collective-permute-start.7 = (bf16[32,1024]{1,0:T(8,128)(2,1)S(1)}, bf16[32,1024]{1,0:T(8,128)(2,1)S(1)}, u32[]{:S(2)}, u32[]{:S(2)}) collective-permute-start(bf16[32,1024]{1,0:T(8,128)(2,1)S(1)} %collective-permute-done.4.refs_3_.refs_4_), channel_id=1, source_target_pairs={{0,2},{2,0},{4,6},{6,4},{8,10},{10,8},{12,14},{14,12},{1,3},{3,1},... | collective-permute-start | bytes 196616 | tf_op jit(solution)/shard_map/ppermute | solution.py:485
  19.0 0.0 collective-permute-done.1.far_info_ref
  19.0 0.0 collective-permute-done.2.refs_0_.refs_1_
  19.0 2.4 %far_tables.1 = (bf16[512,2048]{1,0:T(8,128)(2,1)S(1)}, bf16[512,2048]{1,0:T(8,128)(2,1)S(1)}, f32[2,32,2048]{2,1,0:T(8,128)S(1)}, f32[2,32,2048]{2,1,0:T(8,128)...) custom-call(f32[2,24,256]{2,1,0:T(8,128)S(1)} %get-tuple-element.22.info_ref, ...), custom_call_target="tpu_custom_call" | custom-call | flops 3000000000 | bytes 30000000 | tf_op jit(solution)/shard_map/far_tables/pallas_call | solution.py:541
  21.4 0.0 collective-permute-done.5.refs_5_
  21.4 0.5 %collective-permute-done.6.refs_6_ = bf16[32,1024]{1,0:T(8,128)(2,1)S(1)} collective-permute-done((bf16[32,1024]{1,0:T(8,128)(2,1)S(1)}, bf16[32,1024]{1,0:T(8,128)(2,1)S(1)}, u32[]{:S(2)}, u32[]{:S(2)}) %collective-permute-start.6) | collective-permute-done | bytes 65568 | tf_op jit(solution)/shard_map/ppermute | solution.py:485
  21.8 0.7 %collective-permute-done.7.refs_7_ = bf16[32,1024]{1,0:T(8,128)(2,1)S(1)} collective-permute-done((bf16[32,1024]{1,0:T(8,128)(2,1)S(1)}, bf16[32,1024]{1,0:T(8,128)(2,1)S(1)}, u32[]{:S(2)}, u32[]{:S(2)}) %collective-permute-start.7) | collective-permute-done | bytes 65568 | tf_op jit(solution)/shard_map/ppermute | solution.py:485
  22.5 1.2 %focus.1 = (bf16[32,1024]{1,0:T(8,128)(2,1)S(1)}, f32[2]{0:T(128)}) custom-call(bf16[2,512,256]{2,1,0:T(8,128)(2,1)S(1)} %get-tuple-element.23.tall_ref, bf16[2,32,512]{2,1,0:T(8,128)(2,1)S(1)} %get-tuple-element.26.flat_ref, f32[2,256,256]{2,1,0:T(8,128)S(1)} %get-tuple-element.27.spot_ref, f32[2,8,128]{2,1,0:T(8,128)S(1)} %get-tuple-element.28.gain_ref, ...), custom_call_target="tpu_custom_call" | custom-call | flops 100000000 | bytes 1000000 | tf_op jit(solution)/shard_map/focus/pallas_call | solution.py:549
  23.8 0.1 collective-permute-start.8
  23.8 1.4 %gradient_own.1.refs_5_ = f32[32,2048]{1,0:T(8,128)S(1)} custom-call(bf16[32,1024]{1,0:T(8,128)(2,1)S(1)} %get-tuple-element.33.back_ref, bf16[2048,512]{1,0:T(8,128)(2,1)S(1)} %get-tuple-element.37.refs_0_, bf16[2048,512]{1,0:T(8,128)(2,1)S(1)} %get-tuple-element.38.refs_1_, f32[2,32,2048]{2,1,0:T(8,128)S(1)} %get-tuple-element.39.refs_2_, ...), custom_call_target="tpu_custom_call" | custom-call | flops 1000000000 | bytes 10000000 | tf_op jit(solution)/shard_map/gradient_own/pallas_call | solution.py:564
  25.2 0.0 collective-permute-done.8.refs_0_
  25.2 1.6 %gradient_far.1 = f32[32,2048]{1,0:T(8,128)} custom-call(bf16[32,1024]{1,0:T(8,128)(2,1)S(1)} %collective-permute-done.8.refs_0_, bf16[512,2048]{1,0:T(8,128)(2,1)S(1)} %get-tuple-element.34.refs_1_, bf16[512,2048]{1,0:T(8,128)(2,1)S(1)} %get-tuple-element.35.refs_2_, f32[2,32,2048]{2,1,0:T(8,128)S(1)} %get-tuple-element.32.after_ref.refs_3_, ...), custom_call_target="tpu_custom_call" | custom-call | flops 1000000000 | bytes 10000000 | tf_op jit(solution)/shard_map/gradient_far/pallas_call | solution.py:569
Async XLA Ops:
  4.7 8.4 %collective-permute-start = (bf16[32,1024]{1,0:T(8,128)(2,1)S(1)}, bf16[32,1024]{1,0:T(8,128)(2,1)S(1)}, u32[]{:S(2)}, u32[]{:S(2)}) collective-permute-start(bf16[32,1024]{1,0:T(8,128)(2,1)S(1)} %get-tuple-element.24.refs_0_), channel_id=1, source_target_pairs={{0,12},{2,14},{4,8},{6,10},{8,4},{10,6},{12,0},{14,2},{1,13},{3,15... | collective-permute-start | bytes 196616 | tf_op jit(solution)/shard_map/ppermute | solution.py:485
  9.9 5.6 %collective-permute-start.3 = (bf16[32,1024]{1,0:T(8,128)(2,1)S(1)}, bf16[32,1024]{1,0:T(8,128)(2,1)S(1)}, u32[]{:S(2)}, u32[]{:S(2)}) collective-permute-start(bf16[32,1024]{1,0:T(8,128)(2,1)S(1)} %get-tuple-element.24.refs_0_), channel_id=1, source_target_pairs={{0,8},{2,10},{4,12},{6,14},{8,0},{10,2},{12,4},{14,6},{1,9},{3,11}... | collective-permute-start | bytes 196616 | tf_op jit(solution)/shard_map/ppermute | solution.py:485
  9.9 5.6 %collective-permute-start.4 = (bf16[32,1024]{1,0:T(8,128)(2,1)S(1)}, bf16[32,1024]{1,0:T(8,128)(2,1)S(1)}, u32[]{:S(2)}, u32[]{:S(2)}) collective-permute-start(bf16[32,1024]{1,0:T(8,128)(2,1)S(1)} %get-tuple-element.24.refs_0_), channel_id=1, source_target_pairs={{0,4},{2,6},{4,0},{6,2},{8,12},{10,14},{12,8},{14,10},{1,5},{3,7},... | collective-permute-start | bytes 196616 | tf_op jit(solution)/shard_map/ppermute | solution.py:485
  10.5 8.5 %collective-permute-start.2 = (bf16[32,1024]{1,0:T(8,128)(2,1)S(1)}, bf16[32,1024]{1,0:T(8,128)(2,1)S(1)}, u32[]{:S(2)}, u32[]{:S(2)}) collective-permute-start(bf16[32,1024]{1,0:T(8,128)(2,1)S(1)} %get-tuple-element.24.refs_0_), channel_id=1, source_target_pairs={{0,2},{2,0},{4,6},{6,4},{8,10},{10,8},{12,14},{14,12},{1,3},{3,1},... | collective-permute-start | bytes 196616 | tf_op jit(solution)/shard_map/ppermute | solution.py:485
  12.1 6.9 %collective-permute-start.1 = (f32[2,24,256]{2,1,0:T(8,128)S(1)}, f32[2,24,256]{2,1,0:T(8,128)S(1)}, u32[]{:S(2)}, u32[]{:S(2)}) collective-permute-start(f32[2,24,256]{2,1,0:T(8,128)S(1)} %get-tuple-element.22.info_ref), channel_id=1, source_target_pairs={{0,1},{1,0},{2,3},{3,2},{4,5},{5,4},{6,7},{7,6},{8,9},{9,8},{10,11... | collective-permute-start | bytes 147464 | tf_op jit(solution)/shard_map/ppermute | solution.py:488
  15.5 5.9 %collective-permute-start.5 = (bf16[32,1024]{1,0:T(8,128)(2,1)S(1)}, bf16[32,1024]{1,0:T(8,128)(2,1)S(1)}, u32[]{:S(2)}, u32[]{:S(2)}) collective-permute-start(bf16[32,1024]{1,0:T(8,128)(2,1)S(1)} %collective-permute-done.refs_1_.refs_2_), channel_id=1, source_target_pairs={{0,2},{2,0},{4,6},{6,4},{8,10},{10,8},{12,14},{14,12},{1,3},{3,1},... | collective-permute-start | bytes 196616 | tf_op jit(solution)/shard_map/ppermute | solution.py:485
  17.0 4.9 %collective-permute-start.6 = (bf16[32,1024]{1,0:T(8,128)(2,1)S(1)}, bf16[32,1024]{1,0:T(8,128)(2,1)S(1)}, u32[]{:S(2)}, u32[]{:S(2)}) collective-permute-start(bf16[32,1024]{1,0:T(8,128)(2,1)S(1)} %collective-permute-done.3.refs_2_.refs_3_), channel_id=1, source_target_pairs={{0,2},{2,0},{4,6},{6,4},{8,10},{10,8},{12,14},{14,12},{1,3},{3,1},... | collective-permute-start | bytes 196616 | tf_op jit(solution)/shard_map/ppermute | solution.py:485
  17.5 5.0 %collective-permute-start.7 = (bf16[32,1024]{1,0:T(8,128)(2,1)S(1)}, bf16[32,1024]{1,0:T(8,128)(2,1)S(1)}, u32[]{:S(2)}, u32[]{:S(2)}) collective-permute-start(bf16[32,1024]{1,0:T(8,128)(2,1)S(1)} %collective-permute-done.4.refs_3_.refs_4_), channel_id=1, source_target_pairs={{0,2},{2,0},{4,6},{6,4},{8,10},{10,8},{12,14},{14,12},{1,3},{3,1},... | collective-permute-start | bytes 196616 | tf_op jit(solution)/shard_map/ppermute | solution.py:485
  23.8 1.5 %collective-permute-start.8 = (bf16[32,1024]{1,0:T(8,128)(2,1)S(1)}, bf16[32,1024]{1,0:T(8,128)(2,1)S(1)}, u32[]{:S(2)}, u32[]{:S(2)}) collective-permute-start(bf16[32,1024]{1,0:T(8,128)(2,1)S(1)} %get-tuple-element.33.back_ref), channel_id=1, source_target_pairs={{0,1},{1,0},{2,3},{3,2},{4,5},{5,4},{6,7},{7,6},{8,9},{9,8},{10,11... | collective-permute-start | bytes 196616 | tf_op jit(solution)/shard_map/ppermute | solution.py:488

commit v12 on v10

--- a/solution.py
+++ b/solution.py
@@ -19,7 +19,7 @@
 PIECE = 16
 VMEM_LIMIT = 16 * 1024 * 1024
 WAVE_ROW, ANGLE_ROW, AIM_ROW, INFO_ROWS = 16, 17, 18, 24
-DIRECT = 16
+CUBE = 8
 
 COS = (
     1.0, -19.7392088015709, 64.93939395773512, -85.45681453397417, 60.24458621302471,
@@ -329,16 +329,17 @@
         score_ref[pair] = jnp.sum(ratio * gain)
         scale = gain * 2.0 / all_power
         for rows in pieces:
+            lower = slice(rows.start + FOCAL, rows.stop + FOCAL)
             weight = scale * (spot_ref[pair, rows, :] - ratio)
-            stack_ref[pair, rows, :FOCAL] = (weight * field_ref[pair, 0, rows, :]).astype(jnp.bfloat16)
-            stack_ref[pair, rows, FOCAL:] = (weight * field_ref[pair, 1, rows, :]).astype(jnp.bfloat16)
-        flat = jnp.concatenate([flat_ref[pair, :, :FOCAL], flat_ref[pair, :, FOCAL:]], axis=0)
-        back = jnp.dot(flat, stack_ref[pair], preferred_element_type=jnp.float32)
-        real = back[:rows_dev, :FOCAL] + back[rows_dev:, FOCAL:]
-        imag = back[:rows_dev, FOCAL:] - back[rows_dev:, :FOCAL]
+            real = (weight * field_ref[pair, 0, rows, :]).astype(jnp.bfloat16)
+            imag = (weight * field_ref[pair, 1, rows, :]).astype(jnp.bfloat16)
+            stack_ref[pair, rows, :FOCAL] = real
+            stack_ref[pair, rows, FOCAL:] = imag
+            stack_ref[pair, lower, :FOCAL] = imag
+            stack_ref[pair, lower, FOCAL:] = -real
+        back = jnp.dot(flat_ref[pair], stack_ref[pair], preferred_element_type=jnp.float32)
         lane = 2 * pair * FOCAL
-        back_ref[:, lane : lane + FOCAL] = real.astype(jnp.bfloat16)
-        back_ref[:, lane + FOCAL : lane + 2 * FOCAL] = imag.astype(jnp.bfloat16)
+        back_ref[:, lane : lane + 2 * FOCAL] = back.astype(jnp.bfloat16)
 
 
 def table_kernel(scale, cols, info_ref, far_info_ref, width_ref, *refs):
@@ -507,16 +508,18 @@
         ),
         [VMEM], (VMEM,) * 4, [], 10**8, 10**6,
     )(info)
-    if peers <= DIRECT:
-        steps = list(range(peers - 2, 0, -2))
-        got = [exchange(mine, step) for step in steps]
+    if peers == CUBE:
+        across = exchange(mine, 4)
+        beside = exchange(mine, 2)
         near = exchange(mine, 1)
-        first, flat = lax.optimization_barrier((got[0], flat))
-        joined = call(join_kernel, "join", shape(((len(steps) - 1) * rows_dev, lanes), bf16),
-                      [VMEM] * (len(steps) - 1), VMEM, [], 10**6, 10**6)(*got[1:])
-        sections = [mine, near, first, joined, exchange(first, 1), exchange(joined, 1)]
-        steps = [0, 1, *steps, *(step ^ 1 for step in steps)]
-        after = [near, joined]
+        across, flat = lax.optimization_barrier((across, flat))
+        relayed = exchange(across, 2)
+        joined = call(
+            join_kernel, "join", shape((2 * rows_dev, lanes), bf16), [VMEM] * 2, VMEM, [], 10**6, 10**6
+        )(across, beside)
+        sections = [mine, near, joined, relayed, exchange(joined, 1), exchange(relayed, 1)]
+        steps = [0, 1, 4, 2, 6, 5, 3, 7]
+        after = [near, joined, relayed]
     else:
         blocks = jnp.tile(mine[None], (peers, 1, 1))
         blocks = lax.all_to_all(blocks, "aperture", 0, 0, tiled=True)
@@ -538,7 +541,7 @@
             pltpu.VMEM((rows, lanes), bf16),
             pltpu.VMEM((pairs_dev, 2 * FOCAL, 2 * FOCAL), f32),
             pltpu.VMEM((pairs_dev, 2, FOCAL, FOCAL), f32),
-            pltpu.VMEM((pairs_dev, FOCAL, 2 * FOCAL), bf16),
+            pltpu.VMEM((pairs_dev, 2 * FOCAL, 2 * FOCAL), bf16),
         ],
         10**8, 10**6,
     )(tall, flat, spots, gains, far_slopes[0], *sections)

time: 25.1 us -> 26.6 us (1.060)
  starting transfers between devices: 10.1 us -> 11.1 us
  waiting for transfers between devices: 2.37 us -> 2.99 us
    ppermute x6, starting transfers between devices: 10 us -> 11 us  [exchange(): lax.ppermute(value, 'aperture', [(index, index ^ step) for index in range...]
    ppermute x6, waiting for transfers between devices: 2.36 us -> 2.98 us  [exchange(): lax.ppermute(value, 'aperture', [(index, index ^ step) for index in range...]
  transfers between devices with their start and end apart: 8 -> 8, of which waited for: 2 -> 4; matrix products, arithmetic and copies ran while one was open for 0% -> 0% of each run, Pallas kernels for 19% -> 18%
where the time goes in v12:
time: 26.6 us; the launch traced here: 26.4 us
  Pallas kernels  11.6 us (44%)
  starting transfers between devices  11.1 us (42%)
  waiting for transfers between devices  2.99 us (11%)
  between operations  0.68 us (3%)
    ppermute x6, starting transfers between devices, exchange(): lax.ppermute(value, 'aperture', [(index, index ^ step) for index in range...  11 us
    pallas_call x1, Pallas kernels, on_device(): call(forward_kernel, 'forward', (shape((rows_dev, lanes), bf16), shape((p...  4.01 us
    ppermute x6, waiting for transfers between devices, exchange(): lax.ppermute(value, 'aperture', [(index, index ^ step) for index in range...  2.98 us
    pallas_call x1, Pallas kernels, on_device(): call(functools.partial(table_kernel, math.sqrt(rows * cols), cols), 'far_...  2.37 us
    pallas_call x1, Pallas kernels, on_device(): call(functools.partial(last_grad_kernel, pairs_dev), 'gradient_far', out,...  1.61 us
    pallas_call x1, Pallas kernels, on_device(): call(functools.partial(grad_kernel, pairs_dev, across=False), 'gradient_o...  1.38 us
    pallas_call x1, Pallas kernels, on_device(): call(functools.partial(focus_kernel, steps), 'focus', (shape((rows_dev, l...  1.21 us
    pallas_call x1, Pallas kernels, on_device(): call(row_kernel, 'row_tables', (shape((pairs_dev, 2 * FOCAL, rows), bf16)...  1.04 us
  transfers between devices with their start and end apart: 8, of which 4 were waited for; matrix products, arithmetic and copies ran while one was open for 0% of the time, Pallas kernels for 18%

profile of v12, /device:TPU:0, one launch (start us, length us, event | category | flops | bytes accessed | tf_op | source)
XLA Modules:
  0.0 26.4 jit_solution(3972223131781553975)
XLA Ops:
  0.6 4.0 %forward.1 = (bf16[32,1024]{1,0:T(8,128)(2,1)S(1)}, f32[2,24,256]{2,1,0:T(8,128)S(1)}, f32[32,2048]{1,0:T(8,128)S(1)}, bf16[2048,512]{1,0:T(8,128)(2,1)S(1)}, bf16[2048,512]{1,0:T(8,128)(2,1)S(1)}) custom-call(s32[2]{0:T(128)} %wave_hbm.1, s32[2]{0:T(128)} %angle_hbm.1, s32[2,2]{1,0:T(2,128)} %aim_hbm.1, f32[16,256]{1,0:T(8,128)} %bitcast.1, ...), custom_call_target="tpu_custom_call" | custom-call | flops 1000000000 | bytes 10000000 | tf_op jit(solution)/shard_map/forward/pallas_call | solution.py:478
  4.7 4.1 %collective-permute-start = (bf16[32,1024]{1,0:T(8,128)(2,1)S(1)}, bf16[32,1024]{1,0:T(8,128)(2,1)S(1)}, u32[]{:S(2)}, u32[]{:S(2)}) collective-permute-start(bf16[32,1024]{1,0:T(8,128)(2,1)S(1)} %get-tuple-element.23.refs_0_), channel_id=1, source_target_pairs={{0,8},{2,10},{4,12},{6,14},{8,0},{10,2},{12,4},{14,6},{1,9},{3,11}... | collective-permute-start | bytes 196616 | tf_op jit(solution)/shard_map/ppermute | solution.py:469
  8.8 1.6 %collective-permute-start.3 = (bf16[32,1024]{1,0:T(8,128)(2,1)S(1)}, bf16[32,1024]{1,0:T(8,128)(2,1)S(1)}, u32[]{:S(2)}, u32[]{:S(2)}) collective-permute-start(bf16[32,1024]{1,0:T(8,128)(2,1)S(1)} %get-tuple-element.23.refs_0_), channel_id=1, source_target_pairs={{0,4},{2,6},{4,0},{6,2},{8,12},{10,14},{12,8},{14,10},{1,5},{3,7},... | collective-permute-start | bytes 196616 | tf_op jit(solution)/shard_map/ppermute | solution.py:469
  10.3 1.0 %row_tables.1 = (bf16[2,512,256]{2,1,0:T(8,128)(2,1)S(1)}, bf16[2,32,512]{2,1,0:T(8,128)(2,1)S(1)}, f32[2,256,256]{2,1,0:T(8,128)S(1)}, f32[2,8,128]{2,1,0:T(8,128)S(1)}) custom-call(f32[2,24,256]{2,1,0:T(8,128)S(1)} %get-tuple-element.21.info_ref), custom_call_target="tpu_custom_call" | custom-call | flops 100000000 | bytes 1000000 | tf_op jit(solution)/shard_map/row_tables/pallas_call | solution.py:503
  11.4 0.4 %collective-permute-done.refs_0_ = bf16[32,1024]{1,0:T(8,128)(2,1)S(1)} collective-permute-done((bf16[32,1024]{1,0:T(8,128)(2,1)S(1)}, bf16[32,1024]{1,0:T(8,128)(2,1)S(1)}, u32[]{:S(2)}, u32[]{:S(2)}) %collective-permute-start) | collective-permute-done | bytes 65568 | tf_op jit(solution)/shard_map/ppermute | solution.py:469
  11.8 1.4 %collective-permute-start.4 = (bf16[32,1024]{1,0:T(8,128)(2,1)S(1)}, bf16[32,1024]{1,0:T(8,128)(2,1)S(1)}, u32[]{:S(2)}, u32[]{:S(2)}) collective-permute-start(bf16[32,1024]{1,0:T(8,128)(2,1)S(1)} %collective-permute-done.refs_0_), channel_id=1, source_target_pairs={{0,4},{2,6},{4,0},{6,2},{8,12},{10,14},{12,8},{14,10},{1,5},{3,7},... | collective-permute-start | bytes 196616 | tf_op jit(solution)/shard_map/ppermute | solution.py:469
  13.2 1.5 %collective-permute-start.2 = (bf16[32,1024]{1,0:T(8,128)(2,1)S(1)}, bf16[32,1024]{1,0:T(8,128)(2,1)S(1)}, u32[]{:S(2)}, u32[]{:S(2)}) collective-permute-start(bf16[32,1024]{1,0:T(8,128)(2,1)S(1)} %get-tuple-element.23.refs_0_), channel_id=1, source_target_pairs={{0,2},{2,0},{4,6},{6,4},{8,10},{10,8},{12,14},{14,12},{1,3},{3,1},... | collective-permute-start | bytes 196616 | tf_op jit(solution)/shard_map/ppermute | solution.py:469
  14.7 0.0 collective-permute-start.1
  14.7 0.0 collective-permute-done.3.refs_1_
  14.7 0.6 %collective-permute-start.5 = (bf16[64,1024]{1,0:T(8,128)(2,1)S(1)}, bf16[64,1024]{1,0:T(8,128)(2,1)S(1)}, u32[]{:S(2)}, u32[]{:S(2)}) collective-permute-start(bf16[64,1024]{1,0:T(8,128)(2,1)S(1)} %join.1.refs_1_.refs_2_), channel_id=1, source_target_pairs={{0,2},{2,0},{4,6},{6,4},{8,10},{10,8},{12,14},{14,12},{1,3},{3,1},... | collective-permute-start | bytes 393224 | tf_op jit(solution)/shard_map/ppermute | solution.py:469
  15.3 0.8 %collective-permute-done.4.refs_2_.refs_3_ = bf16[32,1024]{1,0:T(8,128)(2,1)S(1)} collective-permute-done((bf16[32,1024]{1,0:T(8,128)(2,1)S(1)}, bf16[32,1024]{1,0:T(8,128)(2,1)S(1)}, u32[]{:S(2)}, u32[]{:S(2)}) %collective-permute-start.4) | collective-permute-done | bytes 65568 | tf_op jit(solution)/shard_map/ppermute | solution.py:469
  16.1 1.8 %collective-permute-start.6 = (bf16[32,1024]{1,0:T(8,128)(2,1)S(1)}, bf16[32,1024]{1,0:T(8,128)(2,1)S(1)}, u32[]{:S(2)}, u32[]{:S(2)}) collective-permute-start(bf16[32,1024]{1,0:T(8,128)(2,1)S(1)} %collective-permute-done.4.refs_2_.refs_3_), channel_id=1, source_target_pairs={{0,2},{2,0},{4,6},{6,4},{8,10},{10,8},{12,14},{14,12},{1,3},{3,1},... | collective-permute-start | bytes 196616 | tf_op jit(solution)/shard_map/ppermute | solution.py:469
  17.9 0.0 collective-permute-done.1.far_info_ref
  17.9 0.0 collective-permute-done.2.refs_0_.refs_1_
  17.9 2.4 %far_tables.1 = (bf16[512,2048]{1,0:T(8,128)(2,1)S(1)}, bf16[512,2048]{1,0:T(8,128)(2,1)S(1)}, f32[2,32,2048]{2,1,0:T(8,128)S(1)}, f32[2,32,2048]{2,1,0:T(8,128)...) custom-call(f32[2,24,256]{2,1,0:T(8,128)S(1)} %get-tuple-element.21.info_ref, ...), custom_call_target="tpu_custom_call" | custom-call | flops 3000000000 | bytes 30000000 | tf_op jit(solution)/shard_map/far_tables/pallas_call | solution.py:528
  20.3 0.7 %collective-permute-done.5.refs_4_ = bf16[64,1024]{1,0:T(8,128)(2,1)S(1)} collective-permute-done((bf16[64,1024]{1,0:T(8,128)(2,1)S(1)}, bf16[64,1024]{1,0:T(8,128)(2,1)S(1)}, u32[]{:S(2)}, u32[]{:S(2)}) %collective-permute-start.5) | collective-permute-done | bytes 131104 | tf_op jit(solution)/shard_map/ppermute | solution.py:469
  21.0 1.0 %collective-permute-done.6.refs_5_ = bf16[32,1024]{1,0:T(8,128)(2,1)S(1)} collective-permute-done((bf16[32,1024]{1,0:T(8,128)(2,1)S(1)}, bf16[32,1024]{1,0:T(8,128)(2,1)S(1)}, u32[]{:S(2)}, u32[]{:S(2)}) %collective-permute-start.6) | collective-permute-done | bytes 65568 | tf_op jit(solution)/shard_map/ppermute | solution.py:469
  22.1 1.2 %focus.1 = (bf16[32,1024]{1,0:T(8,128)(2,1)S(1)}, f32[2]{0:T(128)}) custom-call(bf16[2,512,256]{2,1,0:T(8,128)(2,1)S(1)} %get-tuple-element.22.tall_ref, bf16[2,32,512]{2,1,0:T(8,128)(2,1)S(1)} %get-tuple-element.25.flat_ref, f32[2,256,256]{2,1,0:T(8,128)S(1)} %get-tuple-element.26.spot_ref, f32[2,8,128]{2,1,0:T(8,128)S(1)} %get-tuple-element.27.gain_ref, ...), custom_call_target="tpu_custom_call" | custom-call | flops 100000000 | bytes 1000000 | tf_op jit(solution)/shard_map/focus/pallas_call | solution.py:536
  23.3 0.1 collective-permute-start.7
  23.4 1.4 %gradient_own.1.refs_5_ = f32[32,2048]{1,0:T(8,128)S(1)} custom-call(bf16[32,1024]{1,0:T(8,128)(2,1)S(1)} %get-tuple-element.31.back_ref, bf16[2048,512]{1,0:T(8,128)(2,1)S(1)} %get-tuple-element.35.refs_0_, bf16[2048,512]{1,0:T(8,128)(2,1)S(1)} %get-tuple-element.36.refs_1_, f32[2,32,2048]{2,1,0:T(8,128)S(1)} %get-tuple-element.37.refs_2_, ...), custom_call_target="tpu_custom_call" | custom-call | flops 1000000000 | bytes 10000000 | tf_op jit(solution)/shard_map/gradient_own/pallas_call | solution.py:551
  24.7 0.0 collective-permute-done.7.refs_0_
  24.8 1.6 %gradient_far.1 = f32[32,2048]{1,0:T(8,128)} custom-call(bf16[32,1024]{1,0:T(8,128)(2,1)S(1)} %collective-permute-done.7.refs_0_, bf16[512,2048]{1,0:T(8,128)(2,1)S(1)} %get-tuple-element.32.refs_1_, bf16[512,2048]{1,0:T(8,128)(2,1)S(1)} %get-tuple-element.33.refs_2_, f32[2,32,2048]{2,1,0:T(8,128)S(1)} %get-tuple-element.30.after_ref.refs_3_, ...), custom_call_target="tpu_custom_call" | custom-call | flops 1000000000 | bytes 10000000 | tf_op jit(solution)/shard_map/gradient_far/pallas_call | solution.py:556
  (1 shorter events, 0.0 us)
Async XLA Ops:
  4.7 7.2 %collective-permute-start = (bf16[32,1024]{1,0:T(8,128)(2,1)S(1)}, bf16[32,1024]{1,0:T(8,128)(2,1)S(1)}, u32[]{:S(2)}, u32[]{:S(2)}) collective-permute-start(bf16[32,1024]{1,0:T(8,128)(2,1)S(1)} %get-tuple-element.23.refs_0_), channel_id=1, source_target_pairs={{0,8},{2,10},{4,12},{6,14},{8,0},{10,2},{12,4},{14,6},{1,9},{3,11}... | collective-permute-start | bytes 196616 | tf_op jit(solution)/shard_map/ppermute | solution.py:469
  8.8 5.9 %collective-permute-start.3 = (bf16[32,1024]{1,0:T(8,128)(2,1)S(1)}, bf16[32,1024]{1,0:T(8,128)(2,1)S(1)}, u32[]{:S(2)}, u32[]{:S(2)}) collective-permute-start(bf16[32,1024]{1,0:T(8,128)(2,1)S(1)} %get-tuple-element.23.refs_0_), channel_id=1, source_target_pairs={{0,4},{2,6},{4,0},{6,2},{8,12},{10,14},{12,8},{14,10},{1,5},{3,7},... | collective-permute-start | bytes 196616 | tf_op jit(solution)/shard_map/ppermute | solution.py:469
  11.8 4.3 %collective-permute-start.4 = (bf16[32,1024]{1,0:T(8,128)(2,1)S(1)}, bf16[32,1024]{1,0:T(8,128)(2,1)S(1)}, u32[]{:S(2)}, u32[]{:S(2)}) collective-permute-start(bf16[32,1024]{1,0:T(8,128)(2,1)S(1)} %collective-permute-done.refs_0_), channel_id=1, source_target_pairs={{0,4},{2,6},{4,0},{6,2},{8,12},{10,14},{12,8},{14,10},{1,5},{3,7},... | collective-permute-start | bytes 196616 | tf_op jit(solution)/shard_map/ppermute | solution.py:469
  13.2 4.8 %collective-permute-start.2 = (bf16[32,1024]{1,0:T(8,128)(2,1)S(1)}, bf16[32,1024]{1,0:T(8,128)(2,1)S(1)}, u32[]{:S(2)}, u32[]{:S(2)}) collective-permute-start(bf16[32,1024]{1,0:T(8,128)(2,1)S(1)} %get-tuple-element.23.refs_0_), channel_id=1, source_target_pairs={{0,2},{2,0},{4,6},{6,4},{8,10},{10,8},{12,14},{14,12},{1,3},{3,1},... | collective-permute-start | bytes 196616 | tf_op jit(solution)/shard_map/ppermute | solution.py:469
  14.7 3.3 %collective-permute-start.1 = (f32[2,24,256]{2,1,0:T(8,128)S(1)}, f32[2,24,256]{2,1,0:T(8,128)S(1)}, u32[]{:S(2)}, u32[]{:S(2)}) collective-permute-start(f32[2,24,256]{2,1,0:T(8,128)S(1)} %get-tuple-element.21.info_ref), channel_id=1, source_target_pairs={{0,1},{1,0},{2,3},{3,2},{4,5},{5,4},{6,7},{7,6},{8,9},{9,8},{10,11... | collective-permute-start | bytes 147464 | tf_op jit(solution)/shard_map/ppermute | solution.py:472
  14.7 6.4 %collective-permute-start.5 = (bf16[64,1024]{1,0:T(8,128)(2,1)S(1)}, bf16[64,1024]{1,0:T(8,128)(2,1)S(1)}, u32[]{:S(2)}, u32[]{:S(2)}) collective-permute-start(bf16[64,1024]{1,0:T(8,128)(2,1)S(1)} %join.1.refs_1_.refs_2_), channel_id=1, source_target_pairs={{0,2},{2,0},{4,6},{6,4},{8,10},{10,8},{12,14},{14,12},{1,3},{3,1},... | collective-permute-start | bytes 393224 | tf_op jit(solution)/shard_map/ppermute | solution.py:469
  16.1 6.0 %collective-permute-start.6 = (bf16[32,1024]{1,0:T(8,128)(2,1)S(1)}, bf16[32,1024]{1,0:T(8,128)(2,1)S(1)}, u32[]{:S(2)}, u32[]{:S(2)}) collective-permute-start(bf16[32,1024]{1,0:T(8,128)(2,1)S(1)} %collective-permute-done.4.refs_2_.refs_3_), channel_id=1, source_target_pairs={{0,2},{2,0},{4,6},{6,4},{8,10},{10,8},{12,14},{14,12},{1,3},{3,1},... | collective-permute-start | bytes 196616 | tf_op jit(solution)/shard_map/ppermute | solution.py:469
  23.3 1.5 %collective-permute-start.7 = (bf16[32,1024]{1,0:T(8,128)(2,1)S(1)}, bf16[32,1024]{1,0:T(8,128)(2,1)S(1)}, u32[]{:S(2)}, u32[]{:S(2)}) collective-permute-start(bf16[32,1024]{1,0:T(8,128)(2,1)S(1)} %get-tuple-element.31.back_ref), channel_id=1, source_target_pairs={{0,1},{1,0},{2,3},{3,2},{4,5},{5,4},{6,7},{7,6},{8,9},{9,8},{10,11... | collective-permute-start | bytes 196616 | tf_op jit(solution)/shard_map/ppermute | solution.py:472

commit v13 on v10

--- a/solution.py
+++ b/solution.py
@@ -17,6 +17,7 @@
 GRAIN = 16
 LANES = 128
 PIECE = 16
+SUBLANES = 8
 VMEM_LIMIT = 16 * 1024 * 1024
 WAVE_ROW, ANGLE_ROW, AIM_ROW, INFO_ROWS = 16, 17, 18, 24
 DIRECT = 16
@@ -95,30 +96,43 @@
     return jnp.concatenate(rows, axis=0)
 
 
+def as_tiles(rows):
+    return jnp.broadcast_to(rows[:, None, :], (rows.shape[0], SUBLANES, rows.shape[1]))
+
+
+def split_rows(value):
+    return value.reshape(value.shape[0] // SUBLANES, SUBLANES, value.shape[1])
+
+
+def join_rows(value):
+    return value.reshape(value.shape[0] * SUBLANES, value.shape[2])
+
+
 def near_fields(s, power_ref, pairs):
+    s = split_rows(s)
     outs = []
     for pair, part in itertools.product(range(pairs), range(2)):
         row = (part + 1) * TERMS - 1
-        value = power_ref[pair, row : row + 1, :] * s + power_ref[pair, row - 1 : row, :]
+        value = power_ref[pair, row] * s + power_ref[pair, row - 1]
         for row in range(row - 2, part * TERMS - 1, -1):
-            value = value * s + power_ref[pair, row : row + 1, :]
-        outs.append(value)
+            value = value * s + power_ref[pair, row]
+        outs.append(join_rows(value))
     return [outs[2 * pair : 2 * pair + 2] for pair in range(pairs)]
 
 
 def near_slopes(s, coef_ref, pairs):
-    def coef(pair, row):
-        return coef_ref[pair, row : row + 1, :]
-
+    s = split_rows(s)
     twice = s + s
     before, current = jnp.ones_like(s), twice
-    outs = [[coef(p, k) + coef(p, k + 1) * twice for k in (1, TERMS + 1)] for p in range(pairs)]
+    outs = [
+        [coef_ref[pair, row] + coef_ref[pair, row + 1] * twice for row in (1, TERMS + 1)] for pair in range(pairs)
+    ]
     for order in range(3, TERMS):
         before, current = current, twice * current - before
         for pair, out in enumerate(outs):
-            out[0] = out[0] + coef(pair, order) * current
-            out[1] = out[1] + coef(pair, TERMS + order) * current
-    return outs
+            out[0] = out[0] + coef_ref[pair, order] * current
+            out[1] = out[1] + coef_ref[pair, TERMS + order] * current
+    return [[join_rows(part) for part in out] for out in outs]
 
 
 def turn_round(value):
@@ -172,7 +186,7 @@
         coef = pick_coef(coef_ref[...], wave_ref[pair])
         coef = jnp.broadcast_to(coef, (WAVE_ROW, FOCAL))
         info_ref[pair, :WAVE_ROW, :] = coef
-        power_ref[pair] = power_coefs(coef[:, :LANES])
+        power_ref[pair] = as_tiles(power_coefs(coef[:, :LANES]))
         row = iota((INFO_ROWS - WAVE_ROW, FOCAL), 0) + WAVE_ROW
         ids = jnp.where(row == WAVE_ROW, wave_ref[pair], 0)
         ids = jnp.where(row == ANGLE_ROW, angle_ref[pair], ids)
@@ -186,6 +200,9 @@
     own_ref[...] = jnp.where(core == 1, right, left)
     far_ref[...] = jnp.where(core == 1, pltpu.roll(left, 1, 1), pltpu.roll(right, half - 1, 1))
 
+    alone = jnp.where(core == 1, 0, half)
+    column = width_ref[:, pl.ds(pl.multiple_of(alone, LANES), LANES)]
+    columns = near_fields(column, power_ref, pairs)
     void = jnp.where(core == 1, 0, half - 1)
     for index in range(half // (2 * BLOCK)):
         starts = block_starts(half, index)
@@ -212,9 +229,6 @@
                 preferred_element_type=jnp.float32,
             )
             acc_ref[pair] = product if index == 0 else acc_ref[pair] + product
-    alone = jnp.where(core == 1, 0, half)
-    column = width_ref[:, pl.ds(pl.multiple_of(alone, LANES), LANES)]
-    columns = near_fields(column, power_ref, pairs)
     for pair in range(pairs):
         acc = [acc_ref[pair, part * rows_dev : (part + 1) * rows_dev, :] for part in range(4)]
         (own_rr, own_ri), (own_ir, own_ii), (far_rr, far_ri), (far_ir, far_ii) = (
@@ -329,16 +343,17 @@
         score_ref[pair] = jnp.sum(ratio * gain)
         scale = gain * 2.0 / all_power
         for rows in pieces:
+            lower = slice(rows.start + FOCAL, rows.stop + FOCAL)
             weight = scale * (spot_ref[pair, rows, :] - ratio)
-            stack_ref[pair, rows, :FOCAL] = (weight * field_ref[pair, 0, rows, :]).astype(jnp.bfloat16)
-            stack_ref[pair, rows, FOCAL:] = (weight * field_ref[pair, 1, rows, :]).astype(jnp.bfloat16)
-        flat = jnp.concatenate([flat_ref[pair, :, :FOCAL], flat_ref[pair, :, FOCAL:]], axis=0)
-        back = jnp.dot(flat, stack_ref[pair], preferred_element_type=jnp.float32)
-        real = back[:rows_dev, :FOCAL] + back[rows_dev:, FOCAL:]
-        imag = back[:rows_dev, FOCAL:] - back[rows_dev:, :FOCAL]
+            real = (weight * field_ref[pair, 0, rows, :]).astype(jnp.bfloat16)
+            imag = (weight * field_ref[pair, 1, rows, :]).astype(jnp.bfloat16)
+            stack_ref[pair, rows, :FOCAL] = real
+            stack_ref[pair, rows, FOCAL:] = imag
+            stack_ref[pair, lower, :FOCAL] = imag
+            stack_ref[pair, lower, FOCAL:] = -real
+        back = jnp.dot(flat_ref[pair], stack_ref[pair], preferred_element_type=jnp.float32)
         lane = 2 * pair * FOCAL
-        back_ref[:, lane : lane + FOCAL] = real.astype(jnp.bfloat16)
-        back_ref[:, lane + FOCAL : lane + 2 * FOCAL] = imag.astype(jnp.bfloat16)
+        back_ref[:, lane : lane + 2 * FOCAL] = back.astype(jnp.bfloat16)
 
 
 def table_kernel(scale, cols, info_ref, far_info_ref, width_ref, *refs):
@@ -350,7 +365,8 @@
     for core, ref in enumerate((info_ref, far_info_ref)):
         for pair in range(pairs):
             coef = ref[pair, : 2 * TERMS, :LANES]
-            coef_ref[core * pairs + pair] = coef * ((iota(coef.shape, 0) % TERMS).astype(jnp.float32) * scale)
+            coef = coef * ((iota(coef.shape, 0) % TERMS).astype(jnp.float32) * scale)
+            coef_ref[core * pairs + pair] = as_tiles(coef)
     centres = []
     for pair in range(pairs):
         own_waves(far_info_ref, pair, cols, base_ref.at[pair], centre_ref.at[pair])
@@ -490,7 +506,7 @@
             pltpu.VMEM(widths.shape, f32),
             pltpu.VMEM((rows_dev, own_cols), f32),
             *waves,
-            pltpu.VMEM((pairs_dev, 2 * TERMS, LANES), f32),
+            pltpu.VMEM((pairs_dev, 2 * TERMS, SUBLANES, LANES), f32),
             pltpu.VMEM((pairs_dev, 4 * rows_dev, own_cols), bf16),
             pltpu.VMEM((pairs_dev, 4 * rows_dev, 2 * FOCAL), f32),
             pltpu.SemaphoreType.DMA((5,)),
@@ -525,7 +541,7 @@
     made = call(
         functools.partial(table_kernel, math.sqrt(rows * cols), cols), "far_tables",
         outs, [VMEM] * 3 + [ANY] * len(after), [VMEM] * len(outs),
-        [*waves, pltpu.VMEM((pairs_dev, 2, FOCAL, BLOCK), f32), pltpu.VMEM((copies * pairs_dev, 2 * TERMS, LANES), f32)],
+        [*waves, pltpu.VMEM((pairs_dev, 2, FOCAL, BLOCK), f32), pltpu.VMEM((copies * pairs_dev, 2 * TERMS, SUBLANES, LANES), f32)],
         30 * 10**8, 30 * 10**6,
     )(info, far_info, own, *after)
     far_tables, slopes, far_slopes = made[:pairs_dev], made[pairs_dev : 2 * pairs_dev], made[2 * pairs_dev :]
@@ -538,7 +554,7 @@
             pltpu.VMEM((rows, lanes), bf16),
             pltpu.VMEM((pairs_dev, 2 * FOCAL, 2 * FOCAL), f32),
             pltpu.VMEM((pairs_dev, 2, FOCAL, FOCAL), f32),
-            pltpu.VMEM((pairs_dev, FOCAL, 2 * FOCAL), bf16),
+            pltpu.VMEM((pairs_dev, 2 * FOCAL, 2 * FOCAL), bf16),
         ],
         10**8, 10**6,
     )(tall, flat, spots, gains, far_slopes[0], *sections)

time: 25.1 us -> 25 us (level)
  no operation moved by 1% of the time
where the time goes in v13:
time: 25 us; the launch traced here: 24.8 us
  Pallas kernels  11.6 us (46%)
  starting transfers between devices  10.1 us (40%)
  waiting for transfers between devices  2.35 us (9%)
  between operations  0.7 us (3%)
    ppermute x6, starting transfers between devices, exchange(): lax.ppermute(value, 'aperture', [(index, index ^ step) for index in range...  10 us
    pallas_call x1, Pallas kernels, on_device(): call(forward_kernel, 'forward', (shape((rows_dev, lanes), bf16), shape((p...  3.98 us
    pallas_call x1, Pallas kernels, on_device(): call(functools.partial(table_kernel, math.sqrt(rows * cols), cols), 'far_...  2.39 us
    ppermute x6, waiting for transfers between devices, exchange(): lax.ppermute(value, 'aperture', [(index, index ^ step) for index in range...  2.35 us
    pallas_call x1, Pallas kernels, on_device(): call(functools.partial(last_grad_kernel, pairs_dev), 'gradient_far', out,...  1.61 us
    pallas_call x1, Pallas kernels, on_device(): call(functools.partial(grad_kernel, pairs_dev, across=False), 'gradient_o...  1.38 us
    pallas_call x1, Pallas kernels, on_device(): call(functools.partial(focus_kernel, steps), 'focus', (shape((rows_dev, l...  1.21 us
    pallas_call x1, Pallas kernels, on_device(): call(row_kernel, 'row_tables', (shape((pairs_dev, 2 * FOCAL, rows), bf16)...  1.04 us
  transfers between devices with their start and end apart: 8, of which 2 were waited for; matrix products, arithmetic and copies ran while one was open for 0% of the time, Pallas kernels for 19%

profile of v13, /device:TPU:0, one launch (start us, length us, event | category | flops | bytes accessed | tf_op | source)
XLA Modules:
  0.0 24.8 jit_solution(709589872347578809)
XLA Ops:
  0.6 4.0 %forward.1 = (bf16[32,1024]{1,0:T(8,128)(2,1)S(1)}, f32[2,24,256]{2,1,0:T(8,128)S(1)}, f32[32,2048]{1,0:T(8,128)S(1)}, bf16[2048,512]{1,0:T(8,128)(2,1)S(1)}, bf16[2048,512]{1,0:T(8,128)(2,1)S(1)}) custom-call(s32[2]{0:T(128)} %wave_hbm.1, s32[2]{0:T(128)} %angle_hbm.1, s32[2,2]{1,0:T(2,128)} %aim_hbm.1, f32[16,256]{1,0:T(8,128)} %bitcast.1, ...), custom_call_target="tpu_custom_call" | custom-call | flops 1000000000 | bytes 10000000 | tf_op jit(solution)/shard_map/forward/pallas_call | solution.py:493
  4.6 5.1 %collective-permute-start = (bf16[32,1024]{1,0:T(8,128)(2,1)S(1)}, bf16[32,1024]{1,0:T(8,128)(2,1)S(1)}, u32[]{:S(2)}, u32[]{:S(2)}) collective-permute-start(bf16[32,1024]{1,0:T(8,128)(2,1)S(1)} %get-tuple-element.23.refs_0_), channel_id=1, source_target_pairs={{0,12},{2,14},{4,8},{6,10},{8,4},{10,6},{12,0},{14,2},{1,13},{3,15... | collective-permute-start | bytes 196616 | tf_op jit(solution)/shard_map/ppermute | solution.py:484
  9.7 0.0 collective-permute-start.3
  9.7 0.6 %collective-permute-start.4 = (bf16[32,1024]{1,0:T(8,128)(2,1)S(1)}, bf16[32,1024]{1,0:T(8,128)(2,1)S(1)}, u32[]{:S(2)}, u32[]{:S(2)}) collective-permute-start(bf16[32,1024]{1,0:T(8,128)(2,1)S(1)} %get-tuple-element.23.refs_0_), channel_id=1, source_target_pairs={{0,4},{2,6},{4,0},{6,2},{8,12},{10,14},{12,8},{14,10},{1,5},{3,7},... | collective-permute-start | bytes 196616 | tf_op jit(solution)/shard_map/ppermute | solution.py:484
  10.4 1.6 %collective-permute-start.2 = (bf16[32,1024]{1,0:T(8,128)(2,1)S(1)}, bf16[32,1024]{1,0:T(8,128)(2,1)S(1)}, u32[]{:S(2)}, u32[]{:S(2)}) collective-permute-start(bf16[32,1024]{1,0:T(8,128)(2,1)S(1)} %get-tuple-element.23.refs_0_), channel_id=1, source_target_pairs={{0,2},{2,0},{4,6},{6,4},{8,10},{10,8},{12,14},{14,12},{1,3},{3,1},... | collective-permute-start | bytes 196616 | tf_op jit(solution)/shard_map/ppermute | solution.py:484
  12.0 0.0 collective-permute-start.1
  12.0 1.0 %row_tables.1 = (bf16[2,512,256]{2,1,0:T(8,128)(2,1)S(1)}, bf16[2,32,512]{2,1,0:T(8,128)(2,1)S(1)}, f32[2,256,256]{2,1,0:T(8,128)S(1)}, f32[2,8,128]{2,1,0:T(8,128)S(1)}) custom-call(f32[2,24,256]{2,1,0:T(8,128)S(1)} %get-tuple-element.21.info_ref), custom_call_target="tpu_custom_call" | custom-call | flops 100000000 | bytes 1000000 | tf_op jit(solution)/shard_map/row_tables/pallas_call | solution.py:518
  13.1 0.0 collective-permute-done.refs_2_
  13.1 1.1 %collective-permute-start.5 = (bf16[32,1024]{1,0:T(8,128)(2,1)S(1)}, bf16[32,1024]{1,0:T(8,128)(2,1)S(1)}, u32[]{:S(2)}, u32[]{:S(2)}) collective-permute-start(bf16[32,1024]{1,0:T(8,128)(2,1)S(1)} %collective-permute-done.refs_2_), channel_id=1, source_target_pairs={{0,2},{2,0},{4,6},{6,4},{8,10},{10,8},{12,14},{14,12},{1,3},{3,1},... | collective-permute-start | bytes 196616 | tf_op jit(solution)/shard_map/ppermute | solution.py:484
  14.2 1.2 %collective-permute-done.3.refs_0_ = bf16[32,1024]{1,0:T(8,128)(2,1)S(1)} collective-permute-done((bf16[32,1024]{1,0:T(8,128)(2,1)S(1)}, bf16[32,1024]{1,0:T(8,128)(2,1)S(1)}, u32[]{:S(2)}, u32[]{:S(2)}) %collective-permute-start.3) | collective-permute-done | bytes 65568 | tf_op jit(solution)/shard_map/ppermute | solution.py:484
  15.3 0.0 collective-permute-done.4.refs_1_
  15.4 1.6 %collective-permute-start.6 = (bf16[64,1024]{1,0:T(8,128)(2,1)S(1)}, bf16[64,1024]{1,0:T(8,128)(2,1)S(1)}, u32[]{:S(2)}, u32[]{:S(2)}) collective-permute-start(bf16[64,1024]{1,0:T(8,128)(2,1)S(1)} %join.1.refs_1_.refs_3_), channel_id=1, source_target_pairs={{0,2},{2,0},{4,6},{6,4},{8,10},{10,8},{12,14},{14,12},{1,3},{3,1},... | collective-permute-start | bytes 393224 | tf_op jit(solution)/shard_map/ppermute | solution.py:484
  16.9 0.0 collective-permute-done.1.far_info_ref
  16.9 0.0 collective-permute-done.2.refs_0_.refs_1_
  16.9 2.4 %far_tables.1 = (bf16[512,2048]{1,0:T(8,128)(2,1)S(1)}, bf16[512,2048]{1,0:T(8,128)(2,1)S(1)}, f32[2,32,2048]{2,1,0:T(8,128)S(1)}, f32[2,32,2048]{2,1,0:T(8,128)...) custom-call(f32[2,24,256]{2,1,0:T(8,128)S(1)} %get-tuple-element.21.info_ref, ...), custom_call_target="tpu_custom_call" | custom-call | flops 3000000000 | bytes 30000000 | tf_op jit(solution)/shard_map/far_tables/pallas_call | solution.py:541
  19.3 0.0 collective-permute-done.5.refs_4_
  19.3 1.2 %collective-permute-done.6.refs_5_ = bf16[64,1024]{1,0:T(8,128)(2,1)S(1)} collective-permute-done((bf16[64,1024]{1,0:T(8,128)(2,1)S(1)}, bf16[64,1024]{1,0:T(8,128)(2,1)S(1)}, u32[]{:S(2)}, u32[]{:S(2)}) %collective-permute-start.6) | collective-permute-done | bytes 131104 | tf_op jit(solution)/shard_map/ppermute | solution.py:484
  20.5 1.2 %focus.1 = (bf16[32,1024]{1,0:T(8,128)(2,1)S(1)}, f32[2]{0:T(128)}) custom-call(bf16[2,512,256]{2,1,0:T(8,128)(2,1)S(1)} %get-tuple-element.22.tall_ref, bf16[2,32,512]{2,1,0:T(8,128)(2,1)S(1)} %get-tuple-element.25.flat_ref, f32[2,256,256]{2,1,0:T(8,128)S(1)} %get-tuple-element.26.spot_ref, f32[2,8,128]{2,1,0:T(8,128)S(1)} %get-tuple-element.27.gain_ref, ...), custom_call_target="tpu_custom_call" | custom-call | flops 100000000 | bytes 1000000 | tf_op jit(solution)/shard_map/focus/pallas_call | solution.py:549
  21.7 0.1 collective-permute-start.7
  21.8 1.4 %gradient_own.1.refs_5_ = f32[32,2048]{1,0:T(8,128)S(1)} custom-call(bf16[32,1024]{1,0:T(8,128)(2,1)S(1)} %get-tuple-element.31.back_ref, bf16[2048,512]{1,0:T(8,128)(2,1)S(1)} %get-tuple-element.35.refs_0_, bf16[2048,512]{1,0:T(8,128)(2,1)S(1)} %get-tuple-element.36.refs_1_, f32[2,32,2048]{2,1,0:T(8,128)S(1)} %get-tuple-element.37.refs_2_, ...), custom_call_target="tpu_custom_call" | custom-call | flops 1000000000 | bytes 10000000 | tf_op jit(solution)/shard_map/gradient_own/pallas_call | solution.py:564
  23.2 0.0 collective-permute-done.7.refs_0_
  23.2 1.6 %gradient_far.1 = f32[32,2048]{1,0:T(8,128)} custom-call(bf16[32,1024]{1,0:T(8,128)(2,1)S(1)} %collective-permute-done.7.refs_0_, bf16[512,2048]{1,0:T(8,128)(2,1)S(1)} %get-tuple-element.32.refs_1_, bf16[512,2048]{1,0:T(8,128)(2,1)S(1)} %get-tuple-element.33.refs_2_, f32[2,32,2048]{2,1,0:T(8,128)S(1)} %get-tuple-element.29.after_ref.refs_3_, ...), custom_call_target="tpu_custom_call" | custom-call | flops 1000000000 | bytes 10000000 | tf_op jit(solution)/shard_map/gradient_far/pallas_call | solution.py:569
  (1 shorter events, 0.0 us)
Async XLA Ops:
  4.6 8.4 %collective-permute-start = (bf16[32,1024]{1,0:T(8,128)(2,1)S(1)}, bf16[32,1024]{1,0:T(8,128)(2,1)S(1)}, u32[]{:S(2)}, u32[]{:S(2)}) collective-permute-start(bf16[32,1024]{1,0:T(8,128)(2,1)S(1)} %get-tuple-element.23.refs_0_), channel_id=1, source_target_pairs={{0,12},{2,14},{4,8},{6,10},{8,4},{10,6},{12,0},{14,2},{1,13},{3,15... | collective-permute-start | bytes 196616 | tf_op jit(solution)/shard_map/ppermute | solution.py:484
  9.7 5.6 %collective-permute-start.3 = (bf16[32,1024]{1,0:T(8,128)(2,1)S(1)}, bf16[32,1024]{1,0:T(8,128)(2,1)S(1)}, u32[]{:S(2)}, u32[]{:S(2)}) collective-permute-start(bf16[32,1024]{1,0:T(8,128)(2,1)S(1)} %get-tuple-element.23.refs_0_), channel_id=1, source_target_pairs={{0,8},{2,10},{4,12},{6,14},{8,0},{10,2},{12,4},{14,6},{1,9},{3,11}... | collective-permute-start | bytes 196616 | tf_op jit(solution)/shard_map/ppermute | solution.py:484
  9.7 5.6 %collective-permute-start.4 = (bf16[32,1024]{1,0:T(8,128)(2,1)S(1)}, bf16[32,1024]{1,0:T(8,128)(2,1)S(1)}, u32[]{:S(2)}, u32[]{:S(2)}) collective-permute-start(bf16[32,1024]{1,0:T(8,128)(2,1)S(1)} %get-tuple-element.23.refs_0_), channel_id=1, source_target_pairs={{0,4},{2,6},{4,0},{6,2},{8,12},{10,14},{12,8},{14,10},{1,5},{3,7},... | collective-permute-start | bytes 196616 | tf_op jit(solution)/shard_map/ppermute | solution.py:484
  10.4 6.5 %collective-permute-start.2 = (bf16[32,1024]{1,0:T(8,128)(2,1)S(1)}, bf16[32,1024]{1,0:T(8,128)(2,1)S(1)}, u32[]{:S(2)}, u32[]{:S(2)}) collective-permute-start(bf16[32,1024]{1,0:T(8,128)(2,1)S(1)} %get-tuple-element.23.refs_0_), channel_id=1, source_target_pairs={{0,2},{2,0},{4,6},{6,4},{8,10},{10,8},{12,14},{14,12},{1,3},{3,1},... | collective-permute-start | bytes 196616 | tf_op jit(solution)/shard_map/ppermute | solution.py:484
  12.0 4.9 %collective-permute-start.1 = (f32[2,24,256]{2,1,0:T(8,128)S(1)}, f32[2,24,256]{2,1,0:T(8,128)S(1)}, u32[]{:S(2)}, u32[]{:S(2)}) collective-permute-start(f32[2,24,256]{2,1,0:T(8,128)S(1)} %get-tuple-element.21.info_ref), channel_id=1, source_target_pairs={{0,1},{1,0},{2,3},{3,2},{4,5},{5,4},{6,7},{7,6},{8,9},{9,8},{10,11... | collective-permute-start | bytes 147464 | tf_op jit(solution)/shard_map/ppermute | solution.py:487
  13.1 6.2 %collective-permute-start.5 = (bf16[32,1024]{1,0:T(8,128)(2,1)S(1)}, bf16[32,1024]{1,0:T(8,128)(2,1)S(1)}, u32[]{:S(2)}, u32[]{:S(2)}) collective-permute-start(bf16[32,1024]{1,0:T(8,128)(2,1)S(1)} %collective-permute-done.refs_2_), channel_id=1, source_target_pairs={{0,2},{2,0},{4,6},{6,4},{8,10},{10,8},{12,14},{14,12},{1,3},{3,1},... | collective-permute-start | bytes 196616 | tf_op jit(solution)/shard_map/ppermute | solution.py:484
  15.4 5.1 %collective-permute-start.6 = (bf16[64,1024]{1,0:T(8,128)(2,1)S(1)}, bf16[64,1024]{1,0:T(8,128)(2,1)S(1)}, u32[]{:S(2)}, u32[]{:S(2)}) collective-permute-start(bf16[64,1024]{1,0:T(8,128)(2,1)S(1)} %join.1.refs_1_.refs_3_), channel_id=1, source_target_pairs={{0,2},{2,0},{4,6},{6,4},{8,10},{10,8},{12,14},{14,12},{1,3},{3,1},... | collective-permute-start | bytes 393224 | tf_op jit(solution)/shard_map/ppermute | solution.py:484
  21.7 1.5 %collective-permute-start.7 = (bf16[32,1024]{1,0:T(8,128)(2,1)S(1)}, bf16[32,1024]{1,0:T(8,128)(2,1)S(1)}, u32[]{:S(2)}, u32[]{:S(2)}) collective-permute-start(bf16[32,1024]{1,0:T(8,128)(2,1)S(1)} %get-tuple-element.31.back_ref), channel_id=1, source_target_pairs={{0,1},{1,0},{2,3},{3,2},{4,5},{5,4},{6,7},{7,6},{8,9},{9,8},{10,11... | collective-permute-start | bytes 196616 | tf_op jit(solution)/shard_map/ppermute | solution.py:487

commit v14 on v13

--- a/solution.py
+++ b/solution.py
@@ -523,20 +523,8 @@
         ),
         [VMEM], (VMEM,) * 4, [], 10**8, 10**6,
     )(info)
-    if peers <= DIRECT:
-        steps = list(range(peers - 2, 0, -2))
-        got = [exchange(mine, step) for step in steps]
-        near = exchange(mine, 1)
-        first, flat = lax.optimization_barrier((got[0], flat))
-        joined = call(join_kernel, "join", shape(((len(steps) - 1) * rows_dev, lanes), bf16),
-                      [VMEM] * (len(steps) - 1), VMEM, [], 10**6, 10**6)(*got[1:])
-        sections = [mine, near, first, joined, exchange(first, 1), exchange(joined, 1)]
-        steps = [0, 1, *steps, *(step ^ 1 for step in steps)]
-        after = [near, joined]
-    else:
-        blocks = jnp.tile(mine[None], (peers, 1, 1))
-        blocks = lax.all_to_all(blocks, "aperture", 0, 0, tiled=True)
-        sections, steps, after = [blocks.reshape(rows, lanes)], None, []
+    gathered = lax.all_gather(mine, "aperture", axis=0, tiled=True)
+    sections, steps, after = [gathered], None, []
     outs = [shape((2 * FOCAL, own_cols), bf16)] * pairs_dev + [shape((2, rows_dev, own_cols), f32)] * 2 * pairs_dev
     made = call(
         functools.partial(table_kernel, math.sqrt(rows * cols), cols), "far_tables",

time: 25 us -> 45.7 us (1.83)
  blocking collectives: 0 us -> 32.7 us
  starting transfers between devices: 10.1 us -> 0.59 us
  waiting for transfers between devices: 2.35 us -> 0.01 us
    all_gather x0 -> x1, blocking collectives: none -> 32.7 us  [on_device(): gathered = lax.all_gather(mine, 'aperture', axis=0, tiled=True)]
    ppermute x6 -> x0, starting transfers between devices: 10 us -> none  [exchange(): lax.ppermute(value, 'aperture', [(index, index ^ step) for index in range...]
    ppermute x6 -> x0, waiting for transfers between devices: 2.35 us -> none  [exchange(): lax.ppermute(value, 'aperture', [(index, index ^ step) for index in range...]
    ppermute x2, starting transfers between devices: 0.07 us -> 0.59 us  [to_core(): lax.ppermute(value, 'wave', [(index, (index + 1) % copies) for index in r...]
  transfers between devices with their start and end apart: 8 -> 2, of which waited for: 2 -> 0; matrix products, arithmetic and copies ran while one was open for 0% -> 0% of each run, Pallas kernels for 19% -> 5%
where the time goes in v14:
time: 45.7 us; the launch traced here: 45.6 us
  blocking collectives  32.7 us (72%)
  Pallas kernels  11.6 us (25%)
  between operations  0.68 us (1%)
  starting transfers between devices  0.59 us (1%)
    all_gather x1, blocking collectives, on_device(): gathered = lax.all_gather(mine, 'aperture', axis=0, tiled=True)  32.7 us
    pallas_call x1, Pallas kernels, on_device(): call(forward_kernel, 'forward', (shape((rows_dev, lanes), bf16), shape((p...  3.98 us
    pallas_call x1, Pallas kernels, on_device(): call(functools.partial(table_kernel, math.sqrt(rows * cols), cols), 'far_...  2.39 us
    pallas_call x1, Pallas kernels, on_device(): call(functools.partial(last_grad_kernel, pairs_dev), 'gradient_far', out,...  1.6 us
    pallas_call x1, Pallas kernels, on_device(): call(functools.partial(grad_kernel, pairs_dev, across=False), 'gradient_o...  1.38 us
    pallas_call x1, Pallas kernels, on_device(): call(functools.partial(focus_kernel, steps), 'focus', (shape((rows_dev, l...  1.16 us
    pallas_call x1, Pallas kernels, on_device(): call(row_kernel, 'row_tables', (shape((pairs_dev, 2 * FOCAL, rows), bf16)...  1.04 us
  transfers between devices with their start and end apart: 2, of which 0 were waited for; matrix products, arithmetic and copies ran while one was open for 0% of the time, Pallas kernels for 5%

profile of v14, /device:TPU:0, one launch (start us, length us, event | category | flops | bytes accessed | tf_op | source)
XLA Modules:
  0.0 45.6 jit_solution(10517803421674924236)
XLA Ops:
  0.6 4.0 %forward.1 = (bf16[32,1024]{1,0:T(8,128)(2,1)S(1)}, f32[2,24,256]{2,1,0:T(8,128)S(1)}, f32[32,2048]{1,0:T(8,128)S(1)}, bf16[2048,512]{1,0:T(8,128)(2,1)S(1)}, bf16[2048,512]{1,0:T(8,128)(2,1)S(1)}) custom-call(s32[2]{0:T(128)} %wave_hbm.1, s32[2]{0:T(128)} %angle_hbm.1, s32[2,2]{1,0:T(2,128)} %aim_hbm.1, f32[16,256]{1,0:T(8,128)} %bitcast.1, ...), custom_call_target="tpu_custom_call" | custom-call | flops 1000000000 | bytes 10000000 | tf_op jit(solution)/shard_map/forward/pallas_call | solution.py:493
  4.6 0.5 %collective-permute-start = (f32[2,24,256]{2,1,0:T(8,128)S(1)}, f32[2,24,256]{2,1,0:T(8,128)S(1)}, u32[]{:S(2)}, u32[]{:S(2)}) collective-permute-start(f32[2,24,256]{2,1,0:T(8,128)S(1)} %get-tuple-element.19.info_ref), channel_id=1, source_target_pairs={{0,1},{1,0},{2,3},{3,2},{4,5},{5,4},{6,7},{7,6},{8,9},{9,8},{10,11... | collective-permute-start | bytes 147464 | tf_op jit(solution)/shard_map/ppermute | solution.py:487
  5.1 32.7 %all_gather.3.refs_0_ = bf16[256,1024]{1,0:T(8,128)(2,1)S(1)} all-gather(bf16[32,1024]{1,0:T(8,128)(2,1)S(1)} %get-tuple-element.26), channel_id=1, replica_groups=mesh['group'=2,'aperture'=8,'wave'=2] {'aperture'}, dimensions={0}, use_global_device_ids=true | all-gather | bytes 589824 | tf_op jit(solution)/shard_map/all_gather | solution.py:526
  37.9 1.0 %row_tables.1 = (bf16[2,512,256]{2,1,0:T(8,128)(2,1)S(1)}, bf16[2,32,512]{2,1,0:T(8,128)(2,1)S(1)}, f32[2,256,256]{2,1,0:T(8,128)S(1)}, f32[2,8,128]{2,1,0:T(8,128)S(1)}) custom-call(f32[2,24,256]{2,1,0:T(8,128)S(1)} %get-tuple-element.19.info_ref), custom_call_target="tpu_custom_call" | custom-call | flops 100000000 | bytes 1000000 | tf_op jit(solution)/shard_map/row_tables/pallas_call | solution.py:518
  38.9 0.0 collective-permute-done.far_info_ref
  38.9 2.4 %far_tables.1 = (bf16[512,2048]{1,0:T(8,128)(2,1)S(1)}, bf16[512,2048]{1,0:T(8,128)(2,1)S(1)}, f32[2,32,2048]{2,1,0:T(8,128)S(1)}, f32[2,32,2048]{2,1,0:T(8,128)...) custom-call(f32[2,24,256]{2,1,0:T(8,128)S(1)} %get-tuple-element.19.info_ref, ...), custom_call_target="tpu_custom_call" | custom-call | flops 3000000000 | bytes 30000000 | tf_op jit(solution)/shard_map/far_tables/pallas_call | solution.py:529
  41.3 1.2 %focus.1 = (bf16[32,1024]{1,0:T(8,128)(2,1)S(1)}, f32[2]{0:T(128)}) custom-call(bf16[2,512,256]{2,1,0:T(8,128)(2,1)S(1)} %get-tuple-element.20.tall_ref, bf16[2,32,512]{2,1,0:T(8,128)(2,1)S(1)} %get-tuple-element.21.flat_ref, f32[2,256,256]{2,1,0:T(8,128)S(1)} %get-tuple-element.22.spot_ref, f32[2,8,128]{2,1,0:T(8,128)S(1)} %get-tuple-element.23.gain_ref, ...), custom_call_target="tpu_custom_call" | custom-call | flops 100000000 | bytes 1000000 | tf_op jit(solution)/shard_map/focus/pallas_call | solution.py:537
  42.5 0.1 collective-permute-start.1
  42.6 1.4 %gradient_own.1.refs_5_ = f32[32,2048]{1,0:T(8,128)S(1)} custom-call(bf16[32,1024]{1,0:T(8,128)(2,1)S(1)} %get-tuple-element.27.back_ref, bf16[2048,512]{1,0:T(8,128)(2,1)S(1)} %get-tuple-element.31.refs_0_, bf16[2048,512]{1,0:T(8,128)(2,1)S(1)} %get-tuple-element.32.refs_1_, f32[2,32,2048]{2,1,0:T(8,128)S(1)} %get-tuple-element.33.refs_2_, ...), custom_call_target="tpu_custom_call" | custom-call | flops 1000000000 | bytes 10000000 | tf_op jit(solution)/shard_map/gradient_own/pallas_call | solution.py:552
  43.9 0.0 collective-permute-done.1.refs_0_
  43.9 1.6 %gradient_far.1 = f32[32,2048]{1,0:T(8,128)} custom-call(bf16[32,1024]{1,0:T(8,128)(2,1)S(1)} %collective-permute-done.1.refs_0_, bf16[512,2048]{1,0:T(8,128)(2,1)S(1)} %get-tuple-element.28.refs_1_, bf16[512,2048]{1,0:T(8,128)(2,1)S(1)} %get-tuple-element.29.refs_2_, f32[2,32,2048]{2,1,0:T(8,128)S(1)} %get-tuple-element.25.after_ref.refs_3_, ...), custom_call_target="tpu_custom_call" | custom-call | flops 1000000000 | bytes 10000000 | tf_op jit(solution)/shard_map/gradient_far/pallas_call | solution.py:557
Async XLA Ops:
  4.6 34.3 %collective-permute-start = (f32[2,24,256]{2,1,0:T(8,128)S(1)}, f32[2,24,256]{2,1,0:T(8,128)S(1)}, u32[]{:S(2)}, u32[]{:S(2)}) collective-permute-start(f32[2,24,256]{2,1,0:T(8,128)S(1)} %get-tuple-element.19.info_ref), channel_id=1, source_target_pairs={{0,1},{1,0},{2,3},{3,2},{4,5},{5,4},{6,7},{7,6},{8,9},{9,8},{10,11... | collective-permute-start | bytes 147464 | tf_op jit(solution)/shard_map/ppermute | solution.py:487
  42.5 1.5 %collective-permute-start.1 = (bf16[32,1024]{1,0:T(8,128)(2,1)S(1)}, bf16[32,1024]{1,0:T(8,128)(2,1)S(1)}, u32[]{:S(2)}, u32[]{:S(2)}) collective-permute-start(bf16[32,1024]{1,0:T(8,128)(2,1)S(1)} %get-tuple-element.27.back_ref), channel_id=1, source_target_pairs={{0,1},{1,0},{2,3},{3,2},{4,5},{5,4},{6,7},{7,6},{8,9},{9,8},{10,11... | collective-permute-start | bytes 196616 | tf_op jit(solution)/shard_map/ppermute | solution.py:487

commit v15 on v13

--- a/solution.py
+++ b/solution.py
@@ -120,19 +120,16 @@
     return [outs[2 * pair : 2 * pair + 2] for pair in range(pairs)]
 
 
-def near_slopes(s, coef_ref, pairs):
+def near_slopes(s, power_ref, pairs):
     s = split_rows(s)
-    twice = s + s
-    before, current = jnp.ones_like(s), twice
-    outs = [
-        [coef_ref[pair, row] + coef_ref[pair, row + 1] * twice for row in (1, TERMS + 1)] for pair in range(pairs)
-    ]
-    for order in range(3, TERMS):
-        before, current = current, twice * current - before
-        for pair, out in enumerate(outs):
-            out[0] = out[0] + coef_ref[pair, order] * current
-            out[1] = out[1] + coef_ref[pair, TERMS + order] * current
-    return [[join_rows(part) for part in out] for out in outs]
+    outs = []
+    for pair, part in itertools.product(range(pairs), range(2)):
+        row = (part + 1) * TERMS - 1
+        value = power_ref[pair, row] * s + power_ref[pair, row - 1]
+        for row in range(row - 2, part * TERMS, -1):
+            value = value * s + power_ref[pair, row]
+        outs.append(join_rows(value))
+    return [outs[2 * pair : 2 * pair + 2] for pair in range(pairs)]
 
 
 def turn_round(value):
@@ -164,10 +161,9 @@
     wave_hbm, angle_hbm, aim_hbm, coef_hbm, width_hbm, mine_ref, info_ref, own_ref, *refs
 ):
     pairs = info_ref.shape[0]
-    table_refs, refs = refs[:pairs], refs[pairs:]
     (
-        wave_ref, angle_ref, aim_ref, coef_ref, width_ref, far_ref, base_ref, centre_ref, power_ref, near_ref, acc_ref,
-        sems,
+        wave_ref, angle_ref, aim_ref, coef_ref, width_ref, far_ref, base_ref, centre_ref, power_ref, near_ref, table_ref,
+        acc_ref, sems,
     ) = refs
     rows_dev, cols = width_ref.shape
     half = cols // 2
@@ -221,11 +217,11 @@
                 base_r, base_i = (base_ref[pair, part, row : row + GRAIN, :] for part in range(2))
                 for start, table in zip(starts, both_blocks(base_r, base_i, cent_r, cent_i)):
                     rows = slice(start + row, start + row + GRAIN)
-                    table_refs[pair][rows, :FOCAL] = table[0].astype(jnp.bfloat16)
-                    table_refs[pair][rows, FOCAL:] = table[1].astype(jnp.bfloat16)
+                    table_ref[pair, rows, :FOCAL] = table[0].astype(jnp.bfloat16)
+                    table_ref[pair, rows, FOCAL:] = table[1].astype(jnp.bfloat16)
             product = jnp.dot(
                 jnp.concatenate([near_ref[pair, :, start : start + BLOCK] for start in starts], axis=1),
-                jnp.concatenate([table_refs[pair][start : start + BLOCK, :] for start in starts], axis=0),
+                jnp.concatenate([table_ref[pair, start : start + BLOCK, :] for start in starts], axis=0),
                 preferred_element_type=jnp.float32,
             )
             acc_ref[pair] = product if index == 0 else acc_ref[pair] + product
@@ -303,73 +299,72 @@
         out_ref[index * count : (index + 1) * count, :] = ref[...]
 
 
-def focus_kernel(steps, tall_ref, flat_ref, spot_ref, gain_ref, after_ref, *refs):
+def focus_kernel(pair, steps, tall_ref, flat_ref, spot_ref, gain_ref, after_ref, *refs):
     del after_ref
-    *sect_refs, back_ref, score_ref, rows_ref, mixed_ref, field_ref, stack_ref = refs
-    pairs = tall_ref.shape[0]
+    last = pair == tall_ref.shape[0] - 1
+    *in_refs, back_ref, score_ref, rows_ref, mixed_ref, field_ref, stack_ref = refs
+    before_refs, sect_refs = in_refs[:pair], in_refs[pair:]
     rows_dev = back_ref.shape[0]
+    lanes = slice(2 * pair * FOCAL, 2 * (pair + 1) * FOCAL)
     if steps is None:
-        rows_ref = sect_refs[0]
+        section = sect_refs[0][:, lanes]
     else:
         me = lax.axis_index("aperture")
         blocks = [
-            ref[index * rows_dev : (index + 1) * rows_dev, :]
+            ref[index * rows_dev : (index + 1) * rows_dev, lanes]
             for ref in sect_refs
             for index in range(ref.shape[0] // rows_dev)
         ]
         for step, block in zip(steps, blocks, strict=True):
             start = pl.multiple_of((me ^ step) * rows_dev, rows_dev)
             rows_ref[pl.ds(start, rows_dev), :] = block
-    for pair in range(pairs):
-        lane = 2 * pair * FOCAL
-        section = rows_ref[:, lane : lane + 2 * FOCAL]
-        mixed_ref[pair] = jnp.dot(tall_ref[pair], section, preferred_element_type=jnp.float32)
+        section = rows_ref[...]
+    mixed_ref[...] = jnp.dot(tall_ref[pair], section, preferred_element_type=jnp.float32)
     pieces = [slice(row, row + PIECE) for row in range(0, FOCAL, PIECE)]
-    sums = []
-    for pair in range(pairs):
-        totals = [jnp.zeros((PIECE, FOCAL), jnp.float32) for _ in range(2)]
-        for rows in pieces:
-            lower = slice(rows.start + FOCAL, rows.stop + FOCAL)
-            real = mixed_ref[pair, rows, :FOCAL] - mixed_ref[pair, lower, FOCAL:]
-            imag = mixed_ref[pair, rows, FOCAL:] + mixed_ref[pair, lower, :FOCAL]
-            field_ref[pair, 0, rows, :] = real
-            field_ref[pair, 1, rows, :] = imag
-            power = real * real + imag * imag
-            totals = [totals[0] + spot_ref[pair, rows, :] * power, totals[1] + power]
-        sums.append((total_of(totals[0]), total_of(totals[1]) + 1e-06))
-    for pair, (spot_power, all_power) in enumerate(sums):
-        ratio = spot_power / all_power
-        gain = gain_ref[pair, :1, :1]
+    totals = [jnp.zeros((PIECE, FOCAL), jnp.float32) for _ in range(2)]
+    for rows in pieces:
+        lower = slice(rows.start + FOCAL, rows.stop + FOCAL)
+        real = mixed_ref[rows, :FOCAL] - mixed_ref[lower, FOCAL:]
+        imag = mixed_ref[rows, FOCAL:] + mixed_ref[lower, :FOCAL]
+        field_ref[0, rows, :] = real
+        field_ref[1, rows, :] = imag
+        power = real * real + imag * imag
+        totals = [totals[0] + spot_ref[pair, rows, :] * power, totals[1] + power]
+    spot_power, all_power = total_of(totals[0]), total_of(totals[1]) + 1e-06
+    ratio = spot_power / all_power
+    gain = gain_ref[pair, :1, :1]
+    if last:
+        for index, ref in enumerate(before_refs):
+            score_ref[index] = jnp.sum(ref[:1, :1])
         score_ref[pair] = jnp.sum(ratio * gain)
-        scale = gain * 2.0 / all_power
-        for rows in pieces:
-            lower = slice(rows.start + FOCAL, rows.stop + FOCAL)
-            weight = scale * (spot_ref[pair, rows, :] - ratio)
-            real = (weight * field_ref[pair, 0, rows, :]).astype(jnp.bfloat16)
-            imag = (weight * field_ref[pair, 1, rows, :]).astype(jnp.bfloat16)
-            stack_ref[pair, rows, :FOCAL] = real
-            stack_ref[pair, rows, FOCAL:] = imag
-            stack_ref[pair, lower, :FOCAL] = imag
-            stack_ref[pair, lower, FOCAL:] = -real
-        back = jnp.dot(flat_ref[pair], stack_ref[pair], preferred_element_type=jnp.float32)
-        lane = 2 * pair * FOCAL
-        back_ref[:, lane : lane + 2 * FOCAL] = back.astype(jnp.bfloat16)
+    else:
+        score_ref[...] = jnp.broadcast_to(ratio * gain, score_ref.shape)
+    scale = gain * 2.0 / all_power
+    for rows in pieces:
+        lower = slice(rows.start + FOCAL, rows.stop + FOCAL)
+        weight = scale * (spot_ref[pair, rows, :] - ratio)
+        real = (weight * field_ref[0, rows, :]).astype(jnp.bfloat16)
+        imag = (weight * field_ref[1, rows, :]).astype(jnp.bfloat16)
+        stack_ref[rows, :FOCAL] = real
+        stack_ref[rows, FOCAL:] = imag
+        stack_ref[lower, :FOCAL] = imag
+        stack_ref[lower, FOCAL:] = -real
+    back = jnp.dot(flat_ref[pair], stack_ref[...], preferred_element_type=jnp.float32)
+    back_ref[...] = back.astype(jnp.bfloat16)
 
 
 def table_kernel(scale, cols, info_ref, far_info_ref, width_ref, *refs):
-    *out_refs, base_ref, centre_ref, turned_ref, coef_ref = refs
-    pairs = base_ref.shape[0]
-    out_refs = out_refs[-3 * pairs :]
+    *out_refs, base_ref, centre_ref, turned_ref, power_ref = refs
+    pairs = power_ref.shape[0]
+    out_refs = out_refs[-2 * pairs :]
     table_refs, slope_refs = out_refs[:pairs], out_refs[pairs:]
     own_cols = width_ref.shape[1]
-    for core, ref in enumerate((info_ref, far_info_ref)):
-        for pair in range(pairs):
-            coef = ref[pair, : 2 * TERMS, :LANES]
-            coef = coef * ((iota(coef.shape, 0) % TERMS).astype(jnp.float32) * scale)
-            coef_ref[core * pairs + pair] = as_tiles(coef)
+    sources = [(ref, pair) for ref in (info_ref, far_info_ref) for pair in range(pairs // 2)]
     centres = []
-    for pair in range(pairs):
-        own_waves(far_info_ref, pair, cols, base_ref.at[pair], centre_ref.at[pair])
+    for pair, (ref, source) in enumerate(sources):
+        power = power_coefs(ref[source, : 2 * TERMS, :LANES])
+        power_ref[pair] = as_tiles(power * ((iota(power.shape, 0) % TERMS).astype(jnp.float32) * scale))
+        own_waves(ref, source, cols, base_ref.at[pair], centre_ref.at[pair])
         for part, row, lane in itertools.product(range(2), range(0, BLOCK, LANES), range(0, FOCAL, LANES)):
             tile = base_ref[pair, part, row : row + LANES, lane : lane + LANES]
             turned_ref[pair, part, lane : lane + LANES, row : row + LANES] = tile.T
@@ -387,7 +382,7 @@
                         table_refs[pair][place, start : start + BLOCK] = value.astype(jnp.bfloat16)
         for start in (start + step for start in starts for step in range(0, BLOCK, LANES)):
             place = slice(start, start + LANES)
-            slopes = near_slopes(width_ref[:, place], coef_ref, 2 * pairs)
+            slopes = near_slopes(width_ref[:, place], power_ref, pairs)
             for ref, slope in zip(slope_refs, slopes):
                 ref[0, :, place] = slope[0]
                 ref[1, :, place] = slope[1]
@@ -413,15 +408,15 @@
         move.wait()
 
 
-def grad_kernel(pairs, back_ref, *refs, send=None, across=True):
+def grad_kernel(pairs, *refs, send=None):
     *in_refs, out_ref = refs
-    table_refs, slope_refs, total_ref = in_refs[:pairs], in_refs[pairs : 2 * pairs], in_refs[2 * pairs :]
+    back_refs, table_refs, slope_refs = (in_refs[first * pairs : (first + 1) * pairs] for first in range(3))
+    total_ref = in_refs[3 * pairs :]
     rows_dev, own_cols = out_ref.shape
     core = lax.axis_index("wave")
     lefts = []
-    for pair in range(pairs):
-        lane = 2 * pair * FOCAL
-        real, imag = back_ref[:, lane : lane + FOCAL], back_ref[:, lane + FOCAL : lane + 2 * FOCAL]
+    for ref in back_refs:
+        real, imag = ref[:, :FOCAL], ref[:, FOCAL:]
         above = jnp.where(core == 1, imag, -imag)
         below = jnp.where(core == 1, -real, real)
         lefts.append(
@@ -433,14 +428,10 @@
     for start in range(0, own_cols, size):
         place = slice(start, start + size)
         total = total_ref[0][:, place] if total_ref else jnp.zeros((rows_dev, size), jnp.float32)
-        for pair in range(pairs):
-            if across:
-                table, dims = table_refs[pair][:, place], ((1,), (0,))
-            else:
-                table, dims = table_refs[pair][place, :], ((1,), (1,))
-            grad = lax.dot_general(lefts[pair], table, (dims, ((), ())), preferred_element_type=jnp.float32)
-            total += grad[:rows_dev] * slope_refs[pair][0, :, place]
-            total += grad[rows_dev:] * slope_refs[pair][1, :, place]
+        for left, table_ref, slope_ref in zip(lefts, table_refs, slope_refs):
+            grad = jnp.dot(left, table_ref[:, place], preferred_element_type=jnp.float32)
+            total += grad[:rows_dev] * slope_ref[0, :, place]
+            total += grad[rows_dev:] * slope_ref[1, :, place]
         if send is None:
             out_ref[:, place] = total
         else:
@@ -472,6 +463,7 @@
     peers = lax.axis_size("aperture")
     copies = lax.axis_size("wave")
     rows = rows_dev * peers
+    pairs = pairs_dev * copies
     own_cols = cols // copies
     lanes = 2 * pairs_dev * FOCAL
     f32, bf16 = jnp.float32, jnp.bfloat16
@@ -490,14 +482,13 @@
         pltpu.VMEM((pairs_dev, 2, BLOCK, FOCAL), f32),
         pltpu.VMEM((pairs_dev, 2, 8, FOCAL), f32),
     ]
-    mine, info, own, *tables = call(
+    mine, info, own = call(
         forward_kernel, "forward",
         (
             shape((rows_dev, lanes), bf16),
             shape((pairs_dev, INFO_ROWS, FOCAL), f32), shape((rows_dev, own_cols), f32),
-            *[shape((own_cols, 2 * FOCAL), bf16)] * pairs_dev,
         ),
-        [HBM] * 5, (VMEM,) * (3 + pairs_dev),
+        [HBM] * 5, (VMEM,) * 3,
         [
             pltpu.SMEM(wave_ids.shape, jnp.int32),
             pltpu.SMEM(angle_ids.shape, jnp.int32),
@@ -508,6 +499,7 @@
             *waves,
             pltpu.VMEM((pairs_dev, 2 * TERMS, SUBLANES, LANES), f32),
             pltpu.VMEM((pairs_dev, 4 * rows_dev, own_cols), bf16),
+            pltpu.VMEM((pairs_dev, own_cols, 2 * FOCAL), bf16),
             pltpu.VMEM((pairs_dev, 4 * rows_dev, 2 * FOCAL), f32),
             pltpu.SemaphoreType.DMA((5,)),
         ],
@@ -537,41 +529,54 @@
         blocks = jnp.tile(mine[None], (peers, 1, 1))
         blocks = lax.all_to_all(blocks, "aperture", 0, 0, tiled=True)
         sections, steps, after = [blocks.reshape(rows, lanes)], None, []
-    outs = [shape((2 * FOCAL, own_cols), bf16)] * pairs_dev + [shape((2, rows_dev, own_cols), f32)] * 2 * pairs_dev
+    outs = [shape((2 * FOCAL, own_cols), bf16)] * pairs + [shape((2, rows_dev, own_cols), f32)] * pairs
     made = call(
-        functools.partial(table_kernel, math.sqrt(rows * cols), cols), "far_tables",
+        functools.partial(table_kernel, math.sqrt(rows * cols), cols), "column_tables",
         outs, [VMEM] * 3 + [ANY] * len(after), [VMEM] * len(outs),
-        [*waves, pltpu.VMEM((pairs_dev, 2, FOCAL, BLOCK), f32), pltpu.VMEM((copies * pairs_dev, 2 * TERMS, SUBLANES, LANES), f32)],
+        [
+            pltpu.VMEM((pairs, 2, BLOCK, FOCAL), f32),
+            pltpu.VMEM((pairs, 2, 8, FOCAL), f32),
+            pltpu.VMEM((pairs, 2, FOCAL, BLOCK), f32),
+            pltpu.VMEM((pairs, 2 * TERMS, SUBLANES, LANES), f32),
+        ],
         30 * 10**8, 30 * 10**6,
     )(info, far_info, own, *after)
-    far_tables, slopes, far_slopes = made[:pairs_dev], made[pairs_dev : 2 * pairs_dev], made[2 * pairs_dev :]
-
-    back, scores = call(
-        functools.partial(focus_kernel, steps), "focus",
-        (shape((rows_dev, lanes), bf16), shape((pairs_dev,), f32)),
-        [VMEM] * 4 + [ANY] + [VMEM] * len(sections), (VMEM, SMEM),
-        [
-            pltpu.VMEM((rows, lanes), bf16),
-            pltpu.VMEM((pairs_dev, 2 * FOCAL, 2 * FOCAL), f32),
-            pltpu.VMEM((pairs_dev, 2, FOCAL, FOCAL), f32),
-            pltpu.VMEM((pairs_dev, 2 * FOCAL, 2 * FOCAL), bf16),
-        ],
-        10**8, 10**6,
-    )(tall, flat, spots, gains, far_slopes[0], *sections)
+    tables, slopes = made[:pairs], made[pairs:]
+
+    backs, scores, last = [], [], slopes[0]
+    for pair in range(pairs_dev):
+        final = pair == pairs_dev - 1
+        score = shape((pairs_dev,), f32) if final else shape((SUBLANES, LANES), f32)
+        last, score = call(
+            functools.partial(focus_kernel, pair, steps), f"focus_{pair}",
+            (shape((rows_dev, 2 * FOCAL), bf16), score),
+            [VMEM] * 4 + [ANY] + [VMEM] * (pair + len(sections)), (VMEM, SMEM if final else VMEM),
+            [
+                pltpu.VMEM((rows, 2 * FOCAL), bf16),
+                pltpu.VMEM((2 * FOCAL, 2 * FOCAL), f32),
+                pltpu.VMEM((2, FOCAL, FOCAL), f32),
+                pltpu.VMEM((2 * FOCAL, 2 * FOCAL), bf16),
+            ],
+            10**8, 10**6,
+        )(tall, flat, spots, gains, last, *scores, *sections)
+        backs.append(last)
+        scores.append(score)
+    backs = backs + [to_core(back) for back in backs]
 
     out = shape((rows_dev, own_cols), f32)
-    ins = [back, *tables, *slopes]
-    grad = call(
-        functools.partial(grad_kernel, pairs_dev, across=False), "gradient_own",
-        out, [VMEM] * len(ins), VMEM, [], 10**9, 10**7,
-    )(*ins)
-    ins = [to_core(back), *far_tables, *far_slopes, grad]
-    grad = call(
-        functools.partial(last_grad_kernel, pairs_dev), "gradient_far",
-        out, [VMEM] * len(ins), HBM,
-        [pltpu.VMEM(out.shape, f32), pltpu.SemaphoreType.DMA((own_cols // (2 * BLOCK),))], 10**9, 10**7,
-    )(*ins)
-    return grad, scores
+    grad = ()
+    for first, count in ((0, pairs_dev), *((pair, 1) for pair in range(pairs_dev, pairs))):
+        some = slice(first, first + count)
+        ins = [*backs[some], *tables[some], *slopes[some], *grad]
+        final = first + count == pairs
+        result = call(
+            functools.partial(last_grad_kernel if final else grad_kernel, count), f"gradient_{first}",
+            out, [VMEM] * len(ins), HBM if final else VMEM,
+            [pltpu.VMEM(out.shape, f32), pltpu.SemaphoreType.DMA((own_cols // (2 * BLOCK),))] if final else [],
+            10**9, 10**7,
+        )(*ins)
+        grad = (result,)
+    return result, scores[-1]
 
 
 def solution(mesh):

time: 25 us -> 25.6 us (1.024)
  Pallas kernels: 11.6 us -> 12.6 us
  waiting for transfers between devices: 2.35 us -> 1.4 us
  starting transfers between devices: 10.1 us -> 10.6 us
    pallas_call x4 -> x6, Pallas kernels: 6.59 us -> 7.76 us  [the longest x1 3.33 us: on_device(): call(functools.partial(table_kernel, math.sqrt(rows * cols), cols), 'colu...]
    ppermute x6, waiting for transfers between devices: 2.35 us -> 1.39 us  [exchange(): lax.ppermute(value, 'aperture', [(index, index ^ step) for index in range...]
    ppermute x2 -> x3, starting transfers between devices: 0.07 us -> 0.59 us  [to_core(): lax.ppermute(value, 'wave', [(index, (index + 1) % copies) for index in r...]
  transfers between devices with their start and end apart: 8 -> 9, of which waited for: 2 -> 2; matrix products, arithmetic and copies ran while one was open for 0% -> 0% of each run, Pallas kernels for 19% -> 27%
where the time goes in v15:
time: 25.6 us; the launch traced here: 25.4 us
  Pallas kernels  12.6 us (49%)
  starting transfers between devices  10.6 us (41%)
  waiting for transfers between devices  1.4 us (5%)
  between operations  0.72 us (3%)
    ppermute x6, starting transfers between devices, exchange(): lax.ppermute(value, 'aperture', [(index, index ^ step) for index in range...  10 us
    pallas_call x1, Pallas kernels, on_device(): call(forward_kernel, 'forward', (shape((rows_dev, lanes), bf16), shape((p...  3.84 us
    pallas_call x1, Pallas kernels, on_device(): call(functools.partial(table_kernel, math.sqrt(rows * cols), cols), 'colu...  3.33 us
    pallas_call x3, Pallas kernels, on_device(): call(functools.partial(last_grad_kernel if final else grad_kernel, count)...  2.57 us
    pallas_call x2, Pallas kernels, on_device(): call(functools.partial(focus_kernel, pair, steps), f'focus_{pair}', (shap...  1.86 us
    ppermute x6, waiting for transfers between devices, exchange(): lax.ppermute(value, 'aperture', [(index, index ^ step) for index in range...  1.39 us
    pallas_call x1, Pallas kernels, on_device(): call(row_kernel, 'row_tables', (shape((pairs_dev, 2 * FOCAL, rows), bf16)...  1.04 us
    ppermute x3, starting transfers between devices, to_core(): lax.ppermute(value, 'wave', [(index, (index + 1) % copies) for index in r...  0.59 us
  transfers between devices with their start and end apart: 9, of which 2 were waited for; matrix products, arithmetic and copies ran while one was open for 0% of the time, Pallas kernels for 27%

profile of v15, /device:TPU:0, one launch (start us, length us, event | category | flops | bytes accessed | tf_op | source)
XLA Modules:
  0.0 25.4 jit_solution(13169341254177956510)
XLA Ops:
  0.6 3.8 %forward.1 = (bf16[32,1024]{1,0:T(8,128)(2,1)S(1)}, f32[2,24,256]{2,1,0:T(8,128)S(1)}, f32[32,2048]{1,0:T(8,128)S(1)}) custom-call(s32[2]{0:T(128)} %wave_hbm.1, s32[2]{0:T(128)} %angle_hbm.1, s32[2,2]{1,0:T(2,128)} %aim_hbm.1, f32[16,256]{1,0:T(8,128)} %bitcast.1, f32[32,4096]{1,0:T(8,128)} %width_hbm.1), custom_call_target="tpu_custom_call" | custom-call | flops 1000000000 | bytes 10000000 | tf_op jit(solution)/shard_map/forward/pallas_call | solution.py:485
  4.5 5.1 %collective-permute-start = (bf16[32,1024]{1,0:T(8,128)(2,1)S(1)}, bf16[32,1024]{1,0:T(8,128)(2,1)S(1)}, u32[]{:S(2)}, u32[]{:S(2)}) collective-permute-start(bf16[32,1024]{1,0:T(8,128)(2,1)S(1)} %get-tuple-element.25.refs_0_.refs_1_), channel_id=1, source_target_pairs={{0,12},{2,14},{4,8},{6,10},{8,4},{10,6},{12,0},{14,2},{1,13},{3,15... | collective-permute-start | bytes 196616 | tf_op jit(solution)/shard_map/ppermute | solution.py:476
  9.6 0.0 collective-permute-start.3
  9.6 0.6 %collective-permute-start.4 = (bf16[32,1024]{1,0:T(8,128)(2,1)S(1)}, bf16[32,1024]{1,0:T(8,128)(2,1)S(1)}, u32[]{:S(2)}, u32[]{:S(2)}) collective-permute-start(bf16[32,1024]{1,0:T(8,128)(2,1)S(1)} %get-tuple-element.25.refs_0_.refs_1_), channel_id=1, source_target_pairs={{0,4},{2,6},{4,0},{6,2},{8,12},{10,14},{12,8},{14,10},{1,5},{3,7},... | collective-permute-start | bytes 196616 | tf_op jit(solution)/shard_map/ppermute | solution.py:476
  10.2 1.6 %collective-permute-start.2 = (bf16[32,1024]{1,0:T(8,128)(2,1)S(1)}, bf16[32,1024]{1,0:T(8,128)(2,1)S(1)}, u32[]{:S(2)}, u32[]{:S(2)}) collective-permute-start(bf16[32,1024]{1,0:T(8,128)(2,1)S(1)} %get-tuple-element.25.refs_0_.refs_1_), channel_id=1, source_target_pairs={{0,2},{2,0},{4,6},{6,4},{8,10},{10,8},{12,14},{14,12},{1,3},{3,1},... | collective-permute-start | bytes 196616 | tf_op jit(solution)/shard_map/ppermute | solution.py:476
  11.9 0.0 collective-permute-start.1
  11.9 1.0 %row_tables.1 = (bf16[2,512,256]{2,1,0:T(8,128)(2,1)S(1)}, bf16[2,32,512]{2,1,0:T(8,128)(2,1)S(1)}, f32[2,256,256]{2,1,0:T(8,128)S(1)}, f32[2,8,128]{2,1,0:T(8,128)S(1)}) custom-call(f32[2,24,256]{2,1,0:T(8,128)S(1)} %get-tuple-element.23.info_ref), custom_call_target="tpu_custom_call" | custom-call | flops 100000000 | bytes 1000000 | tf_op jit(solution)/shard_map/row_tables/pallas_call | solution.py:510
  12.9 0.0 collective-permute-done.refs_2_.refs_3_
  12.9 1.1 %collective-permute-start.5 = (bf16[32,1024]{1,0:T(8,128)(2,1)S(1)}, bf16[32,1024]{1,0:T(8,128)(2,1)S(1)}, u32[]{:S(2)}, u32[]{:S(2)}) collective-permute-start(bf16[32,1024]{1,0:T(8,128)(2,1)S(1)} %collective-permute-done.refs_2_.refs_3_), channel_id=1, source_target_pairs={{0,2},{2,0},{4,6},{6,4},{8,10},{10,8},{12,14},{14,12},{1,3},{3,1},... | collective-permute-start | bytes 196616 | tf_op jit(solution)/shard_map/ppermute | solution.py:476
  14.0 1.2 %collective-permute-done.3.refs_0_ = bf16[32,1024]{1,0:T(8,128)(2,1)S(1)} collective-permute-done((bf16[32,1024]{1,0:T(8,128)(2,1)S(1)}, bf16[32,1024]{1,0:T(8,128)(2,1)S(1)}, u32[]{:S(2)}, u32[]{:S(2)}) %collective-permute-start.3) | collective-permute-done | bytes 65568 | tf_op jit(solution)/shard_map/ppermute | solution.py:476
  15.2 0.0 collective-permute-done.4.refs_1_
  15.2 1.6 %collective-permute-start.6 = (bf16[64,1024]{1,0:T(8,128)(2,1)S(1)}, bf16[64,1024]{1,0:T(8,128)(2,1)S(1)}, u32[]{:S(2)}, u32[]{:S(2)}) collective-permute-start(bf16[64,1024]{1,0:T(8,128)(2,1)S(1)} %join.1.refs_1_.refs_3_.refs_4_), channel_id=1, source_target_pairs={{0,2},{2,0},{4,6},{6,4},{8,10},{10,8},{12,14},{14,12},{1,3},{3,1},... | collective-permute-start | bytes 393224 | tf_op jit(solution)/shard_map/ppermute | solution.py:476
  16.8 0.0 collective-permute-done.1.far_info_ref
  16.8 0.0 collective-permute-done.2.refs_0_.refs_1_.refs_2_
  16.8 3.3 %column_tables.1 = (bf16[512,2048]{1,0:T(8,128)(2,1)S(1)}, bf16[512,2048]{1,0:T(8,128)(2,1)S(1)}, bf16[512,2048]{1,0:T(8,128)(2,1)S(1)}, bf16[512,2048]{1,0:T(8,...) custom-call(f32[2,24,256]{2,1,0:T(8,128)S(1)} %get-tuple-element.23., ...), custom_call_target="tpu_custom_call" | custom-call | flops 3000000000 | bytes 30000000 | tf_op jit(solution)/shard_map/column_tables/pallas_call | solution.py:533
  20.1 0.0 collective-permute-done.5.refs_4_.refs_5_
  20.1 0.2 collective-permute-done.6.refs_5_.refs_6_
  20.3 0.8 %focus_0.1 = (bf16[32,512]{1,0:T(8,128)(2,1)S(1)}, f32[8,128]{1,0:T(8,128)S(1)}) custom-call(bf16[2,512,256]{2,1,0:T(8,128)(2,1)S(1)} %get-tuple-element.24.tall_ref, bf16[2,32,512]{2,1,0:T(8,128)(2,1)S(1)} %get-tuple-element.27.flat_ref, f32[2,256,256]{2,1,0:T(8,128)S(1)} %get-tuple-element.28.spot_ref, f32[2,8,128]{2,1,0:T(8,128)S(1)} %get-tuple-element.29.gain_ref, ...), custom_call_target="tpu_custom_call" | custom-call | flops 100000000 | bytes 1000000 | tf_op jit(solution)/shard_map/focus_0/pallas_call | solution.py:550
  21.2 0.0 collective-permute-start.8
  21.2 1.1 %focus_1.1 = (bf16[32,512]{1,0:T(8,128)(2,1)S(1)}, f32[2]{0:T(128)}) custom-call(bf16[2,512,256]{2,1,0:T(8,128)(2,1)S(1)} %get-tuple-element.24.tall_ref, bf16[2,32,512]{2,1,0:T(8,128)(2,1)S(1)} %get-tuple-element.27.flat_ref, f32[2,256,256]{2,1,0:T(8,128)S(1)} %get-tuple-element.28.spot_ref, f32[2,8,128]{2,1,0:T(8,128)S(1)} %get-tuple-element.29.gain_ref, ...), custom_call_target="tpu_custom_call" | custom-call | flops 100000000 | bytes 1000000 | tf_op jit(solution)/shard_map/focus_1/pallas_call | solution.py:550
  22.2 0.6 %collective-permute-start.7 = (bf16[32,512]{1,0:T(8,128)(2,1)S(1)}, bf16[32,512]{1,0:T(8,128)(2,1)S(1)}, u32[]{:S(2)}, u32[]{:S(2)}) collective-permute-start(bf16[32,512]{1,0:T(8,128)(2,1)S(1)} %get-tuple-element.35.refs_1_), channel_id=1, source_target_pairs={{0,1},{1,0},{2,3},{3,2},{4,5},{5,4},{6,7},{7,6},{8,9},{9,8},{10,11... | collective-permute-start | bytes 98312 | tf_op jit(solution)/shard_map/ppermute | solution.py:479
  22.8 0.8 %gradient_0.1.refs_3_ = f32[32,2048]{1,0:T(8,128)S(1)} custom-call(bf16[32,512]{1,0:T(8,128)(2,1)S(1)} %get-tuple-element.33.after_ref.refs_0_, bf16[32,512]{1,0:T(8,128)(2,1)S(1)} %get-tuple-element.35.refs_1_, bf16[512,2048]{1,0:T(8,128)(2,1)S(1)} %get-tuple-element.40.refs_2_, bf16[512,2048]{1,0:T(8,128)(2,1)S(1)} %get-tuple-element.41.refs_3_, ...), custom_call_target="tpu_custom_call" | custom-call | flops 1000000000 | bytes 10000000 | tf_op jit(solution)/shard_map/gradient_0/pallas_call | solution.py:572
  23.7 0.0 collective-permute-done.8.refs_0_
  23.7 0.5 %gradient_2.1.refs_3_ = f32[32,2048]{1,0:T(8,128)S(1)} custom-call(bf16[32,512]{1,0:T(8,128)(2,1)S(1)} %collective-permute-done.8.refs_0_, bf16[512,2048]{1,0:T(8,128)(2,1)S(1)} %get-tuple-element.38.refs_1_, f32[2,32,2048]{2,1,0:T(8,128)S(1)} %get-tuple-element.39.refs_2_, f32[32,2048]{1,0:T(8,128)S(1)} %gradient_0.1.refs_3_), custom_call_target="tpu_custom_call" | custom-call | flops 1000000000 | bytes 10000000 | tf_op jit(solution)/shard_map/gradient_2/pallas_call | solution.py:572
  24.2 0.0 collective-permute-done.7.refs_0_
  24.2 1.2 %gradient_3.1 = f32[32,2048]{1,0:T(8,128)} custom-call(bf16[32,512]{1,0:T(8,128)(2,1)S(1)} %collective-permute-done.7.refs_0_, bf16[512,2048]{1,0:T(8,128)(2,1)S(1)} %get-tuple-element.36.refs_1_, f32[2,32,2048]{2,1,0:T(8,128)S(1)} %get-tuple-element.37.refs_2_, f32[32,2048]{1,0:T(8,128)S(1)} %gradient_2.1.refs_3_), custom_call_target="tpu_custom_call" | custom-call | flops 1000000000 | bytes 10000000 | tf_op jit(solution)/shard_map/gradient_3/pallas_call | solution.py:572
  (1 shorter events, 0.0 us)
Async XLA Ops:
  4.5 8.4 %collective-permute-start = (bf16[32,1024]{1,0:T(8,128)(2,1)S(1)}, bf16[32,1024]{1,0:T(8,128)(2,1)S(1)}, u32[]{:S(2)}, u32[]{:S(2)}) collective-permute-start(bf16[32,1024]{1,0:T(8,128)(2,1)S(1)} %get-tuple-element.25.refs_0_.refs_1_), channel_id=1, source_target_pairs={{0,12},{2,14},{4,8},{6,10},{8,4},{10,6},{12,0},{14,2},{1,13},{3,15... | collective-permute-start | bytes 196616 | tf_op jit(solution)/shard_map/ppermute | solution.py:476
  9.6 5.6 %collective-permute-start.3 = (bf16[32,1024]{1,0:T(8,128)(2,1)S(1)}, bf16[32,1024]{1,0:T(8,128)(2,1)S(1)}, u32[]{:S(2)}, u32[]{:S(2)}) collective-permute-start(bf16[32,1024]{1,0:T(8,128)(2,1)S(1)} %get-tuple-element.25.refs_0_.refs_1_), channel_id=1, source_target_pairs={{0,8},{2,10},{4,12},{6,14},{8,0},{10,2},{12,4},{14,6},{1,9},{3,11}... | collective-permute-start | bytes 196616 | tf_op jit(solution)/shard_map/ppermute | solution.py:476
  9.6 5.6 %collective-permute-start.4 = (bf16[32,1024]{1,0:T(8,128)(2,1)S(1)}, bf16[32,1024]{1,0:T(8,128)(2,1)S(1)}, u32[]{:S(2)}, u32[]{:S(2)}) collective-permute-start(bf16[32,1024]{1,0:T(8,128)(2,1)S(1)} %get-tuple-element.25.refs_0_.refs_1_), channel_id=1, source_target_pairs={{0,4},{2,6},{4,0},{6,2},{8,12},{10,14},{12,8},{14,10},{1,5},{3,7},... | collective-permute-start | bytes 196616 | tf_op jit(solution)/shard_map/ppermute | solution.py:476
  10.2 6.5 %collective-permute-start.2 = (bf16[32,1024]{1,0:T(8,128)(2,1)S(1)}, bf16[32,1024]{1,0:T(8,128)(2,1)S(1)}, u32[]{:S(2)}, u32[]{:S(2)}) collective-permute-start(bf16[32,1024]{1,0:T(8,128)(2,1)S(1)} %get-tuple-element.25.refs_0_.refs_1_), channel_id=1, source_target_pairs={{0,2},{2,0},{4,6},{6,4},{8,10},{10,8},{12,14},{14,12},{1,3},{3,1},... | collective-permute-start | bytes 196616 | tf_op jit(solution)/shard_map/ppermute | solution.py:476
  11.9 4.9 %collective-permute-start.1 = (f32[2,24,256]{2,1,0:T(8,128)S(1)}, f32[2,24,256]{2,1,0:T(8,128)S(1)}, u32[]{:S(2)}, u32[]{:S(2)}) collective-permute-start(f32[2,24,256]{2,1,0:T(8,128)S(1)} %get-tuple-element.23.info_ref), channel_id=1, source_target_pairs={{0,1},{1,0},{2,3},{3,2},{4,5},{5,4},{6,7},{7,6},{8,9},{9,8},{10,11... | collective-permute-start | bytes 147464 | tf_op jit(solution)/shard_map/ppermute | solution.py:479
  12.9 7.2 %collective-permute-start.5 = (bf16[32,1024]{1,0:T(8,128)(2,1)S(1)}, bf16[32,1024]{1,0:T(8,128)(2,1)S(1)}, u32[]{:S(2)}, u32[]{:S(2)}) collective-permute-start(bf16[32,1024]{1,0:T(8,128)(2,1)S(1)} %collective-permute-done.refs_2_.refs_3_), channel_id=1, source_target_pairs={{0,2},{2,0},{4,6},{6,4},{8,10},{10,8},{12,14},{14,12},{1,3},{3,1},... | collective-permute-start | bytes 196616 | tf_op jit(solution)/shard_map/ppermute | solution.py:476
  15.2 5.1 %collective-permute-start.6 = (bf16[64,1024]{1,0:T(8,128)(2,1)S(1)}, bf16[64,1024]{1,0:T(8,128)(2,1)S(1)}, u32[]{:S(2)}, u32[]{:S(2)}) collective-permute-start(bf16[64,1024]{1,0:T(8,128)(2,1)S(1)} %join.1.refs_1_.refs_3_.refs_4_), channel_id=1, source_target_pairs={{0,2},{2,0},{4,6},{6,4},{8,10},{10,8},{12,14},{14,12},{1,3},{3,1},... | collective-permute-start | bytes 393224 | tf_op jit(solution)/shard_map/ppermute | solution.py:476
  21.2 2.5 %collective-permute-start.8 = (bf16[32,512]{1,0:T(8,128)(2,1)S(1)}, bf16[32,512]{1,0:T(8,128)(2,1)S(1)}, u32[]{:S(2)}, u32[]{:S(2)}) collective-permute-start(bf16[32,512]{1,0:T(8,128)(2,1)S(1)} %get-tuple-element.33.after_ref.refs_0_), channel_id=1, source_target_pairs={{0,1},{1,0},{2,3},{3,2},{4,5},{5,4},{6,7},{7,6},{8,9},{9,8},{10,11... | collective-permute-start | bytes 98312 | tf_op jit(solution)/shard_map/ppermute | solution.py:479
  22.2 1.9 %collective-permute-start.7 = (bf16[32,512]{1,0:T(8,128)(2,1)S(1)}, bf16[32,512]{1,0:T(8,128)(2,1)S(1)}, u32[]{:S(2)}, u32[]{:S(2)}) collective-permute-start(bf16[32,512]{1,0:T(8,128)(2,1)S(1)} %get-tuple-element.35.refs_1_), channel_id=1, source_target_pairs={{0,1},{1,0},{2,3},{3,2},{4,5},{5,4},{6,7},{7,6},{8,9},{9,8},{10,11... | collective-permute-start | bytes 98312 | tf_op jit(solution)/shard_map/ppermute | solution.py:479

commit v16 on v13

--- a/solution.py
+++ b/solution.py
@@ -120,19 +120,16 @@
     return [outs[2 * pair : 2 * pair + 2] for pair in range(pairs)]
 
 
-def near_slopes(s, coef_ref, pairs):
+def near_slopes(s, power_ref, pairs):
     s = split_rows(s)
-    twice = s + s
-    before, current = jnp.ones_like(s), twice
-    outs = [
-        [coef_ref[pair, row] + coef_ref[pair, row + 1] * twice for row in (1, TERMS + 1)] for pair in range(pairs)
-    ]
-    for order in range(3, TERMS):
-        before, current = current, twice * current - before
-        for pair, out in enumerate(outs):
-            out[0] = out[0] + coef_ref[pair, order] * current
-            out[1] = out[1] + coef_ref[pair, TERMS + order] * current
-    return [[join_rows(part) for part in out] for out in outs]
+    outs = []
+    for pair, part in itertools.product(range(pairs), range(2)):
+        row = (part + 1) * TERMS - 1
+        value = power_ref[pair, row] * s + power_ref[pair, row - 1]
+        for row in range(row - 2, part * TERMS, -1):
+            value = value * s + power_ref[pair, row]
+        outs.append(join_rows(value))
+    return [outs[2 * pair : 2 * pair + 2] for pair in range(pairs)]
 
 
 def turn_round(value):
@@ -164,10 +161,9 @@
     wave_hbm, angle_hbm, aim_hbm, coef_hbm, width_hbm, mine_ref, info_ref, own_ref, *refs
 ):
     pairs = info_ref.shape[0]
-    table_refs, refs = refs[:pairs], refs[pairs:]
     (
-        wave_ref, angle_ref, aim_ref, coef_ref, width_ref, far_ref, base_ref, centre_ref, power_ref, near_ref, acc_ref,
-        sems,
+        wave_ref, angle_ref, aim_ref, coef_ref, width_ref, far_ref, base_ref, centre_ref, power_ref, near_ref, table_ref,
+        acc_ref, sems,
     ) = refs
     rows_dev, cols = width_ref.shape
     half = cols // 2
@@ -221,11 +217,11 @@
                 base_r, base_i = (base_ref[pair, part, row : row + GRAIN, :] for part in range(2))
                 for start, table in zip(starts, both_blocks(base_r, base_i, cent_r, cent_i)):
                     rows = slice(start + row, start + row + GRAIN)
-                    table_refs[pair][rows, :FOCAL] = table[0].astype(jnp.bfloat16)
-                    table_refs[pair][rows, FOCAL:] = table[1].astype(jnp.bfloat16)
+                    table_ref[pair, rows, :FOCAL] = table[0].astype(jnp.bfloat16)
+                    table_ref[pair, rows, FOCAL:] = table[1].astype(jnp.bfloat16)
             product = jnp.dot(
                 jnp.concatenate([near_ref[pair, :, start : start + BLOCK] for start in starts], axis=1),
-                jnp.concatenate([table_refs[pair][start : start + BLOCK, :] for start in starts], axis=0),
+                jnp.concatenate([table_ref[pair, start : start + BLOCK, :] for start in starts], axis=0),
                 preferred_element_type=jnp.float32,
             )
             acc_ref[pair] = product if index == 0 else acc_ref[pair] + product
@@ -340,7 +336,7 @@
     for pair, (spot_power, all_power) in enumerate(sums):
         ratio = spot_power / all_power
         gain = gain_ref[pair, :1, :1]
-        score_ref[pair] = jnp.sum(ratio * gain)
+        score_ref[pair] = jnp.broadcast_to(ratio * gain, score_ref.shape[1:])
         scale = gain * 2.0 / all_power
         for rows in pieces:
             lower = slice(rows.start + FOCAL, rows.stop + FOCAL)
@@ -357,19 +353,17 @@
 
 
 def table_kernel(scale, cols, info_ref, far_info_ref, width_ref, *refs):
-    *out_refs, base_ref, centre_ref, turned_ref, coef_ref = refs
-    pairs = base_ref.shape[0]
-    out_refs = out_refs[-3 * pairs :]
+    *out_refs, base_ref, centre_ref, turned_ref, power_ref = refs
+    pairs = power_ref.shape[0]
+    out_refs = out_refs[-2 * pairs :]
     table_refs, slope_refs = out_refs[:pairs], out_refs[pairs:]
     own_cols = width_ref.shape[1]
-    for core, ref in enumerate((info_ref, far_info_ref)):
-        for pair in range(pairs):
-            coef = ref[pair, : 2 * TERMS, :LANES]
-            coef = coef * ((iota(coef.shape, 0) % TERMS).astype(jnp.float32) * scale)
-            coef_ref[core * pairs + pair] = as_tiles(coef)
+    sources = [(ref, pair) for ref in (info_ref, far_info_ref) for pair in range(pairs // 2)]
     centres = []
-    for pair in range(pairs):
-        own_waves(far_info_ref, pair, cols, base_ref.at[pair], centre_ref.at[pair])
+    for pair, (ref, source) in enumerate(sources):
+        power = power_coefs(ref[source, : 2 * TERMS, :LANES])
+        power_ref[pair] = as_tiles(power * ((iota(power.shape, 0) % TERMS).astype(jnp.float32) * scale))
+        own_waves(ref, source, cols, base_ref.at[pair], centre_ref.at[pair])
         for part, row, lane in itertools.product(range(2), range(0, BLOCK, LANES), range(0, FOCAL, LANES)):
             tile = base_ref[pair, part, row : row + LANES, lane : lane + LANES]
             turned_ref[pair, part, lane : lane + LANES, row : row + LANES] = tile.T
@@ -387,20 +381,27 @@
                         table_refs[pair][place, start : start + BLOCK] = value.astype(jnp.bfloat16)
         for start in (start + step for start in starts for step in range(0, BLOCK, LANES)):
             place = slice(start, start + LANES)
-            slopes = near_slopes(width_ref[:, place], coef_ref, 2 * pairs)
+            slopes = near_slopes(width_ref[:, place], power_ref, pairs)
             for ref, slope in zip(slope_refs, slopes):
                 ref[0, :, place] = slope[0]
                 ref[1, :, place] = slope[1]
 
 
-def last_grad_kernel(pairs, *refs):
-    *in_refs, out_hbm, out_ref, sems = refs
-    rows_dev, own_cols = out_ref.shape
-    size = 2 * BLOCK
+def own_grad_kernel(*refs):
+    *in_refs, tile_ref, out_ref, score_ref = refs
+    for pair in range(score_ref.shape[0]):
+        score_ref[pair] = jnp.sum(tile_ref[pair, :1, :1])
+    add_grads(in_refs, None, out_ref, 2 * BLOCK)
+
+
+def last_grad_kernel(*refs):
+    *in_refs, total_ref, out_hbm, out_ref, sems = refs
+    own_cols = out_ref.shape[1]
     core = lax.axis_index("wave")
     moves = []
 
     def send(start, total):
+        size = total.shape[1]
         place = pl.multiple_of(jnp.where(core == 1, start, own_cols - size - start), size)
         place = pl.ds(place, size)
         out_ref[:, place] = jnp.where(core == 1, total, turn_round(total))
@@ -408,14 +409,15 @@
         moves.append(pltpu.make_async_copy(out_ref.at[:, place], out_hbm.at[:, place], sems.at[index]))
         moves[-1].start()
 
-    grad_kernel(pairs, *in_refs, out_ref, send=send)
+    add_grads(in_refs, total_ref, out_ref, BLOCK, send)
     for move in moves:
         move.wait()
 
 
-def grad_kernel(pairs, back_ref, *refs, send=None, across=True):
-    *in_refs, out_ref = refs
-    table_refs, slope_refs, total_ref = in_refs[:pairs], in_refs[pairs : 2 * pairs], in_refs[2 * pairs :]
+def add_grads(in_refs, total_ref, out_ref, size, send=None):
+    back_ref, *in_refs = in_refs
+    pairs = len(in_refs) // 2
+    table_refs, slope_refs = in_refs[:pairs], in_refs[pairs:]
     rows_dev, own_cols = out_ref.shape
     core = lax.axis_index("wave")
     lefts = []
@@ -429,18 +431,13 @@
                 [jnp.concatenate([real, above], axis=1), jnp.concatenate([imag, below], axis=1)], axis=0
             )
         )
-    size = 2 * BLOCK
     for start in range(0, own_cols, size):
         place = slice(start, start + size)
-        total = total_ref[0][:, place] if total_ref else jnp.zeros((rows_dev, size), jnp.float32)
-        for pair in range(pairs):
-            if across:
-                table, dims = table_refs[pair][:, place], ((1,), (0,))
-            else:
-                table, dims = table_refs[pair][place, :], ((1,), (1,))
-            grad = lax.dot_general(lefts[pair], table, (dims, ((), ())), preferred_element_type=jnp.float32)
-            total += grad[:rows_dev] * slope_refs[pair][0, :, place]
-            total += grad[rows_dev:] * slope_refs[pair][1, :, place]
+        total = jnp.zeros((rows_dev, size), jnp.float32) if total_ref is None else total_ref[:, place]
+        for left, table_ref, slope_ref in zip(lefts, table_refs, slope_refs):
+            grad = jnp.dot(left, table_ref[:, place], preferred_element_type=jnp.float32)
+            total += grad[:rows_dev] * slope_ref[0, :, place]
+            total += grad[rows_dev:] * slope_ref[1, :, place]
         if send is None:
             out_ref[:, place] = total
         else:
@@ -472,6 +469,7 @@
     peers = lax.axis_size("aperture")
     copies = lax.axis_size("wave")
     rows = rows_dev * peers
+    pairs = pairs_dev * copies
     own_cols = cols // copies
     lanes = 2 * pairs_dev * FOCAL
     f32, bf16 = jnp.float32, jnp.bfloat16
@@ -490,14 +488,13 @@
         pltpu.VMEM((pairs_dev, 2, BLOCK, FOCAL), f32),
         pltpu.VMEM((pairs_dev, 2, 8, FOCAL), f32),
     ]
-    mine, info, own, *tables = call(
+    mine, info, own = call(
         forward_kernel, "forward",
         (
             shape((rows_dev, lanes), bf16),
             shape((pairs_dev, INFO_ROWS, FOCAL), f32), shape((rows_dev, own_cols), f32),
-            *[shape((own_cols, 2 * FOCAL), bf16)] * pairs_dev,
         ),
-        [HBM] * 5, (VMEM,) * (3 + pairs_dev),
+        [HBM] * 5, (VMEM,) * 3,
         [
             pltpu.SMEM(wave_ids.shape, jnp.int32),
             pltpu.SMEM(angle_ids.shape, jnp.int32),
@@ -508,6 +505,7 @@
             *waves,
             pltpu.VMEM((pairs_dev, 2 * TERMS, SUBLANES, LANES), f32),
             pltpu.VMEM((pairs_dev, 4 * rows_dev, own_cols), bf16),
+            pltpu.VMEM((pairs_dev, own_cols, 2 * FOCAL), bf16),
             pltpu.VMEM((pairs_dev, 4 * rows_dev, 2 * FOCAL), f32),
             pltpu.SemaphoreType.DMA((5,)),
         ],
@@ -537,19 +535,24 @@
         blocks = jnp.tile(mine[None], (peers, 1, 1))
         blocks = lax.all_to_all(blocks, "aperture", 0, 0, tiled=True)
         sections, steps, after = [blocks.reshape(rows, lanes)], None, []
-    outs = [shape((2 * FOCAL, own_cols), bf16)] * pairs_dev + [shape((2, rows_dev, own_cols), f32)] * 2 * pairs_dev
+    outs = [shape((2 * FOCAL, own_cols), bf16)] * pairs + [shape((2, rows_dev, own_cols), f32)] * pairs
     made = call(
-        functools.partial(table_kernel, math.sqrt(rows * cols), cols), "far_tables",
+        functools.partial(table_kernel, math.sqrt(rows * cols), cols), "column_tables",
         outs, [VMEM] * 3 + [ANY] * len(after), [VMEM] * len(outs),
-        [*waves, pltpu.VMEM((pairs_dev, 2, FOCAL, BLOCK), f32), pltpu.VMEM((copies * pairs_dev, 2 * TERMS, SUBLANES, LANES), f32)],
+        [
+            pltpu.VMEM((pairs, 2, BLOCK, FOCAL), f32),
+            pltpu.VMEM((pairs, 2, 8, FOCAL), f32),
+            pltpu.VMEM((pairs, 2, FOCAL, BLOCK), f32),
+            pltpu.VMEM((pairs, 2 * TERMS, SUBLANES, LANES), f32),
+        ],
         30 * 10**8, 30 * 10**6,
     )(info, far_info, own, *after)
-    far_tables, slopes, far_slopes = made[:pairs_dev], made[pairs_dev : 2 * pairs_dev], made[2 * pairs_dev :]
+    tables, slopes = made[:pairs], made[pairs:]
 
     back, scores = call(
         functools.partial(focus_kernel, steps), "focus",
-        (shape((rows_dev, lanes), bf16), shape((pairs_dev,), f32)),
-        [VMEM] * 4 + [ANY] + [VMEM] * len(sections), (VMEM, SMEM),
+        (shape((rows_dev, lanes), bf16), shape((pairs_dev, SUBLANES, LANES), f32)),
+        [VMEM] * 4 + [ANY] + [VMEM] * len(sections), (VMEM, VMEM),
         [
             pltpu.VMEM((rows, lanes), bf16),
             pltpu.VMEM((pairs_dev, 2 * FOCAL, 2 * FOCAL), f32),
@@ -557,19 +560,18 @@
             pltpu.VMEM((pairs_dev, 2 * FOCAL, 2 * FOCAL), bf16),
         ],
         10**8, 10**6,
-    )(tall, flat, spots, gains, far_slopes[0], *sections)
+    )(tall, flat, spots, gains, slopes[0], *sections)
 
     out = shape((rows_dev, own_cols), f32)
-    ins = [back, *tables, *slopes]
+    ins = [back, *tables[:pairs_dev], *slopes[:pairs_dev], scores]
+    grad, scores = call(
+        own_grad_kernel, "gradient_own", (out, shape((pairs_dev,), f32)),
+        [VMEM] * len(ins), (VMEM, SMEM), [], 10**9, 10**7,
+    )(*ins)
+    ins = [to_core(back), *tables[pairs_dev:], *slopes[pairs_dev:], grad]
     grad = call(
-        functools.partial(grad_kernel, pairs_dev, across=False), "gradient_own",
-        out, [VMEM] * len(ins), VMEM, [], 10**9, 10**7,
-    )(*ins)
-    ins = [to_core(back), *far_tables, *far_slopes, grad]
-    grad = call(
-        functools.partial(last_grad_kernel, pairs_dev), "gradient_far",
-        out, [VMEM] * len(ins), HBM,
-        [pltpu.VMEM(out.shape, f32), pltpu.SemaphoreType.DMA((own_cols // (2 * BLOCK),))], 10**9, 10**7,
+        last_grad_kernel, "gradient_far", out, [VMEM] * len(ins), HBM,
+        [pltpu.VMEM(out.shape, f32), pltpu.SemaphoreType.DMA((own_cols // BLOCK,))], 10**9, 10**7,
     )(*ins)
     return grad, scores
 

time: 25 us -> 24.7 us (0.988)
  waiting for transfers between devices: 2.35 us -> 1.4 us
  Pallas kernels: 11.6 us -> 12.3 us
    ppermute x6, waiting for transfers between devices: 2.35 us -> 1.39 us  [exchange(): lax.ppermute(value, 'aperture', [(index, index ^ step) for index in range...]
    pallas_call x3, Pallas kernels: 5.38 us -> 6.3 us  [the longest x1 3.33 us: on_device(): call(functools.partial(table_kernel, math.sqrt(rows * cols), cols), 'colu...]
  transfers between devices with their start and end apart: 8 -> 8, of which waited for: 2 -> 2; matrix products, arithmetic and copies ran while one was open for 0% -> 0% of each run, Pallas kernels for 19% -> 23%
where the time goes in v16:
time: 24.7 us; the launch traced here: 24.5 us
  Pallas kernels  12.3 us (50%)
  starting transfers between devices  10.1 us (41%)
  waiting for transfers between devices  1.4 us (6%)
  between operations  0.7 us (3%)
    ppermute x6, starting transfers between devices, exchange(): lax.ppermute(value, 'aperture', [(index, index ^ step) for index in range...  10 us
    pallas_call x1, Pallas kernels, on_device(): call(forward_kernel, 'forward', (shape((rows_dev, lanes), bf16), shape((p...  3.84 us
    pallas_call x1, Pallas kernels, on_device(): call(functools.partial(table_kernel, math.sqrt(rows * cols), cols), 'colu...  3.33 us
    pallas_call x1, Pallas kernels, on_device(): call(last_grad_kernel, 'gradient_far', out, [VMEM] * len(ins), HBM, [pltp...  1.68 us
    ppermute x6, waiting for transfers between devices, exchange(): lax.ppermute(value, 'aperture', [(index, index ^ step) for index in range...  1.39 us
    pallas_call x1, Pallas kernels, on_device(): call(own_grad_kernel, 'gradient_own', (out, shape((pairs_dev,), f32)), [V...  1.28 us
    pallas_call x1, Pallas kernels, on_device(): call(functools.partial(focus_kernel, steps), 'focus', (shape((rows_dev, l...  1.07 us
    pallas_call x1, Pallas kernels, on_device(): call(row_kernel, 'row_tables', (shape((pairs_dev, 2 * FOCAL, rows), bf16)...  1.04 us
  transfers between devices with their start and end apart: 8, of which 2 were waited for; matrix products, arithmetic and copies ran while one was open for 0% of the time, Pallas kernels for 23%

profile of v16, /device:TPU:0, one launch (start us, length us, event | category | flops | bytes accessed | tf_op | source)
XLA Modules:
  0.0 24.5 jit_solution(15333800412431363550)
XLA Ops:
  0.6 3.8 %forward.1 = (bf16[32,1024]{1,0:T(8,128)(2,1)S(1)}, f32[2,24,256]{2,1,0:T(8,128)S(1)}, f32[32,2048]{1,0:T(8,128)S(1)}) custom-call(s32[2]{0:T(128)} %wave_hbm.1, s32[2]{0:T(128)} %angle_hbm.1, s32[2,2]{1,0:T(2,128)} %aim_hbm.1, f32[16,256]{1,0:T(8,128)} %bitcast.1, f32[32,4096]{1,0:T(8,128)} %width_hbm.1), custom_call_target="tpu_custom_call" | custom-call | flops 1000000000 | bytes 10000000 | tf_op jit(solution)/shard_map/forward/pallas_call | solution.py:491
  4.5 5.1 %collective-permute-start = (bf16[32,1024]{1,0:T(8,128)(2,1)S(1)}, bf16[32,1024]{1,0:T(8,128)(2,1)S(1)}, u32[]{:S(2)}, u32[]{:S(2)}) collective-permute-start(bf16[32,1024]{1,0:T(8,128)(2,1)S(1)} %get-tuple-element.25.refs_0_), channel_id=1, source_target_pairs={{0,12},{2,14},{4,8},{6,10},{8,4},{10,6},{12,0},{14,2},{1,13},{3,15... | collective-permute-start | bytes 196616 | tf_op jit(solution)/shard_map/ppermute | solution.py:482
  9.6 0.0 collective-permute-start.3
  9.6 0.6 %collective-permute-start.4 = (bf16[32,1024]{1,0:T(8,128)(2,1)S(1)}, bf16[32,1024]{1,0:T(8,128)(2,1)S(1)}, u32[]{:S(2)}, u32[]{:S(2)}) collective-permute-start(bf16[32,1024]{1,0:T(8,128)(2,1)S(1)} %get-tuple-element.25.refs_0_), channel_id=1, source_target_pairs={{0,4},{2,6},{4,0},{6,2},{8,12},{10,14},{12,8},{14,10},{1,5},{3,7},... | collective-permute-start | bytes 196616 | tf_op jit(solution)/shard_map/ppermute | solution.py:482
  10.2 1.6 %collective-permute-start.2 = (bf16[32,1024]{1,0:T(8,128)(2,1)S(1)}, bf16[32,1024]{1,0:T(8,128)(2,1)S(1)}, u32[]{:S(2)}, u32[]{:S(2)}) collective-permute-start(bf16[32,1024]{1,0:T(8,128)(2,1)S(1)} %get-tuple-element.25.refs_0_), channel_id=1, source_target_pairs={{0,2},{2,0},{4,6},{6,4},{8,10},{10,8},{12,14},{14,12},{1,3},{3,1},... | collective-permute-start | bytes 196616 | tf_op jit(solution)/shard_map/ppermute | solution.py:482
  11.9 0.0 collective-permute-start.1
  11.9 1.0 %row_tables.1 = (bf16[2,512,256]{2,1,0:T(8,128)(2,1)S(1)}, bf16[2,32,512]{2,1,0:T(8,128)(2,1)S(1)}, f32[2,256,256]{2,1,0:T(8,128)S(1)}, f32[2,8,128]{2,1,0:T(8,128)S(1)}) custom-call(f32[2,24,256]{2,1,0:T(8,128)S(1)} %get-tuple-element.23.info_ref), custom_call_target="tpu_custom_call" | custom-call | flops 100000000 | bytes 1000000 | tf_op jit(solution)/shard_map/row_tables/pallas_call | solution.py:516
  12.9 0.0 collective-permute-done.refs_2_
  12.9 1.1 %collective-permute-start.5 = (bf16[32,1024]{1,0:T(8,128)(2,1)S(1)}, bf16[32,1024]{1,0:T(8,128)(2,1)S(1)}, u32[]{:S(2)}, u32[]{:S(2)}) collective-permute-start(bf16[32,1024]{1,0:T(8,128)(2,1)S(1)} %collective-permute-done.refs_2_), channel_id=1, source_target_pairs={{0,2},{2,0},{4,6},{6,4},{8,10},{10,8},{12,14},{14,12},{1,3},{3,1},... | collective-permute-start | bytes 196616 | tf_op jit(solution)/shard_map/ppermute | solution.py:482
  14.0 1.2 %collective-permute-done.3.refs_0_ = bf16[32,1024]{1,0:T(8,128)(2,1)S(1)} collective-permute-done((bf16[32,1024]{1,0:T(8,128)(2,1)S(1)}, bf16[32,1024]{1,0:T(8,128)(2,1)S(1)}, u32[]{:S(2)}, u32[]{:S(2)}) %collective-permute-start.3) | collective-permute-done | bytes 65568 | tf_op jit(solution)/shard_map/ppermute | solution.py:482
  15.2 0.0 collective-permute-done.4.refs_1_
  15.2 1.6 %collective-permute-start.6 = (bf16[64,1024]{1,0:T(8,128)(2,1)S(1)}, bf16[64,1024]{1,0:T(8,128)(2,1)S(1)}, u32[]{:S(2)}, u32[]{:S(2)}) collective-permute-start(bf16[64,1024]{1,0:T(8,128)(2,1)S(1)} %join.1.refs_1_.refs_3_), channel_id=1, source_target_pairs={{0,2},{2,0},{4,6},{6,4},{8,10},{10,8},{12,14},{14,12},{1,3},{3,1},... | collective-permute-start | bytes 393224 | tf_op jit(solution)/shard_map/ppermute | solution.py:482
  16.8 0.0 collective-permute-done.1.far_info_ref
  16.8 0.0 collective-permute-done.2.refs_0_.refs_1_
  16.8 3.3 %column_tables.1 = (bf16[512,2048]{1,0:T(8,128)(2,1)S(1)}, bf16[512,2048]{1,0:T(8,128)(2,1)S(1)}, bf16[512,2048]{1,0:T(8,128)(2,1)S(1)}, bf16[512,2048]{1,0:T(8,...) custom-call(f32[2,24,256]{2,1,0:T(8,128)S(1)} %get-tuple-element.23., ...), custom_call_target="tpu_custom_call" | custom-call | flops 3000000000 | bytes 30000000 | tf_op jit(solution)/shard_map/column_tables/pallas_call | solution.py:539
  20.1 0.0 collective-permute-done.5.refs_4_
  20.1 0.2 collective-permute-done.6.refs_5_
  20.3 1.1 %focus.1 = (bf16[32,1024]{1,0:T(8,128)(2,1)S(1)}, f32[2,8,128]{2,1,0:T(8,128)S(1)}) custom-call(bf16[2,512,256]{2,1,0:T(8,128)(2,1)S(1)} %get-tuple-element.24.tall_ref, bf16[2,32,512]{2,1,0:T(8,128)(2,1)S(1)} %get-tuple-element.27.flat_ref, f32[2,256,256]{2,1,0:T(8,128)S(1)} %get-tuple-element.28.spot_ref, f32[2,8,128]{2,1,0:T(8,128)S(1)} %get-tuple-element.29.gain_ref, ...), custom_call_target="tpu_custom_call" | custom-call | flops 100000000 | bytes 1000000 | tf_op jit(solution)/shard_map/focus/pallas_call | solution.py:552
  21.4 0.1 collective-permute-start.7
  21.5 1.3 %gradient_own.1 = (f32[32,2048]{1,0:T(8,128)S(1)}, f32[2]{0:T(128)}) custom-call(bf16[32,1024]{1,0:T(8,128)(2,1)S(1)} %get-tuple-element.33.refs_0_, bf16[512,2048]{1,0:T(8,128)(2,1)S(1)} %get-tuple-element.38.refs_1_, bf16[512,2048]{1,0:T(8,128)(2,1)S(1)} %get-tuple-element.39.refs_2_, f32[2,32,2048]{2,1,0:T(8,128)S(1)} %get-tuple-element.31.after_ref.refs_3_, ...), custom_call_target="tpu_custom_call" | custom-call | flops 1000000000 | bytes 10000000 | tf_op jit(solution)/shard_map/gradient_own/pallas_call | solution.py:567
  22.8 0.0 collective-permute-done.7.refs_0_
  22.8 1.7 %gradient_far.1 = f32[32,2048]{1,0:T(8,128)} custom-call(bf16[32,1024]{1,0:T(8,128)(2,1)S(1)} %collective-permute-done.7.refs_0_, bf16[512,2048]{1,0:T(8,128)(2,1)S(1)} %get-tuple-element.34.refs_1_, bf16[512,2048]{1,0:T(8,128)(2,1)S(1)} %get-tuple-element.35.refs_2_, f32[2,32,2048]{2,1,0:T(8,128)S(1)} %get-tuple-element.36.refs_3_, ...), custom_call_target="tpu_custom_call" | custom-call | flops 1000000000 | bytes 10000000 | tf_op jit(solution)/shard_map/gradient_far/pallas_call | solution.py:572
  (1 shorter events, 0.0 us)
Async XLA Ops:
  4.5 8.4 %collective-permute-start = (bf16[32,1024]{1,0:T(8,128)(2,1)S(1)}, bf16[32,1024]{1,0:T(8,128)(2,1)S(1)}, u32[]{:S(2)}, u32[]{:S(2)}) collective-permute-start(bf16[32,1024]{1,0:T(8,128)(2,1)S(1)} %get-tuple-element.25.refs_0_), channel_id=1, source_target_pairs={{0,12},{2,14},{4,8},{6,10},{8,4},{10,6},{12,0},{14,2},{1,13},{3,15... | collective-permute-start | bytes 196616 | tf_op jit(solution)/shard_map/ppermute | solution.py:482
  9.6 5.6 %collective-permute-start.3 = (bf16[32,1024]{1,0:T(8,128)(2,1)S(1)}, bf16[32,1024]{1,0:T(8,128)(2,1)S(1)}, u32[]{:S(2)}, u32[]{:S(2)}) collective-permute-start(bf16[32,1024]{1,0:T(8,128)(2,1)S(1)} %get-tuple-element.25.refs_0_), channel_id=1, source_target_pairs={{0,8},{2,10},{4,12},{6,14},{8,0},{10,2},{12,4},{14,6},{1,9},{3,11}... | collective-permute-start | bytes 196616 | tf_op jit(solution)/shard_map/ppermute | solution.py:482
  9.6 5.6 %collective-permute-start.4 = (bf16[32,1024]{1,0:T(8,128)(2,1)S(1)}, bf16[32,1024]{1,0:T(8,128)(2,1)S(1)}, u32[]{:S(2)}, u32[]{:S(2)}) collective-permute-start(bf16[32,1024]{1,0:T(8,128)(2,1)S(1)} %get-tuple-element.25.refs_0_), channel_id=1, source_target_pairs={{0,4},{2,6},{4,0},{6,2},{8,12},{10,14},{12,8},{14,10},{1,5},{3,7},... | collective-permute-start | bytes 196616 | tf_op jit(solution)/shard_map/ppermute | solution.py:482
  10.2 6.5 %collective-permute-start.2 = (bf16[32,1024]{1,0:T(8,128)(2,1)S(1)}, bf16[32,1024]{1,0:T(8,128)(2,1)S(1)}, u32[]{:S(2)}, u32[]{:S(2)}) collective-permute-start(bf16[32,1024]{1,0:T(8,128)(2,1)S(1)} %get-tuple-element.25.refs_0_), channel_id=1, source_target_pairs={{0,2},{2,0},{4,6},{6,4},{8,10},{10,8},{12,14},{14,12},{1,3},{3,1},... | collective-permute-start | bytes 196616 | tf_op jit(solution)/shard_map/ppermute | solution.py:482
  11.9 4.9 %collective-permute-start.1 = (f32[2,24,256]{2,1,0:T(8,128)S(1)}, f32[2,24,256]{2,1,0:T(8,128)S(1)}, u32[]{:S(2)}, u32[]{:S(2)}) collective-permute-start(f32[2,24,256]{2,1,0:T(8,128)S(1)} %get-tuple-element.23.info_ref), channel_id=1, source_target_pairs={{0,1},{1,0},{2,3},{3,2},{4,5},{5,4},{6,7},{7,6},{8,9},{9,8},{10,11... | collective-permute-start | bytes 147464 | tf_op jit(solution)/shard_map/ppermute | solution.py:485
  12.9 7.2 %collective-permute-start.5 = (bf16[32,1024]{1,0:T(8,128)(2,1)S(1)}, bf16[32,1024]{1,0:T(8,128)(2,1)S(1)}, u32[]{:S(2)}, u32[]{:S(2)}) collective-permute-start(bf16[32,1024]{1,0:T(8,128)(2,1)S(1)} %collective-permute-done.refs_2_), channel_id=1, source_target_pairs={{0,2},{2,0},{4,6},{6,4},{8,10},{10,8},{12,14},{14,12},{1,3},{3,1},... | collective-permute-start | bytes 196616 | tf_op jit(solution)/shard_map/ppermute | solution.py:482
  15.2 5.1 %collective-permute-start.6 = (bf16[64,1024]{1,0:T(8,128)(2,1)S(1)}, bf16[64,1024]{1,0:T(8,128)(2,1)S(1)}, u32[]{:S(2)}, u32[]{:S(2)}) collective-permute-start(bf16[64,1024]{1,0:T(8,128)(2,1)S(1)} %join.1.refs_1_.refs_3_), channel_id=1, source_target_pairs={{0,2},{2,0},{4,6},{6,4},{8,10},{10,8},{12,14},{14,12},{1,3},{3,1},... | collective-permute-start | bytes 393224 | tf_op jit(solution)/shard_map/ppermute | solution.py:482
  21.4 1.4 %collective-permute-start.7 = (bf16[32,1024]{1,0:T(8,128)(2,1)S(1)}, bf16[32,1024]{1,0:T(8,128)(2,1)S(1)}, u32[]{:S(2)}, u32[]{:S(2)}) collective-permute-start(bf16[32,1024]{1,0:T(8,128)(2,1)S(1)} %get-tuple-element.33.refs_0_), channel_id=1, source_target_pairs={{0,1},{1,0},{2,3},{3,2},{4,5},{5,4},{6,7},{7,6},{8,9},{9,8},{10,11... | collective-permute-start | bytes 196616 | tf_op jit(solution)/shard_map/ppermute | solution.py:485

commit v17 on v16

--- a/solution.py
+++ b/solution.py
@@ -167,12 +167,12 @@
     ) = refs
     rows_dev, cols = width_ref.shape
     half = cols // 2
+    copies = [(wave_hbm, wave_ref), (angle_hbm, angle_ref), (aim_hbm, aim_ref), (coef_hbm, coef_ref)]
+    for row in range(0, rows_dev, SUBLANES):
+        place = slice(row, row + SUBLANES)
+        copies.append((width_hbm.at[place, :], width_ref.at[place, :]))
     moves = [
-        pltpu.make_async_copy(source, target, sems.at[index])
-        for index, (source, target) in enumerate((
-            (wave_hbm, wave_ref), (angle_hbm, angle_ref), (aim_hbm, aim_ref),
-            (coef_hbm, coef_ref), (width_hbm, width_ref),
-        ))
+        pltpu.make_async_copy(source, target, sems.at[index]) for index, (source, target) in enumerate(copies)
     ]
     for move in moves:
         move.start()
@@ -388,10 +388,13 @@
 
 
 def own_grad_kernel(*refs):
-    *in_refs, tile_ref, out_ref, score_ref = refs
+    *in_refs, tile_ref, out_ref, score_hbm, score_ref, sem = refs
     for pair in range(score_ref.shape[0]):
         score_ref[pair] = jnp.sum(tile_ref[pair, :1, :1])
+    move = pltpu.make_async_copy(score_ref, score_hbm, sem)
+    move.start()
     add_grads(in_refs, None, out_ref, 2 * BLOCK)
+    move.wait()
 
 
 def last_grad_kernel(*refs):
@@ -409,7 +412,7 @@
         moves.append(pltpu.make_async_copy(out_ref.at[:, place], out_hbm.at[:, place], sems.at[index]))
         moves[-1].start()
 
-    add_grads(in_refs, total_ref, out_ref, BLOCK, send)
+    add_grads(in_refs, total_ref, out_ref, 2 * BLOCK, send)
     for move in moves:
         move.wait()
 
@@ -507,7 +510,7 @@
             pltpu.VMEM((pairs_dev, 4 * rows_dev, own_cols), bf16),
             pltpu.VMEM((pairs_dev, own_cols, 2 * FOCAL), bf16),
             pltpu.VMEM((pairs_dev, 4 * rows_dev, 2 * FOCAL), f32),
-            pltpu.SemaphoreType.DMA((5,)),
+            pltpu.SemaphoreType.DMA((4 + rows_dev // SUBLANES,)),
         ],
         10**9, 10**7,
     )(*(in_hbm(value) for value in (wave_ids, angle_ids, targets, coef_table.T, widths)))
@@ -566,12 +569,13 @@
     ins = [back, *tables[:pairs_dev], *slopes[:pairs_dev], scores]
     grad, scores = call(
         own_grad_kernel, "gradient_own", (out, shape((pairs_dev,), f32)),
-        [VMEM] * len(ins), (VMEM, SMEM), [], 10**9, 10**7,
+        [VMEM] * len(ins), (VMEM, HBM),
+        [pltpu.SMEM((pairs_dev,), f32), pltpu.SemaphoreType.DMA], 10**9, 10**7,
     )(*ins)
     ins = [to_core(back), *tables[pairs_dev:], *slopes[pairs_dev:], grad]
     grad = call(
         last_grad_kernel, "gradient_far", out, [VMEM] * len(ins), HBM,
-        [pltpu.VMEM(out.shape, f32), pltpu.SemaphoreType.DMA((own_cols // BLOCK,))], 10**9, 10**7,
+        [pltpu.VMEM(out.shape, f32), pltpu.SemaphoreType.DMA((own_cols // (2 * BLOCK),))], 10**9, 10**7,
     )(*ins)
     return grad, scores
 

time: 24.7 us -> 24.7 us (level)
  no operation moved by 1% of the time
where the time goes in v17:
time: 24.7 us; the launch traced here: 24.5 us
  Pallas kernels  12.3 us (50%)
  starting transfers between devices  10.1 us (41%)
  waiting for transfers between devices  1.4 us (6%)
  between operations  0.7 us (3%)
    ppermute x6, starting transfers between devices, exchange(): lax.ppermute(value, 'aperture', [(index, index ^ step) for index in range...  10 us
    pallas_call x1, Pallas kernels, on_device(): call(forward_kernel, 'forward', (shape((rows_dev, lanes), bf16), shape((p...  3.91 us
    pallas_call x1, Pallas kernels, on_device(): call(functools.partial(table_kernel, math.sqrt(rows * cols), cols), 'colu...  3.33 us
    pallas_call x1, Pallas kernels, on_device(): call(last_grad_kernel, 'gradient_far', out, [VMEM] * len(ins), HBM, [pltp...  1.62 us
    ppermute x6, waiting for transfers between devices, exchange(): lax.ppermute(value, 'aperture', [(index, index ^ step) for index in range...  1.39 us
    pallas_call x1, Pallas kernels, on_device(): call(own_grad_kernel, 'gradient_own', (out, shape((pairs_dev,), f32)), [V...  1.29 us
    pallas_call x1, Pallas kernels, on_device(): call(functools.partial(focus_kernel, steps), 'focus', (shape((rows_dev, l...  1.06 us
    pallas_call x1, Pallas kernels, on_device(): call(row_kernel, 'row_tables', (shape((pairs_dev, 2 * FOCAL, rows), bf16)...  1.04 us
  transfers between devices with their start and end apart: 8, of which 2 were waited for; matrix products, arithmetic and copies ran while one was open for 0% of the time, Pallas kernels for 23%

profile of v17, /device:TPU:0, one launch (start us, length us, event | category | flops | bytes accessed | tf_op | source)
XLA Modules:
  0.0 24.5 jit_solution(7066129267590351017)
XLA Ops:
  0.6 3.9 %forward.1 = (bf16[32,1024]{1,0:T(8,128)(2,1)S(1)}, f32[2,24,256]{2,1,0:T(8,128)S(1)}, f32[32,2048]{1,0:T(8,128)S(1)}) custom-call(s32[2]{0:T(128)} %wave_hbm.1, s32[2]{0:T(128)} %angle_hbm.1, s32[2,2]{1,0:T(2,128)} %aim_hbm.1, f32[16,256]{1,0:T(8,128)} %bitcast.1, f32[32,4096]{1,0:T(8,128)} %width_hbm.1), custom_call_target="tpu_custom_call" | custom-call | flops 1000000000 | bytes 10000000 | tf_op jit(solution)/shard_map/forward/pallas_call | solution.py:494
  4.6 5.1 %collective-permute-start = (bf16[32,1024]{1,0:T(8,128)(2,1)S(1)}, bf16[32,1024]{1,0:T(8,128)(2,1)S(1)}, u32[]{:S(2)}, u32[]{:S(2)}) collective-permute-start(bf16[32,1024]{1,0:T(8,128)(2,1)S(1)} %get-tuple-element.25.refs_0_), channel_id=1, source_target_pairs={{0,12},{2,14},{4,8},{6,10},{8,4},{10,6},{12,0},{14,2},{1,13},{3,15... | collective-permute-start | bytes 196616 | tf_op jit(solution)/shard_map/ppermute | solution.py:485
  9.7 0.0 collective-permute-start.3
  9.7 0.6 %collective-permute-start.4 = (bf16[32,1024]{1,0:T(8,128)(2,1)S(1)}, bf16[32,1024]{1,0:T(8,128)(2,1)S(1)}, u32[]{:S(2)}, u32[]{:S(2)}) collective-permute-start(bf16[32,1024]{1,0:T(8,128)(2,1)S(1)} %get-tuple-element.25.refs_0_), channel_id=1, source_target_pairs={{0,4},{2,6},{4,0},{6,2},{8,12},{10,14},{12,8},{14,10},{1,5},{3,7},... | collective-permute-start | bytes 196616 | tf_op jit(solution)/shard_map/ppermute | solution.py:485
  10.3 1.6 %collective-permute-start.2 = (bf16[32,1024]{1,0:T(8,128)(2,1)S(1)}, bf16[32,1024]{1,0:T(8,128)(2,1)S(1)}, u32[]{:S(2)}, u32[]{:S(2)}) collective-permute-start(bf16[32,1024]{1,0:T(8,128)(2,1)S(1)} %get-tuple-element.25.refs_0_), channel_id=1, source_target_pairs={{0,2},{2,0},{4,6},{6,4},{8,10},{10,8},{12,14},{14,12},{1,3},{3,1},... | collective-permute-start | bytes 196616 | tf_op jit(solution)/shard_map/ppermute | solution.py:485
  11.9 0.0 collective-permute-start.1
  11.9 1.0 %row_tables.1 = (bf16[2,512,256]{2,1,0:T(8,128)(2,1)S(1)}, bf16[2,32,512]{2,1,0:T(8,128)(2,1)S(1)}, f32[2,256,256]{2,1,0:T(8,128)S(1)}, f32[2,8,128]{2,1,0:T(8,128)S(1)}) custom-call(f32[2,24,256]{2,1,0:T(8,128)S(1)} %get-tuple-element.23.info_ref), custom_call_target="tpu_custom_call" | custom-call | flops 100000000 | bytes 1000000 | tf_op jit(solution)/shard_map/row_tables/pallas_call | solution.py:519
  13.0 0.0 collective-permute-done.refs_2_
  13.0 1.1 %collective-permute-start.5 = (bf16[32,1024]{1,0:T(8,128)(2,1)S(1)}, bf16[32,1024]{1,0:T(8,128)(2,1)S(1)}, u32[]{:S(2)}, u32[]{:S(2)}) collective-permute-start(bf16[32,1024]{1,0:T(8,128)(2,1)S(1)} %collective-permute-done.refs_2_), channel_id=1, source_target_pairs={{0,2},{2,0},{4,6},{6,4},{8,10},{10,8},{12,14},{14,12},{1,3},{3,1},... | collective-permute-start | bytes 196616 | tf_op jit(solution)/shard_map/ppermute | solution.py:485
  14.1 1.2 %collective-permute-done.3.refs_0_ = bf16[32,1024]{1,0:T(8,128)(2,1)S(1)} collective-permute-done((bf16[32,1024]{1,0:T(8,128)(2,1)S(1)}, bf16[32,1024]{1,0:T(8,128)(2,1)S(1)}, u32[]{:S(2)}, u32[]{:S(2)}) %collective-permute-start.3) | collective-permute-done | bytes 65568 | tf_op jit(solution)/shard_map/ppermute | solution.py:485
  15.3 0.0 collective-permute-done.4.refs_1_
  15.3 1.6 %collective-permute-start.6 = (bf16[64,1024]{1,0:T(8,128)(2,1)S(1)}, bf16[64,1024]{1,0:T(8,128)(2,1)S(1)}, u32[]{:S(2)}, u32[]{:S(2)}) collective-permute-start(bf16[64,1024]{1,0:T(8,128)(2,1)S(1)} %join.1.refs_1_.refs_3_), channel_id=1, source_target_pairs={{0,2},{2,0},{4,6},{6,4},{8,10},{10,8},{12,14},{14,12},{1,3},{3,1},... | collective-permute-start | bytes 393224 | tf_op jit(solution)/shard_map/ppermute | solution.py:485
  16.8 0.0 collective-permute-done.1.far_info_ref
  16.8 0.0 collective-permute-done.2.refs_0_.refs_1_
  16.9 3.3 %column_tables.1 = (bf16[512,2048]{1,0:T(8,128)(2,1)S(1)}, bf16[512,2048]{1,0:T(8,128)(2,1)S(1)}, bf16[512,2048]{1,0:T(8,128)(2,1)S(1)}, bf16[512,2048]{1,0:T(8,...) custom-call(f32[2,24,256]{2,1,0:T(8,128)S(1)} %get-tuple-element.23., ...), custom_call_target="tpu_custom_call" | custom-call | flops 3000000000 | bytes 30000000 | tf_op jit(solution)/shard_map/column_tables/pallas_call | solution.py:542
  20.2 0.0 collective-permute-done.5.refs_4_
  20.2 0.2 collective-permute-done.6.refs_5_
  20.4 1.1 %focus.1 = (bf16[32,1024]{1,0:T(8,128)(2,1)S(1)}, f32[2,8,128]{2,1,0:T(8,128)S(1)}) custom-call(bf16[2,512,256]{2,1,0:T(8,128)(2,1)S(1)} %get-tuple-element.24.tall_ref, bf16[2,32,512]{2,1,0:T(8,128)(2,1)S(1)} %get-tuple-element.27.flat_ref, f32[2,256,256]{2,1,0:T(8,128)S(1)} %get-tuple-element.28.spot_ref, f32[2,8,128]{2,1,0:T(8,128)S(1)} %get-tuple-element.29.gain_ref, ...), custom_call_target="tpu_custom_call" | custom-call | flops 100000000 | bytes 1000000 | tf_op jit(solution)/shard_map/focus/pallas_call | solution.py:555
  21.5 0.1 collective-permute-start.7
  21.6 1.3 %gradient_own.1 = (f32[32,2048]{1,0:T(8,128)S(1)}, f32[2]{0:T(128)}) custom-call(bf16[32,1024]{1,0:T(8,128)(2,1)S(1)} %get-tuple-element.33.refs_0_, bf16[512,2048]{1,0:T(8,128)(2,1)S(1)} %get-tuple-element.38.refs_1_, bf16[512,2048]{1,0:T(8,128)(2,1)S(1)} %get-tuple-element.39.refs_2_, f32[2,32,2048]{2,1,0:T(8,128)S(1)} %get-tuple-element.31.after_ref.refs_3_, ...), custom_call_target="tpu_custom_call" | custom-call | flops 1000000000 | bytes 10000000 | tf_op jit(solution)/shard_map/gradient_own/pallas_call | solution.py:570
  22.9 0.0 collective-permute-done.7.refs_0_
  22.9 1.6 %gradient_far.1 = f32[32,2048]{1,0:T(8,128)} custom-call(bf16[32,1024]{1,0:T(8,128)(2,1)S(1)} %collective-permute-done.7.refs_0_, bf16[512,2048]{1,0:T(8,128)(2,1)S(1)} %get-tuple-element.34.refs_1_, bf16[512,2048]{1,0:T(8,128)(2,1)S(1)} %get-tuple-element.35.refs_2_, f32[2,32,2048]{2,1,0:T(8,128)S(1)} %get-tuple-element.36.refs_3_, ...), custom_call_target="tpu_custom_call" | custom-call | flops 1000000000 | bytes 10000000 | tf_op jit(solution)/shard_map/gradient_far/pallas_call | solution.py:576
  (1 shorter events, 0.0 us)
Async XLA Ops:
  4.6 8.4 %collective-permute-start = (bf16[32,1024]{1,0:T(8,128)(2,1)S(1)}, bf16[32,1024]{1,0:T(8,128)(2,1)S(1)}, u32[]{:S(2)}, u32[]{:S(2)}) collective-permute-start(bf16[32,1024]{1,0:T(8,128)(2,1)S(1)} %get-tuple-element.25.refs_0_), channel_id=1, source_target_pairs={{0,12},{2,14},{4,8},{6,10},{8,4},{10,6},{12,0},{14,2},{1,13},{3,15... | collective-permute-start | bytes 196616 | tf_op jit(solution)/shard_map/ppermute | solution.py:485
  9.7 5.6 %collective-permute-start.3 = (bf16[32,1024]{1,0:T(8,128)(2,1)S(1)}, bf16[32,1024]{1,0:T(8,128)(2,1)S(1)}, u32[]{:S(2)}, u32[]{:S(2)}) collective-permute-start(bf16[32,1024]{1,0:T(8,128)(2,1)S(1)} %get-tuple-element.25.refs_0_), channel_id=1, source_target_pairs={{0,8},{2,10},{4,12},{6,14},{8,0},{10,2},{12,4},{14,6},{1,9},{3,11}... | collective-permute-start | bytes 196616 | tf_op jit(solution)/shard_map/ppermute | solution.py:485
  9.7 5.6 %collective-permute-start.4 = (bf16[32,1024]{1,0:T(8,128)(2,1)S(1)}, bf16[32,1024]{1,0:T(8,128)(2,1)S(1)}, u32[]{:S(2)}, u32[]{:S(2)}) collective-permute-start(bf16[32,1024]{1,0:T(8,128)(2,1)S(1)} %get-tuple-element.25.refs_0_), channel_id=1, source_target_pairs={{0,4},{2,6},{4,0},{6,2},{8,12},{10,14},{12,8},{14,10},{1,5},{3,7},... | collective-permute-start | bytes 196616 | tf_op jit(solution)/shard_map/ppermute | solution.py:485
  10.3 6.5 %collective-permute-start.2 = (bf16[32,1024]{1,0:T(8,128)(2,1)S(1)}, bf16[32,1024]{1,0:T(8,128)(2,1)S(1)}, u32[]{:S(2)}, u32[]{:S(2)}) collective-permute-start(bf16[32,1024]{1,0:T(8,128)(2,1)S(1)} %get-tuple-element.25.refs_0_), channel_id=1, source_target_pairs={{0,2},{2,0},{4,6},{6,4},{8,10},{10,8},{12,14},{14,12},{1,3},{3,1},... | collective-permute-start | bytes 196616 | tf_op jit(solution)/shard_map/ppermute | solution.py:485
  11.9 4.9 %collective-permute-start.1 = (f32[2,24,256]{2,1,0:T(8,128)S(1)}, f32[2,24,256]{2,1,0:T(8,128)S(1)}, u32[]{:S(2)}, u32[]{:S(2)}) collective-permute-start(f32[2,24,256]{2,1,0:T(8,128)S(1)} %get-tuple-element.23.info_ref), channel_id=1, source_target_pairs={{0,1},{1,0},{2,3},{3,2},{4,5},{5,4},{6,7},{7,6},{8,9},{9,8},{10,11... | collective-permute-start | bytes 147464 | tf_op jit(solution)/shard_map/ppermute | solution.py:488
  13.0 7.2 %collective-permute-start.5 = (bf16[32,1024]{1,0:T(8,128)(2,1)S(1)}, bf16[32,1024]{1,0:T(8,128)(2,1)S(1)}, u32[]{:S(2)}, u32[]{:S(2)}) collective-permute-start(bf16[32,1024]{1,0:T(8,128)(2,1)S(1)} %collective-permute-done.refs_2_), channel_id=1, source_target_pairs={{0,2},{2,0},{4,6},{6,4},{8,10},{10,8},{12,14},{14,12},{1,3},{3,1},... | collective-permute-start | bytes 196616 | tf_op jit(solution)/shard_map/ppermute | solution.py:485
  15.3 5.1 %collective-permute-start.6 = (bf16[64,1024]{1,0:T(8,128)(2,1)S(1)}, bf16[64,1024]{1,0:T(8,128)(2,1)S(1)}, u32[]{:S(2)}, u32[]{:S(2)}) collective-permute-start(bf16[64,1024]{1,0:T(8,128)(2,1)S(1)} %join.1.refs_1_.refs_3_), channel_id=1, source_target_pairs={{0,2},{2,0},{4,6},{6,4},{8,10},{10,8},{12,14},{14,12},{1,3},{3,1},... | collective-permute-start | bytes 393224 | tf_op jit(solution)/shard_map/ppermute | solution.py:485
  21.5 1.4 %collective-permute-start.7 = (bf16[32,1024]{1,0:T(8,128)(2,1)S(1)}, bf16[32,1024]{1,0:T(8,128)(2,1)S(1)}, u32[]{:S(2)}, u32[]{:S(2)}) collective-permute-start(bf16[32,1024]{1,0:T(8,128)(2,1)S(1)} %get-tuple-element.33.refs_0_), channel_id=1, source_target_pairs={{0,1},{1,0},{2,3},{3,2},{4,5},{5,4},{6,7},{7,6},{8,9},{9,8},{10,11... | collective-permute-start | bytes 196616 | tf_op jit(solution)/shard_map/ppermute | solution.py:488

commit v18 on v16

--- a/solution.py
+++ b/solution.py
@@ -179,15 +179,16 @@
     for move in moves:
         move.wait()
     for pair in range(pairs):
-        coef = pick_coef(coef_ref[...], wave_ref[pair])
+        wave = wave_ref[:, pair : pair + 1]
+        coef = pick_coef(coef_ref[...], wave)
         coef = jnp.broadcast_to(coef, (WAVE_ROW, FOCAL))
         info_ref[pair, :WAVE_ROW, :] = coef
         power_ref[pair] = as_tiles(power_coefs(coef[:, :LANES]))
         row = iota((INFO_ROWS - WAVE_ROW, FOCAL), 0) + WAVE_ROW
-        ids = jnp.where(row == WAVE_ROW, wave_ref[pair], 0)
-        ids = jnp.where(row == ANGLE_ROW, angle_ref[pair], ids)
-        ids = jnp.where(row == AIM_ROW, aim_ref[pair, 0], ids)
-        ids = jnp.where(row == AIM_ROW + 1, aim_ref[pair, 1], ids)
+        ids = jnp.where(row == WAVE_ROW, wave, 0)
+        ids = jnp.where(row == ANGLE_ROW, angle_ref[:, pair : pair + 1], ids)
+        for axis in range(2):
+            ids = jnp.where(row == AIM_ROW + axis, aim_ref[pair : pair + 1, axis : axis + 1], ids)
         info_ref[pair, WAVE_ROW:, :] = ids.astype(jnp.float32)
     for pair in range(pairs):
         own_waves(info_ref, pair, cols, base_ref.at[pair], centre_ref.at[pair])
@@ -388,10 +389,12 @@
 
 
 def own_grad_kernel(*refs):
-    *in_refs, tile_ref, out_ref, score_ref = refs
-    for pair in range(score_ref.shape[0]):
-        score_ref[pair] = jnp.sum(tile_ref[pair, :1, :1])
+    *in_refs, tile_ref, out_ref, score_hbm, score_ref, sem = refs
+    score_ref[...] = jnp.concatenate([tile_ref[pair, :1, :1] for pair in range(tile_ref.shape[0])], axis=1)
+    move = pltpu.make_async_copy(score_ref, score_hbm, sem)
+    move.start()
     add_grads(in_refs, None, out_ref, 2 * BLOCK)
+    move.wait()
 
 
 def last_grad_kernel(*refs):
@@ -409,7 +412,7 @@
         moves.append(pltpu.make_async_copy(out_ref.at[:, place], out_hbm.at[:, place], sems.at[index]))
         moves[-1].start()
 
-    add_grads(in_refs, total_ref, out_ref, BLOCK, send)
+    add_grads(in_refs, total_ref, out_ref, 2 * BLOCK, send)
     for move in moves:
         move.wait()
 
@@ -496,9 +499,9 @@
         ),
         [HBM] * 5, (VMEM,) * 3,
         [
-            pltpu.SMEM(wave_ids.shape, jnp.int32),
-            pltpu.SMEM(angle_ids.shape, jnp.int32),
-            pltpu.SMEM(targets.shape, jnp.int32),
+            pltpu.VMEM((1, pairs_dev), jnp.int32),
+            pltpu.VMEM((1, pairs_dev), jnp.int32),
+            pltpu.VMEM(targets.shape, jnp.int32),
             pltpu.VMEM(coef_table.shape[::-1], f32),
             pltpu.VMEM(widths.shape, f32),
             pltpu.VMEM((rows_dev, own_cols), f32),
@@ -510,7 +513,7 @@
             pltpu.SemaphoreType.DMA((5,)),
         ],
         10**9, 10**7,
-    )(*(in_hbm(value) for value in (wave_ids, angle_ids, targets, coef_table.T, widths)))
+    )(*(in_hbm(value) for value in (wave_ids[None], angle_ids[None], targets, coef_table.T, widths)))
     far_info = to_core(info)
 
     tall, flat, spots, gains = call(
@@ -565,15 +568,16 @@
     out = shape((rows_dev, own_cols), f32)
     ins = [back, *tables[:pairs_dev], *slopes[:pairs_dev], scores]
     grad, scores = call(
-        own_grad_kernel, "gradient_own", (out, shape((pairs_dev,), f32)),
-        [VMEM] * len(ins), (VMEM, SMEM), [], 10**9, 10**7,
+        own_grad_kernel, "gradient_own", (out, shape((1, pairs_dev), f32)),
+        [VMEM] * len(ins), (VMEM, HBM),
+        [pltpu.VMEM((1, pairs_dev), f32), pltpu.SemaphoreType.DMA], 10**9, 10**7,
     )(*ins)
     ins = [to_core(back), *tables[pairs_dev:], *slopes[pairs_dev:], grad]
     grad = call(
         last_grad_kernel, "gradient_far", out, [VMEM] * len(ins), HBM,
-        [pltpu.VMEM(out.shape, f32), pltpu.SemaphoreType.DMA((own_cols // BLOCK,))], 10**9, 10**7,
+        [pltpu.VMEM(out.shape, f32), pltpu.SemaphoreType.DMA((own_cols // (2 * BLOCK),))], 10**9, 10**7,
     )(*ins)
-    return grad, scores
+    return grad, scores[0]
 
 
 def solution(mesh):

time: 24.7 us -> 24.8 us (level)
  no operation moved by 1% of the time
where the time goes in v18:
time: 24.8 us; the launch traced here: 24.6 us
  Pallas kernels  12.4 us (50%)
  starting transfers between devices  10.1 us (41%)
  waiting for transfers between devices  1.41 us (6%)
  between operations  0.7 us (3%)
    ppermute x6, starting transfers between devices, exchange(): lax.ppermute(value, 'aperture', [(index, index ^ step) for index in range...  10 us
    pallas_call x1, Pallas kernels, on_device(): call(forward_kernel, 'forward', (shape((rows_dev, lanes), bf16), shape((p...  4.03 us
    pallas_call x1, Pallas kernels, on_device(): call(functools.partial(table_kernel, math.sqrt(rows * cols), cols), 'colu...  3.33 us
    pallas_call x1, Pallas kernels, on_device(): call(last_grad_kernel, 'gradient_far', out, [VMEM] * len(ins), HBM, [pltp...  1.61 us
    ppermute x6, waiting for transfers between devices, exchange(): lax.ppermute(value, 'aperture', [(index, index ^ step) for index in range...  1.4 us
    pallas_call x1, Pallas kernels, on_device(): call(own_grad_kernel, 'gradient_own', (out, shape((1, pairs_dev), f32)),...  1.3 us
    pallas_call x1, Pallas kernels, on_device(): call(functools.partial(focus_kernel, steps), 'focus', (shape((rows_dev, l...  1.06 us
    pallas_call x1, Pallas kernels, on_device(): call(row_kernel, 'row_tables', (shape((pairs_dev, 2 * FOCAL, rows), bf16)...  1.04 us
  transfers between devices with their start and end apart: 8, of which 2 were waited for; matrix products, arithmetic and copies ran while one was open for 0% of the time, Pallas kernels for 23%

profile of v18, /device:TPU:0, one launch (start us, length us, event | category | flops | bytes accessed | tf_op | source)
XLA Modules:
  0.0 24.6 jit_solution(2116973838219419193)
XLA Ops:
  0.6 4.0 %forward.1 = (bf16[32,1024]{1,0:T(8,128)(2,1)S(1)}, f32[2,24,256]{2,1,0:T(8,128)S(1)}, f32[32,2048]{1,0:T(8,128)S(1)}) custom-call(s32[1,2]{1,0:T(1,128)} %bitcast.5, s32[1,2]{1,0:T(1,128)} %bitcast.6, s32[2,2]{1,0:T(2,128)} %aim_hbm.1, f32[16,256]{1,0:T(8,128)} %bitcast.4, f32[32,4096]{1,0:T(8,128)} %width_hbm.1), custom_call_target="tpu_custom_call" | custom-call | flops 1000000000 | bytes 10000000 | tf_op jit(solution)/shard_map/forward/pallas_call | solution.py:494
  4.7 5.1 %collective-permute-start = (bf16[32,1024]{1,0:T(8,128)(2,1)S(1)}, bf16[32,1024]{1,0:T(8,128)(2,1)S(1)}, u32[]{:S(2)}, u32[]{:S(2)}) collective-permute-start(bf16[32,1024]{1,0:T(8,128)(2,1)S(1)} %get-tuple-element.25.refs_0_), channel_id=1, source_target_pairs={{0,12},{2,14},{4,8},{6,10},{8,4},{10,6},{12,0},{14,2},{1,13},{3,15... | collective-permute-start | bytes 196616 | tf_op jit(solution)/shard_map/ppermute | solution.py:485
  9.8 0.0 collective-permute-start.3
  9.8 0.6 %collective-permute-start.4 = (bf16[32,1024]{1,0:T(8,128)(2,1)S(1)}, bf16[32,1024]{1,0:T(8,128)(2,1)S(1)}, u32[]{:S(2)}, u32[]{:S(2)}) collective-permute-start(bf16[32,1024]{1,0:T(8,128)(2,1)S(1)} %get-tuple-element.25.refs_0_), channel_id=1, source_target_pairs={{0,4},{2,6},{4,0},{6,2},{8,12},{10,14},{12,8},{14,10},{1,5},{3,7},... | collective-permute-start | bytes 196616 | tf_op jit(solution)/shard_map/ppermute | solution.py:485
  10.4 1.6 %collective-permute-start.2 = (bf16[32,1024]{1,0:T(8,128)(2,1)S(1)}, bf16[32,1024]{1,0:T(8,128)(2,1)S(1)}, u32[]{:S(2)}, u32[]{:S(2)}) collective-permute-start(bf16[32,1024]{1,0:T(8,128)(2,1)S(1)} %get-tuple-element.25.refs_0_), channel_id=1, source_target_pairs={{0,2},{2,0},{4,6},{6,4},{8,10},{10,8},{12,14},{14,12},{1,3},{3,1},... | collective-permute-start | bytes 196616 | tf_op jit(solution)/shard_map/ppermute | solution.py:485
  12.1 0.0 collective-permute-start.1
  12.1 1.0 %row_tables.1 = (bf16[2,512,256]{2,1,0:T(8,128)(2,1)S(1)}, bf16[2,32,512]{2,1,0:T(8,128)(2,1)S(1)}, f32[2,256,256]{2,1,0:T(8,128)S(1)}, f32[2,8,128]{2,1,0:T(8,128)S(1)}) custom-call(f32[2,24,256]{2,1,0:T(8,128)S(1)} %get-tuple-element.23.info_ref), custom_call_target="tpu_custom_call" | custom-call | flops 100000000 | bytes 1000000 | tf_op jit(solution)/shard_map/row_tables/pallas_call | solution.py:519
  13.1 0.0 collective-permute-done.refs_2_
  13.1 1.1 %collective-permute-start.5 = (bf16[32,1024]{1,0:T(8,128)(2,1)S(1)}, bf16[32,1024]{1,0:T(8,128)(2,1)S(1)}, u32[]{:S(2)}, u32[]{:S(2)}) collective-permute-start(bf16[32,1024]{1,0:T(8,128)(2,1)S(1)} %collective-permute-done.refs_2_), channel_id=1, source_target_pairs={{0,2},{2,0},{4,6},{6,4},{8,10},{10,8},{12,14},{14,12},{1,3},{3,1},... | collective-permute-start | bytes 196616 | tf_op jit(solution)/shard_map/ppermute | solution.py:485
  14.2 1.2 %collective-permute-done.3.refs_0_ = bf16[32,1024]{1,0:T(8,128)(2,1)S(1)} collective-permute-done((bf16[32,1024]{1,0:T(8,128)(2,1)S(1)}, bf16[32,1024]{1,0:T(8,128)(2,1)S(1)}, u32[]{:S(2)}, u32[]{:S(2)}) %collective-permute-start.3) | collective-permute-done | bytes 65568 | tf_op jit(solution)/shard_map/ppermute | solution.py:485
  15.4 0.0 collective-permute-done.4.refs_1_
  15.4 1.6 %collective-permute-start.6 = (bf16[64,1024]{1,0:T(8,128)(2,1)S(1)}, bf16[64,1024]{1,0:T(8,128)(2,1)S(1)}, u32[]{:S(2)}, u32[]{:S(2)}) collective-permute-start(bf16[64,1024]{1,0:T(8,128)(2,1)S(1)} %join.1.refs_1_.refs_3_), channel_id=1, source_target_pairs={{0,2},{2,0},{4,6},{6,4},{8,10},{10,8},{12,14},{14,12},{1,3},{3,1},... | collective-permute-start | bytes 393224 | tf_op jit(solution)/shard_map/ppermute | solution.py:485
  17.0 0.0 collective-permute-done.1.far_info_ref
  17.0 0.0 collective-permute-done.2.refs_0_.refs_1_
  17.0 3.3 %column_tables.1 = (bf16[512,2048]{1,0:T(8,128)(2,1)S(1)}, bf16[512,2048]{1,0:T(8,128)(2,1)S(1)}, bf16[512,2048]{1,0:T(8,128)(2,1)S(1)}, bf16[512,2048]{1,0:T(8,...) custom-call(f32[2,24,256]{2,1,0:T(8,128)S(1)} %get-tuple-element.23., ...), custom_call_target="tpu_custom_call" | custom-call | flops 3000000000 | bytes 30000000 | tf_op jit(solution)/shard_map/column_tables/pallas_call | solution.py:542
  20.3 0.0 collective-permute-done.5.refs_4_
  20.3 0.2 collective-permute-done.6.refs_5_
  20.5 1.1 %focus.1 = (bf16[32,1024]{1,0:T(8,128)(2,1)S(1)}, f32[2,8,128]{2,1,0:T(8,128)S(1)}) custom-call(bf16[2,512,256]{2,1,0:T(8,128)(2,1)S(1)} %get-tuple-element.24.tall_ref, bf16[2,32,512]{2,1,0:T(8,128)(2,1)S(1)} %get-tuple-element.27.flat_ref, f32[2,256,256]{2,1,0:T(8,128)S(1)} %get-tuple-element.28.spot_ref, f32[2,8,128]{2,1,0:T(8,128)S(1)} %get-tuple-element.29.gain_ref, ...), custom_call_target="tpu_custom_call" | custom-call | flops 100000000 | bytes 1000000 | tf_op jit(solution)/shard_map/focus/pallas_call | solution.py:555
  21.6 0.1 collective-permute-start.7
  21.7 1.3 %gradient_own.1 = (f32[32,2048]{1,0:T(8,128)S(1)}, f32[1,2]{1,0:T(1,128)}) custom-call(bf16[32,1024]{1,0:T(8,128)(2,1)S(1)} %get-tuple-element.33.refs_0_, bf16[512,2048]{1,0:T(8,128)(2,1)S(1)} %get-tuple-element.38.refs_1_, bf16[512,2048]{1,0:T(8,128)(2,1)S(1)} %get-tuple-element.39.refs_2_, f32[2,32,2048]{2,1,0:T(8,128)S(1)} %get-tuple-element.31.after_ref.refs_3_, ...), custom_call_target="tpu_custom_call" | custom-call | flops 1000000000 | bytes 10000000 | tf_op jit(solution)/shard_map/gradient_own/pallas_call | solution.py:570
  23.0 0.0 collective-permute-done.7.refs_0_
  23.0 1.6 %gradient_far.1 = f32[32,2048]{1,0:T(8,128)} custom-call(bf16[32,1024]{1,0:T(8,128)(2,1)S(1)} %collective-permute-done.7.refs_0_, bf16[512,2048]{1,0:T(8,128)(2,1)S(1)} %get-tuple-element.34.refs_1_, bf16[512,2048]{1,0:T(8,128)(2,1)S(1)} %get-tuple-element.35.refs_2_, f32[2,32,2048]{2,1,0:T(8,128)S(1)} %get-tuple-element.36.refs_3_, ...), custom_call_target="tpu_custom_call" | custom-call | flops 1000000000 | bytes 10000000 | tf_op jit(solution)/shard_map/gradient_far/pallas_call | solution.py:576
  (1 shorter events, 0.0 us)
Async XLA Ops:
  4.7 8.4 %collective-permute-start = (bf16[32,1024]{1,0:T(8,128)(2,1)S(1)}, bf16[32,1024]{1,0:T(8,128)(2,1)S(1)}, u32[]{:S(2)}, u32[]{:S(2)}) collective-permute-start(bf16[32,1024]{1,0:T(8,128)(2,1)S(1)} %get-tuple-element.25.refs_0_), channel_id=1, source_target_pairs={{0,12},{2,14},{4,8},{6,10},{8,4},{10,6},{12,0},{14,2},{1,13},{3,15... | collective-permute-start | bytes 196616 | tf_op jit(solution)/shard_map/ppermute | solution.py:485
  9.8 5.6 %collective-permute-start.3 = (bf16[32,1024]{1,0:T(8,128)(2,1)S(1)}, bf16[32,1024]{1,0:T(8,128)(2,1)S(1)}, u32[]{:S(2)}, u32[]{:S(2)}) collective-permute-start(bf16[32,1024]{1,0:T(8,128)(2,1)S(1)} %get-tuple-element.25.refs_0_), channel_id=1, source_target_pairs={{0,8},{2,10},{4,12},{6,14},{8,0},{10,2},{12,4},{14,6},{1,9},{3,11}... | collective-permute-start | bytes 196616 | tf_op jit(solution)/shard_map/ppermute | solution.py:485
  9.8 5.6 %collective-permute-start.4 = (bf16[32,1024]{1,0:T(8,128)(2,1)S(1)}, bf16[32,1024]{1,0:T(8,128)(2,1)S(1)}, u32[]{:S(2)}, u32[]{:S(2)}) collective-permute-start(bf16[32,1024]{1,0:T(8,128)(2,1)S(1)} %get-tuple-element.25.refs_0_), channel_id=1, source_target_pairs={{0,4},{2,6},{4,0},{6,2},{8,12},{10,14},{12,8},{14,10},{1,5},{3,7},... | collective-permute-start | bytes 196616 | tf_op jit(solution)/shard_map/ppermute | solution.py:485
  10.4 6.5 %collective-permute-start.2 = (bf16[32,1024]{1,0:T(8,128)(2,1)S(1)}, bf16[32,1024]{1,0:T(8,128)(2,1)S(1)}, u32[]{:S(2)}, u32[]{:S(2)}) collective-permute-start(bf16[32,1024]{1,0:T(8,128)(2,1)S(1)} %get-tuple-element.25.refs_0_), channel_id=1, source_target_pairs={{0,2},{2,0},{4,6},{6,4},{8,10},{10,8},{12,14},{14,12},{1,3},{3,1},... | collective-permute-start | bytes 196616 | tf_op jit(solution)/shard_map/ppermute | solution.py:485
  12.1 4.9 %collective-permute-start.1 = (f32[2,24,256]{2,1,0:T(8,128)S(1)}, f32[2,24,256]{2,1,0:T(8,128)S(1)}, u32[]{:S(2)}, u32[]{:S(2)}) collective-permute-start(f32[2,24,256]{2,1,0:T(8,128)S(1)} %get-tuple-element.23.info_ref), channel_id=1, source_target_pairs={{0,1},{1,0},{2,3},{3,2},{4,5},{5,4},{6,7},{7,6},{8,9},{9,8},{10,11... | collective-permute-start | bytes 147464 | tf_op jit(solution)/shard_map/ppermute | solution.py:488
  13.1 7.2 %collective-permute-start.5 = (bf16[32,1024]{1,0:T(8,128)(2,1)S(1)}, bf16[32,1024]{1,0:T(8,128)(2,1)S(1)}, u32[]{:S(2)}, u32[]{:S(2)}) collective-permute-start(bf16[32,1024]{1,0:T(8,128)(2,1)S(1)} %collective-permute-done.refs_2_), channel_id=1, source_target_pairs={{0,2},{2,0},{4,6},{6,4},{8,10},{10,8},{12,14},{14,12},{1,3},{3,1},... | collective-permute-start | bytes 196616 | tf_op jit(solution)/shard_map/ppermute | solution.py:485
  15.4 5.1 %collective-permute-start.6 = (bf16[64,1024]{1,0:T(8,128)(2,1)S(1)}, bf16[64,1024]{1,0:T(8,128)(2,1)S(1)}, u32[]{:S(2)}, u32[]{:S(2)}) collective-permute-start(bf16[64,1024]{1,0:T(8,128)(2,1)S(1)} %join.1.refs_1_.refs_3_), channel_id=1, source_target_pairs={{0,2},{2,0},{4,6},{6,4},{8,10},{10,8},{12,14},{14,12},{1,3},{3,1},... | collective-permute-start | bytes 393224 | tf_op jit(solution)/shard_map/ppermute | solution.py:485
  21.6 1.4 %collective-permute-start.7 = (bf16[32,1024]{1,0:T(8,128)(2,1)S(1)}, bf16[32,1024]{1,0:T(8,128)(2,1)S(1)}, u32[]{:S(2)}, u32[]{:S(2)}) collective-permute-start(bf16[32,1024]{1,0:T(8,128)(2,1)S(1)} %get-tuple-element.33.refs_0_), channel_id=1, source_target_pairs={{0,1},{1,0},{2,3},{3,2},{4,5},{5,4},{6,7},{7,6},{8,9},{9,8},{10,11... | collective-permute-start | bytes 196616 | tf_op jit(solution)/shard_map/ppermute | solution.py:488

commit v19 on v16

--- a/solution.py
+++ b/solution.py
@@ -142,6 +142,29 @@
     return jnp.concatenate(parts, axis=1)
 
 
+def side_pieces(width_ref, core):
+    rows, cols = width_ref.shape
+    half = cols // 2
+    count = half // LANES
+    lane = iota((rows, LANES), 1)
+    shift = jnp.where(core == 1, 1, LANES - 1)
+    edge = jnp.where(core == 1, 0, LANES - 1)
+
+    @functools.cache
+    def turned(piece):
+        right = width_ref[:, half + piece * LANES : half + (piece + 1) * LANES]
+        left = turn_round(width_ref[:, half - (piece + 1) * LANES : half - piece * LANES])
+        other = pltpu.roll(jnp.where(core == 1, left, right), shift, 1)
+        return jnp.where(core == 1, right, left), other
+
+    def sides(piece):
+        own, other = turned(piece)
+        beside = jnp.where(core == 1, turned(max(piece - 1, 0))[1], turned(min(piece + 1, count - 1))[1])
+        return own, jnp.where(lane == edge, beside, other)
+
+    return sides
+
+
 def block_starts(cols, index):
     return cols // 2 - (index + 1) * BLOCK, cols // 2 + index * BLOCK
 
@@ -162,7 +185,7 @@
 ):
     pairs = info_ref.shape[0]
     (
-        wave_ref, angle_ref, aim_ref, coef_ref, width_ref, far_ref, base_ref, centre_ref, power_ref, near_ref, table_ref,
+        wave_ref, angle_ref, aim_ref, coef_ref, width_ref, base_ref, centre_ref, power_ref, near_ref, table_ref,
         acc_ref, sems,
     ) = refs
     rows_dev, cols = width_ref.shape
@@ -192,10 +215,7 @@
     for pair in range(pairs):
         own_waves(info_ref, pair, cols, base_ref.at[pair], centre_ref.at[pair])
     core = lax.axis_index("wave")
-    left, right = turn_round(width_ref[:, :half]), width_ref[:, half:]
-    own_ref[...] = jnp.where(core == 1, right, left)
-    far_ref[...] = jnp.where(core == 1, pltpu.roll(left, 1, 1), pltpu.roll(right, half - 1, 1))
-
+    sides = side_pieces(width_ref, core)
     alone = jnp.where(core == 1, 0, half)
     column = width_ref[:, pl.ds(pl.multiple_of(alone, LANES), LANES)]
     columns = near_fields(column, power_ref, pairs)
@@ -203,8 +223,10 @@
     for index in range(half // (2 * BLOCK)):
         starts = block_starts(half, index)
         for start in (start + step for start in starts for step in range(0, BLOCK, LANES)):
-            for side, ref in enumerate((own_ref, far_ref)):
-                outs = near_fields(ref[:, start : start + LANES], power_ref, pairs)
+            both = sides(start // LANES)
+            own_ref[:, start : start + LANES] = both[0]
+            for side, widths in enumerate(both):
+                outs = near_fields(widths, power_ref, pairs)
                 if side and start in (0, half - LANES):
                     keep = iota((rows_dev, LANES), 1) + start != void
                     outs = [[jnp.where(keep, part, 0.0) for part in out] for out in outs]
@@ -388,17 +410,18 @@
 
 
 def own_grad_kernel(*refs):
-    *in_refs, tile_ref, out_ref, score_ref = refs
+    *in_refs, out_ref = refs
+    add_grads(in_refs, None, out_ref, 2 * BLOCK)
+
+
+def last_grad_kernel(*refs):
+    *in_refs, total_ref, tile_ref, out_hbm, score_hbm, out_ref, score_ref, sems = refs
+    own_cols = out_ref.shape[1]
+    core = lax.axis_index("wave")
     for pair in range(score_ref.shape[0]):
         score_ref[pair] = jnp.sum(tile_ref[pair, :1, :1])
-    add_grads(in_refs, None, out_ref, 2 * BLOCK)
-
-
-def last_grad_kernel(*refs):
-    *in_refs, total_ref, out_hbm, out_ref, sems = refs
-    own_cols = out_ref.shape[1]
-    core = lax.axis_index("wave")
-    moves = []
+    moves = [pltpu.make_async_copy(score_ref, score_hbm, sems.at[own_cols // (2 * BLOCK)])]
+    moves[0].start()
 
     def send(start, total):
         size = total.shape[1]
@@ -409,7 +432,7 @@
         moves.append(pltpu.make_async_copy(out_ref.at[:, place], out_hbm.at[:, place], sems.at[index]))
         moves[-1].start()
 
-    add_grads(in_refs, total_ref, out_ref, BLOCK, send)
+    add_grads(in_refs, total_ref, out_ref, 2 * BLOCK, send)
     for move in moves:
         move.wait()
 
@@ -501,7 +524,6 @@
             pltpu.SMEM(targets.shape, jnp.int32),
             pltpu.VMEM(coef_table.shape[::-1], f32),
             pltpu.VMEM(widths.shape, f32),
-            pltpu.VMEM((rows_dev, own_cols), f32),
             *waves,
             pltpu.VMEM((pairs_dev, 2 * TERMS, SUBLANES, LANES), f32),
             pltpu.VMEM((pairs_dev, 4 * rows_dev, own_cols), bf16),
@@ -563,15 +585,19 @@
     )(tall, flat, spots, gains, slopes[0], *sections)
 
     out = shape((rows_dev, own_cols), f32)
-    ins = [back, *tables[:pairs_dev], *slopes[:pairs_dev], scores]
+    ins = [back, *tables[:pairs_dev], *slopes[:pairs_dev]]
+    grad = call(
+        own_grad_kernel, "gradient_own", out, [VMEM] * len(ins), VMEM, [], 10**9, 10**7,
+    )(*ins)
+    ins = [to_core(back), *tables[pairs_dev:], *slopes[pairs_dev:], grad, scores]
     grad, scores = call(
-        own_grad_kernel, "gradient_own", (out, shape((pairs_dev,), f32)),
-        [VMEM] * len(ins), (VMEM, SMEM), [], 10**9, 10**7,
-    )(*ins)
-    ins = [to_core(back), *tables[pairs_dev:], *slopes[pairs_dev:], grad]
-    grad = call(
-        last_grad_kernel, "gradient_far", out, [VMEM] * len(ins), HBM,
-        [pltpu.VMEM(out.shape, f32), pltpu.SemaphoreType.DMA((own_cols // BLOCK,))], 10**9, 10**7,
+        last_grad_kernel, "gradient_far", (out, shape((pairs_dev,), f32)), [VMEM] * len(ins), (HBM, HBM),
+        [
+            pltpu.VMEM(out.shape, f32),
+            pltpu.SMEM((pairs_dev,), f32),
+            pltpu.SemaphoreType.DMA((own_cols // (2 * BLOCK) + 1,)),
+        ],
+        10**9, 10**7,
     )(*ins)
     return grad, scores
 

time: 24.7 us -> 24.5 us (level)
  Pallas kernels: 12.3 us -> 11.8 us
  waiting for transfers between devices: 1.4 us -> 1.76 us
    pallas_call x2, Pallas kernels: 2.97 us -> 2.48 us  [the longest x1 1.62 us: on_device(): call(last_grad_kernel, 'gradient_far', (out, shape((pairs_dev,), f32)), [...]
    ppermute x2, waiting for transfers between devices: 0.01 us -> 0.37 us  [to_core(): lax.ppermute(value, 'wave', [(index, (index + 1) % copies) for index in r...]
  transfers between devices with their start and end apart: 8 -> 8, of which waited for: 2 -> 3; matrix products, arithmetic and copies ran while one was open for 0% -> 0% of each run, Pallas kernels for 23% -> 22%
where the time goes in v19:
time: 24.5 us; the launch traced here: 24.4 us
  Pallas kernels  11.8 us (48%)
  starting transfers between devices  10.1 us (41%)
  waiting for transfers between devices  1.76 us (7%)
  between operations  0.69 us (3%)
    ppermute x6, starting transfers between devices, exchange(): lax.ppermute(value, 'aperture', [(index, index ^ step) for index in range...  10 us
    pallas_call x1, Pallas kernels, on_device(): call(forward_kernel, 'forward', (shape((rows_dev, lanes), bf16), shape((p...  3.87 us
    pallas_call x1, Pallas kernels, on_device(): call(functools.partial(table_kernel, math.sqrt(rows * cols), cols), 'colu...  3.33 us
    pallas_call x1, Pallas kernels, on_device(): call(last_grad_kernel, 'gradient_far', (out, shape((pairs_dev,), f32)), [...  1.62 us
    ppermute x6, waiting for transfers between devices, exchange(): lax.ppermute(value, 'aperture', [(index, index ^ step) for index in range...  1.39 us
    pallas_call x1, Pallas kernels, on_device(): call(functools.partial(focus_kernel, steps), 'focus', (shape((rows_dev, l...  1.06 us
    pallas_call x1, Pallas kernels, on_device(): call(row_kernel, 'row_tables', (shape((pairs_dev, 2 * FOCAL, rows), bf16)...  1.04 us
    pallas_call x1, Pallas kernels, on_device(): call(own_grad_kernel, 'gradient_own', out, [VMEM] * len(ins), VMEM, [], 1...  0.87 us
  transfers between devices with their start and end apart: 8, of which 3 were waited for; matrix products, arithmetic and copies ran while one was open for 0% of the time, Pallas kernels for 22%

profile of v19, /device:TPU:0, one launch (start us, length us, event | category | flops | bytes accessed | tf_op | source)
XLA Modules:
  0.0 24.4 jit_solution(8217604061632895922)
XLA Ops:
  0.6 3.9 %forward.1 = (bf16[32,1024]{1,0:T(8,128)(2,1)S(1)}, f32[2,24,256]{2,1,0:T(8,128)S(1)}, f32[32,2048]{1,0:T(8,128)S(1)}) custom-call(s32[2]{0:T(128)} %wave_hbm.1, s32[2]{0:T(128)} %angle_hbm.1, s32[2,2]{1,0:T(2,128)} %aim_hbm.1, f32[16,256]{1,0:T(8,128)} %bitcast.1, f32[32,4096]{1,0:T(8,128)} %width_hbm.1), custom_call_target="tpu_custom_call" | custom-call | flops 1000000000 | bytes 10000000 | tf_op jit(solution)/shard_map/forward/pallas_call | solution.py:514
  4.5 5.1 %collective-permute-start = (bf16[32,1024]{1,0:T(8,128)(2,1)S(1)}, bf16[32,1024]{1,0:T(8,128)(2,1)S(1)}, u32[]{:S(2)}, u32[]{:S(2)}) collective-permute-start(bf16[32,1024]{1,0:T(8,128)(2,1)S(1)} %get-tuple-element.23.refs_0_), channel_id=1, source_target_pairs={{0,12},{2,14},{4,8},{6,10},{8,4},{10,6},{12,0},{14,2},{1,13},{3,15... | collective-permute-start | bytes 196616 | tf_op jit(solution)/shard_map/ppermute | solution.py:505
  9.6 0.0 collective-permute-start.3
  9.6 0.6 %collective-permute-start.4 = (bf16[32,1024]{1,0:T(8,128)(2,1)S(1)}, bf16[32,1024]{1,0:T(8,128)(2,1)S(1)}, u32[]{:S(2)}, u32[]{:S(2)}) collective-permute-start(bf16[32,1024]{1,0:T(8,128)(2,1)S(1)} %get-tuple-element.23.refs_0_), channel_id=1, source_target_pairs={{0,4},{2,6},{4,0},{6,2},{8,12},{10,14},{12,8},{14,10},{1,5},{3,7},... | collective-permute-start | bytes 196616 | tf_op jit(solution)/shard_map/ppermute | solution.py:505
  10.3 1.6 %collective-permute-start.2 = (bf16[32,1024]{1,0:T(8,128)(2,1)S(1)}, bf16[32,1024]{1,0:T(8,128)(2,1)S(1)}, u32[]{:S(2)}, u32[]{:S(2)}) collective-permute-start(bf16[32,1024]{1,0:T(8,128)(2,1)S(1)} %get-tuple-element.23.refs_0_), channel_id=1, source_target_pairs={{0,2},{2,0},{4,6},{6,4},{8,10},{10,8},{12,14},{14,12},{1,3},{3,1},... | collective-permute-start | bytes 196616 | tf_op jit(solution)/shard_map/ppermute | solution.py:505
  11.9 0.0 collective-permute-start.1
  11.9 1.0 %row_tables.1 = (bf16[2,512,256]{2,1,0:T(8,128)(2,1)S(1)}, bf16[2,32,512]{2,1,0:T(8,128)(2,1)S(1)}, f32[2,256,256]{2,1,0:T(8,128)S(1)}, f32[2,8,128]{2,1,0:T(8,128)S(1)}) custom-call(f32[2,24,256]{2,1,0:T(8,128)S(1)} %get-tuple-element.21.info_ref), custom_call_target="tpu_custom_call" | custom-call | flops 100000000 | bytes 1000000 | tf_op jit(solution)/shard_map/row_tables/pallas_call | solution.py:538
  12.9 0.0 collective-permute-done.refs_2_
  13.0 1.1 %collective-permute-start.5 = (bf16[32,1024]{1,0:T(8,128)(2,1)S(1)}, bf16[32,1024]{1,0:T(8,128)(2,1)S(1)}, u32[]{:S(2)}, u32[]{:S(2)}) collective-permute-start(bf16[32,1024]{1,0:T(8,128)(2,1)S(1)} %collective-permute-done.refs_2_), channel_id=1, source_target_pairs={{0,2},{2,0},{4,6},{6,4},{8,10},{10,8},{12,14},{14,12},{1,3},{3,1},... | collective-permute-start | bytes 196616 | tf_op jit(solution)/shard_map/ppermute | solution.py:505
  14.1 1.2 %collective-permute-done.3.refs_0_ = bf16[32,1024]{1,0:T(8,128)(2,1)S(1)} collective-permute-done((bf16[32,1024]{1,0:T(8,128)(2,1)S(1)}, bf16[32,1024]{1,0:T(8,128)(2,1)S(1)}, u32[]{:S(2)}, u32[]{:S(2)}) %collective-permute-start.3) | collective-permute-done | bytes 65568 | tf_op jit(solution)/shard_map/ppermute | solution.py:505
  15.2 0.0 collective-permute-done.4.refs_1_
  15.2 1.6 %collective-permute-start.6 = (bf16[64,1024]{1,0:T(8,128)(2,1)S(1)}, bf16[64,1024]{1,0:T(8,128)(2,1)S(1)}, u32[]{:S(2)}, u32[]{:S(2)}) collective-permute-start(bf16[64,1024]{1,0:T(8,128)(2,1)S(1)} %join.1.refs_1_.refs_3_), channel_id=1, source_target_pairs={{0,2},{2,0},{4,6},{6,4},{8,10},{10,8},{12,14},{14,12},{1,3},{3,1},... | collective-permute-start | bytes 393224 | tf_op jit(solution)/shard_map/ppermute | solution.py:505
  16.8 0.0 collective-permute-done.1.far_info_ref
  16.8 0.0 collective-permute-done.2.refs_0_.refs_1_
  16.8 3.3 %column_tables.1 = (bf16[512,2048]{1,0:T(8,128)(2,1)S(1)}, bf16[512,2048]{1,0:T(8,128)(2,1)S(1)}, bf16[512,2048]{1,0:T(8,128)(2,1)S(1)}, bf16[512,2048]{1,0:T(8,...) custom-call(f32[2,24,256]{2,1,0:T(8,128)S(1)} %get-tuple-element.21., ...), custom_call_target="tpu_custom_call" | custom-call | flops 3000000000 | bytes 30000000 | tf_op jit(solution)/shard_map/column_tables/pallas_call | solution.py:561
  20.1 0.0 collective-permute-done.5.refs_4_
  20.2 0.2 collective-permute-done.6.refs_5_
  20.4 1.1 %focus.1 = (bf16[32,1024]{1,0:T(8,128)(2,1)S(1)}, f32[2,8,128]{2,1,0:T(8,128)S(1)}) custom-call(bf16[2,512,256]{2,1,0:T(8,128)(2,1)S(1)} %get-tuple-element.22.tall_ref, bf16[2,32,512]{2,1,0:T(8,128)(2,1)S(1)} %get-tuple-element.25.flat_ref, f32[2,256,256]{2,1,0:T(8,128)S(1)} %get-tuple-element.26.spot_ref, f32[2,8,128]{2,1,0:T(8,128)S(1)} %get-tuple-element.27.gain_ref, ...), custom_call_target="tpu_custom_call" | custom-call | flops 100000000 | bytes 1000000 | tf_op jit(solution)/shard_map/focus/pallas_call | solution.py:574
  21.4 0.1 collective-permute-start.7
  21.5 0.9 %gradient_own.1.refs_5_ = f32[32,2048]{1,0:T(8,128)S(1)} custom-call(bf16[32,1024]{1,0:T(8,128)(2,1)S(1)} %get-tuple-element.31.refs_0_, bf16[512,2048]{1,0:T(8,128)(2,1)S(1)} %get-tuple-element.36.refs_1_, bf16[512,2048]{1,0:T(8,128)(2,1)S(1)} %get-tuple-element.37.refs_2_, f32[2,32,2048]{2,1,0:T(8,128)S(1)} %get-tuple-element.29.after_ref.refs_3_, ...), custom_call_target="tpu_custom_call" | custom-call | flops 1000000000 | bytes 10000000 | tf_op jit(solution)/shard_map/gradient_own/pallas_call | solution.py:589
  22.4 0.4 %collective-permute-done.7.refs_0_ = bf16[32,1024]{1,0:T(8,128)(2,1)S(1)} collective-permute-done((bf16[32,1024]{1,0:T(8,128)(2,1)S(1)}, bf16[32,1024]{1,0:T(8,128)(2,1)S(1)}, u32[]{:S(2)}, u32[]{:S(2)}) %collective-permute-start.7) | collective-permute-done | bytes 65568 | tf_op jit(solution)/shard_map/ppermute | solution.py:508
  22.7 1.6 %gradient_far.1 = (f32[32,2048]{1,0:T(8,128)}, f32[2]{0:T(128)}) custom-call(bf16[32,1024]{1,0:T(8,128)(2,1)S(1)} %collective-permute-done.7.refs_0_, bf16[512,2048]{1,0:T(8,128)(2,1)S(1)} %get-tuple-element.32.refs_1_, bf16[512,2048]{1,0:T(8,128)(2,1)S(1)} %get-tuple-element.33.refs_2_, f32[2,32,2048]{2,1,0:T(8,128)S(1)} %get-tuple-element.34.refs_3_, ...), custom_call_target="tpu_custom_call" | custom-call | flops 1000000000 | bytes 10000000 | tf_op jit(solution)/shard_map/gradient_far/pallas_call | solution.py:593
  (1 shorter events, 0.0 us)
Async XLA Ops:
  4.5 8.4 %collective-permute-start = (bf16[32,1024]{1,0:T(8,128)(2,1)S(1)}, bf16[32,1024]{1,0:T(8,128)(2,1)S(1)}, u32[]{:S(2)}, u32[]{:S(2)}) collective-permute-start(bf16[32,1024]{1,0:T(8,128)(2,1)S(1)} %get-tuple-element.23.refs_0_), channel_id=1, source_target_pairs={{0,12},{2,14},{4,8},{6,10},{8,4},{10,6},{12,0},{14,2},{1,13},{3,15... | collective-permute-start | bytes 196616 | tf_op jit(solution)/shard_map/ppermute | solution.py:505
  9.6 5.6 %collective-permute-start.3 = (bf16[32,1024]{1,0:T(8,128)(2,1)S(1)}, bf16[32,1024]{1,0:T(8,128)(2,1)S(1)}, u32[]{:S(2)}, u32[]{:S(2)}) collective-permute-start(bf16[32,1024]{1,0:T(8,128)(2,1)S(1)} %get-tuple-element.23.refs_0_), channel_id=1, source_target_pairs={{0,8},{2,10},{4,12},{6,14},{8,0},{10,2},{12,4},{14,6},{1,9},{3,11}... | collective-permute-start | bytes 196616 | tf_op jit(solution)/shard_map/ppermute | solution.py:505
  9.6 5.6 %collective-permute-start.4 = (bf16[32,1024]{1,0:T(8,128)(2,1)S(1)}, bf16[32,1024]{1,0:T(8,128)(2,1)S(1)}, u32[]{:S(2)}, u32[]{:S(2)}) collective-permute-start(bf16[32,1024]{1,0:T(8,128)(2,1)S(1)} %get-tuple-element.23.refs_0_), channel_id=1, source_target_pairs={{0,4},{2,6},{4,0},{6,2},{8,12},{10,14},{12,8},{14,10},{1,5},{3,7},... | collective-permute-start | bytes 196616 | tf_op jit(solution)/shard_map/ppermute | solution.py:505
  10.3 6.5 %collective-permute-start.2 = (bf16[32,1024]{1,0:T(8,128)(2,1)S(1)}, bf16[32,1024]{1,0:T(8,128)(2,1)S(1)}, u32[]{:S(2)}, u32[]{:S(2)}) collective-permute-start(bf16[32,1024]{1,0:T(8,128)(2,1)S(1)} %get-tuple-element.23.refs_0_), channel_id=1, source_target_pairs={{0,2},{2,0},{4,6},{6,4},{8,10},{10,8},{12,14},{14,12},{1,3},{3,1},... | collective-permute-start | bytes 196616 | tf_op jit(solution)/shard_map/ppermute | solution.py:505
  11.9 4.9 %collective-permute-start.1 = (f32[2,24,256]{2,1,0:T(8,128)S(1)}, f32[2,24,256]{2,1,0:T(8,128)S(1)}, u32[]{:S(2)}, u32[]{:S(2)}) collective-permute-start(f32[2,24,256]{2,1,0:T(8,128)S(1)} %get-tuple-element.21.info_ref), channel_id=1, source_target_pairs={{0,1},{1,0},{2,3},{3,2},{4,5},{5,4},{6,7},{7,6},{8,9},{9,8},{10,11... | collective-permute-start | bytes 147464 | tf_op jit(solution)/shard_map/ppermute | solution.py:508
  13.0 7.2 %collective-permute-start.5 = (bf16[32,1024]{1,0:T(8,128)(2,1)S(1)}, bf16[32,1024]{1,0:T(8,128)(2,1)S(1)}, u32[]{:S(2)}, u32[]{:S(2)}) collective-permute-start(bf16[32,1024]{1,0:T(8,128)(2,1)S(1)} %collective-permute-done.refs_2_), channel_id=1, source_target_pairs={{0,2},{2,0},{4,6},{6,4},{8,10},{10,8},{12,14},{14,12},{1,3},{3,1},... | collective-permute-start | bytes 196616 | tf_op jit(solution)/shard_map/ppermute | solution.py:505
  15.2 5.1 %collective-permute-start.6 = (bf16[64,1024]{1,0:T(8,128)(2,1)S(1)}, bf16[64,1024]{1,0:T(8,128)(2,1)S(1)}, u32[]{:S(2)}, u32[]{:S(2)}) collective-permute-start(bf16[64,1024]{1,0:T(8,128)(2,1)S(1)} %join.1.refs_1_.refs_3_), channel_id=1, source_target_pairs={{0,2},{2,0},{4,6},{6,4},{8,10},{10,8},{12,14},{14,12},{1,3},{3,1},... | collective-permute-start | bytes 393224 | tf_op jit(solution)/shard_map/ppermute | solution.py:505
  21.4 1.3 %collective-permute-start.7 = (bf16[32,1024]{1,0:T(8,128)(2,1)S(1)}, bf16[32,1024]{1,0:T(8,128)(2,1)S(1)}, u32[]{:S(2)}, u32[]{:S(2)}) collective-permute-start(bf16[32,1024]{1,0:T(8,128)(2,1)S(1)} %get-tuple-element.31.refs_0_), channel_id=1, source_target_pairs={{0,1},{1,0},{2,3},{3,2},{4,5},{5,4},{6,7},{7,6},{8,9},{9,8},{10,11... | collective-permute-start | bytes 196616 | tf_op jit(solution)/shard_map/ppermute | solution.py:508

commit v20 on v19

--- a/solution.py
+++ b/solution.py
@@ -335,8 +335,10 @@
             for ref in sect_refs
             for index in range(ref.shape[0] // rows_dev)
         ]
-        for step, block in zip(steps, blocks, strict=True):
-            start = pl.multiple_of((me ^ step) * rows_dev, rows_dev)
+        length = rows_ref.shape[0] // rows_dev // 2
+        for (turn, flip), block in zip(steps, blocks, strict=True):
+            source = 2 * ((me // 2 + (length - turn)) % length) + ((me % 2) ^ flip)
+            start = pl.multiple_of(source * rows_dev, rows_dev)
             rows_ref[pl.ds(start, rows_dev), :] = block
     for pair in range(pairs):
         lane = 2 * pair * FOCAL
@@ -544,15 +546,22 @@
         [VMEM], (VMEM,) * 4, [], 10**8, 10**6,
     )(info)
     if peers <= DIRECT:
-        steps = list(range(peers - 2, 0, -2))
-        got = [exchange(mine, step) for step in steps]
+        length = peers // 2
+
+        def rotate(value, turn):
+            return lax.ppermute(
+                value, "aperture", [(2 * z + x, 2 * ((z + turn) % length) + x) for z in range(length) for x in range(2)]
+            )
+
+        got = [rotate(mine, turn) for turn in range(1, length)]
         near = exchange(mine, 1)
-        first, flat = lax.optimization_barrier((got[0], flat))
-        joined = call(join_kernel, "join", shape(((len(steps) - 1) * rows_dev, lanes), bf16),
-                      [VMEM] * (len(steps) - 1), VMEM, [], 10**6, 10**6)(*got[1:])
-        sections = [mine, near, first, joined, exchange(first, 1), exchange(joined, 1)]
-        steps = [0, 1, *steps, *(step ^ 1 for step in steps)]
-        after = [near, joined]
+        got[0], flat = lax.optimization_barrier((got[0], flat))
+        joined = call(join_kernel, "join", shape(((length - 2) * rows_dev, lanes), bf16),
+                      [VMEM] * (length - 2), VMEM, [], 10**6, 10**6)(*got[:-1])
+        sections = [mine, near, joined, got[-1], exchange(joined, 1), exchange(got[-1], 1)]
+        turns = list(range(1, length))
+        steps = [(0, 0), (0, 1), *((turn, 0) for turn in turns), *((turn, 1) for turn in turns)]
+        after = [near, joined, got[-1]]
     else:
         blocks = jnp.tile(mine[None], (peers, 1, 1))
         blocks = lax.all_to_all(blocks, "aperture", 0, 0, tiled=True)

time: 24.5 us -> 25.6 us (1.045)
  starting transfers between devices: 10.1 us -> 10.7 us
  waiting for transfers between devices: 1.76 us -> 2.33 us
    ppermute x0 -> x3, starting transfers between devices: none -> 7.02 us  [rotate(): lax.ppermute(value, 'aperture', [(2 * z + x, 2 * ((z + turn) % length) +...]
    ppermute x6 -> x3, starting transfers between devices: 10 us -> 3.58 us  [exchange(): lax.ppermute(value, 'aperture', [(index, index ^ step) for index in range...]
    ppermute x0 -> x3, waiting for transfers between devices: none -> 0.6 us  [rotate(): lax.ppermute(value, 'aperture', [(2 * z + x, 2 * ((z + turn) % length) +...]
    ppermute x6 -> x3, waiting for transfers between devices: 1.39 us -> 1.36 us  [exchange(): lax.ppermute(value, 'aperture', [(index, index ^ step) for index in range...]
  transfers between devices with their start and end apart: 8 -> 8, of which waited for: 3 -> 3; matrix products, arithmetic and copies ran while one was open for 0% -> 0% of each run, Pallas kernels for 22% -> 21%
where the time goes in v20:
time: 25.6 us; the launch traced here: 25.5 us
  Pallas kernels  11.8 us (46%)
  starting transfers between devices  10.7 us (42%)
  waiting for transfers between devices  2.33 us (9%)
  between operations  0.69 us (3%)
    ppermute x3, starting transfers between devices, rotate(): lax.ppermute(value, 'aperture', [(2 * z + x, 2 * ((z + turn) % length) +...  7.02 us
    pallas_call x1, Pallas kernels, on_device(): call(forward_kernel, 'forward', (shape((rows_dev, lanes), bf16), shape((p...  3.87 us
    ppermute x3, starting transfers between devices, exchange(): lax.ppermute(value, 'aperture', [(index, index ^ step) for index in range...  3.58 us
    pallas_call x1, Pallas kernels, on_device(): call(functools.partial(table_kernel, math.sqrt(rows * cols), cols), 'colu...  3.33 us
    pallas_call x1, Pallas kernels, on_device(): call(last_grad_kernel, 'gradient_far', (out, shape((pairs_dev,), f32)), [...  1.62 us
    ppermute x3, waiting for transfers between devices, exchange(): lax.ppermute(value, 'aperture', [(index, index ^ step) for index in range...  1.36 us
    pallas_call x1, Pallas kernels, on_device(): call(functools.partial(focus_kernel, steps), 'focus', (shape((rows_dev, l...  1.08 us
    pallas_call x1, Pallas kernels, on_device(): call(row_kernel, 'row_tables', (shape((pairs_dev, 2 * FOCAL, rows), bf16)...  1.04 us
  transfers between devices with their start and end apart: 8, of which 3 were waited for; matrix products, arithmetic and copies ran while one was open for 0% of the time, Pallas kernels for 21%

profile of v20, /device:TPU:0, one launch (start us, length us, event | category | flops | bytes accessed | tf_op | source)
XLA Modules:
  0.0 25.5 jit_solution(14432256273184996730)
XLA Ops:
  0.6 3.9 %forward.1 = (bf16[32,1024]{1,0:T(8,128)(2,1)S(1)}, f32[2,24,256]{2,1,0:T(8,128)S(1)}, f32[32,2048]{1,0:T(8,128)S(1)}) custom-call(s32[2]{0:T(128)} %wave_hbm.1, s32[2]{0:T(128)} %angle_hbm.1, s32[2,2]{1,0:T(2,128)} %aim_hbm.1, f32[16,256]{1,0:T(8,128)} %bitcast.1, f32[32,4096]{1,0:T(8,128)} %width_hbm.1), custom_call_target="tpu_custom_call" | custom-call | flops 1000000000 | bytes 10000000 | tf_op jit(solution)/shard_map/forward/pallas_call | solution.py:516
  4.5 3.1 %collective-permute-start = (bf16[32,1024]{1,0:T(8,128)(2,1)S(1)}, bf16[32,1024]{1,0:T(8,128)(2,1)S(1)}, u32[]{:S(2)}, u32[]{:S(2)}) collective-permute-start(bf16[32,1024]{1,0:T(8,128)(2,1)S(1)} %get-tuple-element.23.refs_0_), channel_id=1, source_target_pairs={{0,4},{2,6},{4,8},{6,10},{8,12},{10,14},{12,0},{14,2},{1,5},{3,7},... | collective-permute-start | bytes 196616 | tf_op jit(solution)/shard_map/ppermute | solution.py:552
  7.6 2.6 %collective-permute-start.3 = (bf16[32,1024]{1,0:T(8,128)(2,1)S(1)}, bf16[32,1024]{1,0:T(8,128)(2,1)S(1)}, u32[]{:S(2)}, u32[]{:S(2)}) collective-permute-start(bf16[32,1024]{1,0:T(8,128)(2,1)S(1)} %get-tuple-element.23.refs_0_), channel_id=1, source_target_pairs={{0,8},{2,10},{4,12},{6,14},{8,0},{10,2},{12,4},{14,6},{1,9},{3,11}... | collective-permute-start | bytes 196616 | tf_op jit(solution)/shard_map/ppermute | solution.py:552
  10.2 1.4 %collective-permute-start.4 = (bf16[32,1024]{1,0:T(8,128)(2,1)S(1)}, bf16[32,1024]{1,0:T(8,128)(2,1)S(1)}, u32[]{:S(2)}, u32[]{:S(2)}) collective-permute-start(bf16[32,1024]{1,0:T(8,128)(2,1)S(1)} %get-tuple-element.23.refs_0_), channel_id=1, source_target_pairs={{0,12},{2,14},{4,0},{6,2},{8,4},{10,6},{12,8},{14,10},{1,13},{3,15... | collective-permute-start | bytes 196616 | tf_op jit(solution)/shard_map/ppermute | solution.py:552
  11.5 1.5 %collective-permute-start.2 = (bf16[32,1024]{1,0:T(8,128)(2,1)S(1)}, bf16[32,1024]{1,0:T(8,128)(2,1)S(1)}, u32[]{:S(2)}, u32[]{:S(2)}) collective-permute-start(bf16[32,1024]{1,0:T(8,128)(2,1)S(1)} %get-tuple-element.23.refs_0_), channel_id=1, source_target_pairs={{0,2},{2,0},{4,6},{6,4},{8,10},{10,8},{12,14},{14,12},{1,3},{3,1},... | collective-permute-start | bytes 196616 | tf_op jit(solution)/shard_map/ppermute | solution.py:507
  13.0 0.0 collective-permute-start.1
  13.0 1.0 %row_tables.1 = (bf16[2,512,256]{2,1,0:T(8,128)(2,1)S(1)}, bf16[2,32,512]{2,1,0:T(8,128)(2,1)S(1)}, f32[2,256,256]{2,1,0:T(8,128)S(1)}, f32[2,8,128]{2,1,0:T(8,128)S(1)}) custom-call(f32[2,24,256]{2,1,0:T(8,128)S(1)} %get-tuple-element.21.info_ref), custom_call_target="tpu_custom_call" | custom-call | flops 100000000 | bytes 1000000 | tf_op jit(solution)/shard_map/row_tables/pallas_call | solution.py:540
  14.1 0.0 collective-permute-done.refs_0_
  14.1 0.6 %collective-permute-done.3.refs_1_ = bf16[32,1024]{1,0:T(8,128)(2,1)S(1)} collective-permute-done((bf16[32,1024]{1,0:T(8,128)(2,1)S(1)}, bf16[32,1024]{1,0:T(8,128)(2,1)S(1)}, u32[]{:S(2)}, u32[]{:S(2)}) %collective-permute-start.3) | collective-permute-done | bytes 65568 | tf_op jit(solution)/shard_map/ppermute | solution.py:552
  14.7 1.8 %collective-permute-start.5 = (bf16[64,1024]{1,0:T(8,128)(2,1)S(1)}, bf16[64,1024]{1,0:T(8,128)(2,1)S(1)}, u32[]{:S(2)}, u32[]{:S(2)}) collective-permute-start(bf16[64,1024]{1,0:T(8,128)(2,1)S(1)} %join.1.refs_1_.refs_2_), channel_id=1, source_target_pairs={{0,2},{2,0},{4,6},{6,4},{8,10},{10,8},{12,14},{14,12},{1,3},{3,1},... | collective-permute-start | bytes 393224 | tf_op jit(solution)/shard_map/ppermute | solution.py:507
  16.5 0.0 collective-permute-done.4.refs_2_.refs_3_
  16.5 0.3 %collective-permute-start.6 = (bf16[32,1024]{1,0:T(8,128)(2,1)S(1)}, bf16[32,1024]{1,0:T(8,128)(2,1)S(1)}, u32[]{:S(2)}, u32[]{:S(2)}) collective-permute-start(bf16[32,1024]{1,0:T(8,128)(2,1)S(1)} %collective-permute-done.4.refs_2_.refs_3_), channel_id=1, source_target_pairs={{0,2},{2,0},{4,6},{6,4},{8,10},{10,8},{12,14},{14,12},{1,3},{3,1},... | collective-permute-start | bytes 196616 | tf_op jit(solution)/shard_map/ppermute | solution.py:507
  16.8 0.0 collective-permute-done.1.far_info_ref
  16.8 0.0 collective-permute-done.2.refs_0_.refs_1_
  16.8 3.3 %column_tables.1 = (bf16[512,2048]{1,0:T(8,128)(2,1)S(1)}, bf16[512,2048]{1,0:T(8,128)(2,1)S(1)}, bf16[512,2048]{1,0:T(8,128)(2,1)S(1)}, bf16[512,2048]{1,0:T(8,...) custom-call(f32[2,24,256]{2,1,0:T(8,128)S(1)} %get-tuple-element.21., ...), custom_call_target="tpu_custom_call" | custom-call | flops 3000000000 | bytes 30000000 | tf_op jit(solution)/shard_map/column_tables/pallas_call | solution.py:570
  20.1 1.4 %collective-permute-done.6.refs_5_ = bf16[32,1024]{1,0:T(8,128)(2,1)S(1)} collective-permute-done((bf16[32,1024]{1,0:T(8,128)(2,1)S(1)}, bf16[32,1024]{1,0:T(8,128)(2,1)S(1)}, u32[]{:S(2)}, u32[]{:S(2)}) %collective-permute-start.6) | collective-permute-done | bytes 65568 | tf_op jit(solution)/shard_map/ppermute | solution.py:507
  21.5 0.0 collective-permute-done.5.refs_4_
  21.5 1.1 %focus.1 = (bf16[32,1024]{1,0:T(8,128)(2,1)S(1)}, f32[2,8,128]{2,1,0:T(8,128)S(1)}) custom-call(bf16[2,512,256]{2,1,0:T(8,128)(2,1)S(1)} %get-tuple-element.22.tall_ref, bf16[2,32,512]{2,1,0:T(8,128)(2,1)S(1)} %get-tuple-element.25.flat_ref, f32[2,256,256]{2,1,0:T(8,128)S(1)} %get-tuple-element.26.spot_ref, f32[2,8,128]{2,1,0:T(8,128)S(1)} %get-tuple-element.27.gain_ref, ...), custom_call_target="tpu_custom_call" | custom-call | flops 100000000 | bytes 1000000 | tf_op jit(solution)/shard_map/focus/pallas_call | solution.py:583
  22.6 0.1 collective-permute-start.7
  22.6 0.9 %gradient_own.1.refs_5_ = f32[32,2048]{1,0:T(8,128)S(1)} custom-call(bf16[32,1024]{1,0:T(8,128)(2,1)S(1)} %get-tuple-element.31.refs_0_, bf16[512,2048]{1,0:T(8,128)(2,1)S(1)} %get-tuple-element.36.refs_1_, bf16[512,2048]{1,0:T(8,128)(2,1)S(1)} %get-tuple-element.37.refs_2_, f32[2,32,2048]{2,1,0:T(8,128)S(1)} %get-tuple-element.30.after_ref.refs_3_, ...), custom_call_target="tpu_custom_call" | custom-call | flops 1000000000 | bytes 10000000 | tf_op jit(solution)/shard_map/gradient_own/pallas_call | solution.py:598
  23.5 0.4 %collective-permute-done.7.refs_0_ = bf16[32,1024]{1,0:T(8,128)(2,1)S(1)} collective-permute-done((bf16[32,1024]{1,0:T(8,128)(2,1)S(1)}, bf16[32,1024]{1,0:T(8,128)(2,1)S(1)}, u32[]{:S(2)}, u32[]{:S(2)}) %collective-permute-start.7) | collective-permute-done | bytes 65568 | tf_op jit(solution)/shard_map/ppermute | solution.py:510
  23.9 1.6 %gradient_far.1 = (f32[32,2048]{1,0:T(8,128)}, f32[2]{0:T(128)}) custom-call(bf16[32,1024]{1,0:T(8,128)(2,1)S(1)} %collective-permute-done.7.refs_0_, bf16[512,2048]{1,0:T(8,128)(2,1)S(1)} %get-tuple-element.32.refs_1_, bf16[512,2048]{1,0:T(8,128)(2,1)S(1)} %get-tuple-element.33.refs_2_, f32[2,32,2048]{2,1,0:T(8,128)S(1)} %get-tuple-element.34.refs_3_, ...), custom_call_target="tpu_custom_call" | custom-call | flops 1000000000 | bytes 10000000 | tf_op jit(solution)/shard_map/gradient_far/pallas_call | solution.py:602
  (1 shorter events, 0.0 us)
Async XLA Ops:
  4.5 9.6 %collective-permute-start = (bf16[32,1024]{1,0:T(8,128)(2,1)S(1)}, bf16[32,1024]{1,0:T(8,128)(2,1)S(1)}, u32[]{:S(2)}, u32[]{:S(2)}) collective-permute-start(bf16[32,1024]{1,0:T(8,128)(2,1)S(1)} %get-tuple-element.23.refs_0_), channel_id=1, source_target_pairs={{0,4},{2,6},{4,8},{6,10},{8,12},{10,14},{12,0},{14,2},{1,5},{3,7},... | collective-permute-start | bytes 196616 | tf_op jit(solution)/shard_map/ppermute | solution.py:552
  7.6 7.1 %collective-permute-start.3 = (bf16[32,1024]{1,0:T(8,128)(2,1)S(1)}, bf16[32,1024]{1,0:T(8,128)(2,1)S(1)}, u32[]{:S(2)}, u32[]{:S(2)}) collective-permute-start(bf16[32,1024]{1,0:T(8,128)(2,1)S(1)} %get-tuple-element.23.refs_0_), channel_id=1, source_target_pairs={{0,8},{2,10},{4,12},{6,14},{8,0},{10,2},{12,4},{14,6},{1,9},{3,11}... | collective-permute-start | bytes 196616 | tf_op jit(solution)/shard_map/ppermute | solution.py:552
  10.2 6.3 %collective-permute-start.4 = (bf16[32,1024]{1,0:T(8,128)(2,1)S(1)}, bf16[32,1024]{1,0:T(8,128)(2,1)S(1)}, u32[]{:S(2)}, u32[]{:S(2)}) collective-permute-start(bf16[32,1024]{1,0:T(8,128)(2,1)S(1)} %get-tuple-element.23.refs_0_), channel_id=1, source_target_pairs={{0,12},{2,14},{4,0},{6,2},{8,4},{10,6},{12,8},{14,10},{1,13},{3,15... | collective-permute-start | bytes 196616 | tf_op jit(solution)/shard_map/ppermute | solution.py:552
  11.5 5.3 %collective-permute-start.2 = (bf16[32,1024]{1,0:T(8,128)(2,1)S(1)}, bf16[32,1024]{1,0:T(8,128)(2,1)S(1)}, u32[]{:S(2)}, u32[]{:S(2)}) collective-permute-start(bf16[32,1024]{1,0:T(8,128)(2,1)S(1)} %get-tuple-element.23.refs_0_), channel_id=1, source_target_pairs={{0,2},{2,0},{4,6},{6,4},{8,10},{10,8},{12,14},{14,12},{1,3},{3,1},... | collective-permute-start | bytes 196616 | tf_op jit(solution)/shard_map/ppermute | solution.py:507
  13.0 3.8 %collective-permute-start.1 = (f32[2,24,256]{2,1,0:T(8,128)S(1)}, f32[2,24,256]{2,1,0:T(8,128)S(1)}, u32[]{:S(2)}, u32[]{:S(2)}) collective-permute-start(f32[2,24,256]{2,1,0:T(8,128)S(1)} %get-tuple-element.21.info_ref), channel_id=1, source_target_pairs={{0,1},{1,0},{2,3},{3,2},{4,5},{5,4},{6,7},{7,6},{8,9},{9,8},{10,11... | collective-permute-start | bytes 147464 | tf_op jit(solution)/shard_map/ppermute | solution.py:510
  14.7 6.8 %collective-permute-start.5 = (bf16[64,1024]{1,0:T(8,128)(2,1)S(1)}, bf16[64,1024]{1,0:T(8,128)(2,1)S(1)}, u32[]{:S(2)}, u32[]{:S(2)}) collective-permute-start(bf16[64,1024]{1,0:T(8,128)(2,1)S(1)} %join.1.refs_1_.refs_2_), channel_id=1, source_target_pairs={{0,2},{2,0},{4,6},{6,4},{8,10},{10,8},{12,14},{14,12},{1,3},{3,1},... | collective-permute-start | bytes 393224 | tf_op jit(solution)/shard_map/ppermute | solution.py:507
  16.5 5.0 %collective-permute-start.6 = (bf16[32,1024]{1,0:T(8,128)(2,1)S(1)}, bf16[32,1024]{1,0:T(8,128)(2,1)S(1)}, u32[]{:S(2)}, u32[]{:S(2)}) collective-permute-start(bf16[32,1024]{1,0:T(8,128)(2,1)S(1)} %collective-permute-done.4.refs_2_.refs_3_), channel_id=1, source_target_pairs={{0,2},{2,0},{4,6},{6,4},{8,10},{10,8},{12,14},{14,12},{1,3},{3,1},... | collective-permute-start | bytes 196616 | tf_op jit(solution)/shard_map/ppermute | solution.py:507
  22.6 1.3 %collective-permute-start.7 = (bf16[32,1024]{1,0:T(8,128)(2,1)S(1)}, bf16[32,1024]{1,0:T(8,128)(2,1)S(1)}, u32[]{:S(2)}, u32[]{:S(2)}) collective-permute-start(bf16[32,1024]{1,0:T(8,128)(2,1)S(1)} %get-tuple-element.31.refs_0_), channel_id=1, source_target_pairs={{0,1},{1,0},{2,3},{3,2},{4,5},{5,4},{6,7},{7,6},{8,9},{9,8},{10,11... | collective-permute-start | bytes 196616 | tf_op jit(solution)/shard_map/ppermute | solution.py:510

commit v21 on v19

--- a/solution.py
+++ b/solution.py
@@ -193,13 +193,13 @@
     moves = [
         pltpu.make_async_copy(source, target, sems.at[index])
         for index, (source, target) in enumerate((
-            (wave_hbm, wave_ref), (angle_hbm, angle_ref), (aim_hbm, aim_ref),
-            (coef_hbm, coef_ref), (width_hbm, width_ref),
+            (width_hbm, width_ref), (wave_hbm, wave_ref), (angle_hbm, angle_ref),
+            (coef_hbm, coef_ref), (aim_hbm, aim_ref),
         ))
     ]
     for move in moves:
         move.start()
-    for move in moves:
+    for move in moves[1:]:
         move.wait()
     for pair in range(pairs):
         coef = pick_coef(coef_ref[...], wave_ref[pair])
@@ -215,6 +215,7 @@
     for pair in range(pairs):
         own_waves(info_ref, pair, cols, base_ref.at[pair], centre_ref.at[pair])
     core = lax.axis_index("wave")
+    moves[0].wait()
     sides = side_pieces(width_ref, core)
     alone = jnp.where(core == 1, 0, half)
     column = width_ref[:, pl.ds(pl.multiple_of(alone, LANES), LANES)]

time: 24.5 us -> 24.4 us (level)
  no operation moved by 1% of the time
where the time goes in v21:
time: 24.4 us; the launch traced here: 24.2 us
  Pallas kernels  11.6 us (48%)
  starting transfers between devices  10.1 us (41%)
  waiting for transfers between devices  1.77 us (7%)
  between operations  0.69 us (3%)
    ppermute x6, starting transfers between devices, exchange(): lax.ppermute(value, 'aperture', [(index, index ^ step) for index in range...  10 us
    pallas_call x1, Pallas kernels, on_device(): call(forward_kernel, 'forward', (shape((rows_dev, lanes), bf16), shape((p...  3.72 us
    pallas_call x1, Pallas kernels, on_device(): call(functools.partial(table_kernel, math.sqrt(rows * cols), cols), 'colu...  3.33 us
    pallas_call x1, Pallas kernels, on_device(): call(last_grad_kernel, 'gradient_far', (out, shape((pairs_dev,), f32)), [...  1.62 us
    ppermute x6, waiting for transfers between devices, exchange(): lax.ppermute(value, 'aperture', [(index, index ^ step) for index in range...  1.4 us
    pallas_call x1, Pallas kernels, on_device(): call(functools.partial(focus_kernel, steps), 'focus', (shape((rows_dev, l...  1.06 us
    pallas_call x1, Pallas kernels, on_device(): call(row_kernel, 'row_tables', (shape((pairs_dev, 2 * FOCAL, rows), bf16)...  1.04 us
    pallas_call x1, Pallas kernels, on_device(): call(own_grad_kernel, 'gradient_own', out, [VMEM] * len(ins), VMEM, [], 1...  0.87 us
  transfers between devices with their start and end apart: 8, of which 3 were waited for; matrix products, arithmetic and copies ran while one was open for 0% of the time, Pallas kernels for 22%

profile of v21, /device:TPU:0, one launch (start us, length us, event | category | flops | bytes accessed | tf_op | source)
XLA Modules:
  0.0 24.2 jit_solution(3542246389074943322)
XLA Ops:
  0.6 3.7 %forward.1 = (bf16[32,1024]{1,0:T(8,128)(2,1)S(1)}, f32[2,24,256]{2,1,0:T(8,128)S(1)}, f32[32,2048]{1,0:T(8,128)S(1)}) custom-call(s32[2]{0:T(128)} %wave_hbm.1, s32[2]{0:T(128)} %angle_hbm.1, s32[2,2]{1,0:T(2,128)} %aim_hbm.1, f32[16,256]{1,0:T(8,128)} %bitcast.1, f32[32,4096]{1,0:T(8,128)} %width_hbm.1), custom_call_target="tpu_custom_call" | custom-call | flops 1000000000 | bytes 10000000 | tf_op jit(solution)/shard_map/forward/pallas_call | solution.py:515
  4.4 5.1 %collective-permute-start = (bf16[32,1024]{1,0:T(8,128)(2,1)S(1)}, bf16[32,1024]{1,0:T(8,128)(2,1)S(1)}, u32[]{:S(2)}, u32[]{:S(2)}) collective-permute-start(bf16[32,1024]{1,0:T(8,128)(2,1)S(1)} %get-tuple-element.23.refs_0_), channel_id=1, source_target_pairs={{0,12},{2,14},{4,8},{6,10},{8,4},{10,6},{12,0},{14,2},{1,13},{3,15... | collective-permute-start | bytes 196616 | tf_op jit(solution)/shard_map/ppermute | solution.py:506
  9.5 0.0 collective-permute-start.3
  9.5 0.6 %collective-permute-start.4 = (bf16[32,1024]{1,0:T(8,128)(2,1)S(1)}, bf16[32,1024]{1,0:T(8,128)(2,1)S(1)}, u32[]{:S(2)}, u32[]{:S(2)}) collective-permute-start(bf16[32,1024]{1,0:T(8,128)(2,1)S(1)} %get-tuple-element.23.refs_0_), channel_id=1, source_target_pairs={{0,4},{2,6},{4,0},{6,2},{8,12},{10,14},{12,8},{14,10},{1,5},{3,7},... | collective-permute-start | bytes 196616 | tf_op jit(solution)/shard_map/ppermute | solution.py:506
  10.1 1.6 %collective-permute-start.2 = (bf16[32,1024]{1,0:T(8,128)(2,1)S(1)}, bf16[32,1024]{1,0:T(8,128)(2,1)S(1)}, u32[]{:S(2)}, u32[]{:S(2)}) collective-permute-start(bf16[32,1024]{1,0:T(8,128)(2,1)S(1)} %get-tuple-element.23.refs_0_), channel_id=1, source_target_pairs={{0,2},{2,0},{4,6},{6,4},{8,10},{10,8},{12,14},{14,12},{1,3},{3,1},... | collective-permute-start | bytes 196616 | tf_op jit(solution)/shard_map/ppermute | solution.py:506
  11.8 0.0 collective-permute-start.1
  11.8 1.0 %row_tables.1 = (bf16[2,512,256]{2,1,0:T(8,128)(2,1)S(1)}, bf16[2,32,512]{2,1,0:T(8,128)(2,1)S(1)}, f32[2,256,256]{2,1,0:T(8,128)S(1)}, f32[2,8,128]{2,1,0:T(8,128)S(1)}) custom-call(f32[2,24,256]{2,1,0:T(8,128)S(1)} %get-tuple-element.21.info_ref), custom_call_target="tpu_custom_call" | custom-call | flops 100000000 | bytes 1000000 | tf_op jit(solution)/shard_map/row_tables/pallas_call | solution.py:539
  12.8 0.0 collective-permute-done.refs_2_
  12.8 1.1 %collective-permute-start.5 = (bf16[32,1024]{1,0:T(8,128)(2,1)S(1)}, bf16[32,1024]{1,0:T(8,128)(2,1)S(1)}, u32[]{:S(2)}, u32[]{:S(2)}) collective-permute-start(bf16[32,1024]{1,0:T(8,128)(2,1)S(1)} %collective-permute-done.refs_2_), channel_id=1, source_target_pairs={{0,2},{2,0},{4,6},{6,4},{8,10},{10,8},{12,14},{14,12},{1,3},{3,1},... | collective-permute-start | bytes 196616 | tf_op jit(solution)/shard_map/ppermute | solution.py:506
  13.9 1.2 %collective-permute-done.3.refs_0_ = bf16[32,1024]{1,0:T(8,128)(2,1)S(1)} collective-permute-done((bf16[32,1024]{1,0:T(8,128)(2,1)S(1)}, bf16[32,1024]{1,0:T(8,128)(2,1)S(1)}, u32[]{:S(2)}, u32[]{:S(2)}) %collective-permute-start.3) | collective-permute-done | bytes 65568 | tf_op jit(solution)/shard_map/ppermute | solution.py:506
  15.1 0.0 collective-permute-done.4.refs_1_
  15.1 1.6 %collective-permute-start.6 = (bf16[64,1024]{1,0:T(8,128)(2,1)S(1)}, bf16[64,1024]{1,0:T(8,128)(2,1)S(1)}, u32[]{:S(2)}, u32[]{:S(2)}) collective-permute-start(bf16[64,1024]{1,0:T(8,128)(2,1)S(1)} %join.1.refs_1_.refs_3_), channel_id=1, source_target_pairs={{0,2},{2,0},{4,6},{6,4},{8,10},{10,8},{12,14},{14,12},{1,3},{3,1},... | collective-permute-start | bytes 393224 | tf_op jit(solution)/shard_map/ppermute | solution.py:506
  16.7 0.0 collective-permute-done.1.far_info_ref
  16.7 0.0 collective-permute-done.2.refs_0_.refs_1_
  16.7 3.3 %column_tables.1 = (bf16[512,2048]{1,0:T(8,128)(2,1)S(1)}, bf16[512,2048]{1,0:T(8,128)(2,1)S(1)}, bf16[512,2048]{1,0:T(8,128)(2,1)S(1)}, bf16[512,2048]{1,0:T(8,...) custom-call(f32[2,24,256]{2,1,0:T(8,128)S(1)} %get-tuple-element.21., ...), custom_call_target="tpu_custom_call" | custom-call | flops 3000000000 | bytes 30000000 | tf_op jit(solution)/shard_map/column_tables/pallas_call | solution.py:562
  20.0 0.0 collective-permute-done.5.refs_4_
  20.0 0.2 collective-permute-done.6.refs_5_
  20.2 1.1 %focus.1 = (bf16[32,1024]{1,0:T(8,128)(2,1)S(1)}, f32[2,8,128]{2,1,0:T(8,128)S(1)}) custom-call(bf16[2,512,256]{2,1,0:T(8,128)(2,1)S(1)} %get-tuple-element.22.tall_ref, bf16[2,32,512]{2,1,0:T(8,128)(2,1)S(1)} %get-tuple-element.25.flat_ref, f32[2,256,256]{2,1,0:T(8,128)S(1)} %get-tuple-element.26.spot_ref, f32[2,8,128]{2,1,0:T(8,128)S(1)} %get-tuple-element.27.gain_ref, ...), custom_call_target="tpu_custom_call" | custom-call | flops 100000000 | bytes 1000000 | tf_op jit(solution)/shard_map/focus/pallas_call | solution.py:575
  21.3 0.1 collective-permute-start.7
  21.4 0.9 %gradient_own.1.refs_5_ = f32[32,2048]{1,0:T(8,128)S(1)} custom-call(bf16[32,1024]{1,0:T(8,128)(2,1)S(1)} %get-tuple-element.31.refs_0_, bf16[512,2048]{1,0:T(8,128)(2,1)S(1)} %get-tuple-element.36.refs_1_, bf16[512,2048]{1,0:T(8,128)(2,1)S(1)} %get-tuple-element.37.refs_2_, f32[2,32,2048]{2,1,0:T(8,128)S(1)} %get-tuple-element.29.after_ref.refs_3_, ...), custom_call_target="tpu_custom_call" | custom-call | flops 1000000000 | bytes 10000000 | tf_op jit(solution)/shard_map/gradient_own/pallas_call | solution.py:590
  22.2 0.4 %collective-permute-done.7.refs_0_ = bf16[32,1024]{1,0:T(8,128)(2,1)S(1)} collective-permute-done((bf16[32,1024]{1,0:T(8,128)(2,1)S(1)}, bf16[32,1024]{1,0:T(8,128)(2,1)S(1)}, u32[]{:S(2)}, u32[]{:S(2)}) %collective-permute-start.7) | collective-permute-done | bytes 65568 | tf_op jit(solution)/shard_map/ppermute | solution.py:509
  22.6 1.6 %gradient_far.1 = (f32[32,2048]{1,0:T(8,128)}, f32[2]{0:T(128)}) custom-call(bf16[32,1024]{1,0:T(8,128)(2,1)S(1)} %collective-permute-done.7.refs_0_, bf16[512,2048]{1,0:T(8,128)(2,1)S(1)} %get-tuple-element.32.refs_1_, bf16[512,2048]{1,0:T(8,128)(2,1)S(1)} %get-tuple-element.33.refs_2_, f32[2,32,2048]{2,1,0:T(8,128)S(1)} %get-tuple-element.34.refs_3_, ...), custom_call_target="tpu_custom_call" | custom-call | flops 1000000000 | bytes 10000000 | tf_op jit(solution)/shard_map/gradient_far/pallas_call | solution.py:594
  (1 shorter events, 0.0 us)
Async XLA Ops:
  4.4 8.4 %collective-permute-start = (bf16[32,1024]{1,0:T(8,128)(2,1)S(1)}, bf16[32,1024]{1,0:T(8,128)(2,1)S(1)}, u32[]{:S(2)}, u32[]{:S(2)}) collective-permute-start(bf16[32,1024]{1,0:T(8,128)(2,1)S(1)} %get-tuple-element.23.refs_0_), channel_id=1, source_target_pairs={{0,12},{2,14},{4,8},{6,10},{8,4},{10,6},{12,0},{14,2},{1,13},{3,15... | collective-permute-start | bytes 196616 | tf_op jit(solution)/shard_map/ppermute | solution.py:506
  9.5 5.6 %collective-permute-start.3 = (bf16[32,1024]{1,0:T(8,128)(2,1)S(1)}, bf16[32,1024]{1,0:T(8,128)(2,1)S(1)}, u32[]{:S(2)}, u32[]{:S(2)}) collective-permute-start(bf16[32,1024]{1,0:T(8,128)(2,1)S(1)} %get-tuple-element.23.refs_0_), channel_id=1, source_target_pairs={{0,8},{2,10},{4,12},{6,14},{8,0},{10,2},{12,4},{14,6},{1,9},{3,11}... | collective-permute-start | bytes 196616 | tf_op jit(solution)/shard_map/ppermute | solution.py:506
  9.5 5.6 %collective-permute-start.4 = (bf16[32,1024]{1,0:T(8,128)(2,1)S(1)}, bf16[32,1024]{1,0:T(8,128)(2,1)S(1)}, u32[]{:S(2)}, u32[]{:S(2)}) collective-permute-start(bf16[32,1024]{1,0:T(8,128)(2,1)S(1)} %get-tuple-element.23.refs_0_), channel_id=1, source_target_pairs={{0,4},{2,6},{4,0},{6,2},{8,12},{10,14},{12,8},{14,10},{1,5},{3,7},... | collective-permute-start | bytes 196616 | tf_op jit(solution)/shard_map/ppermute | solution.py:506
  10.1 6.5 %collective-permute-start.2 = (bf16[32,1024]{1,0:T(8,128)(2,1)S(1)}, bf16[32,1024]{1,0:T(8,128)(2,1)S(1)}, u32[]{:S(2)}, u32[]{:S(2)}) collective-permute-start(bf16[32,1024]{1,0:T(8,128)(2,1)S(1)} %get-tuple-element.23.refs_0_), channel_id=1, source_target_pairs={{0,2},{2,0},{4,6},{6,4},{8,10},{10,8},{12,14},{14,12},{1,3},{3,1},... | collective-permute-start | bytes 196616 | tf_op jit(solution)/shard_map/ppermute | solution.py:506
  11.8 4.9 %collective-permute-start.1 = (f32[2,24,256]{2,1,0:T(8,128)S(1)}, f32[2,24,256]{2,1,0:T(8,128)S(1)}, u32[]{:S(2)}, u32[]{:S(2)}) collective-permute-start(f32[2,24,256]{2,1,0:T(8,128)S(1)} %get-tuple-element.21.info_ref), channel_id=1, source_target_pairs={{0,1},{1,0},{2,3},{3,2},{4,5},{5,4},{6,7},{7,6},{8,9},{9,8},{10,11... | collective-permute-start | bytes 147464 | tf_op jit(solution)/shard_map/ppermute | solution.py:509
  12.8 7.2 %collective-permute-start.5 = (bf16[32,1024]{1,0:T(8,128)(2,1)S(1)}, bf16[32,1024]{1,0:T(8,128)(2,1)S(1)}, u32[]{:S(2)}, u32[]{:S(2)}) collective-permute-start(bf16[32,1024]{1,0:T(8,128)(2,1)S(1)} %collective-permute-done.refs_2_), channel_id=1, source_target_pairs={{0,2},{2,0},{4,6},{6,4},{8,10},{10,8},{12,14},{14,12},{1,3},{3,1},... | collective-permute-start | bytes 196616 | tf_op jit(solution)/shard_map/ppermute | solution.py:506
  15.1 5.1 %collective-permute-start.6 = (bf16[64,1024]{1,0:T(8,128)(2,1)S(1)}, bf16[64,1024]{1,0:T(8,128)(2,1)S(1)}, u32[]{:S(2)}, u32[]{:S(2)}) collective-permute-start(bf16[64,1024]{1,0:T(8,128)(2,1)S(1)} %join.1.refs_1_.refs_3_), channel_id=1, source_target_pairs={{0,2},{2,0},{4,6},{6,4},{8,10},{10,8},{12,14},{14,12},{1,3},{3,1},... | collective-permute-start | bytes 393224 | tf_op jit(solution)/shard_map/ppermute | solution.py:506
  21.3 1.3 %collective-permute-start.7 = (bf16[32,1024]{1,0:T(8,128)(2,1)S(1)}, bf16[32,1024]{1,0:T(8,128)(2,1)S(1)}, u32[]{:S(2)}, u32[]{:S(2)}) collective-permute-start(bf16[32,1024]{1,0:T(8,128)(2,1)S(1)} %get-tuple-element.31.refs_0_), channel_id=1, source_target_pairs={{0,1},{1,0},{2,3},{3,2},{4,5},{5,4},{6,7},{7,6},{8,9},{9,8},{10,11... | collective-permute-start | bytes 196616 | tf_op jit(solution)/shard_map/ppermute | solution.py:509

commit v22 on v21

--- a/solution.py
+++ b/solution.py
@@ -108,28 +108,24 @@
     return value.reshape(value.shape[0] * SUBLANES, value.shape[2])
 
 
+def side_by_side(s, power_ref, pairs, lowest):
+    s = split_rows(s)
+    firsts = [(pair, part * TERMS) for pair, part in itertools.product(range(pairs), range(2))]
+    values = [power_ref[pair, first + TERMS - 1] * s for pair, first in firsts]
+    for power in range(TERMS - 2, lowest - 1, -1):
+        values = [value + power_ref[pair, first + power] for value, (pair, first) in zip(values, firsts)]
+        if power > lowest:
+            values = [value * s for value in values]
+    values = [join_rows(value) for value in values]
+    return [values[2 * pair : 2 * pair + 2] for pair in range(pairs)]
+
+
 def near_fields(s, power_ref, pairs):
-    s = split_rows(s)
-    outs = []
-    for pair, part in itertools.product(range(pairs), range(2)):
-        row = (part + 1) * TERMS - 1
-        value = power_ref[pair, row] * s + power_ref[pair, row - 1]
-        for row in range(row - 2, part * TERMS - 1, -1):
-            value = value * s + power_ref[pair, row]
-        outs.append(join_rows(value))
-    return [outs[2 * pair : 2 * pair + 2] for pair in range(pairs)]
+    return side_by_side(s, power_ref, pairs, 0)
 
 
 def near_slopes(s, power_ref, pairs):
-    s = split_rows(s)
-    outs = []
-    for pair, part in itertools.product(range(pairs), range(2)):
-        row = (part + 1) * TERMS - 1
-        value = power_ref[pair, row] * s + power_ref[pair, row - 1]
-        for row in range(row - 2, part * TERMS, -1):
-            value = value * s + power_ref[pair, row]
-        outs.append(join_rows(value))
-    return [outs[2 * pair : 2 * pair + 2] for pair in range(pairs)]
+    return side_by_side(s, power_ref, pairs, 1)
 
 
 def turn_round(value):

time: 24.4 us -> 24.4 us (level)
  no operation moved by 1% of the time
where the time goes in v22:
time: 24.4 us; the launch traced here: 24.2 us
  Pallas kernels  11.7 us (48%)
  starting transfers between devices  10.1 us (41%)
  waiting for transfers between devices  1.75 us (7%)
  between operations  0.69 us (3%)
    ppermute x6, starting transfers between devices, exchange(): lax.ppermute(value, 'aperture', [(index, index ^ step) for index in range...  10 us
    pallas_call x1, Pallas kernels, on_device(): call(forward_kernel, 'forward', (shape((rows_dev, lanes), bf16), shape((p...  3.72 us
    pallas_call x1, Pallas kernels, on_device(): call(functools.partial(table_kernel, math.sqrt(rows * cols), cols), 'colu...  3.35 us
    pallas_call x1, Pallas kernels, on_device(): call(last_grad_kernel, 'gradient_far', (out, shape((pairs_dev,), f32)), [...  1.62 us
    ppermute x6, waiting for transfers between devices, exchange(): lax.ppermute(value, 'aperture', [(index, index ^ step) for index in range...  1.38 us
    pallas_call x1, Pallas kernels, on_device(): call(functools.partial(focus_kernel, steps), 'focus', (shape((rows_dev, l...  1.06 us
    pallas_call x1, Pallas kernels, on_device(): call(row_kernel, 'row_tables', (shape((pairs_dev, 2 * FOCAL, rows), bf16)...  1.04 us
    pallas_call x1, Pallas kernels, on_device(): call(own_grad_kernel, 'gradient_own', out, [VMEM] * len(ins), VMEM, [], 1...  0.87 us
  transfers between devices with their start and end apart: 8, of which 3 were waited for; matrix products, arithmetic and copies ran while one was open for 0% of the time, Pallas kernels for 22%

profile of v22, /device:TPU:0, one launch (start us, length us, event | category | flops | bytes accessed | tf_op | source)
XLA Modules:
  0.0 24.2 jit_solution(11493679391167357850)
XLA Ops:
  0.6 3.7 %forward.1 = (bf16[32,1024]{1,0:T(8,128)(2,1)S(1)}, f32[2,24,256]{2,1,0:T(8,128)S(1)}, f32[32,2048]{1,0:T(8,128)S(1)}) custom-call(s32[2]{0:T(128)} %wave_hbm.1, s32[2]{0:T(128)} %angle_hbm.1, s32[2,2]{1,0:T(2,128)} %aim_hbm.1, f32[16,256]{1,0:T(8,128)} %bitcast.1, f32[32,4096]{1,0:T(8,128)} %width_hbm.1), custom_call_target="tpu_custom_call" | custom-call | flops 1000000000 | bytes 10000000 | tf_op jit(solution)/shard_map/forward/pallas_call | solution.py:511
  4.4 5.1 %collective-permute-start = (bf16[32,1024]{1,0:T(8,128)(2,1)S(1)}, bf16[32,1024]{1,0:T(8,128)(2,1)S(1)}, u32[]{:S(2)}, u32[]{:S(2)}) collective-permute-start(bf16[32,1024]{1,0:T(8,128)(2,1)S(1)} %get-tuple-element.23.refs_0_), channel_id=1, source_target_pairs={{0,12},{2,14},{4,8},{6,10},{8,4},{10,6},{12,0},{14,2},{1,13},{3,15... | collective-permute-start | bytes 196616 | tf_op jit(solution)/shard_map/ppermute | solution.py:502
  9.5 0.0 collective-permute-start.3
  9.5 0.6 %collective-permute-start.4 = (bf16[32,1024]{1,0:T(8,128)(2,1)S(1)}, bf16[32,1024]{1,0:T(8,128)(2,1)S(1)}, u32[]{:S(2)}, u32[]{:S(2)}) collective-permute-start(bf16[32,1024]{1,0:T(8,128)(2,1)S(1)} %get-tuple-element.23.refs_0_), channel_id=1, source_target_pairs={{0,4},{2,6},{4,0},{6,2},{8,12},{10,14},{12,8},{14,10},{1,5},{3,7},... | collective-permute-start | bytes 196616 | tf_op jit(solution)/shard_map/ppermute | solution.py:502
  10.1 1.6 %collective-permute-start.2 = (bf16[32,1024]{1,0:T(8,128)(2,1)S(1)}, bf16[32,1024]{1,0:T(8,128)(2,1)S(1)}, u32[]{:S(2)}, u32[]{:S(2)}) collective-permute-start(bf16[32,1024]{1,0:T(8,128)(2,1)S(1)} %get-tuple-element.23.refs_0_), channel_id=1, source_target_pairs={{0,2},{2,0},{4,6},{6,4},{8,10},{10,8},{12,14},{14,12},{1,3},{3,1},... | collective-permute-start | bytes 196616 | tf_op jit(solution)/shard_map/ppermute | solution.py:502
  11.8 0.0 collective-permute-start.1
  11.8 1.0 %row_tables.1 = (bf16[2,512,256]{2,1,0:T(8,128)(2,1)S(1)}, bf16[2,32,512]{2,1,0:T(8,128)(2,1)S(1)}, f32[2,256,256]{2,1,0:T(8,128)S(1)}, f32[2,8,128]{2,1,0:T(8,128)S(1)}) custom-call(f32[2,24,256]{2,1,0:T(8,128)S(1)} %get-tuple-element.21.info_ref), custom_call_target="tpu_custom_call" | custom-call | flops 100000000 | bytes 1000000 | tf_op jit(solution)/shard_map/row_tables/pallas_call | solution.py:535
  12.8 0.0 collective-permute-done.refs_2_
  12.8 1.1 %collective-permute-start.5 = (bf16[32,1024]{1,0:T(8,128)(2,1)S(1)}, bf16[32,1024]{1,0:T(8,128)(2,1)S(1)}, u32[]{:S(2)}, u32[]{:S(2)}) collective-permute-start(bf16[32,1024]{1,0:T(8,128)(2,1)S(1)} %collective-permute-done.refs_2_), channel_id=1, source_target_pairs={{0,2},{2,0},{4,6},{6,4},{8,10},{10,8},{12,14},{14,12},{1,3},{3,1},... | collective-permute-start | bytes 196616 | tf_op jit(solution)/shard_map/ppermute | solution.py:502
  13.9 1.2 %collective-permute-done.3.refs_0_ = bf16[32,1024]{1,0:T(8,128)(2,1)S(1)} collective-permute-done((bf16[32,1024]{1,0:T(8,128)(2,1)S(1)}, bf16[32,1024]{1,0:T(8,128)(2,1)S(1)}, u32[]{:S(2)}, u32[]{:S(2)}) %collective-permute-start.3) | collective-permute-done | bytes 65568 | tf_op jit(solution)/shard_map/ppermute | solution.py:502
  15.1 0.0 collective-permute-done.4.refs_1_
  15.1 1.6 %collective-permute-start.6 = (bf16[64,1024]{1,0:T(8,128)(2,1)S(1)}, bf16[64,1024]{1,0:T(8,128)(2,1)S(1)}, u32[]{:S(2)}, u32[]{:S(2)}) collective-permute-start(bf16[64,1024]{1,0:T(8,128)(2,1)S(1)} %join.1.refs_1_.refs_3_), channel_id=1, source_target_pairs={{0,2},{2,0},{4,6},{6,4},{8,10},{10,8},{12,14},{14,12},{1,3},{3,1},... | collective-permute-start | bytes 393224 | tf_op jit(solution)/shard_map/ppermute | solution.py:502
  16.7 0.0 collective-permute-done.1.far_info_ref
  16.7 0.0 collective-permute-done.2.refs_0_.refs_1_
  16.7 3.4 %column_tables.1 = (bf16[512,2048]{1,0:T(8,128)(2,1)S(1)}, bf16[512,2048]{1,0:T(8,128)(2,1)S(1)}, bf16[512,2048]{1,0:T(8,128)(2,1)S(1)}, bf16[512,2048]{1,0:T(8,...) custom-call(f32[2,24,256]{2,1,0:T(8,128)S(1)} %get-tuple-element.21., ...), custom_call_target="tpu_custom_call" | custom-call | flops 3000000000 | bytes 30000000 | tf_op jit(solution)/shard_map/column_tables/pallas_call | solution.py:558
  20.0 0.0 collective-permute-done.5.refs_4_
  20.0 0.2 collective-permute-done.6.refs_5_
  20.2 1.1 %focus.1 = (bf16[32,1024]{1,0:T(8,128)(2,1)S(1)}, f32[2,8,128]{2,1,0:T(8,128)S(1)}) custom-call(bf16[2,512,256]{2,1,0:T(8,128)(2,1)S(1)} %get-tuple-element.22.tall_ref, bf16[2,32,512]{2,1,0:T(8,128)(2,1)S(1)} %get-tuple-element.25.flat_ref, f32[2,256,256]{2,1,0:T(8,128)S(1)} %get-tuple-element.26.spot_ref, f32[2,8,128]{2,1,0:T(8,128)S(1)} %get-tuple-element.27.gain_ref, ...), custom_call_target="tpu_custom_call" | custom-call | flops 100000000 | bytes 1000000 | tf_op jit(solution)/shard_map/focus/pallas_call | solution.py:571
  21.3 0.1 collective-permute-start.7
  21.4 0.9 %gradient_own.1.refs_5_ = f32[32,2048]{1,0:T(8,128)S(1)} custom-call(bf16[32,1024]{1,0:T(8,128)(2,1)S(1)} %get-tuple-element.31.refs_0_, bf16[512,2048]{1,0:T(8,128)(2,1)S(1)} %get-tuple-element.36.refs_1_, bf16[512,2048]{1,0:T(8,128)(2,1)S(1)} %get-tuple-element.37.refs_2_, f32[2,32,2048]{2,1,0:T(8,128)S(1)} %get-tuple-element.29.after_ref.refs_3_, ...), custom_call_target="tpu_custom_call" | custom-call | flops 1000000000 | bytes 10000000 | tf_op jit(solution)/shard_map/gradient_own/pallas_call | solution.py:586
  22.2 0.4 %collective-permute-done.7.refs_0_ = bf16[32,1024]{1,0:T(8,128)(2,1)S(1)} collective-permute-done((bf16[32,1024]{1,0:T(8,128)(2,1)S(1)}, bf16[32,1024]{1,0:T(8,128)(2,1)S(1)}, u32[]{:S(2)}, u32[]{:S(2)}) %collective-permute-start.7) | collective-permute-done | bytes 65568 | tf_op jit(solution)/shard_map/ppermute | solution.py:505
  22.6 1.6 %gradient_far.1 = (f32[32,2048]{1,0:T(8,128)}, f32[2]{0:T(128)}) custom-call(bf16[32,1024]{1,0:T(8,128)(2,1)S(1)} %collective-permute-done.7.refs_0_, bf16[512,2048]{1,0:T(8,128)(2,1)S(1)} %get-tuple-element.32.refs_1_, bf16[512,2048]{1,0:T(8,128)(2,1)S(1)} %get-tuple-element.33.refs_2_, f32[2,32,2048]{2,1,0:T(8,128)S(1)} %get-tuple-element.34.refs_3_, ...), custom_call_target="tpu_custom_call" | custom-call | flops 1000000000 | bytes 10000000 | tf_op jit(solution)/shard_map/gradient_far/pallas_call | solution.py:590
  (1 shorter events, 0.0 us)
Async XLA Ops:
  4.4 8.4 %collective-permute-start = (bf16[32,1024]{1,0:T(8,128)(2,1)S(1)}, bf16[32,1024]{1,0:T(8,128)(2,1)S(1)}, u32[]{:S(2)}, u32[]{:S(2)}) collective-permute-start(bf16[32,1024]{1,0:T(8,128)(2,1)S(1)} %get-tuple-element.23.refs_0_), channel_id=1, source_target_pairs={{0,12},{2,14},{4,8},{6,10},{8,4},{10,6},{12,0},{14,2},{1,13},{3,15... | collective-permute-start | bytes 196616 | tf_op jit(solution)/shard_map/ppermute | solution.py:502
  9.5 5.6 %collective-permute-start.3 = (bf16[32,1024]{1,0:T(8,128)(2,1)S(1)}, bf16[32,1024]{1,0:T(8,128)(2,1)S(1)}, u32[]{:S(2)}, u32[]{:S(2)}) collective-permute-start(bf16[32,1024]{1,0:T(8,128)(2,1)S(1)} %get-tuple-element.23.refs_0_), channel_id=1, source_target_pairs={{0,8},{2,10},{4,12},{6,14},{8,0},{10,2},{12,4},{14,6},{1,9},{3,11}... | collective-permute-start | bytes 196616 | tf_op jit(solution)/shard_map/ppermute | solution.py:502
  9.5 5.6 %collective-permute-start.4 = (bf16[32,1024]{1,0:T(8,128)(2,1)S(1)}, bf16[32,1024]{1,0:T(8,128)(2,1)S(1)}, u32[]{:S(2)}, u32[]{:S(2)}) collective-permute-start(bf16[32,1024]{1,0:T(8,128)(2,1)S(1)} %get-tuple-element.23.refs_0_), channel_id=1, source_target_pairs={{0,4},{2,6},{4,0},{6,2},{8,12},{10,14},{12,8},{14,10},{1,5},{3,7},... | collective-permute-start | bytes 196616 | tf_op jit(solution)/shard_map/ppermute | solution.py:502
  10.1 6.5 %collective-permute-start.2 = (bf16[32,1024]{1,0:T(8,128)(2,1)S(1)}, bf16[32,1024]{1,0:T(8,128)(2,1)S(1)}, u32[]{:S(2)}, u32[]{:S(2)}) collective-permute-start(bf16[32,1024]{1,0:T(8,128)(2,1)S(1)} %get-tuple-element.23.refs_0_), channel_id=1, source_target_pairs={{0,2},{2,0},{4,6},{6,4},{8,10},{10,8},{12,14},{14,12},{1,3},{3,1},... | collective-permute-start | bytes 196616 | tf_op jit(solution)/shard_map/ppermute | solution.py:502
  11.8 4.9 %collective-permute-start.1 = (f32[2,24,256]{2,1,0:T(8,128)S(1)}, f32[2,24,256]{2,1,0:T(8,128)S(1)}, u32[]{:S(2)}, u32[]{:S(2)}) collective-permute-start(f32[2,24,256]{2,1,0:T(8,128)S(1)} %get-tuple-element.21.info_ref), channel_id=1, source_target_pairs={{0,1},{1,0},{2,3},{3,2},{4,5},{5,4},{6,7},{7,6},{8,9},{9,8},{10,11... | collective-permute-start | bytes 147464 | tf_op jit(solution)/shard_map/ppermute | solution.py:505
  12.8 7.2 %collective-permute-start.5 = (bf16[32,1024]{1,0:T(8,128)(2,1)S(1)}, bf16[32,1024]{1,0:T(8,128)(2,1)S(1)}, u32[]{:S(2)}, u32[]{:S(2)}) collective-permute-start(bf16[32,1024]{1,0:T(8,128)(2,1)S(1)} %collective-permute-done.refs_2_), channel_id=1, source_target_pairs={{0,2},{2,0},{4,6},{6,4},{8,10},{10,8},{12,14},{14,12},{1,3},{3,1},... | collective-permute-start | bytes 196616 | tf_op jit(solution)/shard_map/ppermute | solution.py:502
  15.1 5.1 %collective-permute-start.6 = (bf16[64,1024]{1,0:T(8,128)(2,1)S(1)}, bf16[64,1024]{1,0:T(8,128)(2,1)S(1)}, u32[]{:S(2)}, u32[]{:S(2)}) collective-permute-start(bf16[64,1024]{1,0:T(8,128)(2,1)S(1)} %join.1.refs_1_.refs_3_), channel_id=1, source_target_pairs={{0,2},{2,0},{4,6},{6,4},{8,10},{10,8},{12,14},{14,12},{1,3},{3,1},... | collective-permute-start | bytes 393224 | tf_op jit(solution)/shard_map/ppermute | solution.py:502
  21.3 1.3 %collective-permute-start.7 = (bf16[32,1024]{1,0:T(8,128)(2,1)S(1)}, bf16[32,1024]{1,0:T(8,128)(2,1)S(1)}, u32[]{:S(2)}, u32[]{:S(2)}) collective-permute-start(bf16[32,1024]{1,0:T(8,128)(2,1)S(1)} %get-tuple-element.31.refs_0_), channel_id=1, source_target_pairs={{0,1},{1,0},{2,3},{3,2},{4,5},{5,4},{6,7},{7,6},{8,9},{9,8},{10,11... | collective-permute-start | bytes 196616 | tf_op jit(solution)/shard_map/ppermute | solution.py:505

commit v23 on v21

--- a/solution.py
+++ b/solution.py
@@ -20,7 +20,7 @@
 SUBLANES = 8
 VMEM_LIMIT = 16 * 1024 * 1024
 WAVE_ROW, ANGLE_ROW, AIM_ROW, INFO_ROWS = 16, 17, 18, 24
-DIRECT = 16
+CUBE = 8
 
 COS = (
     1.0, -19.7392088015709, 64.93939395773512, -85.45681453397417, 60.24458621302471,
@@ -181,12 +181,11 @@
 
 
 def forward_kernel(
-    wave_hbm, angle_hbm, aim_hbm, coef_hbm, width_hbm, mine_ref, info_ref, own_ref, *refs
+    wave_hbm, angle_hbm, aim_hbm, coef_hbm, width_hbm, mine_ref, info_ref, own_ref, base_ref, centre_ref, *refs
 ):
     pairs = info_ref.shape[0]
     (
-        wave_ref, angle_ref, aim_ref, coef_ref, width_ref, base_ref, centre_ref, power_ref, near_ref, table_ref,
-        acc_ref, sems,
+        wave_ref, angle_ref, aim_ref, coef_ref, width_ref, power_ref, near_ref, table_ref, acc_ref, sems,
     ) = refs
     rows_dev, cols = width_ref.shape
     half = cols // 2
@@ -315,13 +314,6 @@
         gain_ref[pair] = jnp.broadcast_to(FOCAL * FOCAL / total_of(total), gain_ref.shape[1:])
 
 
-def join_kernel(*refs):
-    *in_refs, out_ref = refs
-    count = in_refs[0].shape[0]
-    for index, ref in enumerate(in_refs):
-        out_ref[index * count : (index + 1) * count, :] = ref[...]
-
-
 def focus_kernel(steps, tall_ref, flat_ref, spot_ref, gain_ref, after_ref, *refs):
     del after_ref
     *sect_refs, back_ref, score_ref, rows_ref, mixed_ref, field_ref, stack_ref = refs
@@ -375,7 +367,7 @@
         back_ref[:, lane : lane + 2 * FOCAL] = back.astype(jnp.bfloat16)
 
 
-def table_kernel(scale, cols, info_ref, far_info_ref, width_ref, *refs):
+def table_kernel(scale, cols, info_ref, far_info_ref, width_ref, own_base_ref, own_centre_ref, *refs):
     *out_refs, base_ref, centre_ref, turned_ref, power_ref = refs
     pairs = power_ref.shape[0]
     out_refs = out_refs[-2 * pairs :]
@@ -386,11 +378,15 @@
     for pair, (ref, source) in enumerate(sources):
         power = power_coefs(ref[source, : 2 * TERMS, :LANES])
         power_ref[pair] = as_tiles(power * ((iota(power.shape, 0) % TERMS).astype(jnp.float32) * scale))
-        own_waves(ref, source, cols, base_ref.at[pair], centre_ref.at[pair])
+        if ref is info_ref:
+            bases, middles = own_base_ref.at[source], own_centre_ref.at[source]
+        else:
+            bases, middles = base_ref.at[source], centre_ref.at[source]
+            own_waves(ref, source, cols, bases, middles)
         for part, row, lane in itertools.product(range(2), range(0, BLOCK, LANES), range(0, FOCAL, LANES)):
-            tile = base_ref[pair, part, row : row + LANES, lane : lane + LANES]
+            tile = bases[part, row : row + LANES, lane : lane + LANES]
             turned_ref[pair, part, lane : lane + LANES, row : row + LANES] = tile.T
-        centres.append([centre_ref[pair, part].T for part in range(2)])
+        centres.append([middles[part].T for part in range(2)])
     for index in range(own_cols // (2 * BLOCK)):
         starts = block_starts(own_cols, index)
         for pair in range(pairs):
@@ -512,20 +508,20 @@
         pltpu.VMEM((pairs_dev, 2, BLOCK, FOCAL), f32),
         pltpu.VMEM((pairs_dev, 2, 8, FOCAL), f32),
     ]
-    mine, info, own = call(
+    mine, info, own, base, centre = call(
         forward_kernel, "forward",
         (
             shape((rows_dev, lanes), bf16),
             shape((pairs_dev, INFO_ROWS, FOCAL), f32), shape((rows_dev, own_cols), f32),
+            *(shape(ref.shape, f32) for ref in waves),
         ),
-        [HBM] * 5, (VMEM,) * 3,
+        [HBM] * 5, (VMEM,) * 5,
         [
             pltpu.SMEM(wave_ids.shape, jnp.int32),
             pltpu.SMEM(angle_ids.shape, jnp.int32),
             pltpu.SMEM(targets.shape, jnp.int32),
             pltpu.VMEM(coef_table.shape[::-1], f32),
             pltpu.VMEM(widths.shape, f32),
-            *waves,
             pltpu.VMEM((pairs_dev, 2 * TERMS, SUBLANES, LANES), f32),
             pltpu.VMEM((pairs_dev, 4 * rows_dev, own_cols), bf16),
             pltpu.VMEM((pairs_dev, own_cols, 2 * FOCAL), bf16),
@@ -544,16 +540,14 @@
         ),
         [VMEM], (VMEM,) * 4, [], 10**8, 10**6,
     )(info)
-    if peers <= DIRECT:
-        steps = list(range(peers - 2, 0, -2))
-        got = [exchange(mine, step) for step in steps]
+    if peers == CUBE:
+        last, middle, beside = (exchange(mine, step) for step in (6, 4, 2))
         near = exchange(mine, 1)
-        first, flat = lax.optimization_barrier((got[0], flat))
-        joined = call(join_kernel, "join", shape(((len(steps) - 1) * rows_dev, lanes), bf16),
-                      [VMEM] * (len(steps) - 1), VMEM, [], 10**6, 10**6)(*got[1:])
-        sections = [mine, near, first, joined, exchange(first, 1), exchange(joined, 1)]
-        steps = [0, 1, *steps, *(step ^ 1 for step in steps)]
-        after = [near, joined]
+        corner = exchange(mine, 3)
+        last, flat = lax.optimization_barrier((last, flat))
+        sections = [mine, near, last, middle, beside, corner, exchange(last, 1), exchange(middle, 1)]
+        steps = [0, 1, 6, 4, 2, 3, 7, 5]
+        after = [near, corner, middle, beside]
     else:
         blocks = jnp.tile(mine[None], (peers, 1, 1))
         blocks = lax.all_to_all(blocks, "aperture", 0, 0, tiled=True)
@@ -561,15 +555,14 @@
     outs = [shape((2 * FOCAL, own_cols), bf16)] * pairs + [shape((2, rows_dev, own_cols), f32)] * pairs
     made = call(
         functools.partial(table_kernel, math.sqrt(rows * cols), cols), "column_tables",
-        outs, [VMEM] * 3 + [ANY] * len(after), [VMEM] * len(outs),
+        outs, [VMEM] * 5 + [ANY] * len(after), [VMEM] * len(outs),
         [
-            pltpu.VMEM((pairs, 2, BLOCK, FOCAL), f32),
-            pltpu.VMEM((pairs, 2, 8, FOCAL), f32),
+            *waves,
             pltpu.VMEM((pairs, 2, FOCAL, BLOCK), f32),
             pltpu.VMEM((pairs, 2 * TERMS, SUBLANES, LANES), f32),
         ],
         30 * 10**8, 30 * 10**6,
-    )(info, far_info, own, *after)
+    )(info, far_info, own, base, centre, *after)
     tables, slopes = made[:pairs], made[pairs:]
 
     back, scores = call(

time: 24.4 us -> 24.6 us (level)
  starting transfers between devices: 10.1 us -> 11.1 us
  waiting for transfers between devices: 1.77 us -> 1.13 us
    ppermute x6 -> x7, starting transfers between devices: 10 us -> 11.1 us  [exchange(): lax.ppermute(value, 'aperture', [(index, index ^ step) for index in range...]
    ppermute x6 -> x7, waiting for transfers between devices: 1.4 us -> 0.56 us  [exchange(): lax.ppermute(value, 'aperture', [(index, index ^ step) for index in range...]
  transfers between devices with their start and end apart: 8 -> 9, of which waited for: 3 -> 3; matrix products, arithmetic and copies ran while one was open for 0% -> 0% of each run, Pallas kernels for 22% -> 21%
where the time goes in v23:
time: 24.6 us; the launch traced here: 24.4 us
  Pallas kernels  11.5 us (47%)
  starting transfers between devices  11.1 us (45%)
  waiting for transfers between devices  1.13 us (5%)
  between operations  0.69 us (3%)
    ppermute x7, starting transfers between devices, exchange(): lax.ppermute(value, 'aperture', [(index, index ^ step) for index in range...  11.1 us
    pallas_call x1, Pallas kernels, on_device(): call(forward_kernel, 'forward', (shape((rows_dev, lanes), bf16), shape((p...  3.67 us
    pallas_call x1, Pallas kernels, on_device(): call(functools.partial(table_kernel, math.sqrt(rows * cols), cols), 'colu...  3.27 us
    pallas_call x1, Pallas kernels, on_device(): call(last_grad_kernel, 'gradient_far', (out, shape((pairs_dev,), f32)), [...  1.61 us
    pallas_call x1, Pallas kernels, on_device(): call(functools.partial(focus_kernel, steps), 'focus', (shape((rows_dev, l...  1.05 us
    pallas_call x1, Pallas kernels, on_device(): call(row_kernel, 'row_tables', (shape((pairs_dev, 2 * FOCAL, rows), bf16)...  1.04 us
    pallas_call x1, Pallas kernels, on_device(): call(own_grad_kernel, 'gradient_own', out, [VMEM] * len(ins), VMEM, [], 1...  0.85 us
    ppermute x2, waiting for transfers between devices, to_core(): lax.ppermute(value, 'wave', [(index, (index + 1) % copies) for index in r...  0.57 us
  transfers between devices with their start and end apart: 9, of which 3 were waited for; matrix products, arithmetic and copies ran while one was open for 0% of the time, Pallas kernels for 21%

profile of v23, /device:TPU:0, one launch (start us, length us, event | category | flops | bytes accessed | tf_op | source)
XLA Modules:
  0.0 24.4 jit_solution(15321549610284486578)
XLA Ops:
  0.6 3.7 %forward.1 = (bf16[32,1024]{1,0:T(8,128)(2,1)S(1)}, f32[2,24,256]{2,1,0:T(8,128)S(1)}, f32[32,2048]{1,0:T(8,128)S(1)}, f32[2,2,256,256]{3,2,1,0:T(8,128)S(1)}, f32[2,2,8,256]{3,2,1,0:T(8,128)S(1)}) custom-call(s32[2]{0:T(128)} %wave_hbm.1, s32[2]{0:T(128)} %angle_hbm.1, s32[2,2]{1,0:T(2,128)} %aim_hbm.1, f32[16,256]{1,0:T(8,128)} %bitcast.1, ...), custom_call_target="tpu_custom_call" | custom-call | flops 1000000000 | bytes 10000000 | tf_op jit(solution)/shard_map/forward/pallas_call | solution.py:511
  4.3 5.1 %collective-permute-start = (bf16[32,1024]{1,0:T(8,128)(2,1)S(1)}, bf16[32,1024]{1,0:T(8,128)(2,1)S(1)}, u32[]{:S(2)}, u32[]{:S(2)}) collective-permute-start(bf16[32,1024]{1,0:T(8,128)(2,1)S(1)} %get-tuple-element.25.refs_0_), channel_id=1, source_target_pairs={{0,12},{2,14},{4,8},{6,10},{8,4},{10,6},{12,0},{14,2},{1,13},{3,15... | collective-permute-start | bytes 196616 | tf_op jit(solution)/shard_map/ppermute | solution.py:502
  9.4 0.0 collective-permute-start.4
  9.4 1.5 %collective-permute-start.2 = (bf16[32,1024]{1,0:T(8,128)(2,1)S(1)}, bf16[32,1024]{1,0:T(8,128)(2,1)S(1)}, u32[]{:S(2)}, u32[]{:S(2)}) collective-permute-start(bf16[32,1024]{1,0:T(8,128)(2,1)S(1)} %get-tuple-element.25.refs_0_), channel_id=1, source_target_pairs={{0,2},{2,0},{4,6},{6,4},{8,10},{10,8},{12,14},{14,12},{1,3},{3,1},... | collective-permute-start | bytes 196616 | tf_op jit(solution)/shard_map/ppermute | solution.py:502
  10.9 0.6 %collective-permute-start.3 = (bf16[32,1024]{1,0:T(8,128)(2,1)S(1)}, bf16[32,1024]{1,0:T(8,128)(2,1)S(1)}, u32[]{:S(2)}, u32[]{:S(2)}) collective-permute-start(bf16[32,1024]{1,0:T(8,128)(2,1)S(1)} %get-tuple-element.25.refs_0_), channel_id=1, source_target_pairs={{0,6},{2,4},{4,2},{6,0},{8,14},{10,12},{12,10},{14,8},{1,7},{3,5},... | collective-permute-start | bytes 196616 | tf_op jit(solution)/shard_map/ppermute | solution.py:502
  11.5 1.4 %collective-permute-start.5 = (bf16[32,1024]{1,0:T(8,128)(2,1)S(1)}, bf16[32,1024]{1,0:T(8,128)(2,1)S(1)}, u32[]{:S(2)}, u32[]{:S(2)}) collective-permute-start(bf16[32,1024]{1,0:T(8,128)(2,1)S(1)} %get-tuple-element.25.refs_0_), channel_id=1, source_target_pairs={{0,4},{2,6},{4,0},{6,2},{8,12},{10,14},{12,8},{14,10},{1,5},{3,7},... | collective-permute-start | bytes 196616 | tf_op jit(solution)/shard_map/ppermute | solution.py:502
  12.9 0.0 collective-permute-done.refs_2_
  12.9 0.0 collective-permute-start.1
  12.9 1.0 %row_tables.1 = (bf16[2,512,256]{2,1,0:T(8,128)(2,1)S(1)}, bf16[2,32,512]{2,1,0:T(8,128)(2,1)S(1)}, f32[2,256,256]{2,1,0:T(8,128)S(1)}, f32[2,8,128]{2,1,0:T(8,128)S(1)}) custom-call(f32[2,24,256]{2,1,0:T(8,128)S(1)} %get-tuple-element.23.info_ref), custom_call_target="tpu_custom_call" | custom-call | flops 100000000 | bytes 1000000 | tf_op jit(solution)/shard_map/row_tables/pallas_call | solution.py:535
  14.0 0.2 collective-permute-done.1.far_info_ref
  14.2 1.5 %collective-permute-start.6 = (bf16[32,1024]{1,0:T(8,128)(2,1)S(1)}, bf16[32,1024]{1,0:T(8,128)(2,1)S(1)}, u32[]{:S(2)}, u32[]{:S(2)}) collective-permute-start(bf16[32,1024]{1,0:T(8,128)(2,1)S(1)} %collective-permute-done.refs_2_), channel_id=1, source_target_pairs={{0,2},{2,0},{4,6},{6,4},{8,10},{10,8},{12,14},{14,12},{1,3},{3,1},... | collective-permute-start | bytes 196616 | tf_op jit(solution)/shard_map/ppermute | solution.py:502
  15.6 0.0 collective-permute-done.4.refs_2_.refs_3_
  15.6 1.0 %collective-permute-start.7 = (bf16[32,1024]{1,0:T(8,128)(2,1)S(1)}, bf16[32,1024]{1,0:T(8,128)(2,1)S(1)}, u32[]{:S(2)}, u32[]{:S(2)}) collective-permute-start(bf16[32,1024]{1,0:T(8,128)(2,1)S(1)} %collective-permute-done.4.refs_2_.refs_3_), channel_id=1, source_target_pairs={{0,2},{2,0},{4,6},{6,4},{8,10},{10,8},{12,14},{14,12},{1,3},{3,1},... | collective-permute-start | bytes 196616 | tf_op jit(solution)/shard_map/ppermute | solution.py:502
  16.6 0.0 collective-permute-done.2.refs_0_.refs_1_
  16.6 0.5 %collective-permute-done.3.refs_1_.refs_5_ = bf16[32,1024]{1,0:T(8,128)(2,1)S(1)} collective-permute-done((bf16[32,1024]{1,0:T(8,128)(2,1)S(1)}, bf16[32,1024]{1,0:T(8,128)(2,1)S(1)}, u32[]{:S(2)}, u32[]{:S(2)}) %collective-permute-start.3) | collective-permute-done | bytes 65568 | tf_op jit(solution)/shard_map/ppermute | solution.py:502
  17.2 0.0 collective-permute-done.5.refs_3_.refs_4_
  17.2 3.3 %column_tables.1 = (bf16[512,2048]{1,0:T(8,128)(2,1)S(1)}, bf16[512,2048]{1,0:T(8,128)(2,1)S(1)}, bf16[512,2048]{1,0:T(8,128)(2,1)S(1)}, bf16[512,2048]{1,0:T(8,...) custom-call(f32[2,24,256]{2,1,0:T(8,128)S(1)} %get-tuple-element.23., ...), custom_call_target="tpu_custom_call" | custom-call | flops 3000000000 | bytes 30000000 | tf_op jit(solution)/shard_map/column_tables/pallas_call | solution.py:556
  20.5 0.0 collective-permute-done.6.refs_6_
  20.5 0.0 collective-permute-done.7.refs_7_
  20.5 1.1 %focus.1 = (bf16[32,1024]{1,0:T(8,128)(2,1)S(1)}, f32[2,8,128]{2,1,0:T(8,128)S(1)}) custom-call(bf16[2,512,256]{2,1,0:T(8,128)(2,1)S(1)} %get-tuple-element.24.tall_ref, bf16[2,32,512]{2,1,0:T(8,128)(2,1)S(1)} %get-tuple-element.27.flat_ref, f32[2,256,256]{2,1,0:T(8,128)S(1)} %get-tuple-element.28.spot_ref, f32[2,8,128]{2,1,0:T(8,128)S(1)} %get-tuple-element.29.gain_ref, ...), custom_call_target="tpu_custom_call" | custom-call | flops 100000000 | bytes 1000000 | tf_op jit(solution)/shard_map/focus/pallas_call | solution.py:568
  21.5 0.1 collective-permute-start.8
  21.6 0.8 %gradient_own.1.refs_5_ = f32[32,2048]{1,0:T(8,128)S(1)} custom-call(bf16[32,1024]{1,0:T(8,128)(2,1)S(1)} %get-tuple-element.35.refs_0_, bf16[512,2048]{1,0:T(8,128)(2,1)S(1)} %get-tuple-element.40.refs_1_, bf16[512,2048]{1,0:T(8,128)(2,1)S(1)} %get-tuple-element.41.refs_2_, f32[2,32,2048]{2,1,0:T(8,128)S(1)} %get-tuple-element.33.after_ref.refs_3_, ...), custom_call_target="tpu_custom_call" | custom-call | flops 1000000000 | bytes 10000000 | tf_op jit(solution)/shard_map/gradient_own/pallas_call | solution.py:583
  22.4 0.4 %collective-permute-done.8.refs_0_ = bf16[32,1024]{1,0:T(8,128)(2,1)S(1)} collective-permute-done((bf16[32,1024]{1,0:T(8,128)(2,1)S(1)}, bf16[32,1024]{1,0:T(8,128)(2,1)S(1)}, u32[]{:S(2)}, u32[]{:S(2)}) %collective-permute-start.8) | collective-permute-done | bytes 65568 | tf_op jit(solution)/shard_map/ppermute | solution.py:505
  22.8 1.6 %gradient_far.1 = (f32[32,2048]{1,0:T(8,128)}, f32[2]{0:T(128)}) custom-call(bf16[32,1024]{1,0:T(8,128)(2,1)S(1)} %collective-permute-done.8.refs_0_, bf16[512,2048]{1,0:T(8,128)(2,1)S(1)} %get-tuple-element.36.refs_1_, bf16[512,2048]{1,0:T(8,128)(2,1)S(1)} %get-tuple-element.37.refs_2_, f32[2,32,2048]{2,1,0:T(8,128)S(1)} %get-tuple-element.38.refs_3_, ...), custom_call_target="tpu_custom_call" | custom-call | flops 1000000000 | bytes 10000000 | tf_op jit(solution)/shard_map/gradient_far/pallas_call | solution.py:587
Async XLA Ops:
  4.3 8.6 %collective-permute-start = (bf16[32,1024]{1,0:T(8,128)(2,1)S(1)}, bf16[32,1024]{1,0:T(8,128)(2,1)S(1)}, u32[]{:S(2)}, u32[]{:S(2)}) collective-permute-start(bf16[32,1024]{1,0:T(8,128)(2,1)S(1)} %get-tuple-element.25.refs_0_), channel_id=1, source_target_pairs={{0,12},{2,14},{4,8},{6,10},{8,4},{10,6},{12,0},{14,2},{1,13},{3,15... | collective-permute-start | bytes 196616 | tf_op jit(solution)/shard_map/ppermute | solution.py:502
  9.4 6.2 %collective-permute-start.4 = (bf16[32,1024]{1,0:T(8,128)(2,1)S(1)}, bf16[32,1024]{1,0:T(8,128)(2,1)S(1)}, u32[]{:S(2)}, u32[]{:S(2)}) collective-permute-start(bf16[32,1024]{1,0:T(8,128)(2,1)S(1)} %get-tuple-element.25.refs_0_), channel_id=1, source_target_pairs={{0,8},{2,10},{4,12},{6,14},{8,0},{10,2},{12,4},{14,6},{1,9},{3,11}... | collective-permute-start | bytes 196616 | tf_op jit(solution)/shard_map/ppermute | solution.py:502
  9.4 7.2 %collective-permute-start.2 = (bf16[32,1024]{1,0:T(8,128)(2,1)S(1)}, bf16[32,1024]{1,0:T(8,128)(2,1)S(1)}, u32[]{:S(2)}, u32[]{:S(2)}) collective-permute-start(bf16[32,1024]{1,0:T(8,128)(2,1)S(1)} %get-tuple-element.25.refs_0_), channel_id=1, source_target_pairs={{0,2},{2,0},{4,6},{6,4},{8,10},{10,8},{12,14},{14,12},{1,3},{3,1},... | collective-permute-start | bytes 196616 | tf_op jit(solution)/shard_map/ppermute | solution.py:502
  10.9 6.3 %collective-permute-start.3 = (bf16[32,1024]{1,0:T(8,128)(2,1)S(1)}, bf16[32,1024]{1,0:T(8,128)(2,1)S(1)}, u32[]{:S(2)}, u32[]{:S(2)}) collective-permute-start(bf16[32,1024]{1,0:T(8,128)(2,1)S(1)} %get-tuple-element.25.refs_0_), channel_id=1, source_target_pairs={{0,6},{2,4},{4,2},{6,0},{8,14},{10,12},{12,10},{14,8},{1,7},{3,5},... | collective-permute-start | bytes 196616 | tf_op jit(solution)/shard_map/ppermute | solution.py:502
  11.5 5.6 %collective-permute-start.5 = (bf16[32,1024]{1,0:T(8,128)(2,1)S(1)}, bf16[32,1024]{1,0:T(8,128)(2,1)S(1)}, u32[]{:S(2)}, u32[]{:S(2)}) collective-permute-start(bf16[32,1024]{1,0:T(8,128)(2,1)S(1)} %get-tuple-element.25.refs_0_), channel_id=1, source_target_pairs={{0,4},{2,6},{4,0},{6,2},{8,12},{10,14},{12,8},{14,10},{1,5},{3,7},... | collective-permute-start | bytes 196616 | tf_op jit(solution)/shard_map/ppermute | solution.py:502
  12.9 1.2 %collective-permute-start.1 = (f32[2,24,256]{2,1,0:T(8,128)S(1)}, f32[2,24,256]{2,1,0:T(8,128)S(1)}, u32[]{:S(2)}, u32[]{:S(2)}) collective-permute-start(f32[2,24,256]{2,1,0:T(8,128)S(1)} %get-tuple-element.23.info_ref), channel_id=1, source_target_pairs={{0,1},{1,0},{2,3},{3,2},{4,5},{5,4},{6,7},{7,6},{8,9},{9,8},{10,11... | collective-permute-start | bytes 147464 | tf_op jit(solution)/shard_map/ppermute | solution.py:505
  14.2 6.3 %collective-permute-start.6 = (bf16[32,1024]{1,0:T(8,128)(2,1)S(1)}, bf16[32,1024]{1,0:T(8,128)(2,1)S(1)}, u32[]{:S(2)}, u32[]{:S(2)}) collective-permute-start(bf16[32,1024]{1,0:T(8,128)(2,1)S(1)} %collective-permute-done.refs_2_), channel_id=1, source_target_pairs={{0,2},{2,0},{4,6},{6,4},{8,10},{10,8},{12,14},{14,12},{1,3},{3,1},... | collective-permute-start | bytes 196616 | tf_op jit(solution)/shard_map/ppermute | solution.py:502
  15.6 4.8 %collective-permute-start.7 = (bf16[32,1024]{1,0:T(8,128)(2,1)S(1)}, bf16[32,1024]{1,0:T(8,128)(2,1)S(1)}, u32[]{:S(2)}, u32[]{:S(2)}) collective-permute-start(bf16[32,1024]{1,0:T(8,128)(2,1)S(1)} %collective-permute-done.4.refs_2_.refs_3_), channel_id=1, source_target_pairs={{0,2},{2,0},{4,6},{6,4},{8,10},{10,8},{12,14},{14,12},{1,3},{3,1},... | collective-permute-start | bytes 196616 | tf_op jit(solution)/shard_map/ppermute | solution.py:502
  21.5 1.3 %collective-permute-start.8 = (bf16[32,1024]{1,0:T(8,128)(2,1)S(1)}, bf16[32,1024]{1,0:T(8,128)(2,1)S(1)}, u32[]{:S(2)}, u32[]{:S(2)}) collective-permute-start(bf16[32,1024]{1,0:T(8,128)(2,1)S(1)} %get-tuple-element.35.refs_0_), channel_id=1, source_target_pairs={{0,1},{1,0},{2,3},{3,2},{4,5},{5,4},{6,7},{7,6},{8,9},{9,8},{10,11... | collective-permute-start | bytes 196616 | tf_op jit(solution)/shard_map/ppermute | solution.py:505

commit v24 on v23

--- a/solution.py
+++ b/solution.py
@@ -547,7 +547,7 @@
         last, flat = lax.optimization_barrier((last, flat))
         sections = [mine, near, last, middle, beside, corner, exchange(last, 1), exchange(middle, 1)]
         steps = [0, 1, 6, 4, 2, 3, 7, 5]
-        after = [near, corner, middle, beside]
+        after = [near, middle]
     else:
         blocks = jnp.tile(mine[None], (peers, 1, 1))
         blocks = lax.all_to_all(blocks, "aperture", 0, 0, tiled=True)

time: 24.6 us -> 24.9 us (1.012)
  starting transfers between devices: 11.1 us -> 12 us
  waiting for transfers between devices: 1.13 us -> 0.52 us
    ppermute x7, starting transfers between devices: 11.1 us -> 12 us  [exchange(): lax.ppermute(value, 'aperture', [(index, index ^ step) for index in range...]
    ppermute x7, waiting for transfers between devices: 0.56 us -> 0.14 us  [exchange(): lax.ppermute(value, 'aperture', [(index, index ^ step) for index in range...]
  transfers between devices with their start and end apart: 9 -> 9, of which waited for: 3 -> 2; matrix products, arithmetic and copies ran while one was open for 0% -> 0% of each run, Pallas kernels for 21% -> 21%
where the time goes in v24:
time: 24.9 us; the launch traced here: 24.8 us
  starting transfers between devices  12 us (48%)
  Pallas kernels  11.5 us (46%)
  between operations  0.7 us (3%)
  waiting for transfers between devices  0.52 us (2%)
    ppermute x7, starting transfers between devices, exchange(): lax.ppermute(value, 'aperture', [(index, index ^ step) for index in range...  12 us
    pallas_call x1, Pallas kernels, on_device(): call(forward_kernel, 'forward', (shape((rows_dev, lanes), bf16), shape((p...  3.67 us
    pallas_call x1, Pallas kernels, on_device(): call(functools.partial(table_kernel, math.sqrt(rows * cols), cols), 'colu...  3.27 us
    pallas_call x1, Pallas kernels, on_device(): call(last_grad_kernel, 'gradient_far', (out, shape((pairs_dev,), f32)), [...  1.6 us
    pallas_call x1, Pallas kernels, on_device(): call(functools.partial(focus_kernel, steps), 'focus', (shape((rows_dev, l...  1.05 us
    pallas_call x1, Pallas kernels, on_device(): call(row_kernel, 'row_tables', (shape((pairs_dev, 2 * FOCAL, rows), bf16)...  1.04 us
    pallas_call x1, Pallas kernels, on_device(): call(own_grad_kernel, 'gradient_own', out, [VMEM] * len(ins), VMEM, [], 1...  0.85 us
  transfers between devices with their start and end apart: 9, of which 2 were waited for; matrix products, arithmetic and copies ran while one was open for 0% of the time, Pallas kernels for 21%

profile of v24, /device:TPU:0, one launch (start us, length us, event | category | flops | bytes accessed | tf_op | source)
XLA Modules:
  0.0 24.8 jit_solution(8899579246450000496)
XLA Ops:
  0.6 3.7 %forward.1 = (bf16[32,1024]{1,0:T(8,128)(2,1)S(1)}, f32[2,24,256]{2,1,0:T(8,128)S(1)}, f32[32,2048]{1,0:T(8,128)S(1)}, f32[2,2,256,256]{3,2,1,0:T(8,128)S(1)}, f32[2,2,8,256]{3,2,1,0:T(8,128)S(1)}) custom-call(s32[2]{0:T(128)} %wave_hbm.1, s32[2]{0:T(128)} %angle_hbm.1, s32[2,2]{1,0:T(2,128)} %aim_hbm.1, f32[16,256]{1,0:T(8,128)} %bitcast.1, ...), custom_call_target="tpu_custom_call" | custom-call | flops 1000000000 | bytes 10000000 | tf_op jit(solution)/shard_map/forward/pallas_call | solution.py:511
  4.3 5.1 %collective-permute-start = (bf16[32,1024]{1,0:T(8,128)(2,1)S(1)}, bf16[32,1024]{1,0:T(8,128)(2,1)S(1)}, u32[]{:S(2)}, u32[]{:S(2)}) collective-permute-start(bf16[32,1024]{1,0:T(8,128)(2,1)S(1)} %get-tuple-element.25.refs_0_), channel_id=1, source_target_pairs={{0,12},{2,14},{4,8},{6,10},{8,4},{10,6},{12,0},{14,2},{1,13},{3,15... | collective-permute-start | bytes 196616 | tf_op jit(solution)/shard_map/ppermute | solution.py:502
  9.4 0.0 collective-permute-start.3
  9.4 1.5 %collective-permute-start.2 = (bf16[32,1024]{1,0:T(8,128)(2,1)S(1)}, bf16[32,1024]{1,0:T(8,128)(2,1)S(1)}, u32[]{:S(2)}, u32[]{:S(2)}) collective-permute-start(bf16[32,1024]{1,0:T(8,128)(2,1)S(1)} %get-tuple-element.25.refs_0_), channel_id=1, source_target_pairs={{0,2},{2,0},{4,6},{6,4},{8,10},{10,8},{12,14},{14,12},{1,3},{3,1},... | collective-permute-start | bytes 196616 | tf_op jit(solution)/shard_map/ppermute | solution.py:502
  10.9 0.0 collective-permute-start.1
  10.9 0.8 %collective-permute-start.4 = (bf16[32,1024]{1,0:T(8,128)(2,1)S(1)}, bf16[32,1024]{1,0:T(8,128)(2,1)S(1)}, u32[]{:S(2)}, u32[]{:S(2)}) collective-permute-start(bf16[32,1024]{1,0:T(8,128)(2,1)S(1)} %get-tuple-element.25.refs_0_), channel_id=1, source_target_pairs={{0,4},{2,6},{4,0},{6,2},{8,12},{10,14},{12,8},{14,10},{1,5},{3,7},... | collective-permute-start | bytes 196616 | tf_op jit(solution)/shard_map/ppermute | solution.py:502
  11.7 1.0 %row_tables.1 = (bf16[2,512,256]{2,1,0:T(8,128)(2,1)S(1)}, bf16[2,32,512]{2,1,0:T(8,128)(2,1)S(1)}, f32[2,256,256]{2,1,0:T(8,128)S(1)}, f32[2,8,128]{2,1,0:T(8,128)S(1)}) custom-call(f32[2,24,256]{2,1,0:T(8,128)S(1)} %get-tuple-element.23.info_ref), custom_call_target="tpu_custom_call" | custom-call | flops 100000000 | bytes 1000000 | tf_op jit(solution)/shard_map/row_tables/pallas_call | solution.py:535
  12.7 0.0 collective-permute-done.refs_2_
  12.8 2.6 %collective-permute-start.5 = (bf16[32,1024]{1,0:T(8,128)(2,1)S(1)}, bf16[32,1024]{1,0:T(8,128)(2,1)S(1)}, u32[]{:S(2)}, u32[]{:S(2)}) collective-permute-start(bf16[32,1024]{1,0:T(8,128)(2,1)S(1)} %get-tuple-element.25.refs_0_), channel_id=1, source_target_pairs={{0,6},{2,4},{4,2},{6,0},{8,14},{10,12},{12,10},{14,8},{1,7},{3,5},... | collective-permute-start | bytes 196616 | tf_op jit(solution)/shard_map/ppermute | solution.py:502
  15.3 0.0 collective-permute-done.1.far_info_ref
  15.3 0.8 %collective-permute-start.6 = (bf16[32,1024]{1,0:T(8,128)(2,1)S(1)}, bf16[32,1024]{1,0:T(8,128)(2,1)S(1)}, u32[]{:S(2)}, u32[]{:S(2)}) collective-permute-start(bf16[32,1024]{1,0:T(8,128)(2,1)S(1)} %collective-permute-done.refs_2_), channel_id=1, source_target_pairs={{0,2},{2,0},{4,6},{6,4},{8,10},{10,8},{12,14},{14,12},{1,3},{3,1},... | collective-permute-start | bytes 196616 | tf_op jit(solution)/shard_map/ppermute | solution.py:502
  16.1 0.0 collective-permute-done.3.refs_1_.refs_3_
  16.1 1.3 %collective-permute-start.7 = (bf16[32,1024]{1,0:T(8,128)(2,1)S(1)}, bf16[32,1024]{1,0:T(8,128)(2,1)S(1)}, u32[]{:S(2)}, u32[]{:S(2)}) collective-permute-start(bf16[32,1024]{1,0:T(8,128)(2,1)S(1)} %collective-permute-done.3.refs_1_.refs_3_), channel_id=1, source_target_pairs={{0,2},{2,0},{4,6},{6,4},{8,10},{10,8},{12,14},{14,12},{1,3},{3,1},... | collective-permute-start | bytes 196616 | tf_op jit(solution)/shard_map/ppermute | solution.py:502
  17.4 0.0 collective-permute-done.2.refs_0_.refs_1_
  17.4 3.3 %column_tables.1 = (bf16[512,2048]{1,0:T(8,128)(2,1)S(1)}, bf16[512,2048]{1,0:T(8,128)(2,1)S(1)}, bf16[512,2048]{1,0:T(8,128)(2,1)S(1)}, bf16[512,2048]{1,0:T(8,...) custom-call(f32[2,24,256]{2,1,0:T(8,128)S(1)} %get-tuple-element.23., ...), custom_call_target="tpu_custom_call" | custom-call | flops 3000000000 | bytes 30000000 | tf_op jit(solution)/shard_map/column_tables/pallas_call | solution.py:556
  20.6 0.0 collective-permute-done.4.refs_4_
  20.7 0.0 collective-permute-done.5.refs_5_
  20.7 0.0 collective-permute-done.6.refs_6_
  20.7 0.1 collective-permute-done.7.refs_7_
  20.8 1.0 %focus.1 = (bf16[32,1024]{1,0:T(8,128)(2,1)S(1)}, f32[2,8,128]{2,1,0:T(8,128)S(1)}) custom-call(bf16[2,512,256]{2,1,0:T(8,128)(2,1)S(1)} %get-tuple-element.24.tall_ref, bf16[2,32,512]{2,1,0:T(8,128)(2,1)S(1)} %get-tuple-element.27.flat_ref, f32[2,256,256]{2,1,0:T(8,128)S(1)} %get-tuple-element.28.spot_ref, f32[2,8,128]{2,1,0:T(8,128)S(1)} %get-tuple-element.29.gain_ref, ...), custom_call_target="tpu_custom_call" | custom-call | flops 100000000 | bytes 1000000 | tf_op jit(solution)/shard_map/focus/pallas_call | solution.py:568
  21.8 0.1 collective-permute-start.8
  21.9 0.9 %gradient_own.1.refs_5_ = f32[32,2048]{1,0:T(8,128)S(1)} custom-call(bf16[32,1024]{1,0:T(8,128)(2,1)S(1)} %get-tuple-element.35.refs_0_, bf16[512,2048]{1,0:T(8,128)(2,1)S(1)} %get-tuple-element.40.refs_1_, bf16[512,2048]{1,0:T(8,128)(2,1)S(1)} %get-tuple-element.41.refs_2_, f32[2,32,2048]{2,1,0:T(8,128)S(1)} %get-tuple-element.33.after_ref.refs_3_, ...), custom_call_target="tpu_custom_call" | custom-call | flops 1000000000 | bytes 10000000 | tf_op jit(solution)/shard_map/gradient_own/pallas_call | solution.py:583
  22.8 0.4 %collective-permute-done.8.refs_0_ = bf16[32,1024]{1,0:T(8,128)(2,1)S(1)} collective-permute-done((bf16[32,1024]{1,0:T(8,128)(2,1)S(1)}, bf16[32,1024]{1,0:T(8,128)(2,1)S(1)}, u32[]{:S(2)}, u32[]{:S(2)}) %collective-permute-start.8) | collective-permute-done | bytes 65568 | tf_op jit(solution)/shard_map/ppermute | solution.py:505
  23.2 1.6 %gradient_far.1 = (f32[32,2048]{1,0:T(8,128)}, f32[2]{0:T(128)}) custom-call(bf16[32,1024]{1,0:T(8,128)(2,1)S(1)} %collective-permute-done.8.refs_0_, bf16[512,2048]{1,0:T(8,128)(2,1)S(1)} %get-tuple-element.36.refs_1_, bf16[512,2048]{1,0:T(8,128)(2,1)S(1)} %get-tuple-element.37.refs_2_, f32[2,32,2048]{2,1,0:T(8,128)S(1)} %get-tuple-element.38.refs_3_, ...), custom_call_target="tpu_custom_call" | custom-call | flops 1000000000 | bytes 10000000 | tf_op jit(solution)/shard_map/gradient_far/pallas_call | solution.py:587
Async XLA Ops:
  4.3 8.4 %collective-permute-start = (bf16[32,1024]{1,0:T(8,128)(2,1)S(1)}, bf16[32,1024]{1,0:T(8,128)(2,1)S(1)}, u32[]{:S(2)}, u32[]{:S(2)}) collective-permute-start(bf16[32,1024]{1,0:T(8,128)(2,1)S(1)} %get-tuple-element.25.refs_0_), channel_id=1, source_target_pairs={{0,12},{2,14},{4,8},{6,10},{8,4},{10,6},{12,0},{14,2},{1,13},{3,15... | collective-permute-start | bytes 196616 | tf_op jit(solution)/shard_map/ppermute | solution.py:502
  9.4 6.7 %collective-permute-start.3 = (bf16[32,1024]{1,0:T(8,128)(2,1)S(1)}, bf16[32,1024]{1,0:T(8,128)(2,1)S(1)}, u32[]{:S(2)}, u32[]{:S(2)}) collective-permute-start(bf16[32,1024]{1,0:T(8,128)(2,1)S(1)} %get-tuple-element.25.refs_0_), channel_id=1, source_target_pairs={{0,8},{2,10},{4,12},{6,14},{8,0},{10,2},{12,4},{14,6},{1,9},{3,11}... | collective-permute-start | bytes 196616 | tf_op jit(solution)/shard_map/ppermute | solution.py:502
  9.4 7.9 %collective-permute-start.2 = (bf16[32,1024]{1,0:T(8,128)(2,1)S(1)}, bf16[32,1024]{1,0:T(8,128)(2,1)S(1)}, u32[]{:S(2)}, u32[]{:S(2)}) collective-permute-start(bf16[32,1024]{1,0:T(8,128)(2,1)S(1)} %get-tuple-element.25.refs_0_), channel_id=1, source_target_pairs={{0,2},{2,0},{4,6},{6,4},{8,10},{10,8},{12,14},{14,12},{1,3},{3,1},... | collective-permute-start | bytes 196616 | tf_op jit(solution)/shard_map/ppermute | solution.py:502
  10.9 4.4 %collective-permute-start.1 = (f32[2,24,256]{2,1,0:T(8,128)S(1)}, f32[2,24,256]{2,1,0:T(8,128)S(1)}, u32[]{:S(2)}, u32[]{:S(2)}) collective-permute-start(f32[2,24,256]{2,1,0:T(8,128)S(1)} %get-tuple-element.23.info_ref), channel_id=1, source_target_pairs={{0,1},{1,0},{2,3},{3,2},{4,5},{5,4},{6,7},{7,6},{8,9},{9,8},{10,11... | collective-permute-start | bytes 147464 | tf_op jit(solution)/shard_map/ppermute | solution.py:505
  10.9 9.7 %collective-permute-start.4 = (bf16[32,1024]{1,0:T(8,128)(2,1)S(1)}, bf16[32,1024]{1,0:T(8,128)(2,1)S(1)}, u32[]{:S(2)}, u32[]{:S(2)}) collective-permute-start(bf16[32,1024]{1,0:T(8,128)(2,1)S(1)} %get-tuple-element.25.refs_0_), channel_id=1, source_target_pairs={{0,4},{2,6},{4,0},{6,2},{8,12},{10,14},{12,8},{14,10},{1,5},{3,7},... | collective-permute-start | bytes 196616 | tf_op jit(solution)/shard_map/ppermute | solution.py:502
  12.8 7.9 %collective-permute-start.5 = (bf16[32,1024]{1,0:T(8,128)(2,1)S(1)}, bf16[32,1024]{1,0:T(8,128)(2,1)S(1)}, u32[]{:S(2)}, u32[]{:S(2)}) collective-permute-start(bf16[32,1024]{1,0:T(8,128)(2,1)S(1)} %get-tuple-element.25.refs_0_), channel_id=1, source_target_pairs={{0,6},{2,4},{4,2},{6,0},{8,14},{10,12},{12,10},{14,8},{1,7},{3,5},... | collective-permute-start | bytes 196616 | tf_op jit(solution)/shard_map/ppermute | solution.py:502
  15.3 5.3 %collective-permute-start.6 = (bf16[32,1024]{1,0:T(8,128)(2,1)S(1)}, bf16[32,1024]{1,0:T(8,128)(2,1)S(1)}, u32[]{:S(2)}, u32[]{:S(2)}) collective-permute-start(bf16[32,1024]{1,0:T(8,128)(2,1)S(1)} %collective-permute-done.refs_2_), channel_id=1, source_target_pairs={{0,2},{2,0},{4,6},{6,4},{8,10},{10,8},{12,14},{14,12},{1,3},{3,1},... | collective-permute-start | bytes 196616 | tf_op jit(solution)/shard_map/ppermute | solution.py:502
  16.1 4.7 %collective-permute-start.7 = (bf16[32,1024]{1,0:T(8,128)(2,1)S(1)}, bf16[32,1024]{1,0:T(8,128)(2,1)S(1)}, u32[]{:S(2)}, u32[]{:S(2)}) collective-permute-start(bf16[32,1024]{1,0:T(8,128)(2,1)S(1)} %collective-permute-done.3.refs_1_.refs_3_), channel_id=1, source_target_pairs={{0,2},{2,0},{4,6},{6,4},{8,10},{10,8},{12,14},{14,12},{1,3},{3,1},... | collective-permute-start | bytes 196616 | tf_op jit(solution)/shard_map/ppermute | solution.py:502
  21.8 1.3 %collective-permute-start.8 = (bf16[32,1024]{1,0:T(8,128)(2,1)S(1)}, bf16[32,1024]{1,0:T(8,128)(2,1)S(1)}, u32[]{:S(2)}, u32[]{:S(2)}) collective-permute-start(bf16[32,1024]{1,0:T(8,128)(2,1)S(1)} %get-tuple-element.35.refs_0_), channel_id=1, source_target_pairs={{0,1},{1,0},{2,3},{3,2},{4,5},{5,4},{6,7},{7,6},{8,9},{9,8},{10,11... | collective-permute-start | bytes 196616 | tf_op jit(solution)/shard_map/ppermute | solution.py:505

commit v25 on v21

--- a/solution.py
+++ b/solution.py
@@ -421,7 +421,7 @@
     core = lax.axis_index("wave")
     for pair in range(score_ref.shape[0]):
         score_ref[pair] = jnp.sum(tile_ref[pair, :1, :1])
-    moves = [pltpu.make_async_copy(score_ref, score_hbm, sems.at[own_cols // (2 * BLOCK)])]
+    moves = [pltpu.make_async_copy(score_ref, score_hbm, sems.at[0])]
     moves[0].start()
 
     def send(start, total):
@@ -429,8 +429,7 @@
         place = pl.multiple_of(jnp.where(core == 1, start, own_cols - size - start), size)
         place = pl.ds(place, size)
         out_ref[:, place] = jnp.where(core == 1, total, turn_round(total))
-        index = start // size
-        moves.append(pltpu.make_async_copy(out_ref.at[:, place], out_hbm.at[:, place], sems.at[index]))
+        moves.append(pltpu.make_async_copy(out_ref.at[:, place], out_hbm.at[:, place], sems.at[len(moves)]))
         moves[-1].start()
 
     add_grads(in_refs, total_ref, out_ref, 2 * BLOCK, send)
@@ -455,9 +454,12 @@
                 [jnp.concatenate([real, above], axis=1), jnp.concatenate([imag, below], axis=1)], axis=0
             )
         )
-    for start in range(0, own_cols, size):
-        place = slice(start, start + size)
-        total = jnp.zeros((rows_dev, size), jnp.float32) if total_ref is None else total_ref[:, place]
+    starts = list(range(0, own_cols, size))
+    if send is not None:
+        starts.append(own_cols - size // 2)
+    for start, stop in zip(starts, [*starts[1:], own_cols]):
+        place = slice(start, stop)
+        total = jnp.zeros((rows_dev, stop - start), jnp.float32) if total_ref is None else total_ref[:, place]
         for left, table_ref, slope_ref in zip(lefts, table_refs, slope_refs):
             grad = jnp.dot(left, table_ref[:, place], preferred_element_type=jnp.float32)
             total += grad[:rows_dev] * slope_ref[0, :, place]
@@ -596,7 +598,7 @@
         [
             pltpu.VMEM(out.shape, f32),
             pltpu.SMEM((pairs_dev,), f32),
-            pltpu.SemaphoreType.DMA((own_cols // (2 * BLOCK) + 1,)),
+            pltpu.SemaphoreType.DMA((own_cols // (2 * BLOCK) + 2,)),
         ],
         10**9, 10**7,
     )(*ins)

time: 24.4 us -> 24.4 us (level)
  no operation moved by 1% of the time
where the time goes in v25:
time: 24.4 us; the launch traced here: 24.2 us
  Pallas kernels  11.6 us (48%)
  starting transfers between devices  10.1 us (41%)
  waiting for transfers between devices  1.77 us (7%)
  between operations  0.69 us (3%)
    ppermute x6, starting transfers between devices, exchange(): lax.ppermute(value, 'aperture', [(index, index ^ step) for index in range...  10 us
    pallas_call x1, Pallas kernels, on_device(): call(forward_kernel, 'forward', (shape((rows_dev, lanes), bf16), shape((p...  3.72 us
    pallas_call x1, Pallas kernels, on_device(): call(functools.partial(table_kernel, math.sqrt(rows * cols), cols), 'colu...  3.33 us
    pallas_call x1, Pallas kernels, on_device(): call(last_grad_kernel, 'gradient_far', (out, shape((pairs_dev,), f32)), [...  1.62 us
    ppermute x6, waiting for transfers between devices, exchange(): lax.ppermute(value, 'aperture', [(index, index ^ step) for index in range...  1.4 us
    pallas_call x1, Pallas kernels, on_device(): call(functools.partial(focus_kernel, steps), 'focus', (shape((rows_dev, l...  1.06 us
    pallas_call x1, Pallas kernels, on_device(): call(row_kernel, 'row_tables', (shape((pairs_dev, 2 * FOCAL, rows), bf16)...  1.04 us
    pallas_call x1, Pallas kernels, on_device(): call(own_grad_kernel, 'gradient_own', out, [VMEM] * len(ins), VMEM, [], 1...  0.87 us
  transfers between devices with their start and end apart: 8, of which 3 were waited for; matrix products, arithmetic and copies ran while one was open for 0% of the time, Pallas kernels for 22%

profile of v25, /device:TPU:0, one launch (start us, length us, event | category | flops | bytes accessed | tf_op | source)
XLA Modules:
  0.0 24.2 jit_solution(7309634155819162996)
XLA Ops:
  0.6 3.7 %forward.1 = (bf16[32,1024]{1,0:T(8,128)(2,1)S(1)}, f32[2,24,256]{2,1,0:T(8,128)S(1)}, f32[32,2048]{1,0:T(8,128)S(1)}) custom-call(s32[2]{0:T(128)} %wave_hbm.1, s32[2]{0:T(128)} %angle_hbm.1, s32[2,2]{1,0:T(2,128)} %aim_hbm.1, f32[16,256]{1,0:T(8,128)} %bitcast.1, f32[32,4096]{1,0:T(8,128)} %width_hbm.1), custom_call_target="tpu_custom_call" | custom-call | flops 1000000000 | bytes 10000000 | tf_op jit(solution)/shard_map/forward/pallas_call | solution.py:517
  4.4 5.1 %collective-permute-start = (bf16[32,1024]{1,0:T(8,128)(2,1)S(1)}, bf16[32,1024]{1,0:T(8,128)(2,1)S(1)}, u32[]{:S(2)}, u32[]{:S(2)}) collective-permute-start(bf16[32,1024]{1,0:T(8,128)(2,1)S(1)} %get-tuple-element.23.refs_0_), channel_id=1, source_target_pairs={{0,12},{2,14},{4,8},{6,10},{8,4},{10,6},{12,0},{14,2},{1,13},{3,15... | collective-permute-start | bytes 196616 | tf_op jit(solution)/shard_map/ppermute | solution.py:508
  9.5 0.0 collective-permute-start.3
  9.5 0.6 %collective-permute-start.4 = (bf16[32,1024]{1,0:T(8,128)(2,1)S(1)}, bf16[32,1024]{1,0:T(8,128)(2,1)S(1)}, u32[]{:S(2)}, u32[]{:S(2)}) collective-permute-start(bf16[32,1024]{1,0:T(8,128)(2,1)S(1)} %get-tuple-element.23.refs_0_), channel_id=1, source_target_pairs={{0,4},{2,6},{4,0},{6,2},{8,12},{10,14},{12,8},{14,10},{1,5},{3,7},... | collective-permute-start | bytes 196616 | tf_op jit(solution)/shard_map/ppermute | solution.py:508
  10.1 1.6 %collective-permute-start.2 = (bf16[32,1024]{1,0:T(8,128)(2,1)S(1)}, bf16[32,1024]{1,0:T(8,128)(2,1)S(1)}, u32[]{:S(2)}, u32[]{:S(2)}) collective-permute-start(bf16[32,1024]{1,0:T(8,128)(2,1)S(1)} %get-tuple-element.23.refs_0_), channel_id=1, source_target_pairs={{0,2},{2,0},{4,6},{6,4},{8,10},{10,8},{12,14},{14,12},{1,3},{3,1},... | collective-permute-start | bytes 196616 | tf_op jit(solution)/shard_map/ppermute | solution.py:508
  11.8 0.0 collective-permute-start.1
  11.8 1.0 %row_tables.1 = (bf16[2,512,256]{2,1,0:T(8,128)(2,1)S(1)}, bf16[2,32,512]{2,1,0:T(8,128)(2,1)S(1)}, f32[2,256,256]{2,1,0:T(8,128)S(1)}, f32[2,8,128]{2,1,0:T(8,128)S(1)}) custom-call(f32[2,24,256]{2,1,0:T(8,128)S(1)} %get-tuple-element.21.info_ref), custom_call_target="tpu_custom_call" | custom-call | flops 100000000 | bytes 1000000 | tf_op jit(solution)/shard_map/row_tables/pallas_call | solution.py:541
  12.8 0.0 collective-permute-done.refs_2_
  12.8 1.1 %collective-permute-start.5 = (bf16[32,1024]{1,0:T(8,128)(2,1)S(1)}, bf16[32,1024]{1,0:T(8,128)(2,1)S(1)}, u32[]{:S(2)}, u32[]{:S(2)}) collective-permute-start(bf16[32,1024]{1,0:T(8,128)(2,1)S(1)} %collective-permute-done.refs_2_), channel_id=1, source_target_pairs={{0,2},{2,0},{4,6},{6,4},{8,10},{10,8},{12,14},{14,12},{1,3},{3,1},... | collective-permute-start | bytes 196616 | tf_op jit(solution)/shard_map/ppermute | solution.py:508
  13.9 1.2 %collective-permute-done.3.refs_0_ = bf16[32,1024]{1,0:T(8,128)(2,1)S(1)} collective-permute-done((bf16[32,1024]{1,0:T(8,128)(2,1)S(1)}, bf16[32,1024]{1,0:T(8,128)(2,1)S(1)}, u32[]{:S(2)}, u32[]{:S(2)}) %collective-permute-start.3) | collective-permute-done | bytes 65568 | tf_op jit(solution)/shard_map/ppermute | solution.py:508
  15.1 0.0 collective-permute-done.4.refs_1_
  15.1 1.6 %collective-permute-start.6 = (bf16[64,1024]{1,0:T(8,128)(2,1)S(1)}, bf16[64,1024]{1,0:T(8,128)(2,1)S(1)}, u32[]{:S(2)}, u32[]{:S(2)}) collective-permute-start(bf16[64,1024]{1,0:T(8,128)(2,1)S(1)} %join.1.refs_1_.refs_3_), channel_id=1, source_target_pairs={{0,2},{2,0},{4,6},{6,4},{8,10},{10,8},{12,14},{14,12},{1,3},{3,1},... | collective-permute-start | bytes 393224 | tf_op jit(solution)/shard_map/ppermute | solution.py:508
  16.7 0.0 collective-permute-done.1.far_info_ref
  16.7 0.0 collective-permute-done.2.refs_0_.refs_1_
  16.7 3.3 %column_tables.1 = (bf16[512,2048]{1,0:T(8,128)(2,1)S(1)}, bf16[512,2048]{1,0:T(8,128)(2,1)S(1)}, bf16[512,2048]{1,0:T(8,128)(2,1)S(1)}, bf16[512,2048]{1,0:T(8,...) custom-call(f32[2,24,256]{2,1,0:T(8,128)S(1)} %get-tuple-element.21., ...), custom_call_target="tpu_custom_call" | custom-call | flops 3000000000 | bytes 30000000 | tf_op jit(solution)/shard_map/column_tables/pallas_call | solution.py:564
  20.0 0.0 collective-permute-done.5.refs_4_
  20.0 0.2 collective-permute-done.6.refs_5_
  20.2 1.1 %focus.1 = (bf16[32,1024]{1,0:T(8,128)(2,1)S(1)}, f32[2,8,128]{2,1,0:T(8,128)S(1)}) custom-call(bf16[2,512,256]{2,1,0:T(8,128)(2,1)S(1)} %get-tuple-element.22.tall_ref, bf16[2,32,512]{2,1,0:T(8,128)(2,1)S(1)} %get-tuple-element.25.flat_ref, f32[2,256,256]{2,1,0:T(8,128)S(1)} %get-tuple-element.26.spot_ref, f32[2,8,128]{2,1,0:T(8,128)S(1)} %get-tuple-element.27.gain_ref, ...), custom_call_target="tpu_custom_call" | custom-call | flops 100000000 | bytes 1000000 | tf_op jit(solution)/shard_map/focus/pallas_call | solution.py:577
  21.3 0.1 collective-permute-start.7
  21.4 0.9 %gradient_own.1.refs_5_ = f32[32,2048]{1,0:T(8,128)S(1)} custom-call(bf16[32,1024]{1,0:T(8,128)(2,1)S(1)} %get-tuple-element.31.refs_0_, bf16[512,2048]{1,0:T(8,128)(2,1)S(1)} %get-tuple-element.36.refs_1_, bf16[512,2048]{1,0:T(8,128)(2,1)S(1)} %get-tuple-element.37.refs_2_, f32[2,32,2048]{2,1,0:T(8,128)S(1)} %get-tuple-element.29.after_ref.refs_3_, ...), custom_call_target="tpu_custom_call" | custom-call | flops 1000000000 | bytes 10000000 | tf_op jit(solution)/shard_map/gradient_own/pallas_call | solution.py:592
  22.2 0.4 %collective-permute-done.7.refs_0_ = bf16[32,1024]{1,0:T(8,128)(2,1)S(1)} collective-permute-done((bf16[32,1024]{1,0:T(8,128)(2,1)S(1)}, bf16[32,1024]{1,0:T(8,128)(2,1)S(1)}, u32[]{:S(2)}, u32[]{:S(2)}) %collective-permute-start.7) | collective-permute-done | bytes 65568 | tf_op jit(solution)/shard_map/ppermute | solution.py:511
  22.6 1.6 %gradient_far.1 = (f32[32,2048]{1,0:T(8,128)}, f32[2]{0:T(128)}) custom-call(bf16[32,1024]{1,0:T(8,128)(2,1)S(1)} %collective-permute-done.7.refs_0_, bf16[512,2048]{1,0:T(8,128)(2,1)S(1)} %get-tuple-element.32.refs_1_, bf16[512,2048]{1,0:T(8,128)(2,1)S(1)} %get-tuple-element.33.refs_2_, f32[2,32,2048]{2,1,0:T(8,128)S(1)} %get-tuple-element.34.refs_3_, ...), custom_call_target="tpu_custom_call" | custom-call | flops 1000000000 | bytes 10000000 | tf_op jit(solution)/shard_map/gradient_far/pallas_call | solution.py:596
  (1 shorter events, 0.0 us)
Async XLA Ops:
  4.4 8.4 %collective-permute-start = (bf16[32,1024]{1,0:T(8,128)(2,1)S(1)}, bf16[32,1024]{1,0:T(8,128)(2,1)S(1)}, u32[]{:S(2)}, u32[]{:S(2)}) collective-permute-start(bf16[32,1024]{1,0:T(8,128)(2,1)S(1)} %get-tuple-element.23.refs_0_), channel_id=1, source_target_pairs={{0,12},{2,14},{4,8},{6,10},{8,4},{10,6},{12,0},{14,2},{1,13},{3,15... | collective-permute-start | bytes 196616 | tf_op jit(solution)/shard_map/ppermute | solution.py:508
  9.5 5.6 %collective-permute-start.3 = (bf16[32,1024]{1,0:T(8,128)(2,1)S(1)}, bf16[32,1024]{1,0:T(8,128)(2,1)S(1)}, u32[]{:S(2)}, u32[]{:S(2)}) collective-permute-start(bf16[32,1024]{1,0:T(8,128)(2,1)S(1)} %get-tuple-element.23.refs_0_), channel_id=1, source_target_pairs={{0,8},{2,10},{4,12},{6,14},{8,0},{10,2},{12,4},{14,6},{1,9},{3,11}... | collective-permute-start | bytes 196616 | tf_op jit(solution)/shard_map/ppermute | solution.py:508
  9.5 5.6 %collective-permute-start.4 = (bf16[32,1024]{1,0:T(8,128)(2,1)S(1)}, bf16[32,1024]{1,0:T(8,128)(2,1)S(1)}, u32[]{:S(2)}, u32[]{:S(2)}) collective-permute-start(bf16[32,1024]{1,0:T(8,128)(2,1)S(1)} %get-tuple-element.23.refs_0_), channel_id=1, source_target_pairs={{0,4},{2,6},{4,0},{6,2},{8,12},{10,14},{12,8},{14,10},{1,5},{3,7},... | collective-permute-start | bytes 196616 | tf_op jit(solution)/shard_map/ppermute | solution.py:508
  10.1 6.5 %collective-permute-start.2 = (bf16[32,1024]{1,0:T(8,128)(2,1)S(1)}, bf16[32,1024]{1,0:T(8,128)(2,1)S(1)}, u32[]{:S(2)}, u32[]{:S(2)}) collective-permute-start(bf16[32,1024]{1,0:T(8,128)(2,1)S(1)} %get-tuple-element.23.refs_0_), channel_id=1, source_target_pairs={{0,2},{2,0},{4,6},{6,4},{8,10},{10,8},{12,14},{14,12},{1,3},{3,1},... | collective-permute-start | bytes 196616 | tf_op jit(solution)/shard_map/ppermute | solution.py:508
  11.8 4.9 %collective-permute-start.1 = (f32[2,24,256]{2,1,0:T(8,128)S(1)}, f32[2,24,256]{2,1,0:T(8,128)S(1)}, u32[]{:S(2)}, u32[]{:S(2)}) collective-permute-start(f32[2,24,256]{2,1,0:T(8,128)S(1)} %get-tuple-element.21.info_ref), channel_id=1, source_target_pairs={{0,1},{1,0},{2,3},{3,2},{4,5},{5,4},{6,7},{7,6},{8,9},{9,8},{10,11... | collective-permute-start | bytes 147464 | tf_op jit(solution)/shard_map/ppermute | solution.py:511
  12.8 7.2 %collective-permute-start.5 = (bf16[32,1024]{1,0:T(8,128)(2,1)S(1)}, bf16[32,1024]{1,0:T(8,128)(2,1)S(1)}, u32[]{:S(2)}, u32[]{:S(2)}) collective-permute-start(bf16[32,1024]{1,0:T(8,128)(2,1)S(1)} %collective-permute-done.refs_2_), channel_id=1, source_target_pairs={{0,2},{2,0},{4,6},{6,4},{8,10},{10,8},{12,14},{14,12},{1,3},{3,1},... | collective-permute-start | bytes 196616 | tf_op jit(solution)/shard_map/ppermute | solution.py:508
  15.1 5.1 %collective-permute-start.6 = (bf16[64,1024]{1,0:T(8,128)(2,1)S(1)}, bf16[64,1024]{1,0:T(8,128)(2,1)S(1)}, u32[]{:S(2)}, u32[]{:S(2)}) collective-permute-start(bf16[64,1024]{1,0:T(8,128)(2,1)S(1)} %join.1.refs_1_.refs_3_), channel_id=1, source_target_pairs={{0,2},{2,0},{4,6},{6,4},{8,10},{10,8},{12,14},{14,12},{1,3},{3,1},... | collective-permute-start | bytes 393224 | tf_op jit(solution)/shard_map/ppermute | solution.py:508
  21.3 1.3 %collective-permute-start.7 = (bf16[32,1024]{1,0:T(8,128)(2,1)S(1)}, bf16[32,1024]{1,0:T(8,128)(2,1)S(1)}, u32[]{:S(2)}, u32[]{:S(2)}) collective-permute-start(bf16[32,1024]{1,0:T(8,128)(2,1)S(1)} %get-tuple-element.31.refs_0_), channel_id=1, source_target_pairs={{0,1},{1,0},{2,3},{3,2},{4,5},{5,4},{6,7},{7,6},{8,9},{9,8},{10,11... | collective-permute-start | bytes 196616 | tf_op jit(solution)/shard_map/ppermute | solution.py:511
